TPU v7x, 32 devices: a whole 2x2x4 slice. The times are simulated.
32 devices in a mesh: segment: 2 (over core), rows: 4 (over z), dp: 4 (over y, x).
Axes of the slice: x: 2, y: 2, z: 4, core: 2. Of those that a mesh axis runs over, the one named last changes fastest.
Arguments:
- coarse: bfloat16 [8, 100, 48, 256], P(('segment', 'dp'), None, 'rows'), may hold values from -6 to 6
- target: bfloat16 [8, 64, 48, 256], P(('segment', 'dp'), None, 'rows'), may hold values from -6 to 6
- noise: bfloat16 [8, 4, 64, 64, 144], P(('segment', 'dp'), 'rows'), may hold values from -6 to 6
- regions: int32 [8, 4, 32, 4], P(('segment', 'dp')), may hold values from 0 to 244, as said below
- reg_conv: bfloat16 [128, 900], replicated, may hold values from -0.1875 to 0.1875
- reg_out: bfloat16 [64, 128], replicated, may hold values from -0.5 to 0.5
- conv_one: bfloat16 [128, 1152], replicated, may hold values from -0.1875 to 0.1875
- conv_two: bfloat16 [128, 1152], replicated, may hold values from -0.1875 to 0.1875
- out_proj: bfloat16 [64, 128], replicated, may hold values from -0.5 to 0.5
- step_embed: float32 [32, 128], replicated, may hold values from -3 to 3
Outputs:
- mean_field: bfloat16 [8, 64, 48, 256], P(('segment', 'dp'), None, 'rows')
- owner_loss: float32 [8, 4], P(('segment', 'dp'), 'rows')
- grad_conv_one: float32 [128, 1152], replicated
- grad_conv_two: float32 [128, 1152], replicated
- grad_out_proj: float32 [64, 128], replicated
- grad_embed: float32 [32, 128], replicated
Inputs may be any that keep to these rules, and one draw needn't show every extreme that they name: `regions`: for sample s, strip i and entry k: entry 0 is the patch's row offset within strip i (0 on the last strip), entry 1 its first column, at most 244, entry 2 its owner, entry 3 its noise level below 32. Every owner receives 2 * 32, 32 or 16 patches of a sample; for each owner with 64 there is one with 32 and two with 16. No strip lists more than 16 patches for one owner, and some strip lists exactly 16 for one owner.
All inputs are finite; a program needn't handle non-finite values.
Results may differ from a plain program's by a relative error of at most 0.0048.
Values may be sent and summed in bfloat16 or wider, within the bound.
No kernel may reach another device: no remote copies, remote signals or barrier semaphores. Data moves between devices by JAX's collectives and lax.ppermute only.
A program may use at most 192 MiB of HBM per device.

v0:
```python
import math

import jax
import jax.numpy as jnp
from jax import lax
from jax.sharding import PartitionSpec as P

PATCH = 12


TAPS = ((-1, -1), (-1, 0), (-1, 1), (0, -1), (0, 0), (0, 1), (1, -1), (1, 0), (1, 1))


def padded_2(cells, sides, width):
    for axis, dim in sides:
        count = lax.axis_size(axis)
        ends = count - 1
        head = lax.slice_in_dim(cells, 0, width, axis=dim)
        tail = lax.slice_in_dim(cells, cells.shape[dim] - width, cells.shape[dim], axis=dim)
        cells = jnp.concatenate(
            [
                lax.ppermute(tail, axis, [(i, (i + 1) % count) for i in range(ends)]),
                cells,
                lax.ppermute(head, axis, [((i + 1) % count, i) for i in range(ends)]),
            ],
            axis=dim,
        )
    return cells


def shifted_2(block, axis, distance):
    devices = range(lax.axis_size(axis))
    route = [(i - distance, i) for i in devices if i - distance in devices]
    return lax.ppermute(block, axis, route)


def shifted(values, row_step, col_step, stride):
    length = values.shape[-1]
    margin = stride + 1
    widths = [(0, 0)] * (values.ndim - 1) + [(margin, margin)]
    padded = jnp.pad(values, widths)
    offset = margin + row_step * stride + col_step
    moved = lax.slice_in_dim(padded, offset, offset + length, axis=values.ndim - 1)
    column = jnp.arange(length, dtype=jnp.int32) % stride + col_step
    inside = (column >= 0) & (column < stride)
    return jnp.where(inside, moved, jnp.zeros((), moved.dtype))


def columns(values, stride):
    return jnp.concatenate(
        [shifted(values, row_step, col_step, stride) for row_step, col_step in TAPS], axis=-2
    )


def fold(gradients, stride):
    width = gradients.shape[-2] // 9
    result = jnp.zeros(gradients.shape[:-2] + (width, gradients.shape[-1]), jnp.float32)
    for position, (row_step, col_step) in enumerate(TAPS):
        piece = gradients[..., position * width : (position + 1) * width, :]
        result = result + shifted(piece, -row_step, -col_step, stride)
    return result


def noise_levels(level_count):
    steps_f = jnp.arange(level_count, dtype=jnp.float32)
    return 0.1 * jnp.exp(steps_f * (math.log(100.0) / (level_count - 1)))


def silu_slope(values):
    gate = jax.nn.sigmoid(values)
    return gate * (1.0 + values * (1.0 - gate))


def product(form, left, right):
    return jnp.einsum(form, left, right, preferred_element_type=jnp.float32)


def regress(grid_rows, reg_conv, reg_out):
    channels, height, width = grid_rows.shape
    flat = grid_rows.reshape(channels, height * width)
    hidden = product("ok,kp->op", reg_conv, columns(flat, width))
    activated = jax.nn.silu(hidden).astype(jnp.bfloat16)
    mean_flat = product("co,op->cp", reg_out, activated).astype(jnp.bfloat16)
    return mean_flat.reshape(reg_out.shape[0], height, width)


def patch_block(mean_part, target_part, noise_part, step_ids, in_use, weights):
    conv_one, conv_two, out_proj, step_embed = weights
    stride = PATCH
    level_count = step_embed.shape[0]
    sigma_table = noise_levels(level_count)
    step_hot = (step_ids[:, None] == jnp.arange(level_count, dtype=jnp.int32)[None, :]).astype(
        jnp.float32
    )
    sigma = jnp.sum(step_hot * sigma_table[None, :], axis=1)
    sigma_sq = sigma * sigma + 1.0
    scale_in = (1.0 / jnp.sqrt(sigma_sq))[:, None, None]
    scale_skip = (1.0 / sigma_sq)[:, None, None]
    scale_out = (sigma / jnp.sqrt(sigma_sq))[:, None, None]
    weight_loss = sigma_sq / (sigma * sigma)
    mean_float = mean_part.astype(jnp.float32)
    residual = target_part.astype(jnp.float32) - mean_float
    noisy = residual + sigma[:, None, None] * noise_part.astype(jnp.float32)
    inputs = jnp.concatenate([scale_in * noisy, mean_float], axis=1).astype(jnp.bfloat16)
    cols_in = columns(inputs, stride)
    embedded = jnp.sum(step_hot[:, :, None] * step_embed[None, :, :], axis=1)
    pre_one = product("ok,bkp->bop", conv_one, cols_in) + embedded[:, :, None]
    act_one = jax.nn.silu(pre_one).astype(jnp.bfloat16)
    cols_one = columns(act_one, stride)
    pre_two = product("ok,bkp->bop", conv_two, cols_one)
    act_two = jax.nn.silu(pre_two).astype(jnp.bfloat16)
    output = product("co,bop->bcp", out_proj, act_two)
    error = scale_skip * noisy + scale_out * output - residual
    losses = weight_loss * jnp.mean(error * error, axis=(1, 2)) * in_use
    factor = 2.0 * weight_loss * in_use / (error.shape[1] * error.shape[2])
    grad_output = (factor[:, None, None] * scale_out * error).astype(jnp.bfloat16)
    grad_proj = product("bcp,bop->co", grad_output, act_two)
    grad_act_two = product("co,bcp->bop", out_proj, grad_output)
    grad_pre_two = (grad_act_two * silu_slope(pre_two)).astype(jnp.bfloat16)
    grad_two = product("bop,bkp->ok", grad_pre_two, cols_one)
    grad_cols = product("ok,bop->bkp", conv_two, grad_pre_two)
    grad_act_one = fold(grad_cols, stride)
    grad_pre_one = (grad_act_one * silu_slope(pre_one)).astype(jnp.bfloat16)
    grad_one = product("bop,bkp->ok", grad_pre_one, cols_in)
    pixel_sums = jnp.sum(grad_pre_one, axis=2, dtype=jnp.float32)
    grad_table = jnp.sum(step_hot[:, :, None] * pixel_sums[:, None, :], axis=0)
    return (losses, (grad_one, grad_two, grad_proj, grad_table))


def run_blocks(mean_part, target_part, noise_part, step_ids, in_use, weights):
    patch_count = mean_part.shape[0]
    blocks = patch_count // 4

    def regroup(values):
        return values.reshape((blocks, 4) + values.shape[1:])

    def advance(running, group_block):
        losses, gradients = patch_block(
            group_block[0], group_block[1], group_block[2], group_block[3], group_block[4], weights
        )
        summed = (
            running[0] + gradients[0],
            running[1] + gradients[1],
            running[2] + gradients[2],
            running[3] + gradients[3],
        )
        return (summed, losses)

    initial = (
        jnp.zeros(weights[0].shape, jnp.float32),
        jnp.zeros(weights[1].shape, jnp.float32),
        jnp.zeros(weights[2].shape, jnp.float32),
        jnp.zeros(weights[3].shape, jnp.float32),
    )
    stacked = (
        regroup(mean_part),
        regroup(target_part),
        regroup(noise_part),
        regroup(step_ids),
        regroup(in_use),
    )
    gradients, losses = lax.scan(advance, initial, stacked)
    return (losses.reshape(patch_count), gradients)


def owner_tables(region_rows, strips):
    owners = region_rows[:, :, 2]
    owner_hot = (owners[:, :, None] == jnp.arange(strips, dtype=jnp.int32)[None, None, :]).astype(
        jnp.int32
    )
    pair_rank = jnp.sum((jnp.cumsum(owner_hot, axis=1) - owner_hot) * owner_hot, axis=2)
    flat_hot = owner_hot.reshape(-1, strips)
    owner_slot = jnp.sum((jnp.cumsum(flat_hot, axis=0) - flat_hot) * flat_hot, axis=1).reshape(
        owners.shape
    )
    return (owners, pair_rank, owner_slot)


def owned_slots(region_rows, owners, pair_rank, owner_slot, strip_index, capacity, most, height):
    strips = region_rows.shape[0]
    slot_hits = (
        (owners == strip_index)[:, :, None]
        & (owner_slot[:, :, None] == jnp.arange(most, dtype=jnp.int32)[None, None, :])
    ).astype(jnp.int32)
    strip_ids = jnp.arange(strips, dtype=jnp.int32)[:, None]
    recv_index = jnp.sum(slot_hits * (strip_ids * capacity + pair_rank)[:, :, None], axis=(0, 1))
    in_use = jnp.sum(slot_hits, axis=(0, 1)).astype(jnp.float32)
    step_ids = jnp.sum(slot_hits * region_rows[:, :, 3][:, :, None], axis=(0, 1))
    row_at = jnp.sum(
        slot_hits * (strip_ids * height + region_rows[:, :, 0])[:, :, None], axis=(0, 1)
    )
    col_at = jnp.sum(slot_hits * region_rows[:, :, 1][:, :, None], axis=(0, 1))
    return (recv_index, in_use, step_ids, row_at, col_at)


def cut_patches(source_grid, row_at, col_at, height):
    zero_index = jnp.zeros((), jnp.int32)

    def cut(row_start, col_start):
        piece = lax.dynamic_slice(
            source_grid,
            (zero_index, zero_index, row_start, col_start),
            (2, source_grid.shape[1], height, height),
        )
        return piece.reshape(2, source_grid.shape[1], height * height)

    return jax.vmap(cut)(row_at, col_at)


def per_device(
    coarse, target, noise, regions, reg_conv, reg_out, conv_one, conv_two, out_proj, step_embed
):
    strips = lax.axis_size("rows")
    strip_index = lax.axis_index("rows")
    region_rows = regions[0]
    per_strip = region_rows.shape[1]
    capacity = max(2, (2 * per_strip + strips - 1) // strips)
    most = 2 * per_strip
    weights = (conv_one, conv_two, out_proj, step_embed)
    rimmed = padded_2(coarse, (("rows", 2),), 1)
    mean_strip = regress(rimmed[0], reg_conv, reg_out)[:, 1:-1]
    height = mean_strip.shape[1]
    pair_strip = jnp.stack([mean_strip, target[0]])
    owners, pair_rank, owner_slot = owner_tables(region_rows, strips)
    own_regions = lax.dynamic_index_in_dim(region_rows, strip_index, 0, keepdims=False)
    own_pairs = lax.dynamic_index_in_dim(pair_rank, strip_index, 0, keepdims=False)
    slot_noise = noise[0, 0]
    below = shifted_2(pair_strip[:, :, : height - 1], "rows", -1)
    extended = jnp.concatenate([pair_strip, below], axis=2)
    patches = cut_patches(extended, own_regions[:, 0], own_regions[:, 1], height)
    outgoing = jnp.zeros((strips, capacity) + patches.shape[1:], patches.dtype)
    outgoing = outgoing.at[own_regions[:, 2], own_pairs].set(patches)
    received = lax.all_to_all(outgoing, "rows", split_axis=0, concat_axis=0, tiled=True)
    flat_recv = received.reshape((strips * capacity,) + patches.shape[1:])
    recv_index, in_use, step_ids, row_at, col_at = owned_slots(
        region_rows, owners, pair_rank, owner_slot, strip_index, capacity, most, height
    )
    gathered = jnp.take(flat_recv, recv_index, axis=0)
    losses, gradients = run_blocks(
        gathered[:, 0], gathered[:, 1], slot_noise, step_ids, in_use, weights
    )
    owner_total = jnp.sum(losses)
    totals = lax.psum(
        (gradients[0], gradients[1], gradients[2], gradients[3]), ("segment", "rows", "dp")
    )
    return (mean_strip[None], owner_total.reshape(1, 1), totals[0], totals[1], totals[2], totals[3])


def solution(mesh):
    placed = (
        P(("segment", "dp"), None, "rows", None),
        P(("segment", "dp"), None, "rows", None),
        P(("segment", "dp"), "rows", None, None, None),
        P(("segment", "dp"), None, None, None),
        P(),
        P(),
        P(),
        P(),
        P(),
        P(),
    )
    return jax.shard_map(
        per_device,
        mesh=mesh,
        in_specs=placed,
        out_specs=(
            P(("segment", "dp"), None, "rows", None),
            P(("segment", "dp"), "rows"),
            P(),
            P(),
            P(),
            P(),
        ),
        check_vma=False,
    )
```

profile of v0, /device:TPU:0, one launch (start us, length us, event | category | flops | bytes accessed | tf_op | source)
XLA Modules:
  0.0 714.2 jit_solution(13689492145728348428)
XLA Ops:
  8.1 4.9 collective-permute-start
  14.4 3.2 copy.76
  19.7 4.4 slice_select_fusion.1
  24.1 41.7 %concatenate.38 = bf16[900,3584]{1,0:T(8,128)(2,1)} concatenate(bf16[100,3584]{1,0:T(8,128)(2,1)} %get-tuple-element.372, bf16[100,3584]{1,0:T(8,128)(2,1)} %get-tuple-element.375, bf16[100,3584]{1,0:T(8,128)(2,1)} %get-tuple-element.365, bf16[100,3584]{1,0:T(8,128)(2,1)} %get-tuple-element.373, bf16[100,3584]{1,0:T(8,128)(2,1)} %get-tuple-element.376, ...), dimensions={0} | concatenate | bytes 12902400 | tf_op jit(solution)/shard_map/concatenate | solution.py:50
  65.9 5.4 fusion.29
  72.7 3.2 copy.75
  76.0 4.9 pad_maximum_fusion.2
  80.8 4.6 copy.77
  87.4 17.1 %collective-permute-done.2 = bf16[2,64,11,256]{3,1,2,0:T(8,128)(2,1)} collective-permute-done((bf16[2,64,11,256]{3,1,2,0:T(8,128)(2,1)}, bf16[2,64,11,256]{3,1,2,0:T(8,128)(2,1)}, u32[]{:S(2)}, u32[]{:S(2)}) %collective-permute-start.2) | collective-permute-done | bytes 720928 | tf_op jit(solution)/shard_map/ppermute | solution.py:34
  104.5 4.7 copy.78
  109.1 8.1 %pad_maximum_fusion.1 = bf16[2,64,23,256]{1,0,3,2:T(2,128)(2,1)} fusion(bf16[2,64,11,256]{1,0,3,2:T(2,128)(2,1)} %copy.78, bf16[1,64,12,256]{1,0,3,2:T(2,128)(2,1)S(1)} %copy.76, bf16[1,64,12,256]{1,0,3,2:T(2,128)(2,1)S(1)} %copy.75), kind=kLoop, calls=%fused_computation.91 | loop fusion | flops 4521984 | bytes 3014656 | tf_op jit(solution)/shard_map/concatenate | solution.py:229
  117.2 8.6 %gather_fusion = bf16[32,2,64,12,12]{2,1,4,3,0:T(2,128)(2,1)S(1)} fusion(bf16[2,64,23,256]{1,0,3,2:T(2,128)(2,1)} %pad_maximum_fusion.1, s32[32]{0:T(128)S(1)} %get-tuple-element.383), kind=kCustom, calls=%fused_computation | custom fusion | bytes 2359808 | tf_op jit(solution)/shard_map/vmap()/gather | solution.py:200
  125.9 3.9 copy.79
  129.8 2.5 broadcast_in_dim.229
  132.3 5.8 scatter_fusion
  138.1 4.9 all-to-all-start
  144.1 90.6 %all-to-all-done = bf16[4,16,2,64,144]{4,3,2,1,0:T(8,128)(2,1)} async-done(((bf16[4,16,2,64,144]{4,3,2,1,0:T(8,128)(2,1)}), bf16[4,16,2,64,144]{4,3,2,1,0:T(8,128)(2,1)}, u32[]{:S(2)}, u32[]{:S(2)}) %all-to-all-start) | async-done | bytes 2359328 | tf_op jit(solution)/shard_map/all_to_all | solution.py:233
  234.7 5.0 gather_fusion.1
  239.7 2.6 broadcast_select_fusion
  242.3 2.5 fusion.60
  244.9 328.0 %while.21 = (s32[]{:T(128)}, f32[128,1152]{1,0:T(8,128)}, f32[128,1152]{1,0:T(8,128)}, f32[64,128]{1,0:T(8,128)S(1)}, f32[32,128]{1,0:T(8,128)S(1)}, /*index=5*/...) while((s32[]{:T(128)}, f32[128,1152]{1,0:T(8,128)}, ...), condition=%wide.region_14.15_spmd.clone, body=%wide.region_8.14_spmd.clone.sunk | while | flops 884677568 | bytes 48410204 | solution.py:162
  248.7 2.3 multiply_convert_fusion.15
  252.3 1.6 multiply_convert_fusion.16
  257.1 1.7 fusion.112
  268.2 2.3 multiply_convert_fusion.15
  271.8 1.6 multiply_convert_fusion.16
  276.6 2.8 fusion.112
  288.8 2.3 multiply_convert_fusion.15
  292.4 1.6 multiply_convert_fusion.16
  297.2 2.8 fusion.112
  309.4 2.3 multiply_convert_fusion.15
  313.0 1.6 multiply_convert_fusion.16
  317.7 2.8 fusion.112
  329.9 2.3 multiply_convert_fusion.15
  333.5 1.6 multiply_convert_fusion.16
  338.3 2.8 fusion.112
  350.5 2.3 multiply_convert_fusion.15
  358.9 2.8 fusion.112
  371.0 2.3 multiply_convert_fusion.15
  379.4 2.8 fusion.112
  391.6 2.3 multiply_convert_fusion.15
  400.0 2.8 fusion.112
  412.2 2.3 multiply_convert_fusion.15
  420.6 2.8 fusion.112
  432.7 2.3 multiply_convert_fusion.15
  441.1 2.8 fusion.112
  453.3 2.3 multiply_convert_fusion.15
  461.7 2.8 fusion.112
  473.9 2.3 multiply_convert_fusion.15
  477.5 1.6 multiply_convert_fusion.16
  482.3 2.8 fusion.112
  494.4 2.3 multiply_convert_fusion.15
  498.1 1.6 multiply_convert_fusion.16
  502.8 2.8 fusion.112
  515.0 2.3 multiply_convert_fusion.15
  523.4 2.8 fusion.112
  535.6 2.3 multiply_convert_fusion.15
  543.9 2.8 fusion.112
  556.1 2.3 multiply_convert_fusion.15
  564.5 2.8 fusion.112
  574.2 38.8 %all-reduce.11 = (f32[64,128]{1,0:T(8,128)}, f32[32,128]{1,0:T(8,128)}) all-reduce(f32[64,128]{1,0:T(8,128)S(1)} %get-tuple-element.201, f32[32,128]{1,0:T(8,128)S(1)} %get-tuple-element.202), channel_id=1, replica_groups=mesh['segment'=2,'rows'=4,'dp'=4] {'segment','rows','dp'}, use_global_device_ids=true, to_apply=%region_18.19 | all-reduce | flops 12288 | bytes 98304 | tf_op jit(solution)/shard_map/psum | solution.py:243
  613.1 90.4 %all-reduce.15.cloned.1.call-done = (f32[128,1152]{1,0:T(8,128)}, f32[128,1152]{1,0:T(8,128)}) async-done(((f32[128,1152]{1,0:T(8,128)}, f32[128,1152]{1,0:T(8,128)}), (f32[128,1152]{1,0:T(8,128)}, f32[128,1152]{1,0:T(8,128)})) %all-reduce.15.cloned.1.call-update) | async-done | bytes 1179664 | tf_op jit(solution)/shard_map/psum | solution.py:243
  703.5 1.9 copy.139
  705.4 1.9 copy.140
  (871 shorter events, 241.5 us)
Async XLA Ops:
  7.2 58.7 %copy-start = (bf16[128,900]{0,1:T(8,128)(2,1)S(1)}, bf16[128,900]{0,1:T(8,128)(2,1)}, u32[]{:S(2)}) copy-start(bf16[128,900]{0,1:T(8,128)(2,1)} %param.16) | copy-start | bytes 691204
  7.2 11.9 %copy-start.9 = (bf16[1,100,12,256]{3,1,2,0:T(8,128)(2,1)S(1)}, bf16[1,100,12,256]{3,1,2,0:T(8,128)(2,1)}, u32[]{:S(2)}) copy-start(bf16[1,100,12,256]{3,1,2,0:T(8,128)(2,1)} %param.12) | copy-start | bytes 1843204
  8.1 9.5 %collective-permute-start = (bf16[1,100,1,256]{3,1,2,0:T(8,128)(2,1)S(1)}, bf16[1,100,1,256]{3,1,2,0:T(8,128)(2,1)S(1)}, u32[]{:S(2)}, u32[]{:S(2)}) collective-permute-start(bf16[1,100,1,256]{3,1,2,0:T(8,128)(2,1)S(1)} %get-tuple-element.378), channel_id=1, source_target_pairs={{0,4},{4,8},{8,12},{1,5},{5,9},{9,13},{2,6},{6,10},{10,14},{3,7},{... | collective-permute-start | bytes 153608 | tf_op jit(solution)/shard_map/ppermute | solution.py:22
  13.0 6.0 collective-permute-start.1
  24.1 41.7 %copy-start.13 = (bf16[64,128]{1,0:T(8,128)(2,1)S(1)}, bf16[64,128]{1,0:T(8,128)(2,1)}, u32[]{:S(2)}) copy-start(bf16[64,128]{1,0:T(8,128)(2,1)} %param.17) | copy-start | bytes 49156
  75.9 11.0 %copy-start.12 = (s32[1,4,32,4]{2,3,1,0:T(4,128)S(1)}, s32[1,4,32,4]{2,3,1,0:T(4,128)}, u32[]{:S(2)}) copy-start(s32[1,4,32,4]{2,3,1,0:T(4,128)} %param.15) | copy-start | bytes 6148
  85.5 19.0 %collective-permute-start.2 = (bf16[2,64,11,256]{3,1,2,0:T(8,128)(2,1)}, bf16[2,64,11,256]{3,1,2,0:T(8,128)(2,1)}, u32[]{:S(2)}, u32[]{:S(2)}) collective-permute-start(bf16[2,64,11,256]{3,1,2,0:T(8,128)(2,1)} %copy.77), channel_id=1, source_target_pairs={{4,0},{8,4},{12,8},{5,1},{9,5},{13,9},{6,2},{10,6},{14,10},{7,3},{... | collective-permute-start | bytes 2162696 | tf_op jit(solution)/shard_map/ppermute | solution.py:34
  129.8 2.5 copy-start.7
  138.1 96.6 %all-to-all-start = ((bf16[4,16,2,64,144]{4,3,2,1,0:T(8,128)(2,1)}), bf16[4,16,2,64,144]{4,3,2,1,0:T(8,128)(2,1)}, u32[]{:S(2)}, u32[]{:S(2)}) async-start(bf16[4,16,2,64,144]{4,3,2,1,0:T(8,128)(2,1)} %scatter_fusion), calls=%async_computation | async-start | bytes 8388608 | tf_op jit(solution)/shard_map/all_to_all | solution.py:233
  142.9 560.6 %all-reduce.15.cloned.1.call-start = ((), (), s32[]{:S(2)}) async-start(), calls=%async_computation.1 | async-start | bytes 2359296 | tf_op jit(solution)/shard_map/psum | solution.py:243
  242.3 2.6 copy-start.8
  242.3 2.6 copy-start.10
  242.3 2.6 copy-start.11
  252.3 2.9 copy-start.2
  255.3 1.8 copy-start.3
  260.7 1.3 copy-start.4
  262.9 1.5 copy-start.5
  271.8 2.9 copy-start.2
  274.8 1.8 copy-start.3
  283.5 1.5 copy-start.5
  292.4 2.9 copy-start.2
  295.3 1.8 copy-start.3
  301.8 1.3 copy-start.4
  304.1 1.5 copy-start.5
  313.0 2.9 copy-start.2
  315.9 1.8 copy-start.3
  324.6 1.5 copy-start.5
  333.5 2.9 copy-start.2
  336.5 1.8 copy-start.3
  345.2 1.5 copy-start.5
  354.1 2.9 copy-start.2
  357.0 1.8 copy-start.3
  365.7 1.5 copy-start.5
  374.7 2.9 copy-start.2
  377.6 1.8 copy-start.3
  386.3 1.5 copy-start.5
  395.2 2.9 copy-start.2
  398.2 1.8 copy-start.3
  406.9 1.5 copy-start.5
  415.8 2.9 copy-start.2
  418.7 1.8 copy-start.3
  427.4 1.5 copy-start.5
  436.4 2.9 copy-start.2
  439.3 1.8 copy-start.3
  448.0 1.5 copy-start.5
  456.9 2.9 copy-start.2
  459.9 1.8 copy-start.3
  468.6 1.5 copy-start.5
  477.5 2.9 copy-start.2
  480.4 1.8 copy-start.3
  489.1 1.5 copy-start.5
  498.0 2.9 copy-start.2
  501.0 1.8 copy-start.3
  509.7 1.5 copy-start.5
  518.6 2.9 copy-start.2
  521.5 1.8 copy-start.3
  530.3 1.5 copy-start.5
  539.2 2.9 copy-start.2
  542.1 1.8 copy-start.3
  550.8 1.5 copy-start.5
  559.7 2.9 copy-start.2
  562.7 1.8 copy-start.3
  571.4 1.5 copy-start.5
  572.9 134.5 %copy-start.1 = (bf16[128,900]{0,1:T(8,128)(2,1)S(1)}, bf16[128,900]{0,1:T(8,128)(2,1)}, u32[]{:S(2)}) copy-start(bf16[128,900]{0,1:T(8,128)(2,1)} %param.16) | copy-start | bytes 691204
  (30 other events, 34.4 us)
Sparse Core Ops, SparseCore 0:
  573.0 130.4 all-reduce.14
where the time goes:
time: 721 us; the launch traced here: 714 us
  waiting for transfers between devices  200 us (28%)
  matrix products  190 us (26%)
  local copies, waits for them, and re-layouts  146 us (20%)
  other arithmetic  109 us (15%)
  blocking collectives  38.8 us (5%)
  between operations  14.4 us (2%)
  starting transfers between devices  12.6 us (2%)
    dot_general x129, matrix products, product(): return jnp.einsum(form, left, right, preferred_element_type=jnp.float32)  190 us
    all_to_all x1, waiting for transfers between devices, per_device(): lax.all_to_all(outgoing, 'rows', split_axis=0, concat_axis=0, tiled=True)  90.6 us
    psum x1, waiting for transfers between devices, per_device(): lax.psum((gradients[0], gradients[1], gradients[2], gradients[3]), ('segm...  90.4 us
    concatenate x1, local copies, waits for them, and re-layouts, columns(): jnp.concatenate([shifted(values, row_step, col_step, stride) for row_step...  41.7 us
    psum x1, blocking collectives, per_device(): lax.psum((gradients[0], gradients[1], gradients[2], gradients[3]), ('segm...  38.8 us
    while x256, other arithmetic  34.1 us
    dynamic_update_slice x16, local copies, waits for them, and re-layouts, run_blocks(): gradients, losses = lax.scan(advance, initial, stacked)  21.3 us
    reduce_sum x16, other arithmetic, patch_block(): pixel_sums = jnp.sum(grad_pre_one, axis=2, dtype=jnp.float32)  20.2 us
  transfers between devices with their start and end apart: 5, of which 4 were waited for; matrix products, arithmetic and copies ran while one was open for 1% of the time, Pallas kernels for 0%

commit v1 on v0

v1 whole, which is shorter than its diff:
```python
import functools
import math

import jax
import jax.numpy as jnp
from jax import lax
from jax.experimental import pallas as pl
from jax.experimental.pallas import tpu as pltpu
from jax.sharding import PartitionSpec as P

BF = jnp.bfloat16
F32 = jnp.float32
TAPS = tuple((a, b) for a in (-1, 0, 1) for b in (-1, 0, 1))
NT_FORM = (((1,), (1,)), ((), ()))
TN_FORM = (((0,), (0,)), ((), ()))
LIMIT = 48 * 1024 * 1024


def matmul(left, right):
    return jnp.dot(left, right, preferred_element_type=F32)


def whole(shape):
    return pl.BlockSpec(memory_space=pltpu.VMEM)


VM = pl.BlockSpec(memory_space=pltpu.VMEM)
SM = pl.BlockSpec(memory_space=pltpu.SMEM)


def call(kernel, outs, ins, specs, scratch=(), cost=0):
    return pl.pallas_call(
        kernel,
        out_shape=outs,
        in_specs=list(specs),
        out_specs=jax.tree.map(lambda _: VM, outs),
        scratch_shapes=list(scratch),
        compiler_params=pltpu.CompilerParams(vmem_limit_bytes=LIMIT),
        cost_estimate=pl.CostEstimate(flops=cost, bytes_accessed=1 << 20, transcendentals=0),
    )(*ins)


def pack_kernel(slots_ref, noise_ref, *out_refs):
    channels, cells = noise_ref.shape[1:]
    half = cells // 2
    row = lax.broadcasted_iota(jnp.int32, (half, cells), 0)
    col = lax.broadcasted_iota(jnp.int32, (half, cells), 1)
    even = (col == 2 * row).astype(BF)
    odd = (col == 2 * row + 1).astype(BF)
    low = lax.broadcasted_iota(jnp.int32, (half, 2 * channels), 1) < channels
    per = out_refs[0].shape[0]
    for index, out_ref in enumerate(out_refs):

        def pair(j, carry, index=index, out_ref=out_ref):
            one = noise_ref[slots_ref[index * per + 2 * j]]
            two = noise_ref[slots_ref[index * per + 2 * j + 1]]
            both = jnp.concatenate([one, two], axis=0)
            first = lax.dot_general(even, both, NT_FORM, preferred_element_type=F32)
            second = lax.dot_general(odd, both, NT_FORM, preferred_element_type=F32)
            out_ref[2 * j] = jnp.where(low, first, pltpu.roll(second, channels, 1)).astype(BF)
            out_ref[2 * j + 1] = jnp.where(low, pltpu.roll(first, channels, 1), second).astype(BF)
            return carry

        lax.fori_loop(0, per // 2, pair, 0, unroll=min(4, per // 2))


def regress_kernel(above_ref, own_ref, below_ref, conv_ref, proj_ref, mean_ref, cols_ref):
    rows, channels, width = own_ref.shape
    deep = cols_ref.shape[1] // 3
    cols_ref[...] = jnp.zeros(cols_ref.shape, BF)
    lane = lax.broadcasted_iota(jnp.int32, (channels, width), 1)

    def put(at, cells):
        wide = cells.astype(F32)
        left = jnp.where(lane == 0, 0.0, pltpu.roll(wide, 1, 1)).astype(BF)
        right = jnp.where(lane == width - 1, 0.0, pltpu.roll(wide, width - 1, 1)).astype(BF)
        cols_ref[at, 0:channels] = left
        cols_ref[at, deep : deep + channels] = cells
        cols_ref[at, 2 * deep : 2 * deep + channels] = right

    put(0, above_ref[0])
    put(rows + 1, below_ref[0])

    def fill(r, carry):
        put(r + 1, own_ref[r])
        return carry

    lax.fori_loop(0, rows, fill, 0)

    def one(r, carry):
        stack = cols_ref[pl.ds(r, 3)].reshape(9 * deep, width)
        hidden = matmul(conv_ref[...], stack)
        act = (hidden * jax.nn.sigmoid(hidden)).astype(BF)
        mean_ref[r] = matmul(proj_ref[...], act).astype(BF)
        return carry

    lax.fori_loop(0, rows, one, 0, unroll=2)


def gather_kernel(
    row_ref, col_ref, mean_ref, mean_low_ref, tgt_ref, tgt_low_ref, mp_ref, tp_ref, img_m, img_t, got_m, got_t
):
    rows, channels, width = mean_ref.shape
    chunks, _, count, _ = mp_ref.shape
    pairs = rows // 2
    eye = (
        lax.broadcasted_iota(jnp.int32, (width, width), 0)
        == lax.broadcasted_iota(jnp.int32, (width, width), 1)
    ).astype(BF)

    def paint(cells, img, at):
        after = pltpu.roll(cells.astype(F32), width - 1, 1).astype(BF)
        both = jnp.concatenate([cells, after], axis=0)
        img[at] = lax.dot_general(eye, both, NT_FORM, preferred_element_type=F32)

    def own(r, carry):
        paint(mean_ref[r], img_m, r)
        paint(tgt_ref[r], img_t, r)
        return carry

    def low(r, carry):
        paint(mean_low_ref[r], img_m, rows + r)
        paint(tgt_low_ref[r], img_t, rows + r)
        return carry

    lax.fori_loop(0, rows, own, 0)
    lax.fori_loop(0, rows - 1, low, 0)
    for chunk in range(chunks):

        def patch(k, carry, chunk=chunk):
            top = row_ref[chunk * count + k]
            left = col_ref[chunk * count + k]
            for r in range(rows):
                for img, got in ((img_m, got_m), (img_t, got_t)):
                    got[pl.ds(r * pairs * count + k, pairs, stride=count), :] = img[
                        top + r, pl.ds(left, pairs, stride=2), :
                    ]
            return carry

        lax.fori_loop(0, count, patch, 0)
        mp_ref[chunk] = got_m[...].astype(BF).reshape(mp_ref.shape[1:])
        tp_ref[chunk] = got_t[...].astype(BF).reshape(tp_ref.shape[1:])


def chunk_kernel(
    chunk,
    last,
    phases,
    *refs,
):
    source_ref, phase_ref, step_ref = refs[:3]
    noise_refs = refs[3 : 3 + phases]
    refs = refs[3 + phases :]
    (mp_ref, tp_ref, fac_ref, embed_ref, w1_ref, w2_ref, v2_ref, po_ref, pg_ref) = refs[:9]
    refs = refs[9:]
    before = None
    if chunk > 0:
        before, refs = refs[0], refs[1:]
    out_ref, loss_ref = refs[:2]
    (nz, xn, xm, x2n, x2m, e1, o1, e2, o2, slope1, res, noisy, act2, gout, gt, emb) = refs[2:]
    _, cells, count, wide = mp_ref.shape
    rows = 12
    pairs = cells // rows
    total = cells * count
    group = 4
    half = wide // 2

    for ref in (xn, xm, e1, o1, e2, o2):
        ref[...] = jnp.zeros(ref.shape, BF)
    for k in range(count):
        at = source_ref[chunk * count + k]
        piece = noise_refs[0][at]
        if phases > 1:
            piece = jnp.where(phase_ref[chunk * count + k] == 0, piece, noise_refs[1][at])
        nz[pl.ds(k, cells, stride=count), :] = piece.astype(F32)
        emb[pl.ds(k, 1), :] = embed_ref[pl.ds(step_ref[chunk * count + k], 1), :]

    def spread(index):
        return fac_ref[index][None]

    scale_in, sigma, skip, scale_out, grad_scale = (spread(i) for i in range(5))
    lane = lax.broadcasted_iota(jnp.int32, (1, 1, count, wide), 3)

    mean_bf = mp_ref[0]
    mean = mean_bf.astype(F32)
    residual = tp_ref[0].astype(F32) - mean
    noised = residual + sigma * nz[...].reshape(cells, count, wide)
    res[...] = residual.reshape(total, wide)
    noisy[...] = noised.reshape(total, wide)
    xn[1 : rows + 1, 1 : pairs + 1] = (scale_in * noised).astype(BF).reshape(rows, pairs, count, wide)
    xm[1 : rows + 1, 1 : pairs + 1] = mean_bf.reshape(rows, pairs, count, wide)
    for src, dst in ((xn, x2n), (xm, x2m)):
        dst[...] = jnp.where(
            lane < half, src[:, 2 : pairs + 2].astype(F32), src[:, 0:pairs].astype(F32)
        ).astype(BF)

    def view(ref, at, many, p0):
        return ref[at : at + many, p0 : p0 + pairs].reshape(many * pairs * count, wide)

    def stack_in(at, many):
        return [view(xn, at, many, 1), view(xm, at, many, 1), view(x2n, at, many, 0), view(x2m, at, many, 0)]

    def stack_eo(even, odd, at, many):
        return [view(even, at, many, 1), view(odd, at, many, 1), view(odd, at, many, 0), view(even, at, many, 2)]

    def shape4(value, many):
        return value.reshape(many, pairs, count, value.shape[-1])

    tile = group * pairs * count
    emb_pair = jnp.concatenate([emb[...], emb[...]], axis=1)[None]
    for r in range(0, rows, group):
        left = jnp.concatenate(sum([stack_in(r + a, group) for a in range(3)], []), axis=1)
        pre = matmul(left, w1_ref[...]).reshape(group * pairs, count, 2 * wide) + emb_pair
        gate = jax.nn.sigmoid(pre)
        act = (pre * gate).astype(BF)
        slope1[r * pairs * count : r * pairs * count + tile, :] = (
            gate * (1.0 + pre * (1.0 - gate))
        ).reshape(tile, 2 * wide)
        act = shape4(act, group)
        e1[r + 1 : r + 1 + group, 1 : pairs + 1] = act[..., :wide]
        o1[r + 1 : r + 1 + group, 1 : pairs + 1] = act[..., wide:]

    loss = jnp.zeros((count, wide), F32)
    for r in range(0, rows, group):
        span = pl.ds(r * pairs * count, tile)
        left = jnp.concatenate(sum([stack_eo(e1, o1, r + a, group) for a in range(3)], []), axis=1)
        pre = matmul(left, w2_ref[...])
        gate = jax.nn.sigmoid(pre)
        act = (pre * gate).astype(BF)
        slope = gate * (1.0 + pre * (1.0 - gate))
        act2[span, :] = act
        output = matmul(act, po_ref[...]).reshape(group * pairs, count, wide)
        error = (
            skip * noisy[span, :].reshape(group * pairs, count, wide)
            + scale_out * output
            - res[span, :].reshape(group * pairs, count, wide)
        )
        loss = loss + jnp.sum(error * error, axis=0)
        grad_output = (grad_scale * error).astype(BF).reshape(tile, wide)
        gout[span, :] = grad_output
        grad_pre = (matmul(grad_output, pg_ref[...]) * slope).astype(BF)
        grad_pre = shape4(grad_pre, group)
        e2[r + 1 : r + 1 + group, 1 : pairs + 1] = grad_pre[..., :wide]
        o2[r + 1 : r + 1 + group, 1 : pairs + 1] = grad_pre[..., wide:]
    loss_ref[...] = loss

    def emit(at, size, value):
        if before is not None:
            value = value + before[at : at + size, :]
        out_ref[at : at + size, :] = value

    depth = wide
    proj = lax.dot_general(gout[...], act2[...], TN_FORM, preferred_element_type=F32)
    emit(18 * depth, half, proj[:half, :wide] + proj[half:, wide:])

    gt[0:depth, :] = jnp.transpose(view(e2, 1, rows, 1))
    gt[depth : 2 * depth, :] = jnp.transpose(view(o2, 1, rows, 1))
    for a in range(3):
        right = jnp.concatenate(stack_eo(e1, o1, a, rows), axis=1)
        got = matmul(gt[...], right)
        h0, h1 = got[:depth], got[depth:]
        base = 9 * depth + 3 * a * depth
        emit(base, depth, h1[:, 0:wide] + h0[:, 2 * wide : 3 * wide])
        emit(base + depth, depth, h0[:, 0:wide] + h1[:, wide : 2 * wide])
        emit(base + 2 * depth, depth, h0[:, wide : 2 * wide] + h1[:, 3 * wide : 4 * wide])

    sums = jnp.zeros((count, 2 * wide), F32)
    for r in range(0, rows, group):
        span = pl.ds(r * pairs * count, tile)
        left = jnp.concatenate(sum([stack_eo(e2, o2, r + a, group) for a in range(3)], []), axis=1)
        grad = (matmul(left, v2_ref[...]) * slope1[span, :]).astype(BF)
        sums = sums + jnp.sum(grad.astype(F32).reshape(group * pairs, count, 2 * wide), axis=0)
        act2[span, :] = grad
    emb[...] = sums[:, :wide] + sums[:, wide:]
    table = 18 * depth + half
    levels = embed_ref.shape[0]
    if before is not None:
        out_ref[table : table + levels, :] = before[table : table + levels, :]
    else:
        out_ref[table : table + levels, :] = jnp.zeros((levels, wide), F32)
    for k in range(count):
        at = table + step_ref[chunk * count + k]
        out_ref[pl.ds(at, 1), :] = out_ref[pl.ds(at, 1), :] + emb[pl.ds(k, 1), :]

    gt[...] = jnp.transpose(act2[...])
    low = lax.broadcasted_iota(jnp.int32, (depth, wide), 1) < half
    for a in range(3):
        right = jnp.concatenate(stack_in(a, rows), axis=1)
        got = matmul(gt[...], right)
        h0, h1 = got[:depth], got[depth:]

        def merged(first, second):
            n = first[:, 0:wide], second[:, 0:wide]
            m = first[:, wide:], second[:, wide:]
            noise_part = n[0] + pltpu.roll(n[1], half, 1)
            mean_part = pltpu.roll(m[0], half, 1) + m[1]
            return jnp.where(low, noise_part, mean_part)

        base = 3 * a * depth
        direct, rim = slice(0, 2 * wide), slice(2 * wide, 4 * wide)
        emit(base, depth, merged(h1[:, direct], h0[:, rim]))
        emit(base + depth, depth, merged(h0[:, direct], h1[:, direct]))
        emit(base + 2 * depth, depth, merged(h1[:, rim], h0[:, direct]))


def pair_weights(taps, split):
    zero = jnp.zeros_like(taps[0][0])
    blocks = []
    for a in range(3):
        low, mid, high = taps[a]

        def rows_of(first, second):
            if not split:
                return [first, second]
            half = first.shape[0] // 2
            return [first[:half], second[:half], first[half:], second[half:]]

        even = jnp.concatenate([mid, low], axis=1)
        odd = jnp.concatenate([high, mid], axis=1)
        before = jnp.concatenate([low, zero], axis=1)
        after = jnp.concatenate([zero, high], axis=1)
        blocks += rows_of(even, odd)
        blocks += rows_of(after, before) if split else rows_of(before, after)
    return jnp.concatenate(blocks, axis=0)


def forward_weights(conv, split):
    depth = conv.shape[1] // 9
    cut = [conv[:, i * depth : (i + 1) * depth].T for i in range(9)]
    return pair_weights([cut[0:3], cut[3:6], cut[6:9]], split)


def backward_weights(conv):
    depth = conv.shape[1] // 9
    cut = [conv[:, (8 - i) * depth : (9 - i) * depth] for i in range(9)]
    return pair_weights([cut[0:3], cut[3:6], cut[6:9]], False)


def by_distance(axis, distance):
    return [(i, i ^ distance) for i in range(lax.axis_size(axis))]


def rounded_to_bf16(values):
    return lax.reduce_precision(values, 8, 7)


def take(pieces, index):
    return lax.dynamic_index_in_dim(pieces, index, 0, keepdims=False)


def scatter_sum(values, axis):
    n = values.shape[0]
    me = lax.axis_index(axis)
    out = take(values, me)
    arrived = [
        lax.ppermute(take(values, me ^ d).astype(BF), axis, by_distance(axis, d)) for d in range(1, n)
    ]
    for piece in arrived:
        out = out + piece.astype(F32)
    return out


def gather_all(piece, axis):
    n = lax.axis_size(axis)
    me = lax.axis_index(axis)
    found = [piece] + [lax.ppermute(piece, axis, by_distance(axis, d)) for d in range(1, n)]
    return jnp.stack([sum_select(found, me, i) for i in range(n)])


def sum_select(found, me, index):
    out = found[0]
    for d in range(1, len(found)):
        out = jnp.where((me ^ d) == index, found[d], out)
    return out


def rows_sum(piece, axis):
    n = lax.axis_size(axis)
    if n > 4:
        return lax.psum(piece, axis)
    values = [rounded_to_bf16(piece).astype(BF)]
    for d in range(1, n):
        values.append(lax.ppermute(values[0], axis, by_distance(axis, d)))
    values = [v.astype(F32) for v in values]
    while len(values) > 1:
        values = [values[i] + values[i + 1] for i in range(0, len(values), 2)]
    return values[0]


def per_device(coarse, target, noise, regions, reg_conv, reg_out, conv_one, conv_two, out_proj, step_embed):
    strips = lax.axis_size("rows")
    me = lax.axis_index("rows")
    region = regions[0]
    per_strip = region.shape[1]
    most = noise.shape[2]
    capacity = max(2, (2 * per_strip + strips - 1) // strips)
    phases = 2
    deep = capacity // phases
    count = per_strip // phases
    exchange = strips <= 4
    channels = target.shape[1]
    height, width = target.shape[2:]
    cells = height * height
    wide = 2 * channels
    depth = conv_one.shape[0]
    levels = step_embed.shape[0]

    down = [(i + 1, i) for i in range(strips - 1)]
    up = [(i, i + 1) for i in range(strips - 1)]
    own_target = jnp.transpose(target[0], (1, 0, 2))
    own_coarse = jnp.transpose(coarse[0], (1, 0, 2))
    target_low = lax.ppermute(own_target[: height - 1], "rows", down)
    coarse_above = lax.ppermute(own_coarse[height - 1 :], "rows", up)
    coarse_below = lax.ppermute(own_coarse[:1], "rows", down)

    ids = jnp.arange(strips, dtype=jnp.int32)
    owners = region[:, :, 2]
    mine = jnp.sum((owners == me).astype(jnp.int32), axis=1)
    starts = jnp.sum(jnp.where(ids[:, None] > ids[None, :], mine[None, :], 0), axis=1)
    distances = ids
    goal = (ids ^ me) if exchange else ids
    goal_start = jnp.sum(jnp.where(goal[:, None] == ids[None, :], starts[None, :], 0), axis=1)
    rank = jnp.arange(capacity, dtype=jnp.int32).reshape(phases, 1, deep)
    slots = jnp.minimum(goal_start[None, :, None] + rank, most - 1).reshape(-1)

    own = lax.dynamic_index_in_dim(region, me, 0, keepdims=False)
    owner = own[:, 2]
    entry = jnp.arange(per_strip, dtype=jnp.int32)
    earlier = entry[None, :] < entry[:, None]
    pair_rank = jnp.sum(((owner[:, None] == owner[None, :]) & earlier).astype(jnp.int32), axis=1)
    early = pair_rank < deep
    early_before = jnp.sum((early[None, :] & earlier).astype(jnp.int32), axis=1)
    first = early & (early_before < count)
    first_before = jnp.sum((first[None, :] & earlier).astype(jnp.int32), axis=1)
    place = jnp.where(first, first_before, count + entry - first_before)
    place_hot = place[None, :] == entry[:, None]

    def ordered(field):
        return jnp.sum(jnp.where(place_hot, field[None, :], 0), axis=1)

    source = ordered(((owner ^ me) if exchange else owner) * deep + pair_rank % deep)
    phase = ordered(pair_rank // deep)
    top, left, step, owner_in_order = (ordered(own[:, i]) for i in (0, 1, 3, 2))

    sigma = 0.1 * jnp.exp(step.astype(F32) * (math.log(100.0) / (levels - 1)))
    u = sigma * sigma + 1.0
    weight = u / (sigma * sigma)
    scale_out = sigma / jnp.sqrt(u)
    grad_scale = 2.0 * weight / (channels * cells) * scale_out
    factors = jnp.stack([1.0 / jnp.sqrt(u), sigma, 1.0 / u, scale_out, grad_scale])
    factors = jnp.broadcast_to(factors[:, :, None], (5, per_strip, wide))

    slot_shape = (cells // 2, wide)
    pieces = phases * strips if exchange else phases
    packed = call(
        pack_kernel,
        [jax.ShapeDtypeStruct((phases * strips * deep // pieces,) + slot_shape, BF)] * pieces,
        (slots, noise[0, 0]),
        (SM, VM),
    )
    arrived = []
    for f in range(phases):
        if exchange:
            parts = [packed[f * strips]]
            for d in range(1, strips):
                parts.append(lax.ppermute(packed[f * strips + d], "rows", by_distance("rows", d)))
            arrived.append(jnp.concatenate(parts, axis=0))
        else:
            arrived.append(lax.all_to_all(packed[f], "rows", 0, 0, tiled=True))

    fill = -(-reg_conv.shape[1] // 9 // 16) * 16
    per_tap = reg_conv.shape[1] // 9
    reg_taps = jnp.pad(reg_conv.reshape(-1, 9, per_tap), ((0, 0), (0, 0), (0, fill - per_tap)))
    mean = call(
        regress_kernel,
        jax.ShapeDtypeStruct((height, channels, width), BF),
        (coarse_above, own_coarse, coarse_below, reg_taps.reshape(-1, 9 * fill), reg_out),
        (VM,) * 5,
        [pltpu.VMEM((height + 2, 3 * fill, width), BF)],
    )
    mean_low = lax.ppermute(mean[: height - 1], "rows", down)
    patch_shape = jax.ShapeDtypeStruct((phases, cells // 2, count, wide), BF)
    mean_p, target_p = call(
        gather_kernel,
        [patch_shape, patch_shape],
        (top, left, mean, mean_low, own_target, target_low),
        (SM, SM) + (VM,) * 4,
        [pltpu.VMEM((2 * height - 1, width, wide), F32)] * 2 + [pltpu.VMEM((cells // 2 * count, wide), F32)] * 2,
    )

    weights_one = forward_weights(conv_one, True)
    weights_two = forward_weights(conv_two, False)
    weights_back = backward_weights(conv_two)
    zero = jnp.zeros_like(out_proj)
    proj_back = jnp.concatenate(
        [jnp.concatenate([out_proj, zero], axis=1), jnp.concatenate([zero, out_proj], axis=1)], axis=0
    )
    proj_out = proj_back.T

    total = cells // 2 * count
    rows_used = 18 * depth + channels + levels
    table = None
    losses = []
    for chunk in range(phases):
        pad = pltpu.VMEM((height + 2, height // 2 + 2, count, wide), BF)
        rim = pltpu.VMEM((height + 2, height // 2, count, wide), BF)
        ins = (source, phase, step) + tuple(arrived[: chunk + 1])
        ins += (mean_p[chunk : chunk + 1], target_p[chunk : chunk + 1])
        ins += (factors[:, chunk * count : (chunk + 1) * count], step_embed)
        ins += (weights_one, weights_two, weights_back, proj_out, proj_back)
        ins += (table,) if chunk > 0 else ()
        table, loss = call(
            functools.partial(chunk_kernel, chunk, chunk == phases - 1, chunk + 1),
            [jax.ShapeDtypeStruct((rows_used, wide), F32), jax.ShapeDtypeStruct((count, wide), F32)],
            ins,
            (SM,) * 3 + (VM,) * (len(ins) - 3),
            [
                pltpu.VMEM((total, wide), F32),
                pad,
                pad,
                rim,
                rim,
                pad,
                pad,
                pad,
                pad,
                pltpu.VMEM((total, 2 * wide), F32),
                pltpu.VMEM((total, wide), F32),
                pltpu.VMEM((total, wide), F32),
                pltpu.VMEM((total, 2 * wide), BF),
                pltpu.VMEM((total, wide), BF),
                pltpu.VMEM((2 * wide, total), BF),
                pltpu.VMEM((count, wide), F32),
            ],
        )
        losses.append(loss)

    patch_loss = weight * (jnp.sum(jnp.concatenate(losses), axis=1) / (channels * cells))
    by_owner = jnp.sum(jnp.where(owner_in_order[None, :] == ids[:, None], patch_loss[None, :], 0.0), axis=1)
    samples = lax.axis_size("segment") * lax.axis_size("dp")
    sample = lax.axis_index("segment") * lax.axis_size("dp") + lax.axis_index("dp")
    spread = jnp.where(jnp.arange(samples)[:, None] == sample, by_owner[None, :], 0.0).reshape(-1)
    loss_rows = -(-samples * strips // wide)
    spread = jnp.pad(spread, (0, loss_rows * wide - samples * strips)).reshape(loss_rows, wide)
    coarse_part = rounded_to_bf16(spread)
    unit = 2 * lax.axis_size("dp") * 16
    rows_all = -(-(rows_used + 2 * loss_rows) // unit) * unit
    table = jnp.concatenate(
        [
            table,
            coarse_part,
            spread - coarse_part,
            jnp.zeros((rows_all - rows_used - 2 * loss_rows, wide), F32),
        ],
        axis=0,
    )

    cores, groups = lax.axis_size("segment"), lax.axis_size("dp")
    kept = scatter_sum(table.reshape(cores, rows_all // cores, wide), "segment")
    kept = scatter_sum(kept.reshape(groups, rows_all // cores // groups, wide), "dp")
    kept = rows_sum(kept, "rows")
    piece_rows = rows_all // cores // groups
    ending = (lax.axis_index("segment") == cores - 1) & (lax.axis_index("dp") == groups - 1)
    at = rows_used - (rows_all - piece_rows)
    exact = kept[at : at + loss_rows] + kept[at + loss_rows : at + 2 * loss_rows]
    rounded = rounded_to_bf16(exact)
    pair = jnp.concatenate([rounded, exact - rounded], axis=0)
    pair = jnp.where(ending, pair, kept[at : at + 2 * loss_rows])
    kept = rounded_to_bf16(lax.dynamic_update_slice_in_dim(kept, pair, at, 0)).astype(BF)
    kept = gather_all(kept, "dp").reshape(rows_all // cores, wide)
    table = gather_all(kept, "segment").reshape(rows_all, wide).astype(F32)

    def assembled(at):
        block = table[at : at + 9 * depth].reshape(9, depth, wide)
        return jnp.transpose(block, (1, 0, 2)).reshape(depth, 9 * wide)

    loss_table = (
        table[rows_used : rows_used + loss_rows] + table[rows_used + loss_rows : rows_used + 2 * loss_rows]
    ).reshape(-1)
    owner_loss = lax.dynamic_slice_in_dim(loss_table, sample * strips + me, 1).reshape(1, 1)
    return (
        jnp.transpose(mean, (1, 0, 2))[None],
        owner_loss,
        assembled(0),
        assembled(9 * depth),
        table[18 * depth : 18 * depth + channels],
        table[18 * depth + channels : rows_used],
    )


def solution(mesh):
    placed = (
        P(("segment", "dp"), None, "rows", None),
        P(("segment", "dp"), None, "rows", None),
        P(("segment", "dp"), "rows", None, None, None),
        P(("segment", "dp"), None, None, None),
        P(),
        P(),
        P(),
        P(),
        P(),
        P(),
    )
    return jax.shard_map(
        per_device,
        mesh=mesh,
        in_specs=placed,
        out_specs=(
            P(("segment", "dp"), None, "rows", None),
            P(("segment", "dp"), "rows"),
            P(),
            P(),
            P(),
            P(),
        ),
        check_vma=False,
    )
```

time: 721 us -> 138 us (0.19)
  matrix products: 190 us -> 0 us
  waiting for transfers between devices: 200 us -> 28.2 us
  local copies, waits for them, and re-layouts: 146 us -> 30.8 us
  other arithmetic: 109 us -> 7.78 us
  blocking collectives: 38.8 us -> 0 us
  Pallas kernels: 0 us -> 35.5 us
  starting transfers between devices: 12.6 us -> 33.7 us
  between operations: 14.4 us -> 1.56 us
    dot_general x129 -> x0, matrix products: 190 us -> none  [product(): return jnp.einsum(form, left, right, preferred_element_type=jnp.float32)]
    all_to_all x1 -> x0, waiting for transfers between devices: 90.6 us -> none  [per_device(): lax.all_to_all(outgoing, 'rows', split_axis=0, concat_axis=0, tiled=True)]
    psum x1 -> x0, waiting for transfers between devices: 90.4 us -> none  [per_device(): lax.psum((gradients[0], gradients[1], gradients[2], gradients[3]), ('segm...]
    psum x1 -> x0, blocking collectives: 38.8 us -> none  [per_device(): lax.psum((gradients[0], gradients[1], gradients[2], gradients[3]), ('segm...]
    concatenate x2 -> x6, local copies, waits for them, and re-layouts: 41.9 us -> 6.12 us  [the longest x1 3.13 us: per_device(): jnp.concatenate([table, coarse_part, spread - coarse_part, jnp.zeros((row...]
    pallas_call x0 -> x5, Pallas kernels: none -> 35.5 us  [call(): pl.pallas_call(kernel, out_shape=outs, in_specs=list(specs), out_specs=ja...]
    while x256 -> x0, other arithmetic: 34.1 us -> none
    ppermute x3 -> x21, starting transfers between devices: 7.67 us -> 33.7 us  [the longest x6 13 us: per_device(): lax.ppermute(packed[f * strips + d], 'rows', by_distance('rows', d))]
  transfers between devices with their start and end apart: 5 -> 21, of which waited for: 4 -> 11; matrix products, arithmetic and copies ran while one was open for 1% -> 15% of each run, Pallas kernels for 0% -> 7%
where the time goes in v1:
time: 138 us; the launch traced here: 137 us
  Pallas kernels  35.5 us (26%)
  starting transfers between devices  33.7 us (24%)
  local copies, waits for them, and re-layouts  30.8 us (22%)
  waiting for transfers between devices  28.2 us (20%)
  other arithmetic  7.78 us (6%)
  between operations  1.56 us (1%)
    pallas_call x5, Pallas kernels, call(): pl.pallas_call(kernel, out_shape=outs, in_specs=list(specs), out_specs=ja...  35.5 us
    unnamed x85, local copies, waits for them, and re-layouts  15.7 us
    ppermute x6, starting transfers between devices, per_device(): lax.ppermute(packed[f * strips + d], 'rows', by_distance('rows', d))  13 us
    ppermute x6, waiting for transfers between devices, per_device(): lax.ppermute(packed[f * strips + d], 'rows', by_distance('rows', d))  12.3 us
    ppermute x4, waiting for transfers between devices, scatter_sum(): lax.ppermute(take(values, me ^ d).astype(BF), axis, by_distance(axis, d))  6.39 us
    ppermute x1, starting transfers between devices, per_device(): coarse_above = lax.ppermute(own_coarse[height - 1:], 'rows', up)  4.92 us
    ppermute x3, waiting for transfers between devices, rows_sum(): values.append(lax.ppermute(values[0], axis, by_distance(axis, d)))  4.83 us
    ppermute x4, waiting for transfers between devices, gather_all(): lax.ppermute(piece, axis, by_distance(axis, d))  4.71 us
  transfers between devices with their start and end apart: 21, of which 11 were waited for; matrix products, arithmetic and copies ran while one was open for 15% of the time, Pallas kernels for 7%

profile of v1, /device:TPU:0, one launch (start us, length us, event | category | flops | bytes accessed | tf_op | source)
XLA Modules:
  0.0 137.5 jit_solution(12552623526142354620)
XLA Ops:
  0.6 1.5 %fusion.30 = (bf16[1,100,256]{2,1,0:T(8,128)(2,1)}, bf16[1,100,256]{2,1,0:T(8,128)(2,1)}) fusion(bf16[12,100,256]{2,1,0:T(8,128)(2,1)} %bitcast.119), kind=kLoop, calls=%fused_computation.191 | loop fusion | bytes 204800 | tf_op jit(solution)/shard_map/slice | solution.py:414
  2.1 4.9 %collective-permute-start = (bf16[1,100,256]{2,1,0:T(8,128)(2,1)}, bf16[1,100,256]{2,1,0:T(8,128)(2,1)S(1)}, u32[]{:S(2)}, u32[]{:S(2)}) collective-permute-start(bf16[1,100,256]{2,1,0:T(8,128)(2,1)} %get-tuple-element.61), channel_id=1, source_target_pairs={{0,4},{4,8},{8,12},{1,5},{5,9},{9,13},{2,6},{6,10},{10,14},{3,7},{... | collective-permute-start | bytes 153608 | tf_op jit(solution)/shard_map/ppermute | solution.py:413
  7.0 1.3 collective-permute-start.1
  8.4 0.9 fusion.21
  9.7 1.6 %copy-done.1 = bf16[1,1,64,64,144]{4,3,2,1,0:T(8,128)(2,1)S(1)} copy-done((bf16[1,1,64,64,144]{4,3,2,1,0:T(8,128)(2,1)S(1)}, bf16[1,1,64,64,144]{4,3,2,1,0:T(8,128)(2,1)}, u32[]{:S(2)}) %copy-start.1) | copy-done | bytes 1179672
  11.3 2.7 %shard_map.146 = (bf16[8,72,128]{2,1,0:T(8,128)(2,1)S(1)}, bf16[8,72,128]{2,1,0:T(8,128)(2,1)}, bf16[8,72,128]{2,1,0:T(8,128)(2,1)}, bf16[8,72,128]{2,1,0:T(8,12...) custom-call(s32[64]{0:T(128)S(1)} %min.12.slots_ref, ...), custom_call_target="tpu_custom_call" | custom-call | bytes 1048576 | tf_op jit(solution)/shard_map/pallas_call | solution.py:32
  14.0 0.7 copy-done.7
  14.6 0.7 copy-done.11
  15.3 0.7 copy-done.13
  16.0 2.6 %collective-permute-start.2 = (bf16[8,72,128]{2,1,0:T(8,128)(2,1)}, bf16[8,72,128]{2,1,0:T(8,128)(2,1)}, u32[]{:S(2)}, u32[]{:S(2)}) collective-permute-start(bf16[8,72,128]{2,1,0:T(8,128)(2,1)} %get-tuple-element.21), channel_id=1, source_target_pairs={{0,4},{4,0},{8,12},{12,8},{1,5},{5,1},{9,13},{13,9},{2,6},{6,2},{1... | collective-permute-start | bytes 442376 | tf_op jit(solution)/shard_map/ppermute | solution.py:466
  18.6 2.6 %collective-permute-start.3 = (bf16[8,72,128]{2,1,0:T(8,128)(2,1)}, bf16[8,72,128]{2,1,0:T(8,128)(2,1)}, u32[]{:S(2)}, u32[]{:S(2)}) collective-permute-start(bf16[8,72,128]{2,1,0:T(8,128)(2,1)} %get-tuple-element.22), channel_id=1, source_target_pairs={{0,8},{4,12},{8,0},{12,4},{1,9},{5,13},{9,1},{13,5},{2,10},{6,14},... | collective-permute-start | bytes 442376 | tf_op jit(solution)/shard_map/ppermute | solution.py:466
  21.2 0.7 fusion.20
  22.3 0.6 select_reduce_fusion
  25.3 0.6 constant_dynamic-update-slice_fusion.39
  25.9 0.7 constant_dynamic-update-slice_fusion.38
  26.6 0.6 constant_dynamic-update-slice_fusion.37
  27.2 0.6 constant_dynamic-update-slice_fusion.36
  27.9 0.6 constant_dynamic-update-slice_fusion.35
  28.5 0.6 constant_dynamic-update-slice_fusion.34
  29.2 0.7 constant_dynamic-update-slice_fusion.33
  29.8 0.6 constant_dynamic-update-slice_fusion.32
  30.5 0.6 constant_dynamic-update-slice_fusion.31
  31.1 0.6 constant_dynamic-update-slice_fusion.30
  31.7 0.6 constant_dynamic-update-slice_fusion.29
  32.4 0.6 constant_dynamic-update-slice_fusion.28
  33.8 1.0 reshape.234
  35.0 0.8 slice.286
  35.7 1.4 %copy.78.refs_9_.refs_10_ = bf16[1536,256]{1,0:T(8,128)(2,1)S(1)} copy(bf16[1536,256]{0,1:T(8,128)(2,1)} %constant_dynamic-update-slice_fusion.28) | data formatting | bytes 1572864 | tf_op jit(solution)/shard_map/concatenate | solution.py:324
  37.3 1.3 collective-permute-start.9
  38.6 2.7 %collective-permute-start.5 = (bf16[8,72,128]{2,1,0:T(8,128)(2,1)}, bf16[8,72,128]{2,1,0:T(8,128)(2,1)S(1)}, u32[]{:S(2)}, u32[]{:S(2)}) collective-permute-start(bf16[8,72,128]{2,1,0:T(8,128)(2,1)} %copy-done.15), channel_id=1, source_target_pairs={{0,4},{4,0},{8,12},{12,8},{1,5},{5,1},{9,13},{13,9},{2,6},{6,2},{1... | collective-permute-start | bytes 442376 | tf_op jit(solution)/shard_map/ppermute | solution.py:466
  41.3 1.1 copy-done.6
  42.4 6.6 %shard_map.145.mean_ref = bf16[12,64,256]{2,1,0:T(8,128)(2,1)} custom-call(bf16[1,100,256]{2,1,0:T(8,128)(2,1)S(1)} %collective-permute-done.above_ref, bf16[12,100,256]{2,1,0:T(8,128)(2,1)S(1)} %bitcast.120, bf16[1,100,256]{2,1,0:T(8,128)(2,1)S(1)} %collective-permute-done.1.below_ref, bf16[128,1008]{1,0:T(8,128)(2,1)S(1)} %copy.66.conv_ref, ...), custom_call_target="tpu_custom_call" | custom-call | bytes 1048576 | tf_op jit(solution)/shard_map/pallas_call | solution.py:32
  49.0 1.1 slice.285
  50.1 1.3 collective-permute-start.8
  51.4 0.9 constant_dynamic-update-slice_fusion.2
  52.4 2.6 %collective-permute-start.6 = (bf16[8,72,128]{2,1,0:T(8,128)(2,1)S(1)}, bf16[8,72,128]{2,1,0:T(8,128)(2,1)S(1)}, u32[]{:S(2)}, u32[]{:S(2)}) collective-permute-start(bf16[8,72,128]{2,1,0:T(8,128)(2,1)S(1)} %copy-done.14), channel_id=1, source_target_pairs={{0,8},{4,12},{8,0},{12,4},{1,9},{5,13},{9,1},{13,5},{2,10},{6,14},... | collective-permute-start | bytes 442376 | tf_op jit(solution)/shard_map/ppermute | solution.py:466
  55.0 2.5 %collective-permute-start.7 = (bf16[8,72,128]{2,1,0:T(8,128)(2,1)S(1)}, bf16[8,72,128]{2,1,0:T(8,128)(2,1)S(1)}, u32[]{:S(2)}, u32[]{:S(2)}) collective-permute-start(bf16[8,72,128]{2,1,0:T(8,128)(2,1)S(1)} %copy-done.12), channel_id=1, source_target_pairs={{0,12},{4,8},{8,4},{12,0},{1,13},{5,9},{9,5},{13,1},{2,14},{6,10},... | collective-permute-start | bytes 442376 | tf_op jit(solution)/shard_map/ppermute | solution.py:466
  57.4 0.9 constant_dynamic-update-slice_fusion.1
  58.4 0.9 constant_dynamic-update-slice_fusion.refs_3_
  59.3 12.2 %collective-permute-done.6 = bf16[8,72,128]{2,1,0:T(8,128)(2,1)S(1)} collective-permute-done((bf16[8,72,128]{2,1,0:T(8,128)(2,1)S(1)}, bf16[8,72,128]{2,1,0:T(8,128)(2,1)S(1)}, u32[]{:S(2)}, u32[]{:S(2)}) %collective-permute-start.6) | collective-permute-done | bytes 147488 | tf_op jit(solution)/shard_map/ppermute | solution.py:466
  71.7 8.8 %shard_map.147 = (bf16[2,72,16,128]{3,2,1,0:T(8,128)(2,1)S(1)}, bf16[2,72,16,128]{3,2,1,0:T(8,128)(2,1)S(1)}) custom-call(s32[32]{0:T(128)S(1)} %get-tuple-element.54.row_ref, s32[32]{0:T(128)S(1)} %get-tuple-element.53.col_ref, bf16[12,64,256]{2,1,0:T(8,128)(2,1)S(1)} %copy-done, bf16[11,64,256]{2,1,0:T(8,128)(2,1)S(1)} %collective-permute-done.8.mean_low_ref, ...), custom_call_target="tpu_custom_call" | custom-call | bytes 1048576 | tf_op jit(solution)/shard_map/pallas_call | solution.py:32
  81.3 8.2 %shard_map.148 = (f32[2400,128]{1,0:T(8,128)S(1)}, f32[16,128]{1,0:T(8,128)S(1)}) custom-call(s32[32]{0:T(128)S(1)} %get-tuple-element.57.refs_0_, s32[32]{0:T(128)S(1)} %get-tuple-element.56.refs_1_, s32[32]{0:T(128)S(1)} %get-tuple-element.55.refs_2_, bf16[32,72,128]{2,1,0:T(8,128)(2,1)S(1)} %constant_dynamic-update-slice_fusion.refs_3_, ...), custom_call_target="tpu_custom_call" | custom-call | bytes 1048576 | tf_op jit(solution)/shard_map/pallas_call | solution.py:32
  89.4 1.0 copy-done.5
  90.6 9.2 %shard_map.149 = (f32[2400,128]{1,0:T(8,128)S(1)}, f32[16,128]{1,0:T(8,128)S(1)}) custom-call(s32[32]{0:T(128)S(1)} %get-tuple-element.57.refs_0_, s32[32]{0:T(128)S(1)} %get-tuple-element.56.refs_1_, s32[32]{0:T(128)S(1)} %get-tuple-element.55.refs_2_, bf16[32,72,128]{2,1,0:T(8,128)(2,1)S(1)} %constant_dynamic-update-slice_fusion.refs_3_, ...), custom_call_target="tpu_custom_call" | custom-call | bytes 1048576 | tf_op jit(solution)/shard_map/pallas_call | solution.py:32
  99.8 1.0 copy-done.4
  101.3 3.1 %concatenate.186 = f32[2432,128]{1,0:T(8,128)S(1)} concatenate(f32[2400,128]{1,0:T(8,128)} %copy-done.4, f32[1,128]{1,0:T(1,128)S(1)} %get-tuple-element.110, f32[1,128]{1,0:T(1,128)S(1)} %get-tuple-element.109, f32[30,128]{1,0:T(8,128)S(1)} %broadcast_in_dim.151), dimensions={0} | concatenate | bytes 2490368 | tf_op jit(solution)/shard_map/concatenate | solution.py:548
  104.6 1.6 %collective-permute-done.10 = bf16[1216,128]{1,0:T(8,128)(2,1)S(1)} collective-permute-done((bf16[1216,128]{1,0:T(8,128)(2,1)S(1)}, bf16[1216,128]{1,0:T(8,128)(2,1)S(1)}, u32[]{:S(2)}, u32[]{:S(2)}) %collective-permute-start.10) | collective-permute-done | bytes 311328 | tf_op jit(solution)/shard_map/ppermute | solution.py:356
  106.2 1.6 %collective-permute-start.11 = (bf16[304,128]{1,0:T(8,128)(2,1)S(1)}, bf16[304,128]{1,0:T(8,128)(2,1)S(1)}, u32[]{:S(2)}, u32[]{:S(2)}) collective-permute-start(bf16[304,128]{1,0:T(8,128)(2,1)S(1)} %get-tuple-element.64), channel_id=1, source_target_pairs={{0,1},{1,0},{2,3},{3,2},{4,5},{5,4},{6,7},{7,6},{8,9},{9,8},{10,11... | collective-permute-start | bytes 233480 | tf_op jit(solution)/shard_map/ppermute | solution.py:356
  107.8 1.5 %collective-permute-start.12 = (bf16[304,128]{1,0:T(8,128)(2,1)S(1)}, bf16[304,128]{1,0:T(8,128)(2,1)S(1)}, u32[]{:S(2)}, u32[]{:S(2)}) collective-permute-start(bf16[304,128]{1,0:T(8,128)(2,1)S(1)} %get-tuple-element.66), channel_id=1, source_target_pairs={{0,2},{1,3},{2,0},{3,1},{4,6},{5,7},{6,4},{7,5},{8,10},{9,11},{10,... | collective-permute-start | bytes 233480 | tf_op jit(solution)/shard_map/ppermute | solution.py:356
  109.8 0.9 collective-permute-done.11
  110.7 1.5 %collective-permute-done.12 = bf16[304,128]{1,0:T(8,128)(2,1)S(1)} collective-permute-done((bf16[304,128]{1,0:T(8,128)(2,1)S(1)}, bf16[304,128]{1,0:T(8,128)(2,1)S(1)}, u32[]{:S(2)}, u32[]{:S(2)}) %collective-permute-start.12) | collective-permute-done | bytes 77856 | tf_op jit(solution)/shard_map/ppermute | solution.py:356
  112.2 2.4 %collective-permute-done.13 = bf16[304,128]{1,0:T(8,128)(2,1)S(1)} collective-permute-done((bf16[304,128]{1,0:T(8,128)(2,1)S(1)}, bf16[304,128]{1,0:T(8,128)(2,1)S(1)}, u32[]{:S(2)}, u32[]{:S(2)}) %collective-permute-start.13) | collective-permute-done | bytes 77856 | tf_op jit(solution)/shard_map/ppermute | solution.py:356
  114.7 2.2 %collective-permute-start.14 = (bf16[304,128]{1,0:T(8,128)(2,1)S(1)}, bf16[304,128]{1,0:T(8,128)(2,1)S(1)}, u32[]{:S(2)}, u32[]{:S(2)}) collective-permute-start(bf16[304,128]{1,0:T(8,128)(2,1)S(1)} %fusion.4), channel_id=1, source_target_pairs={{0,4},{4,0},{8,12},{12,8},{1,5},{5,1},{9,13},{13,9},{2,6},{6,2},{1... | collective-permute-start | bytes 233480 | tf_op jit(solution)/shard_map/ppermute | solution.py:383
  116.8 2.4 %collective-permute-start.16 = (bf16[304,128]{1,0:T(8,128)(2,1)S(1)}, bf16[304,128]{1,0:T(8,128)(2,1)S(1)}, u32[]{:S(2)}, u32[]{:S(2)}) collective-permute-start(bf16[304,128]{1,0:T(8,128)(2,1)S(1)} %fusion.4), channel_id=1, source_target_pairs={{0,12},{4,8},{8,4},{12,0},{1,13},{5,9},{9,5},{13,1},{2,14},{6,10},... | collective-permute-start | bytes 233480 | tf_op jit(solution)/shard_map/ppermute | solution.py:383
  119.3 1.6 %collective-permute-done.14 = bf16[304,128]{1,0:T(8,128)(2,1)S(1)} collective-permute-done((bf16[304,128]{1,0:T(8,128)(2,1)S(1)}, bf16[304,128]{1,0:T(8,128)(2,1)S(1)}, u32[]{:S(2)}, u32[]{:S(2)}) %collective-permute-start.14) | collective-permute-done | bytes 77856 | tf_op jit(solution)/shard_map/ppermute | solution.py:383
  120.9 3.2 %collective-permute-done.15 = bf16[304,128]{1,0:T(8,128)(2,1)S(1)} collective-permute-done((bf16[304,128]{1,0:T(8,128)(2,1)S(1)}, bf16[304,128]{1,0:T(8,128)(2,1)S(1)}, u32[]{:S(2)}, u32[]{:S(2)}) %collective-permute-start.15) | collective-permute-done | bytes 77856 | tf_op jit(solution)/shard_map/ppermute | solution.py:383
  124.2 0.8 collective-permute-start.17
  125.0 1.5 %collective-permute-start.18 = (bf16[304,128]{1,0:T(8,128)(2,1)S(1)}, bf16[304,128]{1,0:T(8,128)(2,1)S(1)}, u32[]{:S(2)}, u32[]{:S(2)}) collective-permute-start(bf16[304,128]{1,0:T(8,128)(2,1)S(1)} %reduce-precision_convert_fusion), channel_id=1, source_target_pairs={{0,2},{1,3},{2,0},{3,1},{4,6},{5,7},{6,4},{7,5},{8,10},{9,11},{10,... | collective-permute-start | bytes 233480 | tf_op jit(solution)/shard_map/ppermute | solution.py:366
  126.5 1.3 collective-permute-start.19
  127.8 1.9 %collective-permute-done.17 = bf16[304,128]{1,0:T(8,128)(2,1)S(1)} collective-permute-done((bf16[304,128]{1,0:T(8,128)(2,1)S(1)}, bf16[304,128]{1,0:T(8,128)(2,1)S(1)}, u32[]{:S(2)}, u32[]{:S(2)}) %collective-permute-start.17) | collective-permute-done | bytes 77856 | tf_op jit(solution)/shard_map/ppermute | solution.py:366
  130.3 0.6 collective-permute-done.19
  131.2 1.6 %collective-permute-done.20 = bf16[1216,128]{1,0:T(8,128)(2,1)S(1)} collective-permute-done((bf16[1216,128]{1,0:T(8,128)(2,1)S(1)}, bf16[1216,128]{1,0:T(8,128)(2,1)S(1)}, u32[]{:S(2)}, u32[]{:S(2)}) %collective-permute-start.20) | collective-permute-done | bytes 311328 | tf_op jit(solution)/shard_map/ppermute | solution.py:366
  134.5 1.1 copy.82
  135.8 1.1 copy.83
  (155 shorter events, 9.4 us)
Async XLA Ops:
  2.1 35.2 %collective-permute-start = (bf16[1,100,256]{2,1,0:T(8,128)(2,1)}, bf16[1,100,256]{2,1,0:T(8,128)(2,1)S(1)}, u32[]{:S(2)}, u32[]{:S(2)}) collective-permute-start(bf16[1,100,256]{2,1,0:T(8,128)(2,1)} %get-tuple-element.61), channel_id=1, source_target_pairs={{0,4},{4,8},{8,12},{1,5},{5,9},{9,13},{2,6},{6,10},{10,14},{3,7},{... | collective-permute-start | bytes 153608 | tf_op jit(solution)/shard_map/ppermute | solution.py:413
  7.0 31.6 %collective-permute-start.1 = (bf16[1,100,256]{2,1,0:T(8,128)(2,1)}, bf16[1,100,256]{2,1,0:T(8,128)(2,1)S(1)}, u32[]{:S(2)}, u32[]{:S(2)}) collective-permute-start(bf16[1,100,256]{2,1,0:T(8,128)(2,1)} %get-tuple-element.60), channel_id=1, source_target_pairs={{4,0},{8,4},{12,8},{5,1},{9,5},{13,9},{6,2},{10,6},{14,10},{7,3},{... | collective-permute-start | bytes 153608 | tf_op jit(solution)/shard_map/ppermute | solution.py:414
  9.7 1.6 %copy-start.1 = (bf16[1,1,64,64,144]{4,3,2,1,0:T(8,128)(2,1)S(1)}, bf16[1,1,64,64,144]{4,3,2,1,0:T(8,128)(2,1)}, u32[]{:S(2)}) copy-start(bf16[1,1,64,64,144]{4,3,2,1,0:T(8,128)(2,1)} %param.12) | copy-start | bytes 3538948
  11.3 11.7 %copy-start.16 = (bf16[128,1152]{1,0:T(8,128)(2,1)S(1)}, bf16[128,1152]{1,0:T(8,128)(2,1)}, u32[]{:S(2)}) copy-start(bf16[128,1152]{1,0:T(8,128)(2,1)} %param.17) | copy-start | bytes 884740
  11.3 11.8 %copy-start.17 = (bf16[128,1152]{1,0:T(8,128)(2,1)S(1)}, bf16[128,1152]{1,0:T(8,128)(2,1)}, u32[]{:S(2)}) copy-start(bf16[128,1152]{1,0:T(8,128)(2,1)} %param.16) | copy-start | bytes 884740
  14.0 0.7 copy-start.7
  14.6 0.7 copy-start.11
  15.3 0.7 copy-start.13
  16.0 7.6 %copy-start.15 = (bf16[8,72,128]{2,1,0:T(8,128)(2,1)}, bf16[8,72,128]{2,1,0:T(8,128)(2,1)S(1)}, u32[]{:S(2)}) copy-start(bf16[8,72,128]{2,1,0:T(8,128)(2,1)S(1)} %get-tuple-element.25) | copy-start | bytes 442372
  16.0 34.1 %collective-permute-start.2 = (bf16[8,72,128]{2,1,0:T(8,128)(2,1)}, bf16[8,72,128]{2,1,0:T(8,128)(2,1)}, u32[]{:S(2)}, u32[]{:S(2)}) collective-permute-start(bf16[8,72,128]{2,1,0:T(8,128)(2,1)} %get-tuple-element.21), channel_id=1, source_target_pairs={{0,4},{4,0},{8,12},{12,8},{1,5},{5,1},{9,13},{13,9},{2,6},{6,2},{1... | collective-permute-start | bytes 442376 | tf_op jit(solution)/shard_map/ppermute | solution.py:466
  18.6 33.7 %collective-permute-start.3 = (bf16[8,72,128]{2,1,0:T(8,128)(2,1)}, bf16[8,72,128]{2,1,0:T(8,128)(2,1)}, u32[]{:S(2)}, u32[]{:S(2)}) collective-permute-start(bf16[8,72,128]{2,1,0:T(8,128)(2,1)} %get-tuple-element.22), channel_id=1, source_target_pairs={{0,8},{4,12},{8,0},{12,4},{1,9},{5,13},{9,1},{13,5},{2,10},{6,14},... | collective-permute-start | bytes 442376 | tf_op jit(solution)/shard_map/ppermute | solution.py:466
  21.2 33.8 %collective-permute-start.4 = (bf16[8,72,128]{2,1,0:T(8,128)(2,1)}, bf16[8,72,128]{2,1,0:T(8,128)(2,1)}, u32[]{:S(2)}, u32[]{:S(2)}) collective-permute-start(bf16[8,72,128]{2,1,0:T(8,128)(2,1)} %get-tuple-element.23), channel_id=1, source_target_pairs={{0,12},{4,8},{8,4},{12,0},{1,13},{5,9},{9,5},{13,1},{2,14},{6,10},... | collective-permute-start | bytes 442376 | tf_op jit(solution)/shard_map/ppermute | solution.py:466
  26.6 6.6 %copy-start.18 = (bf16[64,128]{1,0:T(8,128)(2,1)S(1)}, bf16[64,128]{1,0:T(8,128)(2,1)}, u32[]{:S(2)}) copy-start(bf16[64,128]{1,0:T(8,128)(2,1)} %param.18) | copy-start | bytes 49156
  33.1 1.9 %copy-start.2 = (bf16[1,64,12,256]{3,1,2,0:T(8,128)(2,1)S(1)}, bf16[1,64,12,256]{3,1,2,0:T(8,128)(2,1)}, u32[]{:S(2)}) copy-start(bf16[1,64,12,256]{3,1,2,0:T(8,128)(2,1)} %param.11) | copy-start | bytes 1179652
  35.0 6.3 %copy-start.10 = (bf16[64,128]{1,0:T(8,128)(2,1)S(1)}, bf16[64,128]{1,0:T(8,128)(2,1)}, u32[]{:S(2)}) copy-start(bf16[64,128]{1,0:T(8,128)(2,1)} %proj_ref.1) | copy-start | bytes 49156
  37.3 34.4 %collective-permute-start.9 = (bf16[11,64,256]{2,1,0:T(8,128)(2,1)}, bf16[11,64,256]{2,1,0:T(8,128)(2,1)S(1)}, u32[]{:S(2)}, u32[]{:S(2)}) collective-permute-start(bf16[11,64,256]{2,1,0:T(8,128)(2,1)} %slice.286), channel_id=1, source_target_pairs={{4,0},{8,4},{12,8},{5,1},{9,5},{13,9},{6,2},{10,6},{14,10},{7,3},{... | collective-permute-start | bytes 1081352 | tf_op jit(solution)/shard_map/ppermute | solution.py:412
  38.6 20.7 %collective-permute-start.5 = (bf16[8,72,128]{2,1,0:T(8,128)(2,1)}, bf16[8,72,128]{2,1,0:T(8,128)(2,1)S(1)}, u32[]{:S(2)}, u32[]{:S(2)}) collective-permute-start(bf16[8,72,128]{2,1,0:T(8,128)(2,1)} %copy-done.15), channel_id=1, source_target_pairs={{0,4},{4,0},{8,12},{12,8},{1,5},{5,1},{9,13},{13,9},{2,6},{6,2},{1... | collective-permute-start | bytes 442376 | tf_op jit(solution)/shard_map/ppermute | solution.py:466
  41.3 1.1 copy-start.6
  42.4 10.0 %copy-start.14 = (bf16[8,72,128]{2,1,0:T(8,128)(2,1)S(1)}, bf16[8,72,128]{2,1,0:T(8,128)(2,1)}, u32[]{:S(2)}) copy-start(bf16[8,72,128]{2,1,0:T(8,128)(2,1)} %copy-done.13) | copy-start | bytes 442372
  42.4 12.6 %copy-start.12 = (bf16[8,72,128]{2,1,0:T(8,128)(2,1)S(1)}, bf16[8,72,128]{2,1,0:T(8,128)(2,1)}, u32[]{:S(2)}) copy-start(bf16[8,72,128]{2,1,0:T(8,128)(2,1)} %copy-done.11) | copy-start | bytes 442372
  42.4 29.2 %copy-start.8 = (bf16[8,72,128]{2,1,0:T(8,128)(2,1)S(1)}, bf16[8,72,128]{2,1,0:T(8,128)(2,1)}, u32[]{:S(2)}) copy-start(bf16[8,72,128]{2,1,0:T(8,128)(2,1)} %copy-done.7) | copy-start | bytes 442372
  49.0 22.7 %copy-start = (bf16[12,64,256]{2,1,0:T(8,128)(2,1)S(1)}, bf16[12,64,256]{2,1,0:T(8,128)(2,1)}, u32[]{:S(2)}) copy-start(bf16[12,64,256]{2,1,0:T(8,128)(2,1)} %shard_map.145.mean_ref) | copy-start | bytes 1179652
  49.0 22.7 %copy-start.3 = (bf16[1,64,12,256]{3,1,2,0:T(8,128)(2,1)S(1)}, bf16[1,64,12,256]{3,1,2,0:T(8,128)(2,1)}, u32[]{:S(2)}) copy-start(bf16[1,64,12,256]{3,1,2,0:T(8,128)(2,1)} %param.11) | copy-start | bytes 1179652
  50.1 21.6 %collective-permute-start.8 = (bf16[11,64,256]{2,1,0:T(8,128)(2,1)S(1)}, bf16[11,64,256]{2,1,0:T(8,128)(2,1)S(1)}, u32[]{:S(2)}, u32[]{:S(2)}) collective-permute-start(bf16[11,64,256]{2,1,0:T(8,128)(2,1)S(1)} %slice.285), channel_id=1, source_target_pairs={{4,0},{8,4},{12,8},{5,1},{9,5},{13,9},{6,2},{10,6},{14,10},{7,3},{... | collective-permute-start | bytes 1081352 | tf_op jit(solution)/shard_map/ppermute | solution.py:481
  52.4 19.2 %collective-permute-start.6 = (bf16[8,72,128]{2,1,0:T(8,128)(2,1)S(1)}, bf16[8,72,128]{2,1,0:T(8,128)(2,1)S(1)}, u32[]{:S(2)}, u32[]{:S(2)}) collective-permute-start(bf16[8,72,128]{2,1,0:T(8,128)(2,1)S(1)} %copy-done.14), channel_id=1, source_target_pairs={{0,8},{4,12},{8,0},{12,4},{1,9},{5,13},{9,1},{13,5},{2,10},{6,14},... | collective-permute-start | bytes 442376 | tf_op jit(solution)/shard_map/ppermute | solution.py:466
  55.0 16.6 %collective-permute-start.7 = (bf16[8,72,128]{2,1,0:T(8,128)(2,1)S(1)}, bf16[8,72,128]{2,1,0:T(8,128)(2,1)S(1)}, u32[]{:S(2)}, u32[]{:S(2)}) collective-permute-start(bf16[8,72,128]{2,1,0:T(8,128)(2,1)S(1)} %copy-done.12), channel_id=1, source_target_pairs={{0,12},{4,8},{8,4},{12,0},{1,13},{5,9},{9,5},{13,1},{2,14},{6,10},... | collective-permute-start | bytes 442376 | tf_op jit(solution)/shard_map/ppermute | solution.py:466
  80.5 0.7 copy-start.19
  80.5 0.8 copy-start.9
  89.4 1.1 copy-start.5
  90.6 10.4 %copy-start.21 = (s32[32]{0:T(128)S(1)}, s32[32]{0:T(128)}, u32[]{:S(2)}) copy-start(s32[32]{0:T(128)} %get-tuple-element.52) | copy-start | bytes 388
  90.6 10.5 %copy-start.20 = (pred[8]{0:T(512)(128)(4,1)S(1)}, pred[8]{0:T(512)(128)(4,1)}, u32[]{:S(2)}) copy-start(pred[8]{0:T(512)(128)(4,1)} %iota_compare_fusion.7) | copy-start | bytes 28
  99.8 1.1 copy-start.4
  104.5 1.7 %collective-permute-start.10 = (bf16[1216,128]{1,0:T(8,128)(2,1)S(1)}, bf16[1216,128]{1,0:T(8,128)(2,1)S(1)}, u32[]{:S(2)}, u32[]{:S(2)}) collective-permute-start(bf16[1216,128]{1,0:T(8,128)(2,1)S(1)} %fusion), channel_id=1, source_target_pairs={{0,16},{16,0},{1,17},{17,1},{2,18},{18,2},{3,19},{19,3},{4,20},{20... | collective-permute-start | bytes 933896 | tf_op jit(solution)/shard_map/ppermute | solution.py:356
  106.2 4.5 %collective-permute-start.11 = (bf16[304,128]{1,0:T(8,128)(2,1)S(1)}, bf16[304,128]{1,0:T(8,128)(2,1)S(1)}, u32[]{:S(2)}, u32[]{:S(2)}) collective-permute-start(bf16[304,128]{1,0:T(8,128)(2,1)S(1)} %get-tuple-element.64), channel_id=1, source_target_pairs={{0,1},{1,0},{2,3},{3,2},{4,5},{5,4},{6,7},{7,6},{8,9},{9,8},{10,11... | collective-permute-start | bytes 233480 | tf_op jit(solution)/shard_map/ppermute | solution.py:356
  107.8 4.4 %collective-permute-start.12 = (bf16[304,128]{1,0:T(8,128)(2,1)S(1)}, bf16[304,128]{1,0:T(8,128)(2,1)S(1)}, u32[]{:S(2)}, u32[]{:S(2)}) collective-permute-start(bf16[304,128]{1,0:T(8,128)(2,1)S(1)} %get-tuple-element.66), channel_id=1, source_target_pairs={{0,2},{1,3},{2,0},{3,1},{4,6},{5,7},{6,4},{7,5},{8,10},{9,11},{10,... | collective-permute-start | bytes 233480 | tf_op jit(solution)/shard_map/ppermute | solution.py:356
  109.3 5.3 %collective-permute-start.13 = (bf16[304,128]{1,0:T(8,128)(2,1)S(1)}, bf16[304,128]{1,0:T(8,128)(2,1)S(1)}, u32[]{:S(2)}, u32[]{:S(2)}) collective-permute-start(bf16[304,128]{1,0:T(8,128)(2,1)S(1)} %get-tuple-element.65), channel_id=1, source_target_pairs={{0,3},{1,2},{2,1},{3,0},{4,7},{5,6},{6,5},{7,4},{8,11},{9,10},{10,... | collective-permute-start | bytes 233480 | tf_op jit(solution)/shard_map/ppermute | solution.py:356
  114.7 6.2 %collective-permute-start.14 = (bf16[304,128]{1,0:T(8,128)(2,1)S(1)}, bf16[304,128]{1,0:T(8,128)(2,1)S(1)}, u32[]{:S(2)}, u32[]{:S(2)}) collective-permute-start(bf16[304,128]{1,0:T(8,128)(2,1)S(1)} %fusion.4), channel_id=1, source_target_pairs={{0,4},{4,0},{8,12},{12,8},{1,5},{5,1},{9,13},{13,9},{2,6},{6,2},{1... | collective-permute-start | bytes 233480 | tf_op jit(solution)/shard_map/ppermute | solution.py:383
  116.8 7.3 %collective-permute-start.15 = (bf16[304,128]{1,0:T(8,128)(2,1)S(1)}, bf16[304,128]{1,0:T(8,128)(2,1)S(1)}, u32[]{:S(2)}, u32[]{:S(2)}) collective-permute-start(bf16[304,128]{1,0:T(8,128)(2,1)S(1)} %fusion.4), channel_id=1, source_target_pairs={{0,8},{4,12},{8,0},{12,4},{1,9},{5,13},{9,1},{13,5},{2,10},{6,14},... | collective-permute-start | bytes 233480 | tf_op jit(solution)/shard_map/ppermute | solution.py:383
  116.8 7.3 %collective-permute-start.16 = (bf16[304,128]{1,0:T(8,128)(2,1)S(1)}, bf16[304,128]{1,0:T(8,128)(2,1)S(1)}, u32[]{:S(2)}, u32[]{:S(2)}) collective-permute-start(bf16[304,128]{1,0:T(8,128)(2,1)S(1)} %fusion.4), channel_id=1, source_target_pairs={{0,12},{4,8},{8,4},{12,0},{1,13},{5,9},{9,5},{13,1},{2,14},{6,10},... | collective-permute-start | bytes 233480 | tf_op jit(solution)/shard_map/ppermute | solution.py:383
  124.2 5.5 %collective-permute-start.17 = (bf16[304,128]{1,0:T(8,128)(2,1)S(1)}, bf16[304,128]{1,0:T(8,128)(2,1)S(1)}, u32[]{:S(2)}, u32[]{:S(2)}) collective-permute-start(bf16[304,128]{1,0:T(8,128)(2,1)S(1)} %reduce-precision_convert_fusion), channel_id=1, source_target_pairs={{0,3},{1,2},{2,1},{3,0},{4,7},{5,6},{6,5},{7,4},{8,11},{9,10},{10,... | collective-permute-start | bytes 233480 | tf_op jit(solution)/shard_map/ppermute | solution.py:366
  125.0 5.2 %collective-permute-start.18 = (bf16[304,128]{1,0:T(8,128)(2,1)S(1)}, bf16[304,128]{1,0:T(8,128)(2,1)S(1)}, u32[]{:S(2)}, u32[]{:S(2)}) collective-permute-start(bf16[304,128]{1,0:T(8,128)(2,1)S(1)} %reduce-precision_convert_fusion), channel_id=1, source_target_pairs={{0,2},{1,3},{2,0},{3,1},{4,6},{5,7},{6,4},{7,5},{8,10},{9,11},{10,... | collective-permute-start | bytes 233480 | tf_op jit(solution)/shard_map/ppermute | solution.py:366
  126.5 4.4 %collective-permute-start.19 = (bf16[304,128]{1,0:T(8,128)(2,1)S(1)}, bf16[304,128]{1,0:T(8,128)(2,1)S(1)}, u32[]{:S(2)}, u32[]{:S(2)}) collective-permute-start(bf16[304,128]{1,0:T(8,128)(2,1)S(1)} %reduce-precision_convert_fusion), channel_id=1, source_target_pairs={{0,1},{1,0},{2,3},{3,2},{4,5},{5,4},{6,7},{7,6},{8,9},{9,8},{10,11... | collective-permute-start | bytes 233480 | tf_op jit(solution)/shard_map/ppermute | solution.py:366
  131.1 1.7 %collective-permute-start.20 = (bf16[1216,128]{1,0:T(8,128)(2,1)S(1)}, bf16[1216,128]{1,0:T(8,128)(2,1)S(1)}, u32[]{:S(2)}, u32[]{:S(2)}) collective-permute-start(bf16[1216,128]{1,0:T(8,128)(2,1)S(1)} %bitcast.129), channel_id=1, source_target_pairs={{0,16},{16,0},{1,17},{17,1},{2,18},{18,2},{3,19},{19,3},{4,20},{20... | collective-permute-start | bytes 933896 | tf_op jit(solution)/shard_map/ppermute | solution.py:366

commit v2 on v1

--- a/solution.py
+++ b/solution.py
@@ -13,31 +13,31 @@
 TAPS = tuple((a, b) for a in (-1, 0, 1) for b in (-1, 0, 1))
 NT_FORM = (((1,), (1,)), ((), ()))
 TN_FORM = (((0,), (0,)), ((), ()))
-LIMIT = 48 * 1024 * 1024
+MIB = 1024 * 1024
 
 
 def matmul(left, right):
     return jnp.dot(left, right, preferred_element_type=F32)
 
 
-def whole(shape):
-    return pl.BlockSpec(memory_space=pltpu.VMEM)
-
-
 VM = pl.BlockSpec(memory_space=pltpu.VMEM)
 SM = pl.BlockSpec(memory_space=pltpu.SMEM)
 
 
-def call(kernel, outs, ins, specs, scratch=(), cost=0):
+def call(kernel, outs, ins, specs, scratch=(), cost=0, limit=32):
     return pl.pallas_call(
         kernel,
         out_shape=outs,
         in_specs=list(specs),
         out_specs=jax.tree.map(lambda _: VM, outs),
         scratch_shapes=list(scratch),
-        compiler_params=pltpu.CompilerParams(vmem_limit_bytes=LIMIT),
+        compiler_params=pltpu.CompilerParams(vmem_limit_bytes=limit * MIB),
         cost_estimate=pl.CostEstimate(flops=cost, bytes_accessed=1 << 20, transcendentals=0),
     )(*ins)
+
+
+def after(values, others):
+    return lax.optimization_barrier((values, others))[0]
 
 
 def pack_kernel(slots_ref, noise_ref, *out_refs):
@@ -64,10 +64,16 @@
         lax.fori_loop(0, per // 2, pair, 0, unroll=min(4, per // 2))
 
 
-def regress_kernel(above_ref, own_ref, below_ref, conv_ref, proj_ref, mean_ref, cols_ref):
+def regress_kernel(above_ref, own_ref, below_ref, conv_ref, proj_ref, mean_ref, top_ref, cols_ref, taps_ref):
     rows, channels, width = own_ref.shape
     deep = cols_ref.shape[1] // 3
     cols_ref[...] = jnp.zeros(cols_ref.shape, BF)
+    taps_ref[...] = jnp.zeros(taps_ref.shape, BF)
+    for tap in range(9):
+        taps_ref[tap * deep : tap * deep + channels] = (
+            conv_ref[tap * channels : (tap + 1) * channels].astype(F32).astype(BF)
+        )
+    taps = jnp.transpose(taps_ref[...])
     lane = lax.broadcasted_iota(jnp.int32, (channels, width), 1)
 
     def put(at, cells):
@@ -89,41 +95,55 @@
 
     def one(r, carry):
         stack = cols_ref[pl.ds(r, 3)].reshape(9 * deep, width)
-        hidden = matmul(conv_ref[...], stack)
+        hidden = matmul(taps, stack)
         act = (hidden * jax.nn.sigmoid(hidden)).astype(BF)
         mean_ref[r] = matmul(proj_ref[...], act).astype(BF)
         return carry
 
     lax.fori_loop(0, rows, one, 0, unroll=2)
-
-
-def gather_kernel(
-    row_ref, col_ref, mean_ref, mean_low_ref, tgt_ref, tgt_low_ref, mp_ref, tp_ref, img_m, img_t, got_m, got_t
-):
-    rows, channels, width = mean_ref.shape
-    chunks, _, count, _ = mp_ref.shape
-    pairs = rows // 2
+    top_ref[...] = mean_ref[0 : rows - 1]
+
+
+def painter(width):
     eye = (
         lax.broadcasted_iota(jnp.int32, (width, width), 0)
         == lax.broadcasted_iota(jnp.int32, (width, width), 1)
     ).astype(BF)
 
-    def paint(cells, img, at):
-        after = pltpu.roll(cells.astype(F32), width - 1, 1).astype(BF)
-        both = jnp.concatenate([cells, after], axis=0)
-        img[at] = lax.dot_general(eye, both, NT_FORM, preferred_element_type=F32)
-
-    def own(r, carry):
-        paint(mean_ref[r], img_m, r)
-        paint(tgt_ref[r], img_t, r)
+    def paint(cells):
+        following = pltpu.roll(cells.astype(F32), width - 1, 1).astype(BF)
+        both = jnp.concatenate([cells, following], axis=0)
+        return lax.dot_general(eye, both, NT_FORM, preferred_element_type=F32)
+
+    return paint
+
+
+def paint_kernel(mean_ref, tgt_ref, img_m, img_t):
+    paint = painter(mean_ref.shape[2])
+
+    def one(r, carry):
+        img_m[r] = paint(mean_ref[r]).astype(BF)
+        img_t[r] = paint(tgt_ref[r]).astype(BF)
         return carry
 
+    lax.fori_loop(0, mean_ref.shape[0], one, 0, unroll=2)
+
+
+def gather_kernel(
+    row_ref, col_ref, own_m, own_t, mean_low_ref, tgt_low_ref, mp_ref, tp_ref, img_m, img_t, got_m, got_t
+):
+    rows = own_m.shape[0]
+    chunks, _, count, _ = mp_ref.shape
+    pairs = rows // 2
+    paint = painter(own_m.shape[1])
+    img_m[0:rows] = own_m[...].astype(F32)
+    img_t[0:rows] = own_t[...].astype(F32)
+
     def low(r, carry):
-        paint(mean_low_ref[r], img_m, rows + r)
-        paint(tgt_low_ref[r], img_t, rows + r)
+        img_m[rows + r] = paint(mean_low_ref[r])
+        img_t[rows + r] = paint(tgt_low_ref[r])
         return carry
 
-    lax.fori_loop(0, rows, own, 0)
     lax.fori_loop(0, rows - 1, low, 0)
     for chunk in range(chunks):
 
@@ -142,22 +162,21 @@
         tp_ref[chunk] = got_t[...].astype(BF).reshape(tp_ref.shape[1:])
 
 
-def chunk_kernel(
-    chunk,
-    last,
-    phases,
-    *refs,
-):
-    source_ref, phase_ref, step_ref = refs[:3]
-    noise_refs = refs[3 : 3 + phases]
-    refs = refs[3 + phases :]
+def chunk_kernel(chunk, last, pieces, *refs):
+    source_ref, step_ref, place_ref = refs[:3]
+    noise_refs = refs[3 : 3 + pieces]
+    refs = refs[3 + pieces :]
     (mp_ref, tp_ref, fac_ref, embed_ref, w1_ref, w2_ref, v2_ref, po_ref, pg_ref) = refs[:9]
     refs = refs[9:]
     before = None
     if chunk > 0:
         before, refs = refs[0], refs[1:]
-    out_ref, loss_ref = refs[:2]
-    (nz, xn, xm, x2n, x2m, e1, o1, e2, o2, slope1, res, noisy, act2, gout, gt, emb) = refs[2:]
+    if last:
+        keep_ref, send_ref, out_ref = refs[:3]
+        refs = refs[3:]
+    else:
+        out_ref, refs = refs[0], refs[1:]
+    (stage, nz, xn, xm, x2n, x2m, e1, o1, e2, o2, slope1, res, noisy, act2, gout, gt, emb) = refs
     _, cells, count, wide = mp_ref.shape
     rows = 12
     pairs = cells // rows
@@ -167,11 +186,12 @@
 
     for ref in (xn, xm, e1, o1, e2, o2):
         ref[...] = jnp.zeros(ref.shape, BF)
+    at = 0
+    for ref in noise_refs:
+        stage[at : at + ref.shape[0]] = ref[...]
+        at += ref.shape[0]
     for k in range(count):
-        at = source_ref[chunk * count + k]
-        piece = noise_refs[0][at]
-        if phases > 1:
-            piece = jnp.where(phase_ref[chunk * count + k] == 0, piece, noise_refs[1][at])
+        piece = stage[source_ref[chunk * count + k]]
         nz[pl.ds(k, cells, stride=count), :] = piece.astype(F32)
         emb[pl.ds(k, 1), :] = embed_ref[pl.ds(step_ref[chunk * count + k], 1), :]
 
@@ -242,7 +262,6 @@
         grad_pre = shape4(grad_pre, group)
         e2[r + 1 : r + 1 + group, 1 : pairs + 1] = grad_pre[..., :wide]
         o2[r + 1 : r + 1 + group, 1 : pairs + 1] = grad_pre[..., wide:]
-    loss_ref[...] = loss
 
     def emit(at, size, value):
         if before is not None:
@@ -282,6 +301,21 @@
         at = table + step_ref[chunk * count + k]
         out_ref[pl.ds(at, 1), :] = out_ref[pl.ds(at, 1), :] + emb[pl.ds(k, 1), :]
 
+    levels_end = table + levels
+    spots = lax.broadcasted_iota(jnp.int32, (8, wide), 0) * wide + lax.broadcasted_iota(jnp.int32, (8, wide), 1)
+    sums = jnp.sum(fac_ref[5] * loss, axis=1, keepdims=True)
+    owned = jnp.zeros((8, wide), F32)
+    for k in range(count):
+        owned = owned + jnp.where(spots == place_ref[chunk * count + k], sums[k : k + 1], 0.0)
+    if before is not None:
+        owned = owned + before[levels_end : levels_end + 8, :]
+    out_ref[levels_end:, :] = jnp.zeros((out_ref.shape[0] - levels_end, wide), F32)
+    if last:
+        rounded = owned.astype(BF).astype(F32)
+        out_ref[levels_end + 8 : levels_end + 16, :] = owned - rounded
+        owned = rounded
+    out_ref[levels_end : levels_end + 8, :] = owned
+
     gt[...] = jnp.transpose(act2[...])
     low = lax.broadcasted_iota(jnp.int32, (depth, wide), 1) < half
     for a in range(3):
@@ -302,38 +336,75 @@
         emit(base + depth, depth, merged(h0[:, direct], h1[:, direct]))
         emit(base + 2 * depth, depth, merged(h1[:, rim], h0[:, direct]))
 
-
-def pair_weights(taps, split):
-    zero = jnp.zeros_like(taps[0][0])
-    blocks = []
-    for a in range(3):
-        low, mid, high = taps[a]
-
-        def rows_of(first, second):
-            if not split:
-                return [first, second]
-            half = first.shape[0] // 2
-            return [first[:half], second[:half], first[half:], second[half:]]
-
-        even = jnp.concatenate([mid, low], axis=1)
-        odd = jnp.concatenate([high, mid], axis=1)
-        before = jnp.concatenate([low, zero], axis=1)
-        after = jnp.concatenate([zero, high], axis=1)
-        blocks += rows_of(even, odd)
-        blocks += rows_of(after, before) if split else rows_of(before, after)
-    return jnp.concatenate(blocks, axis=0)
-
-
-def forward_weights(conv, split):
-    depth = conv.shape[1] // 9
-    cut = [conv[:, i * depth : (i + 1) * depth].T for i in range(9)]
-    return pair_weights([cut[0:3], cut[3:6], cut[6:9]], split)
-
-
-def backward_weights(conv):
-    depth = conv.shape[1] // 9
-    cut = [conv[:, (8 - i) * depth : (9 - i) * depth] for i in range(9)]
-    return pair_weights([cut[0:3], cut[3:6], cut[6:9]], False)
+    if last:
+        size = keep_ref.shape[0]
+        core = place_ref[place_ref.shape[0] - 1]
+        keep_ref[...] = out_ref[pl.ds(pl.multiple_of(core * size, 16), size), :]
+        send_ref[...] = out_ref[pl.ds(pl.multiple_of((1 - core) * size, 16), size), :].astype(BF)
+
+
+def unfold_kernel(index_ref, own_ref, other_ref, one_ref, two_ref, proj_ref, embed_ref, loss_ref, full):
+    size, wide = own_ref.shape
+    core = index_ref[0]
+    full[pl.ds(pl.multiple_of(core * size, 16), size), :] = own_ref[...]
+    full[pl.ds(pl.multiple_of((1 - core) * size, 16), size), :] = other_ref[...]
+    depth = one_ref.shape[0]
+    for tap in range(9):
+        span = slice(tap * wide, (tap + 1) * wide)
+        one_ref[:, span] = full[tap * depth : (tap + 1) * depth].astype(F32)
+        two_ref[:, span] = full[(9 + tap) * depth : (10 + tap) * depth].astype(F32)
+    at = 18 * depth
+    for ref in (proj_ref, embed_ref):
+        ref[...] = full[at : at + ref.shape[0]].astype(F32)
+        at += ref.shape[0]
+    spots = lax.broadcasted_iota(jnp.int32, (8, wide), 0) * wide + lax.broadcasted_iota(jnp.int32, (8, wide), 1)
+    both = full[at : at + 16].astype(F32)
+    loss = jnp.where(spots == index_ref[1], both[0:8] + both[8:16], 0.0)
+    loss_ref[...] = jnp.sum(jnp.sum(loss, axis=1, keepdims=True), axis=0, keepdims=True)
+
+
+def weights_kernel(one_ref, two_ref, proj_ref, w1_ref, w2_ref, v2_ref, po_ref, pg_ref):
+    wide = one_ref.shape[0]
+    half = wide // 2
+    left, right = slice(0, wide), slice(wide, 2 * wide)
+    for ref in (w1_ref, w2_ref, v2_ref, po_ref, pg_ref):
+        ref[...] = jnp.zeros(ref.shape, BF)
+
+    def place(ref, a, b, tap, split):
+        base = 4 * wide * a
+
+        def put(member, side):
+            if split:
+                start = {0: 0, 1: half, 3: 2 * wide, 2: 2 * wide + half}[member] + base
+                ref[start : start + half, side] = tap[:half]
+                ref[start + wide : start + wide + half, side] = tap[half:]
+            else:
+                start = base + member * wide
+                ref[start : start + wide, side] = tap
+
+        if b == 0:
+            put(0, left)
+            put(1, right)
+        elif b == 1:
+            put(1, left)
+            put(3, right)
+        else:
+            put(0, right)
+            put(2, left)
+
+    for i, (a, b) in enumerate(TAPS):
+        span = slice(i * wide, (i + 1) * wide)
+        flipped = slice((8 - i) * wide, (9 - i) * wide)
+        place(w1_ref, a + 1, b, jnp.transpose(one_ref[:, span]), True)
+        place(w2_ref, a + 1, b, jnp.transpose(two_ref[:, span]), False)
+        place(v2_ref, a + 1, b, two_ref[:, flipped], False)
+    proj = proj_ref[...]
+    pg_ref[0:half, left] = proj
+    pg_ref[half:, right] = proj
+    flat = jnp.transpose(proj.astype(F32)).astype(BF)
+    zero = jnp.zeros_like(flat)
+    po_ref[left, :] = jnp.concatenate([flat, zero], axis=1)
+    po_ref[right, :] = jnp.concatenate([zero, flat], axis=1)
 
 
 def by_distance(axis, distance):
@@ -438,8 +509,9 @@
     def ordered(field):
         return jnp.sum(jnp.where(place_hot, field[None, :], 0), axis=1)
 
-    source = ordered(((owner ^ me) if exchange else owner) * deep + pair_rank % deep)
-    phase = ordered(pair_rank // deep)
+    source = ordered(
+        (pair_rank // deep) * (strips * deep) + ((owner ^ me) if exchange else owner) * deep + pair_rank % deep
+    )
     top, left, step, owner_in_order = (ordered(own[:, i]) for i in (0, 1, 3, 2))
 
     sigma = 0.1 * jnp.exp(step.astype(F32) * (math.log(100.0) / (levels - 1)))
@@ -447,8 +519,12 @@
     weight = u / (sigma * sigma)
     scale_out = sigma / jnp.sqrt(u)
     grad_scale = 2.0 * weight / (channels * cells) * scale_out
-    factors = jnp.stack([1.0 / jnp.sqrt(u), sigma, 1.0 / u, scale_out, grad_scale])
-    factors = jnp.broadcast_to(factors[:, :, None], (5, per_strip, wide))
+    factors = [1.0 / jnp.sqrt(u), sigma, 1.0 / u, scale_out, grad_scale, weight / (channels * cells)]
+    factors = jnp.broadcast_to(jnp.stack(factors)[:, :, None], (6, per_strip, wide))
+    samples = lax.axis_size("segment") * lax.axis_size("dp")
+    sample = lax.axis_index("segment") * lax.axis_size("dp") + lax.axis_index("dp")
+    core = lax.axis_index("segment")
+    place = jnp.concatenate([sample * strips + owner_in_order, core[None]]).astype(jnp.int32)
 
     slot_shape = (cells // 2, wide)
     pieces = phases * strips if exchange else phases
@@ -458,63 +534,82 @@
         (slots, noise[0, 0]),
         (SM, VM),
     )
+    reg_channels = reg_conv.shape[1] // 9
+    fill = -(-reg_channels // 16) * 16
+    per_row = (channels, width)
+    first_packed = packed[:strips] if exchange else packed[:1]
+    coarse_above, coarse_below = after((coarse_above, coarse_below), tuple(first_packed) + (target_low,))
+    mean, mean_top = call(
+        regress_kernel,
+        [jax.ShapeDtypeStruct((height,) + per_row, BF), jax.ShapeDtypeStruct((height - 1,) + per_row, BF)],
+        (coarse_above, own_coarse, coarse_below, reg_conv.T, reg_out),
+        (VM,) * 5,
+        [pltpu.VMEM((height + 2, 3 * fill, width), BF), pltpu.VMEM((9 * fill, depth), BF)],
+    )
+    mean_low = lax.ppermute(mean_top, "rows", down)
+
     arrived = []
     for f in range(phases):
+        sent = packed[f * strips : (f + 1) * strips] if exchange else packed[f : f + 1]
+        if f > 0:
+            sent = after(tuple(sent), (mean_top,))
         if exchange:
-            parts = [packed[f * strips]]
+            parts = [sent[0]]
             for d in range(1, strips):
-                parts.append(lax.ppermute(packed[f * strips + d], "rows", by_distance("rows", d)))
-            arrived.append(jnp.concatenate(parts, axis=0))
+                parts.append(lax.ppermute(sent[d], "rows", by_distance("rows", d)))
         else:
-            arrived.append(lax.all_to_all(packed[f], "rows", 0, 0, tiled=True))
-
-    fill = -(-reg_conv.shape[1] // 9 // 16) * 16
-    per_tap = reg_conv.shape[1] // 9
-    reg_taps = jnp.pad(reg_conv.reshape(-1, 9, per_tap), ((0, 0), (0, 0), (0, fill - per_tap)))
-    mean = call(
-        regress_kernel,
-        jax.ShapeDtypeStruct((height, channels, width), BF),
-        (coarse_above, own_coarse, coarse_below, reg_taps.reshape(-1, 9 * fill), reg_out),
-        (VM,) * 5,
-        [pltpu.VMEM((height + 2, 3 * fill, width), BF)],
-    )
-    mean_low = lax.ppermute(mean[: height - 1], "rows", down)
+            parts = [lax.all_to_all(sent[0], "rows", 0, 0, tiled=True)]
+        arrived += parts
+
+    conv_one, conv_two, out_proj = after((conv_one, conv_two, out_proj), (mean_top,))
+    image = jax.ShapeDtypeStruct((height, width, wide), BF)
+    image_m, image_t = call(paint_kernel, [image, image], (mean, own_target), (VM,) * 2)
+    stacked = jax.ShapeDtypeStruct((12 * depth, 2 * depth), BF)
+    weights = call(
+        weights_kernel,
+        [stacked] * 3
+        + [jax.ShapeDtypeStruct((2 * depth, wide), BF), jax.ShapeDtypeStruct((wide, 2 * depth), BF)],
+        (conv_one, conv_two, out_proj),
+        (VM,) * 3,
+    )
     patch_shape = jax.ShapeDtypeStruct((phases, cells // 2, count, wide), BF)
     mean_p, target_p = call(
         gather_kernel,
         [patch_shape, patch_shape],
-        (top, left, mean, mean_low, own_target, target_low),
+        (top, left, image_m, image_t, mean_low, target_low),
         (SM, SM) + (VM,) * 4,
         [pltpu.VMEM((2 * height - 1, width, wide), F32)] * 2 + [pltpu.VMEM((cells // 2 * count, wide), F32)] * 2,
     )
 
-    weights_one = forward_weights(conv_one, True)
-    weights_two = forward_weights(conv_two, False)
-    weights_back = backward_weights(conv_two)
-    zero = jnp.zeros_like(out_proj)
-    proj_back = jnp.concatenate(
-        [jnp.concatenate([out_proj, zero], axis=1), jnp.concatenate([zero, out_proj], axis=1)], axis=0
-    )
-    proj_out = proj_back.T
-
+    cores, groups = lax.axis_size("segment"), lax.axis_size("dp")
     total = cells // 2 * count
     rows_used = 18 * depth + channels + levels
-    table = None
-    losses = []
+    unit = cores * groups * 16
+    rows_all = -(-(rows_used + 16) // unit) * unit
+    per_core = rows_all // cores
+    table = jax.ShapeDtypeStruct((rows_all, wide), F32)
+    result = ()
     for chunk in range(phases):
+        last = chunk == phases - 1
         pad = pltpu.VMEM((height + 2, height // 2 + 2, count, wide), BF)
         rim = pltpu.VMEM((height + 2, height // 2, count, wide), BF)
-        ins = (source, phase, step) + tuple(arrived[: chunk + 1])
+        used = arrived[: (chunk + 1) * len(parts)]
+        slots_here = sum(piece.shape[0] for piece in used)
+        ins = (source, step, place) + tuple(used)
         ins += (mean_p[chunk : chunk + 1], target_p[chunk : chunk + 1])
         ins += (factors[:, chunk * count : (chunk + 1) * count], step_embed)
-        ins += (weights_one, weights_two, weights_back, proj_out, proj_back)
-        ins += (table,) if chunk > 0 else ()
-        table, loss = call(
-            functools.partial(chunk_kernel, chunk, chunk == phases - 1, chunk + 1),
-            [jax.ShapeDtypeStruct((rows_used, wide), F32), jax.ShapeDtypeStruct((count, wide), F32)],
+        ins += tuple(weights) + tuple(result)
+        outs = [table]
+        if last:
+            outs = [jax.ShapeDtypeStruct((per_core, wide), F32), jax.ShapeDtypeStruct((per_core, wide), BF)]
+        result = call(
+            functools.partial(chunk_kernel, chunk, last, len(used)),
+            outs,
             ins,
             (SM,) * 3 + (VM,) * (len(ins) - 3),
-            [
+            ([pltpu.VMEM((rows_all, wide), F32)] if last else [])
+            + [
+                pltpu.VMEM((slots_here, cells // 2, wide), BF),
                 pltpu.VMEM((total, wide), F32),
                 pad,
                 pad,
@@ -533,59 +628,36 @@
                 pltpu.VMEM((count, wide), F32),
             ],
         )
-        losses.append(loss)
-
-    patch_loss = weight * (jnp.sum(jnp.concatenate(losses), axis=1) / (channels * cells))
-    by_owner = jnp.sum(jnp.where(owner_in_order[None, :] == ids[:, None], patch_loss[None, :], 0.0), axis=1)
-    samples = lax.axis_size("segment") * lax.axis_size("dp")
-    sample = lax.axis_index("segment") * lax.axis_size("dp") + lax.axis_index("dp")
-    spread = jnp.where(jnp.arange(samples)[:, None] == sample, by_owner[None, :], 0.0).reshape(-1)
-    loss_rows = -(-samples * strips // wide)
-    spread = jnp.pad(spread, (0, loss_rows * wide - samples * strips)).reshape(loss_rows, wide)
-    coarse_part = rounded_to_bf16(spread)
-    unit = 2 * lax.axis_size("dp") * 16
-    rows_all = -(-(rows_used + 2 * loss_rows) // unit) * unit
-    table = jnp.concatenate(
-        [
-            table,
-            coarse_part,
-            spread - coarse_part,
-            jnp.zeros((rows_all - rows_used - 2 * loss_rows, wide), F32),
-        ],
-        axis=0,
-    )
-
-    cores, groups = lax.axis_size("segment"), lax.axis_size("dp")
-    kept = scatter_sum(table.reshape(cores, rows_all // cores, wide), "segment")
-    kept = scatter_sum(kept.reshape(groups, rows_all // cores // groups, wide), "dp")
+
+    kept, sent = result
+    kept = kept + lax.ppermute(sent, "segment", by_distance("segment", 1)).astype(F32)
+    kept = scatter_sum(kept.reshape(groups, per_core // groups, wide), "dp")
     kept = rows_sum(kept, "rows")
-    piece_rows = rows_all // cores // groups
-    ending = (lax.axis_index("segment") == cores - 1) & (lax.axis_index("dp") == groups - 1)
+    piece_rows = per_core // groups
+    ending = (core == cores - 1) & (lax.axis_index("dp") == groups - 1)
     at = rows_used - (rows_all - piece_rows)
-    exact = kept[at : at + loss_rows] + kept[at + loss_rows : at + 2 * loss_rows]
+    exact = kept[at : at + 8] + kept[at + 8 : at + 16]
     rounded = rounded_to_bf16(exact)
     pair = jnp.concatenate([rounded, exact - rounded], axis=0)
-    pair = jnp.where(ending, pair, kept[at : at + 2 * loss_rows])
+    pair = jnp.where(ending, pair, kept[at : at + 16])
     kept = rounded_to_bf16(lax.dynamic_update_slice_in_dim(kept, pair, at, 0)).astype(BF)
-    kept = gather_all(kept, "dp").reshape(rows_all // cores, wide)
-    table = gather_all(kept, "segment").reshape(rows_all, wide).astype(F32)
-
-    def assembled(at):
-        block = table[at : at + 9 * depth].reshape(9, depth, wide)
-        return jnp.transpose(block, (1, 0, 2)).reshape(depth, 9 * wide)
-
-    loss_table = (
-        table[rows_used : rows_used + loss_rows] + table[rows_used + loss_rows : rows_used + 2 * loss_rows]
-    ).reshape(-1)
-    owner_loss = lax.dynamic_slice_in_dim(loss_table, sample * strips + me, 1).reshape(1, 1)
-    return (
-        jnp.transpose(mean, (1, 0, 2))[None],
-        owner_loss,
-        assembled(0),
-        assembled(9 * depth),
-        table[18 * depth : 18 * depth + channels],
-        table[18 * depth + channels : rows_used],
-    )
+    kept = gather_all(kept, "dp").reshape(per_core, wide)
+    other = lax.ppermute(kept, "segment", by_distance("segment", 1))
+    gradient = jax.ShapeDtypeStruct(conv_one.shape, F32)
+    grad_one, grad_two, grad_proj, grad_embed, owner_loss = call(
+        unfold_kernel,
+        [
+            gradient,
+            gradient,
+            jax.ShapeDtypeStruct(out_proj.shape, F32),
+            jax.ShapeDtypeStruct(step_embed.shape, F32),
+            jax.ShapeDtypeStruct((1, 1), F32),
+        ],
+        (jnp.stack([core, sample * strips + me]).astype(jnp.int32), kept, other),
+        (SM, VM, VM),
+        [pltpu.VMEM((rows_all, wide), BF)],
+    )
+    return jnp.transpose(mean, (1, 0, 2))[None], owner_loss, grad_one, grad_two, grad_proj, grad_embed
 
 
 def solution(mesh):

time: 138 us -> 102 us (0.74)
  local copies, waits for them, and re-layouts: 30.8 us -> 8.46 us
  other arithmetic: 7.78 us -> 2.36 us
  waiting for transfers between devices: 28.2 us -> 23.1 us
  starting transfers between devices: 33.7 us -> 30.8 us
    unnamed x85 -> x28, local copies, waits for them, and re-layouts: 15.7 us -> 4.62 us
    concatenate x6 -> x0, local copies, waits for them, and re-layouts: 6.12 us -> none  [the longest x1 3.13 us: per_device(): jnp.concatenate([table, coarse_part, spread - coarse_part, jnp.zeros((row...]
    unnamed x18 -> x0, other arithmetic: 3.94 us -> none
    ppermute x7 -> x9, waiting for transfers between devices: 12.3 us -> 9.18 us  [the longest x1 6.08 us: per_device(): mean_low = lax.ppermute(mean_top, 'rows', down)]
    ppermute x7 -> x9, starting transfers between devices: 14.3 us -> 11.6 us  [the longest x6 10.2 us: per_device(): parts.append(lax.ppermute(sent[d], 'rows', by_distance('rows', d)))]
    slice x6 -> x0, local copies, waits for them, and re-layouts: 2.54 us -> none  [the longest x1 1.08 us: per_device(): mean_low = lax.ppermute(mean[:height - 1], 'rows', down)]
    ppermute x4 -> x3, waiting for transfers between devices: 6.39 us -> 3.85 us  [scatter_sum(): lax.ppermute(take(values, me ^ d).astype(BF), axis, by_distance(axis, d))]
    ppermute x4 -> x3, waiting for transfers between devices: 4.71 us -> 4.37 us  [gather_all(): lax.ppermute(piece, axis, by_distance(axis, d))]
  transfers between devices with their start and end apart: 21 -> 21, of which waited for: 11 -> 11; matrix products, arithmetic and copies ran while one was open for 15% -> 4% of each run, Pallas kernels for 7% -> 25%
where the time goes in v2:
time: 102 us; the launch traced here: 101 us
  Pallas kernels  35.5 us (35%)
  starting transfers between devices  30.8 us (30%)
  waiting for transfers between devices  23.1 us (23%)
  local copies, waits for them, and re-layouts  8.46 us (8%)
  other arithmetic  2.36 us (2%)
  between operations  1.1 us (1%)
    pallas_call x8, Pallas kernels, call(): pl.pallas_call(kernel, out_shape=outs, in_specs=list(specs), out_specs=ja...  35.5 us
    ppermute x6, starting transfers between devices, per_device(): parts.append(lax.ppermute(sent[d], 'rows', by_distance('rows', d)))  10.2 us
    ppermute x1, waiting for transfers between devices, per_device(): mean_low = lax.ppermute(mean_top, 'rows', down)  6.08 us
    ppermute x3, waiting for transfers between devices, rows_sum(): values.append(lax.ppermute(values[0], axis, by_distance(axis, d)))  5.69 us
    ppermute x1, starting transfers between devices, per_device(): coarse_above = lax.ppermute(own_coarse[height - 1:], 'rows', up)  4.92 us
    unnamed x28, local copies, waits for them, and re-layouts  4.62 us
    ppermute x3, starting transfers between devices, rows_sum(): values.append(lax.ppermute(values[0], axis, by_distance(axis, d)))  4.45 us
    ppermute x3, waiting for transfers between devices, gather_all(): lax.ppermute(piece, axis, by_distance(axis, d))  4.37 us
  transfers between devices with their start and end apart: 21, of which 11 were waited for; matrix products, arithmetic and copies ran while one was open for 4% of the time, Pallas kernels for 25%

profile of v2, /device:TPU:0, one launch (start us, length us, event | category | flops | bytes accessed | tf_op | source)
XLA Modules:
  0.0 101.3 jit_solution(16773353853948260071)
XLA Ops:
  0.7 1.5 %fusion.15 = (bf16[1,100,256]{2,1,0:T(8,128)(2,1)S(1)}, bf16[1,100,256]{2,1,0:T(8,128)(2,1)}) fusion(bf16[12,100,256]{2,1,0:T(8,128)(2,1)} %bitcast.73), kind=kLoop, calls=%fused_computation.70 | loop fusion | bytes 204800 | tf_op jit(solution)/shard_map/slice | solution.py:485
  2.2 4.9 %collective-permute-start = (bf16[1,100,256]{2,1,0:T(8,128)(2,1)}, bf16[1,100,256]{2,1,0:T(8,128)(2,1)S(1)}, u32[]{:S(2)}, u32[]{:S(2)}) collective-permute-start(bf16[1,100,256]{2,1,0:T(8,128)(2,1)} %get-tuple-element.82), channel_id=1, source_target_pairs={{0,4},{4,8},{8,12},{1,5},{5,9},{9,13},{2,6},{6,10},{10,14},{3,7},{... | collective-permute-start | bytes 153608 | tf_op jit(solution)/shard_map/ppermute | solution.py:484
  7.1 1.3 %collective-permute-start.1 = (bf16[1,100,256]{2,1,0:T(8,128)(2,1)S(1)}, bf16[1,100,256]{2,1,0:T(8,128)(2,1)S(1)}, u32[]{:S(2)}, u32[]{:S(2)}) collective-permute-start(bf16[1,100,256]{2,1,0:T(8,128)(2,1)S(1)} %get-tuple-element.81), channel_id=1, source_target_pairs={{4,0},{8,4},{12,8},{5,1},{9,5},{13,9},{6,2},{10,6},{14,10},{7,3},{... | collective-permute-start | bytes 153608 | tf_op jit(solution)/shard_map/ppermute | solution.py:485
  8.4 1.1 %slice.74 = bf16[11,64,256]{2,1,0:T(8,128)(2,1)S(1)} slice(bf16[12,64,256]{2,1,0:T(8,128)(2,1)} %bitcast.69), slice={[0:11], [0:64], [0:256]} | slice | bytes 720896 | tf_op jit(solution)/shard_map/slice | solution.py:483
  9.5 1.3 %collective-permute-start.2 = (bf16[11,64,256]{2,1,0:T(8,128)(2,1)S(1)}, bf16[11,64,256]{2,1,0:T(8,128)(2,1)S(1)}, u32[]{:S(2)}, u32[]{:S(2)}) collective-permute-start(bf16[11,64,256]{2,1,0:T(8,128)(2,1)S(1)} %slice.74), channel_id=1, source_target_pairs={{4,0},{8,4},{12,8},{5,1},{9,5},{13,9},{6,2},{10,6},{14,10},{7,3},{... | collective-permute-start | bytes 1081352 | tf_op jit(solution)/shard_map/ppermute | solution.py:483
  10.8 0.9 fusion.11
  11.7 0.1 select_reduce_fusion.6
  11.8 0.2 select_reduce_fusion.5
  12.0 0.1 add_minimum_fusion
  12.1 0.1 min.12.slots_ref
  12.2 1.6 %copy-done = bf16[1,1,64,64,144]{4,3,2,1,0:T(8,128)(2,1)S(1)} copy-done((bf16[1,1,64,64,144]{4,3,2,1,0:T(8,128)(2,1)S(1)}, bf16[1,1,64,64,144]{4,3,2,1,0:T(8,128)(2,1)}, u32[]{:S(2)}) %copy-start) | copy-done | bytes 1179672
  13.8 2.7 %shard_map.145 = (bf16[8,72,128]{2,1,0:T(8,128)(2,1)S(1)}, bf16[8,72,128]{2,1,0:T(8,128)(2,1)}, bf16[8,72,128]{2,1,0:T(8,128)(2,1)}, bf16[8,72,128]{2,1,0:T(8,12...) custom-call(s32[64]{0:T(128)S(1)} %min.12.slots_ref, ...), custom_call_target="tpu_custom_call" | custom-call | bytes 1048576 | tf_op jit(solution)/shard_map/pallas_call | solution.py:28
  16.4 0.7 copy-done.10
  17.1 0.7 copy-done.12
  17.8 0.6 copy-done.13
  18.4 3.3 %collective-permute-start.3 = (bf16[8,72,128]{2,1,0:T(8,128)(2,1)}, bf16[8,72,128]{2,1,0:T(8,128)(2,1)S(1)}, u32[]{:S(2)}, u32[]{:S(2)}) collective-permute-start(bf16[8,72,128]{2,1,0:T(8,128)(2,1)} %get-tuple-element.42), channel_id=1, source_target_pairs={{0,4},{4,0},{8,12},{12,8},{1,5},{5,1},{9,13},{13,9},{2,6},{6,2},{1... | collective-permute-start | bytes 442376 | tf_op jit(solution)/shard_map/ppermute | solution.py:559
  21.7 3.0 %collective-permute-start.4 = (bf16[8,72,128]{2,1,0:T(8,128)(2,1)}, bf16[8,72,128]{2,1,0:T(8,128)(2,1)S(1)}, u32[]{:S(2)}, u32[]{:S(2)}) collective-permute-start(bf16[8,72,128]{2,1,0:T(8,128)(2,1)} %get-tuple-element.43), channel_id=1, source_target_pairs={{0,8},{4,12},{8,0},{12,4},{1,9},{5,13},{9,1},{13,5},{2,10},{6,14},... | collective-permute-start | bytes 442376 | tf_op jit(solution)/shard_map/ppermute | solution.py:559
  24.7 0.7 dynamic-slice_bitcast_fusion
  25.4 0.2 convert_reduce_fusion.2
  25.6 0.1 convert_reduce_fusion.1
  25.7 0.1 convert_reduce_fusion
  25.9 0.2 select_reduce_fusion
  26.1 0.1 collective-permute-start.5
  26.3 6.7 %shard_map.146 = (bf16[12,64,256]{2,1,0:T(8,128)(2,1)}, bf16[11,64,256]{2,1,0:T(8,128)(2,1)S(1)}) custom-call(bf16[1,100,256]{2,1,0:T(8,128)(2,1)S(1)} %collective-permute-done.above_ref, bf16[12,100,256]{2,1,0:T(8,128)(2,1)S(1)} %bitcast.74, bf16[1,100,256]{2,1,0:T(8,128)(2,1)S(1)} %collective-permute-done.1.below_ref, bf16[900,128]{1,0:T(8,128)(2,1)S(1)} %bitcast.76, ...), custom_call_target="tpu_custom_call" | custom-call | bytes 1048576 | tf_op jit(solution)/shard_map/pallas_call | solution.py:28
  33.0 1.3 %collective-permute-start.9 = (bf16[11,64,256]{2,1,0:T(8,128)(2,1)S(1)}, bf16[11,64,256]{2,1,0:T(8,128)(2,1)S(1)}, u32[]{:S(2)}, u32[]{:S(2)}) collective-permute-start(bf16[11,64,256]{2,1,0:T(8,128)(2,1)S(1)} %get-tuple-element.52), channel_id=1, source_target_pairs={{4,0},{8,4},{12,8},{5,1},{9,5},{13,9},{6,2},{10,6},{14,10},{7,3},{... | collective-permute-start | bytes 1081352 | tf_op jit(solution)/shard_map/ppermute | solution.py:549
  34.3 0.1 pad_add_fusion.1.refs_2_
  34.4 0.1 fusion.18
  34.4 2.6 %collective-permute-start.6 = (bf16[8,72,128]{2,1,0:T(8,128)(2,1)}, bf16[8,72,128]{2,1,0:T(8,128)(2,1)S(1)}, u32[]{:S(2)}, u32[]{:S(2)}) collective-permute-start(bf16[8,72,128]{2,1,0:T(8,128)(2,1)} %copy-done.13), channel_id=1, source_target_pairs={{0,4},{4,0},{8,12},{12,8},{1,5},{5,1},{9,13},{13,9},{2,6},{6,2},{1... | collective-permute-start | bytes 442376 | tf_op jit(solution)/shard_map/ppermute | solution.py:559
  37.1 1.0 copy-done.3
  38.1 2.1 %shard_map.147 = (bf16[12,256,128]{2,1,0:T(8,128)(2,1)S(1)}, bf16[12,256,128]{2,1,0:T(8,128)(2,1)S(1)}) custom-call(bf16[12,64,256]{2,1,0:T(8,128)(2,1)S(1)} %copy-done.3, bf16[12,64,256]{2,1,0:T(8,128)(2,1)S(1)} %bitcast.70), custom_call_target="tpu_custom_call" | custom-call | bytes 1048576 | tf_op jit(solution)/shard_map/pallas_call | solution.py:28
  40.3 0.4 shard_map.149
  40.7 6.1 %collective-permute-done.9.mean_low_ref = bf16[11,64,256]{2,1,0:T(8,128)(2,1)S(1)} collective-permute-done((bf16[11,64,256]{2,1,0:T(8,128)(2,1)S(1)}, bf16[11,64,256]{2,1,0:T(8,128)(2,1)S(1)}, u32[]{:S(2)}, u32[]{:S(2)}) %collective-permute-start.9) | collective-permute-done | bytes 360480 | tf_op jit(solution)/shard_map/ppermute | solution.py:549
  46.8 0.1 collective-permute-start.7
  46.9 5.5 %shard_map.148 = (bf16[2,72,16,128]{3,2,1,0:T(8,128)(2,1)S(1)}, bf16[2,72,16,128]{3,2,1,0:T(8,128)(2,1)S(1)}) custom-call(s32[32]{0:T(128)S(1)} %get-tuple-element.77.row_ref, s32[32]{0:T(128)S(1)} %get-tuple-element.76.col_ref, bf16[12,256,128]{2,1,0:T(8,128)(2,1)S(1)} %get-tuple-element.57.own_m, bf16[12,256,128]{2,1,0:T(8,128)(2,1)S(1)} %get-tuple-element.58.own_t, ...), custom_call_target="tpu_custom_call" | custom-call | bytes 1048576 | tf_op jit(solution)/shard_map/pallas_call | solution.py:28
  52.4 0.1 fusion.17
  52.6 1.1 %collective-permute-start.8 = (bf16[8,72,128]{2,1,0:T(8,128)(2,1)S(1)}, bf16[8,72,128]{2,1,0:T(8,128)(2,1)S(1)}, u32[]{:S(2)}, u32[]{:S(2)}) collective-permute-start(bf16[8,72,128]{2,1,0:T(8,128)(2,1)S(1)} %copy-done.11), channel_id=1, source_target_pairs={{0,12},{4,8},{8,4},{12,0},{1,13},{5,9},{9,5},{13,1},{2,14},{6,10},... | collective-permute-start | bytes 442376 | tf_op jit(solution)/shard_map/ppermute | solution.py:559
  53.6 0.1 fusion.16
  53.7 0.1 broadcast_in_dim.97.refs_9_
  53.8 8.1 %shard_map.150.refs_20_ = f32[2432,128]{1,0:T(8,128)S(1)} custom-call(s32[32]{0:T(128)S(1)} %get-tuple-element.80.refs_0_, s32[32]{0:T(128)S(1)} %get-tuple-element.79.refs_1_, s32[33]{0:T(128)S(1)} %pad_add_fusion.1.refs_2_, bf16[8,72,128]{2,1,0:T(8,128)(2,1)S(1)} %get-tuple-element.41.refs_3_, bf16[8,72,128]{2,1,0:T(8,128)(2,1)S(1)} %collective-permute-done.3.refs_4_, ...), custom_call_target="tpu_custom_call" | custom-call | bytes 1048576 | tf_op jit(solution)/shard_map/pallas_call | solution.py:28
  62.0 0.1 broadcast_in_dim.96.refs_13_
  62.1 8.3 %shard_map.151 = (f32[1216,128]{1,0:T(8,128)S(1)}, bf16[1216,128]{1,0:T(8,128)(2,1)S(1)}) custom-call(s32[32]{0:T(128)S(1)} %get-tuple-element.80.refs_0_, s32[32]{0:T(128)S(1)} %get-tuple-element.79.refs_1_, s32[33]{0:T(128)S(1)} %pad_add_fusion.1.refs_2_, bf16[8,72,128]{2,1,0:T(8,128)(2,1)S(1)} %get-tuple-element.41.refs_3_, ...), custom_call_target="tpu_custom_call" | custom-call | bytes 1048576 | tf_op jit(solution)/shard_map/pallas_call | solution.py:28
  70.3 0.1 collective-permute-start.10
  70.4 1.6 %collective-permute-done.10 = bf16[1216,128]{1,0:T(8,128)(2,1)S(1)} collective-permute-done((bf16[1216,128]{1,0:T(8,128)(2,1)S(1)}, bf16[1216,128]{1,0:T(8,128)(2,1)S(1)}, u32[]{:S(2)}, u32[]{:S(2)}) %collective-permute-start.10) | collective-permute-done | bytes 311328 | tf_op jit(solution)/shard_map/ppermute | solution.py:633
  72.1 2.5 %collective-permute-start.13 = (bf16[304,128]{1,0:T(8,128)(2,1)S(1)}, bf16[304,128]{1,0:T(8,128)(2,1)S(1)}, u32[]{:S(2)}, u32[]{:S(2)}) collective-permute-start(bf16[304,128]{1,0:T(8,128)(2,1)S(1)} %get-tuple-element.84), channel_id=1, source_target_pairs={{0,3},{1,2},{2,1},{3,0},{4,7},{5,6},{6,5},{7,4},{8,11},{9,10},{10,... | collective-permute-start | bytes 233480 | tf_op jit(solution)/shard_map/ppermute | solution.py:427
  74.6 0.5 collective-permute-start.12
  75.1 0.5 collective-permute-start.11
  75.7 1.8 %collective-permute-done.13 = bf16[304,128]{1,0:T(8,128)(2,1)S(1)} collective-permute-done((bf16[304,128]{1,0:T(8,128)(2,1)S(1)}, bf16[304,128]{1,0:T(8,128)(2,1)S(1)}, u32[]{:S(2)}, u32[]{:S(2)}) %collective-permute-start.13) | collective-permute-done | bytes 77856 | tf_op jit(solution)/shard_map/ppermute | solution.py:427
  77.5 1.6 %collective-permute-done.12 = bf16[304,128]{1,0:T(8,128)(2,1)S(1)} collective-permute-done((bf16[304,128]{1,0:T(8,128)(2,1)S(1)}, bf16[304,128]{1,0:T(8,128)(2,1)S(1)}, u32[]{:S(2)}, u32[]{:S(2)}) %collective-permute-start.12) | collective-permute-done | bytes 77856 | tf_op jit(solution)/shard_map/ppermute | solution.py:427
  79.1 0.4 collective-permute-done.11
  79.6 2.9 %collective-permute-start.16 = (bf16[304,128]{1,0:T(8,128)(2,1)S(1)}, bf16[304,128]{1,0:T(8,128)(2,1)S(1)}, u32[]{:S(2)}, u32[]{:S(2)}) collective-permute-start(bf16[304,128]{1,0:T(8,128)(2,1)S(1)} %fusion.3), channel_id=1, source_target_pairs={{0,12},{4,8},{8,4},{12,0},{1,13},{5,9},{9,5},{13,1},{2,14},{6,10},... | collective-permute-start | bytes 233480 | tf_op jit(solution)/shard_map/ppermute | solution.py:454
  82.5 1.0 collective-permute-start.15
  83.5 0.6 collective-permute-start.14
  84.0 1.9 %collective-permute-done.16 = bf16[304,128]{1,0:T(8,128)(2,1)S(1)} collective-permute-done((bf16[304,128]{1,0:T(8,128)(2,1)S(1)}, bf16[304,128]{1,0:T(8,128)(2,1)S(1)}, u32[]{:S(2)}, u32[]{:S(2)}) %collective-permute-start.16) | collective-permute-done | bytes 77856 | tf_op jit(solution)/shard_map/ppermute | solution.py:454
  85.9 3.8 %collective-permute-done.15 = bf16[304,128]{1,0:T(8,128)(2,1)S(1)} collective-permute-done((bf16[304,128]{1,0:T(8,128)(2,1)S(1)}, bf16[304,128]{1,0:T(8,128)(2,1)S(1)}, u32[]{:S(2)}, u32[]{:S(2)}) %collective-permute-start.15) | collective-permute-done | bytes 77856 | tf_op jit(solution)/shard_map/ppermute | solution.py:454
  89.8 1.4 %collective-permute-start.17 = (bf16[304,128]{1,0:T(8,128)(2,1)S(1)}, bf16[304,128]{1,0:T(8,128)(2,1)S(1)}, u32[]{:S(2)}, u32[]{:S(2)}) collective-permute-start(bf16[304,128]{1,0:T(8,128)(2,1)S(1)} %reduce-precision_convert_fusion), channel_id=1, source_target_pairs={{0,3},{1,2},{2,1},{3,0},{4,7},{5,6},{6,5},{7,4},{8,11},{9,10},{10,... | collective-permute-start | bytes 233480 | tf_op jit(solution)/shard_map/ppermute | solution.py:437
  91.2 2.2 %collective-permute-start.18 = (bf16[304,128]{1,0:T(8,128)(2,1)S(1)}, bf16[304,128]{1,0:T(8,128)(2,1)S(1)}, u32[]{:S(2)}, u32[]{:S(2)}) collective-permute-start(bf16[304,128]{1,0:T(8,128)(2,1)S(1)} %reduce-precision_convert_fusion), channel_id=1, source_target_pairs={{0,2},{1,3},{2,0},{3,1},{4,6},{5,7},{6,4},{7,5},{8,10},{9,11},{10,... | collective-permute-start | bytes 233480 | tf_op jit(solution)/shard_map/ppermute | solution.py:437
  93.5 1.8 %collective-permute-done.17 = bf16[304,128]{1,0:T(8,128)(2,1)S(1)} collective-permute-done((bf16[304,128]{1,0:T(8,128)(2,1)S(1)}, bf16[304,128]{1,0:T(8,128)(2,1)S(1)}, u32[]{:S(2)}, u32[]{:S(2)}) %collective-permute-start.17) | collective-permute-done | bytes 77856 | tf_op jit(solution)/shard_map/ppermute | solution.py:437
  95.2 1.3 %collective-permute-done.18 = bf16[304,128]{1,0:T(8,128)(2,1)S(1)} collective-permute-done((bf16[304,128]{1,0:T(8,128)(2,1)S(1)}, bf16[304,128]{1,0:T(8,128)(2,1)S(1)}, u32[]{:S(2)}, u32[]{:S(2)}) %collective-permute-start.18) | collective-permute-done | bytes 77856 | tf_op jit(solution)/shard_map/ppermute | solution.py:437
  96.5 1.3 %collective-permute-done.19 = bf16[304,128]{1,0:T(8,128)(2,1)S(1)} collective-permute-done((bf16[304,128]{1,0:T(8,128)(2,1)S(1)}, bf16[304,128]{1,0:T(8,128)(2,1)S(1)}, u32[]{:S(2)}, u32[]{:S(2)}) %collective-permute-start.19) | collective-permute-done | bytes 77856 | tf_op jit(solution)/shard_map/ppermute | solution.py:437
  97.8 0.1 select_bitcast_fusion.3
  98.0 0.1 collective-permute-start.20
  98.1 0.1 pad_add_fusion.index_ref
  98.2 1.5 %collective-permute-done.20.other_ref = bf16[1216,128]{1,0:T(8,128)(2,1)S(1)} collective-permute-done((bf16[1216,128]{1,0:T(8,128)(2,1)S(1)}, bf16[1216,128]{1,0:T(8,128)(2,1)S(1)}, u32[]{:S(2)}, u32[]{:S(2)}) %collective-permute-start.20) | collective-permute-done | bytes 311328 | tf_op jit(solution)/shard_map/ppermute | solution.py:645
  99.7 1.7 %shard_map.152 = (f32[128,1152]{1,0:T(8,128)}, f32[128,1152]{1,0:T(8,128)}, f32[64,128]{1,0:T(8,128)}, f32[32,128]{1,0:T(8,128)}, f32[1,1]{1,0:T(1,128)}) custom-call(s32[2]{0:T(128)S(1)} %pad_add_fusion.index_ref, bf16[1216,128]{1,0:T(8,128)(2,1)S(1)} %bitcast.72, bf16[1216,128]{1,0:T(8,128)(2,1)S(1)} %collective-permute-done.20.other_ref), custom_call_target="tpu_custom_call" | custom-call | bytes 1048576 | tf_op jit(solution)/shard_map/pallas_call | solution.py:28
  (52 shorter events, 0.5 us)
Async XLA Ops:
  0.6 25.6 %copy-start.6 = (bf16[128,900]{0,1:T(8,128)(2,1)S(1)}, bf16[128,900]{0,1:T(8,128)(2,1)}, u32[]{:S(2)}) copy-start(bf16[128,900]{0,1:T(8,128)(2,1)} %param.14) | copy-start | bytes 691204
  0.6 25.6 %copy-start.8 = (bf16[64,128]{1,0:T(8,128)(2,1)S(1)}, bf16[64,128]{1,0:T(8,128)(2,1)}, u32[]{:S(2)}) copy-start(bf16[64,128]{1,0:T(8,128)(2,1)} %proj_ref.1) | copy-start | bytes 49156
  0.7 36.4 %copy-start.1 = (bf16[1,64,12,256]{3,1,2,0:T(8,128)(2,1)S(1)}, bf16[1,64,12,256]{3,1,2,0:T(8,128)(2,1)}, u32[]{:S(2)}) copy-start(bf16[1,64,12,256]{3,1,2,0:T(8,128)(2,1)} %param.11) | copy-start | bytes 1179652
  2.2 23.9 %collective-permute-start = (bf16[1,100,256]{2,1,0:T(8,128)(2,1)}, bf16[1,100,256]{2,1,0:T(8,128)(2,1)S(1)}, u32[]{:S(2)}, u32[]{:S(2)}) collective-permute-start(bf16[1,100,256]{2,1,0:T(8,128)(2,1)} %get-tuple-element.82), channel_id=1, source_target_pairs={{0,4},{4,8},{8,12},{1,5},{5,9},{9,13},{2,6},{6,10},{10,14},{3,7},{... | collective-permute-start | bytes 153608 | tf_op jit(solution)/shard_map/ppermute | solution.py:484
  7.1 19.1 %collective-permute-start.1 = (bf16[1,100,256]{2,1,0:T(8,128)(2,1)S(1)}, bf16[1,100,256]{2,1,0:T(8,128)(2,1)S(1)}, u32[]{:S(2)}, u32[]{:S(2)}) collective-permute-start(bf16[1,100,256]{2,1,0:T(8,128)(2,1)S(1)} %get-tuple-element.81), channel_id=1, source_target_pairs={{4,0},{8,4},{12,8},{5,1},{9,5},{13,9},{6,2},{10,6},{14,10},{7,3},{... | collective-permute-start | bytes 153608 | tf_op jit(solution)/shard_map/ppermute | solution.py:485
  8.4 31.8 %copy-start.4 = (bf16[128,1152]{1,0:T(8,128)(2,1)S(1)}, bf16[128,1152]{1,0:T(8,128)(2,1)}, u32[]{:S(2)}) copy-start(bf16[128,1152]{1,0:T(8,128)(2,1)} %one_ref) | copy-start | bytes 884740
  9.5 30.7 %copy-start.9 = (bf16[64,128]{1,0:T(8,128)(2,1)S(1)}, bf16[64,128]{1,0:T(8,128)(2,1)}, u32[]{:S(2)}) copy-start(bf16[64,128]{1,0:T(8,128)(2,1)} %proj_ref.2) | copy-start | bytes 49156
  9.5 16.7 %collective-permute-start.2 = (bf16[11,64,256]{2,1,0:T(8,128)(2,1)S(1)}, bf16[11,64,256]{2,1,0:T(8,128)(2,1)S(1)}, u32[]{:S(2)}, u32[]{:S(2)}) collective-permute-start(bf16[11,64,256]{2,1,0:T(8,128)(2,1)S(1)} %slice.74), channel_id=1, source_target_pairs={{4,0},{8,4},{12,8},{5,1},{9,5},{13,9},{6,2},{10,6},{14,10},{7,3},{... | collective-permute-start | bytes 1081352 | tf_op jit(solution)/shard_map/ppermute | solution.py:483
  12.2 1.6 %copy-start = (bf16[1,1,64,64,144]{4,3,2,1,0:T(8,128)(2,1)S(1)}, bf16[1,1,64,64,144]{4,3,2,1,0:T(8,128)(2,1)}, u32[]{:S(2)}) copy-start(bf16[1,1,64,64,144]{4,3,2,1,0:T(8,128)(2,1)} %param.12) | copy-start | bytes 3538948
  13.8 12.5 %copy-start.2 = (bf16[1,100,12,256]{3,1,2,0:T(8,128)(2,1)S(1)}, bf16[1,100,12,256]{3,1,2,0:T(8,128)(2,1)}, u32[]{:S(2)}) copy-start(bf16[1,100,12,256]{3,1,2,0:T(8,128)(2,1)} %param.10) | copy-start | bytes 1843204
  13.8 26.5 %copy-start.5 = (bf16[128,1152]{1,0:T(8,128)(2,1)S(1)}, bf16[128,1152]{1,0:T(8,128)(2,1)}, u32[]{:S(2)}) copy-start(bf16[128,1152]{1,0:T(8,128)(2,1)} %two_ref) | copy-start | bytes 884740
  16.4 0.7 copy-start.10
  17.1 0.7 copy-start.12
  17.8 0.6 copy-start.13
  18.4 34.1 %collective-permute-start.3 = (bf16[8,72,128]{2,1,0:T(8,128)(2,1)}, bf16[8,72,128]{2,1,0:T(8,128)(2,1)S(1)}, u32[]{:S(2)}, u32[]{:S(2)}) collective-permute-start(bf16[8,72,128]{2,1,0:T(8,128)(2,1)} %get-tuple-element.42), channel_id=1, source_target_pairs={{0,4},{4,0},{8,12},{12,8},{1,5},{5,1},{9,13},{13,9},{2,6},{6,2},{1... | collective-permute-start | bytes 442376 | tf_op jit(solution)/shard_map/ppermute | solution.py:559
  21.7 32.0 %collective-permute-start.4 = (bf16[8,72,128]{2,1,0:T(8,128)(2,1)}, bf16[8,72,128]{2,1,0:T(8,128)(2,1)S(1)}, u32[]{:S(2)}, u32[]{:S(2)}) collective-permute-start(bf16[8,72,128]{2,1,0:T(8,128)(2,1)} %get-tuple-element.43), channel_id=1, source_target_pairs={{0,8},{4,12},{8,0},{12,4},{1,9},{5,13},{9,1},{13,5},{2,10},{6,14},... | collective-permute-start | bytes 442376 | tf_op jit(solution)/shard_map/ppermute | solution.py:559
  26.1 27.6 %collective-permute-start.5 = (bf16[8,72,128]{2,1,0:T(8,128)(2,1)}, bf16[8,72,128]{2,1,0:T(8,128)(2,1)S(1)}, u32[]{:S(2)}, u32[]{:S(2)}) collective-permute-start(bf16[8,72,128]{2,1,0:T(8,128)(2,1)} %get-tuple-element.44), channel_id=1, source_target_pairs={{0,12},{4,8},{8,4},{12,0},{1,13},{5,9},{9,5},{13,1},{2,14},{6,10},... | collective-permute-start | bytes 442376 | tf_op jit(solution)/shard_map/ppermute | solution.py:559
  33.0 13.8 %collective-permute-start.9 = (bf16[11,64,256]{2,1,0:T(8,128)(2,1)S(1)}, bf16[11,64,256]{2,1,0:T(8,128)(2,1)S(1)}, u32[]{:S(2)}, u32[]{:S(2)}) collective-permute-start(bf16[11,64,256]{2,1,0:T(8,128)(2,1)S(1)} %get-tuple-element.52), channel_id=1, source_target_pairs={{4,0},{8,4},{12,8},{5,1},{9,5},{13,9},{6,2},{10,6},{14,10},{7,3},{... | collective-permute-start | bytes 1081352 | tf_op jit(solution)/shard_map/ppermute | solution.py:549
  34.4 27.5 %collective-permute-start.6 = (bf16[8,72,128]{2,1,0:T(8,128)(2,1)}, bf16[8,72,128]{2,1,0:T(8,128)(2,1)S(1)}, u32[]{:S(2)}, u32[]{:S(2)}) collective-permute-start(bf16[8,72,128]{2,1,0:T(8,128)(2,1)} %copy-done.13), channel_id=1, source_target_pairs={{0,4},{4,0},{8,12},{12,8},{1,5},{5,1},{9,13},{13,9},{2,6},{6,2},{1... | collective-permute-start | bytes 442376 | tf_op jit(solution)/shard_map/ppermute | solution.py:559
  37.1 1.0 copy-start.3
  40.2 12.3 %copy-start.11 = (bf16[8,72,128]{2,1,0:T(8,128)(2,1)S(1)}, bf16[8,72,128]{2,1,0:T(8,128)(2,1)}, u32[]{:S(2)}) copy-start(bf16[8,72,128]{2,1,0:T(8,128)(2,1)} %copy-done.10) | copy-start | bytes 442372
  46.8 15.2 %collective-permute-start.7 = (bf16[8,72,128]{2,1,0:T(8,128)(2,1)}, bf16[8,72,128]{2,1,0:T(8,128)(2,1)S(1)}, u32[]{:S(2)}, u32[]{:S(2)}) collective-permute-start(bf16[8,72,128]{2,1,0:T(8,128)(2,1)} %copy-done.12), channel_id=1, source_target_pairs={{0,8},{4,12},{8,0},{12,4},{1,9},{5,13},{9,1},{13,5},{2,10},{6,14},... | collective-permute-start | bytes 442376 | tf_op jit(solution)/shard_map/ppermute | solution.py:559
  46.9 6.9 %copy-start.7 = (f32[32,128]{1,0:T(8,128)S(1)}, f32[32,128]{1,0:T(8,128)}, u32[]{:S(2)}) copy-start(f32[32,128]{1,0:T(8,128)} %refs_14_.1) | copy-start | bytes 49156
  52.6 9.4 %collective-permute-start.8 = (bf16[8,72,128]{2,1,0:T(8,128)(2,1)S(1)}, bf16[8,72,128]{2,1,0:T(8,128)(2,1)S(1)}, u32[]{:S(2)}, u32[]{:S(2)}) collective-permute-start(bf16[8,72,128]{2,1,0:T(8,128)(2,1)S(1)} %copy-done.11), channel_id=1, source_target_pairs={{0,12},{4,8},{8,4},{12,0},{1,13},{5,9},{9,5},{13,1},{2,14},{6,10},... | collective-permute-start | bytes 442376 | tf_op jit(solution)/shard_map/ppermute | solution.py:559
  70.3 1.7 %collective-permute-start.10 = (bf16[1216,128]{1,0:T(8,128)(2,1)S(1)}, bf16[1216,128]{1,0:T(8,128)(2,1)S(1)}, u32[]{:S(2)}, u32[]{:S(2)}) collective-permute-start(bf16[1216,128]{1,0:T(8,128)(2,1)S(1)} %get-tuple-element.70), channel_id=1, source_target_pairs={{0,16},{16,0},{1,17},{17,1},{2,18},{18,2},{3,19},{19,3},{4,20},{20... | collective-permute-start | bytes 933896 | tf_op jit(solution)/shard_map/ppermute | solution.py:633
  72.1 5.4 %collective-permute-start.13 = (bf16[304,128]{1,0:T(8,128)(2,1)S(1)}, bf16[304,128]{1,0:T(8,128)(2,1)S(1)}, u32[]{:S(2)}, u32[]{:S(2)}) collective-permute-start(bf16[304,128]{1,0:T(8,128)(2,1)S(1)} %get-tuple-element.84), channel_id=1, source_target_pairs={{0,3},{1,2},{2,1},{3,0},{4,7},{5,6},{6,5},{7,4},{8,11},{9,10},{10,... | collective-permute-start | bytes 233480 | tf_op jit(solution)/shard_map/ppermute | solution.py:427
  74.6 4.5 %collective-permute-start.12 = (bf16[304,128]{1,0:T(8,128)(2,1)S(1)}, bf16[304,128]{1,0:T(8,128)(2,1)S(1)}, u32[]{:S(2)}, u32[]{:S(2)}) collective-permute-start(bf16[304,128]{1,0:T(8,128)(2,1)S(1)} %get-tuple-element.85), channel_id=1, source_target_pairs={{0,2},{1,3},{2,0},{3,1},{4,6},{5,7},{6,4},{7,5},{8,10},{9,11},{10,... | collective-permute-start | bytes 233480 | tf_op jit(solution)/shard_map/ppermute | solution.py:427
  75.1 4.4 %collective-permute-start.11 = (bf16[304,128]{1,0:T(8,128)(2,1)S(1)}, bf16[304,128]{1,0:T(8,128)(2,1)S(1)}, u32[]{:S(2)}, u32[]{:S(2)}) collective-permute-start(bf16[304,128]{1,0:T(8,128)(2,1)S(1)} %get-tuple-element.83), channel_id=1, source_target_pairs={{0,1},{1,0},{2,3},{3,2},{4,5},{5,4},{6,7},{7,6},{8,9},{9,8},{10,11... | collective-permute-start | bytes 233480 | tf_op jit(solution)/shard_map/ppermute | solution.py:427
  79.6 6.4 %collective-permute-start.16 = (bf16[304,128]{1,0:T(8,128)(2,1)S(1)}, bf16[304,128]{1,0:T(8,128)(2,1)S(1)}, u32[]{:S(2)}, u32[]{:S(2)}) collective-permute-start(bf16[304,128]{1,0:T(8,128)(2,1)S(1)} %fusion.3), channel_id=1, source_target_pairs={{0,12},{4,8},{8,4},{12,0},{1,13},{5,9},{9,5},{13,1},{2,14},{6,10},... | collective-permute-start | bytes 233480 | tf_op jit(solution)/shard_map/ppermute | solution.py:454
  82.5 7.2 %collective-permute-start.15 = (bf16[304,128]{1,0:T(8,128)(2,1)S(1)}, bf16[304,128]{1,0:T(8,128)(2,1)S(1)}, u32[]{:S(2)}, u32[]{:S(2)}) collective-permute-start(bf16[304,128]{1,0:T(8,128)(2,1)S(1)} %fusion.3), channel_id=1, source_target_pairs={{0,8},{4,12},{8,0},{12,4},{1,9},{5,13},{9,1},{13,5},{2,10},{6,14},... | collective-permute-start | bytes 233480 | tf_op jit(solution)/shard_map/ppermute | solution.py:454
  83.5 6.2 %collective-permute-start.14 = (bf16[304,128]{1,0:T(8,128)(2,1)S(1)}, bf16[304,128]{1,0:T(8,128)(2,1)S(1)}, u32[]{:S(2)}, u32[]{:S(2)}) collective-permute-start(bf16[304,128]{1,0:T(8,128)(2,1)S(1)} %fusion.3), channel_id=1, source_target_pairs={{0,4},{4,0},{8,12},{12,8},{1,5},{5,1},{9,13},{13,9},{2,6},{6,2},{1... | collective-permute-start | bytes 233480 | tf_op jit(solution)/shard_map/ppermute | solution.py:454
  89.8 5.4 %collective-permute-start.17 = (bf16[304,128]{1,0:T(8,128)(2,1)S(1)}, bf16[304,128]{1,0:T(8,128)(2,1)S(1)}, u32[]{:S(2)}, u32[]{:S(2)}) collective-permute-start(bf16[304,128]{1,0:T(8,128)(2,1)S(1)} %reduce-precision_convert_fusion), channel_id=1, source_target_pairs={{0,3},{1,2},{2,1},{3,0},{4,7},{5,6},{6,5},{7,4},{8,11},{9,10},{10,... | collective-permute-start | bytes 233480 | tf_op jit(solution)/shard_map/ppermute | solution.py:437
  91.2 5.3 %collective-permute-start.18 = (bf16[304,128]{1,0:T(8,128)(2,1)S(1)}, bf16[304,128]{1,0:T(8,128)(2,1)S(1)}, u32[]{:S(2)}, u32[]{:S(2)}) collective-permute-start(bf16[304,128]{1,0:T(8,128)(2,1)S(1)} %reduce-precision_convert_fusion), channel_id=1, source_target_pairs={{0,2},{1,3},{2,0},{3,1},{4,6},{5,7},{6,4},{7,5},{8,10},{9,11},{10,... | collective-permute-start | bytes 233480 | tf_op jit(solution)/shard_map/ppermute | solution.py:437
  93.4 4.4 %collective-permute-start.19 = (bf16[304,128]{1,0:T(8,128)(2,1)S(1)}, bf16[304,128]{1,0:T(8,128)(2,1)S(1)}, u32[]{:S(2)}, u32[]{:S(2)}) collective-permute-start(bf16[304,128]{1,0:T(8,128)(2,1)S(1)} %reduce-precision_convert_fusion), channel_id=1, source_target_pairs={{0,1},{1,0},{2,3},{3,2},{4,5},{5,4},{6,7},{7,6},{8,9},{9,8},{10,11... | collective-permute-start | bytes 233480 | tf_op jit(solution)/shard_map/ppermute | solution.py:437
  98.0 1.7 %collective-permute-start.20 = (bf16[1216,128]{1,0:T(8,128)(2,1)S(1)}, bf16[1216,128]{1,0:T(8,128)(2,1)S(1)}, u32[]{:S(2)}, u32[]{:S(2)}) collective-permute-start(bf16[1216,128]{1,0:T(8,128)(2,1)S(1)} %bitcast.71), channel_id=1, source_target_pairs={{0,16},{16,0},{1,17},{17,1},{2,18},{18,2},{3,19},{19,3},{4,20},{20... | collective-permute-start | bytes 933896 | tf_op jit(solution)/shard_map/ppermute | solution.py:645

commit v3 on v2

--- a/solution.py
+++ b/solution.py
@@ -14,6 +14,7 @@
 NT_FORM = (((1,), (1,)), ((), ()))
 TN_FORM = (((0,), (0,)), ((), ()))
 MIB = 1024 * 1024
+GROUP = 4
 
 
 def matmul(left, right):
@@ -24,7 +25,7 @@
 SM = pl.BlockSpec(memory_space=pltpu.SMEM)
 
 
-def call(kernel, outs, ins, specs, scratch=(), cost=0, limit=32):
+def call(kernel, outs, ins, specs, scratch=(), limit=24):
     return pl.pallas_call(
         kernel,
         out_shape=outs,
@@ -32,7 +33,7 @@
         out_specs=jax.tree.map(lambda _: VM, outs),
         scratch_shapes=list(scratch),
         compiler_params=pltpu.CompilerParams(vmem_limit_bytes=limit * MIB),
-        cost_estimate=pl.CostEstimate(flops=cost, bytes_accessed=1 << 20, transcendentals=0),
+        cost_estimate=pl.CostEstimate(flops=1000000000, bytes_accessed=1, transcendentals=0),
     )(*ins)
 
 
@@ -40,7 +41,27 @@
     return lax.optimization_barrier((values, others))[0]
 
 
-def pack_kernel(slots_ref, noise_ref, *out_refs):
+def starts_kernel(region_ref, starts_ref):
+    strips, _, entries = region_ref.shape
+    me = lax.axis_index("rows")
+
+    def strip(i, total):
+        starts_ref[i] = total
+
+        def entry(k, count):
+            return count + jnp.where(region_ref[i, 2, k] == me, 1, 0)
+
+        return lax.fori_loop(0, entries, entry, total, unroll=8)
+
+    lax.fori_loop(0, strips, strip, 0)
+
+
+def pack_kernel(phase, exchange, most, *refs):
+    region_ref, noise_ref = refs[:2]
+    out_refs, starts_ref = refs[2:-1], refs[-1]
+    starts_kernel(region_ref, starts_ref)
+    strips = starts_ref.shape[0]
+    me = lax.axis_index("rows")
     channels, cells = noise_ref.shape[1:]
     half = cells // 2
     row = lax.broadcasted_iota(jnp.int32, (half, cells), 0)
@@ -48,23 +69,70 @@
     even = (col == 2 * row).astype(BF)
     odd = (col == 2 * row + 1).astype(BF)
     low = lax.broadcasted_iota(jnp.int32, (half, 2 * channels), 1) < channels
-    per = out_refs[0].shape[0]
-    for index, out_ref in enumerate(out_refs):
-
-        def pair(j, carry, index=index, out_ref=out_ref):
-            one = noise_ref[slots_ref[index * per + 2 * j]]
-            two = noise_ref[slots_ref[index * per + 2 * j + 1]]
+    deep = out_refs[0].shape[0] * len(out_refs) // strips
+
+    def fill(goal, out_ref, base):
+        first_slot = starts_ref[goal] + phase * deep
+
+        def pair(j, carry):
+            one_at, two_at = 2 * j, jnp.minimum(2 * j + 1, deep - 1)
+            one = noise_ref[jnp.minimum(first_slot + one_at, most - 1)]
+            two = noise_ref[jnp.minimum(first_slot + two_at, most - 1)]
             both = jnp.concatenate([one, two], axis=0)
             first = lax.dot_general(even, both, NT_FORM, preferred_element_type=F32)
             second = lax.dot_general(odd, both, NT_FORM, preferred_element_type=F32)
-            out_ref[2 * j] = jnp.where(low, first, pltpu.roll(second, channels, 1)).astype(BF)
-            out_ref[2 * j + 1] = jnp.where(low, pltpu.roll(first, channels, 1), second).astype(BF)
+            out_ref[base + two_at] = jnp.where(low, pltpu.roll(first, channels, 1), second).astype(BF)
+            out_ref[base + one_at] = jnp.where(low, first, pltpu.roll(second, channels, 1)).astype(BF)
             return carry
 
-        lax.fori_loop(0, per // 2, pair, 0, unroll=min(4, per // 2))
-
-
-def regress_kernel(above_ref, own_ref, below_ref, conv_ref, proj_ref, mean_ref, top_ref, cols_ref, taps_ref):
+        many = (deep + 1) // 2
+        lax.fori_loop(0, many, pair, 0, unroll=many)
+
+    if exchange:
+        for distance, out_ref in enumerate(out_refs):
+            fill(me ^ distance, out_ref, 0)
+    else:
+
+        def goal(i, carry):
+            fill(i, out_refs[0], i * deep)
+            return carry
+
+        lax.fori_loop(0, strips, goal, 0)
+
+
+SOURCE, STEP, PLACE, TOP, LEFT = range(5)
+
+
+def tables_kernel(exchange, deep, count, region_ref, table_ref, seen_ref):
+    strips, _, entries = region_ref.shape
+    me = lax.axis_index("rows")
+    sample = lax.axis_index("segment") * lax.axis_size("dp") + lax.axis_index("dp")
+    for i in range(strips):
+        seen_ref[i] = 0
+
+    def entry(k, carry):
+        first, later = carry
+        owner = region_ref[me, 2, k]
+        rank = seen_ref[owner]
+        seen_ref[owner] = rank + 1
+        phase = rank // deep
+        early = (phase == 0) & (first < count)
+        at = jnp.where(early, first, later)
+        sender = owner ^ me if exchange else owner
+        table_ref[SOURCE, at] = (phase * strips + sender) * deep + rank - phase * deep
+        table_ref[STEP, at] = region_ref[me, 3, k]
+        table_ref[PLACE, at] = sample * strips + owner
+        table_ref[TOP, at] = region_ref[me, 0, k]
+        table_ref[LEFT, at] = region_ref[me, 1, k]
+        step = jnp.where(early, 1, 0)
+        return first + step, later + 1 - step
+
+    lax.fori_loop(0, entries, entry, (0, count))
+
+
+def regress_kernel(
+    even_ref, inward_ref, own_ref, outward_ref, conv_ref, proj_ref, mean_ref, top_ref, last_ref, cols_ref, taps_ref
+):
     rows, channels, width = own_ref.shape
     deep = cols_ref.shape[1] // 3
     cols_ref[...] = jnp.zeros(cols_ref.shape, BF)
@@ -84,8 +152,9 @@
         cols_ref[at, deep : deep + channels] = cells
         cols_ref[at, 2 * deep : 2 * deep + channels] = right
 
-    put(0, above_ref[0])
-    put(rows + 1, below_ref[0])
+    even = even_ref[0]
+    put(even * (rows + 1), inward_ref[0])
+    put((1 - even) * (rows + 1), outward_ref[0])
 
     def fill(r, carry):
         put(r + 1, own_ref[r])
@@ -102,6 +171,7 @@
 
     lax.fori_loop(0, rows, one, 0, unroll=2)
     top_ref[...] = mean_ref[0 : rows - 1]
+    last_ref[...] = mean_ref[rows - 1 : rows]
 
 
 def painter(width):
@@ -118,56 +188,63 @@
     return paint
 
 
-def paint_kernel(mean_ref, tgt_ref, img_m, img_t):
-    paint = painter(mean_ref.shape[2])
+def gather(table_ref, image, got, out_ref):
+    chunks, _, count, _ = out_ref.shape
+    rows = 12
+    pairs = rows // 2
+    for chunk in range(chunks):
+
+        def patch(k, carry, chunk=chunk):
+            top = table_ref[TOP, chunk * count + k]
+            left = table_ref[LEFT, chunk * count + k]
+            for r in range(rows):
+                got[pl.ds(r * pairs * count + k, pairs, stride=count), :] = image[
+                    top + r, pl.ds(left, pairs, stride=2), :
+                ]
+            return carry
+
+        lax.fori_loop(0, count, patch, 0, unroll=2)
+        out_ref[chunk] = got[...].astype(BF).reshape(out_ref.shape[1:])
+
+
+def target_kernel(
+    exchange, deep, region_ref, tgt_ref, tgt_low_ref, top_ref, last_ref, table_ref, tp_ref, img_m, image, got, seen
+):
+    tables_kernel(exchange, deep, tp_ref.shape[2], region_ref, table_ref, seen)
+    paint = painter(tgt_ref.shape[2])
+    rows = tgt_ref.shape[0]
 
     def one(r, carry):
-        img_m[r] = paint(mean_ref[r]).astype(BF)
-        img_t[r] = paint(tgt_ref[r]).astype(BF)
+        img_m[r] = paint(top_ref[r]).astype(BF)
+        image[r] = paint(tgt_ref[r])
+        image[rows + r] = paint(tgt_low_ref[r])
         return carry
 
-    lax.fori_loop(0, mean_ref.shape[0], one, 0, unroll=2)
-
-
-def gather_kernel(
-    row_ref, col_ref, own_m, own_t, mean_low_ref, tgt_low_ref, mp_ref, tp_ref, img_m, img_t, got_m, got_t
-):
-    rows = own_m.shape[0]
-    chunks, _, count, _ = mp_ref.shape
-    pairs = rows // 2
-    paint = painter(own_m.shape[1])
-    img_m[0:rows] = own_m[...].astype(F32)
-    img_t[0:rows] = own_t[...].astype(F32)
+    lax.fori_loop(0, rows - 1, one, 0)
+    img_m[rows - 1] = paint(last_ref[0]).astype(BF)
+    image[rows - 1] = paint(tgt_ref[rows - 1])
+    gather(table_ref, image, got, tp_ref)
+
+
+def mean_kernel(table_ref, own, low_ref, mp_ref, image, got):
+    rows = own.shape[0]
+    paint = painter(own.shape[1])
+    image[0:rows] = own[...].astype(F32)
 
     def low(r, carry):
-        img_m[rows + r] = paint(mean_low_ref[r])
-        img_t[rows + r] = paint(tgt_low_ref[r])
+        image[rows + r] = paint(low_ref[r])
         return carry
 
-    lax.fori_loop(0, rows - 1, low, 0)
-    for chunk in range(chunks):
-
-        def patch(k, carry, chunk=chunk):
-            top = row_ref[chunk * count + k]
-            left = col_ref[chunk * count + k]
-            for r in range(rows):
-                for img, got in ((img_m, got_m), (img_t, got_t)):
-                    got[pl.ds(r * pairs * count + k, pairs, stride=count), :] = img[
-                        top + r, pl.ds(left, pairs, stride=2), :
-                    ]
-            return carry
-
-        lax.fori_loop(0, count, patch, 0)
-        mp_ref[chunk] = got_m[...].astype(BF).reshape(mp_ref.shape[1:])
-        tp_ref[chunk] = got_t[...].astype(BF).reshape(tp_ref.shape[1:])
+    lax.fori_loop(0, rows - 1, low, 0, unroll=11)
+    gather(table_ref, image, got, mp_ref)
 
 
 def chunk_kernel(chunk, last, pieces, *refs):
-    source_ref, step_ref, place_ref = refs[:3]
-    noise_refs = refs[3 : 3 + pieces]
-    refs = refs[3 + pieces :]
-    (mp_ref, tp_ref, fac_ref, embed_ref, w1_ref, w2_ref, v2_ref, po_ref, pg_ref) = refs[:9]
-    refs = refs[9:]
+    table_ref = refs[0]
+    noise_refs = refs[1 : 1 + pieces]
+    refs = refs[1 + pieces :]
+    (mp_ref, tp_ref, embed_ref, w1_ref, w2_ref, v2_ref, po_ref, pg_ref) = refs[:8]
+    refs = refs[8:]
     before = None
     if chunk > 0:
         before, refs = refs[0], refs[1:]
@@ -176,12 +253,26 @@
         refs = refs[3:]
     else:
         out_ref, refs = refs[0], refs[1:]
-    (stage, nz, xn, xm, x2n, x2m, e1, o1, e2, o2, slope1, res, noisy, act2, gout, gt, emb) = refs
+    (stage, nz, xn, xm, x2n, x2m, e1, o1, e2, o2, slope1, res, noisy, act2, gout, gt, emb, fac, by_level) = refs
     _, cells, count, wide = mp_ref.shape
     rows = 12
     pairs = cells // rows
     total = cells * count
-    group = 4
+    levels = embed_ref.shape[0]
+
+    def entry(field, k):
+        return table_ref[field, chunk * count + k]
+
+    values = cells * wide
+    level = lax.broadcasted_iota(jnp.int32, (levels, wide), 0).astype(F32)
+    sig = 0.1 * jnp.exp(level * (math.log(100.0) / (levels - 1)))
+    u = sig * sig + 1.0
+    weight = u / (sig * sig)
+    root = jnp.sqrt(u)
+    scales = [1.0 / root, sig, 1.0 / u, sig / root, 2.0 * weight / values * (sig / root), weight / values]
+    for i, scale in enumerate(scales):
+        by_level[i] = scale
+    group = GROUP
     half = wide // 2
 
     for ref in (xn, xm, e1, o1, e2, o2):
@@ -191,12 +282,15 @@
         stage[at : at + ref.shape[0]] = ref[...]
         at += ref.shape[0]
     for k in range(count):
-        piece = stage[source_ref[chunk * count + k]]
+        piece = stage[entry(SOURCE, k)]
         nz[pl.ds(k, cells, stride=count), :] = piece.astype(F32)
-        emb[pl.ds(k, 1), :] = embed_ref[pl.ds(step_ref[chunk * count + k], 1), :]
+        step = entry(STEP, k)
+        emb[pl.ds(k, 1), :] = embed_ref[pl.ds(step, 1), :]
+        for i in range(len(scales)):
+            fac[i, pl.ds(k, 1), :] = by_level[i, pl.ds(step, 1), :]
 
     def spread(index):
-        return fac_ref[index][None]
+        return fac[index][None]
 
     scale_in, sigma, skip, scale_out, grad_scale = (spread(i) for i in range(5))
     lane = lax.broadcasted_iota(jnp.int32, (1, 1, count, wide), 3)
@@ -292,21 +386,20 @@
         act2[span, :] = grad
     emb[...] = sums[:, :wide] + sums[:, wide:]
     table = 18 * depth + half
-    levels = embed_ref.shape[0]
     if before is not None:
         out_ref[table : table + levels, :] = before[table : table + levels, :]
     else:
         out_ref[table : table + levels, :] = jnp.zeros((levels, wide), F32)
     for k in range(count):
-        at = table + step_ref[chunk * count + k]
+        at = table + entry(STEP, k)
         out_ref[pl.ds(at, 1), :] = out_ref[pl.ds(at, 1), :] + emb[pl.ds(k, 1), :]
 
     levels_end = table + levels
     spots = lax.broadcasted_iota(jnp.int32, (8, wide), 0) * wide + lax.broadcasted_iota(jnp.int32, (8, wide), 1)
-    sums = jnp.sum(fac_ref[5] * loss, axis=1, keepdims=True)
+    sums = jnp.sum(fac[5] * loss, axis=1, keepdims=True)
     owned = jnp.zeros((8, wide), F32)
     for k in range(count):
-        owned = owned + jnp.where(spots == place_ref[chunk * count + k], sums[k : k + 1], 0.0)
+        owned = owned + jnp.where(spots == entry(PLACE, k), sums[k : k + 1], 0.0)
     if before is not None:
         owned = owned + before[levels_end : levels_end + 8, :]
     out_ref[levels_end:, :] = jnp.zeros((out_ref.shape[0] - levels_end, wide), F32)
@@ -338,14 +431,16 @@
 
     if last:
         size = keep_ref.shape[0]
-        core = place_ref[place_ref.shape[0] - 1]
+        core = lax.axis_index("segment")
         keep_ref[...] = out_ref[pl.ds(pl.multiple_of(core * size, 16), size), :]
         send_ref[...] = out_ref[pl.ds(pl.multiple_of((1 - core) * size, 16), size), :].astype(BF)
 
 
-def unfold_kernel(index_ref, own_ref, other_ref, one_ref, two_ref, proj_ref, embed_ref, loss_ref, full):
+def unfold_kernel(own_ref, other_ref, one_ref, two_ref, proj_ref, embed_ref, loss_ref, full):
     size, wide = own_ref.shape
-    core = index_ref[0]
+    core = lax.axis_index("segment")
+    sample = core * lax.axis_size("dp") + lax.axis_index("dp")
+    place = sample * lax.axis_size("rows") + lax.axis_index("rows")
     full[pl.ds(pl.multiple_of(core * size, 16), size), :] = own_ref[...]
     full[pl.ds(pl.multiple_of((1 - core) * size, 16), size), :] = other_ref[...]
     depth = one_ref.shape[0]
@@ -359,7 +454,7 @@
         at += ref.shape[0]
     spots = lax.broadcasted_iota(jnp.int32, (8, wide), 0) * wide + lax.broadcasted_iota(jnp.int32, (8, wide), 1)
     both = full[at : at + 16].astype(F32)
-    loss = jnp.where(spots == index_ref[1], both[0:8] + both[8:16], 0.0)
+    loss = jnp.where(spots == place, both[0:8] + both[8:16], 0.0)
     loss_ref[...] = jnp.sum(jnp.sum(loss, axis=1, keepdims=True), axis=0, keepdims=True)
 
 
@@ -477,93 +572,55 @@
     levels = step_embed.shape[0]
 
     down = [(i + 1, i) for i in range(strips - 1)]
-    up = [(i, i + 1) for i in range(strips - 1)]
     own_target = jnp.transpose(target[0], (1, 0, 2))
     own_coarse = jnp.transpose(coarse[0], (1, 0, 2))
-    target_low = lax.ppermute(own_target[: height - 1], "rows", down)
-    coarse_above = lax.ppermute(own_coarse[height - 1 :], "rows", up)
-    coarse_below = lax.ppermute(own_coarse[:1], "rows", down)
-
-    ids = jnp.arange(strips, dtype=jnp.int32)
-    owners = region[:, :, 2]
-    mine = jnp.sum((owners == me).astype(jnp.int32), axis=1)
-    starts = jnp.sum(jnp.where(ids[:, None] > ids[None, :], mine[None, :], 0), axis=1)
-    distances = ids
-    goal = (ids ^ me) if exchange else ids
-    goal_start = jnp.sum(jnp.where(goal[:, None] == ids[None, :], starts[None, :], 0), axis=1)
-    rank = jnp.arange(capacity, dtype=jnp.int32).reshape(phases, 1, deep)
-    slots = jnp.minimum(goal_start[None, :, None] + rank, most - 1).reshape(-1)
-
-    own = lax.dynamic_index_in_dim(region, me, 0, keepdims=False)
-    owner = own[:, 2]
-    entry = jnp.arange(per_strip, dtype=jnp.int32)
-    earlier = entry[None, :] < entry[:, None]
-    pair_rank = jnp.sum(((owner[:, None] == owner[None, :]) & earlier).astype(jnp.int32), axis=1)
-    early = pair_rank < deep
-    early_before = jnp.sum((early[None, :] & earlier).astype(jnp.int32), axis=1)
-    first = early & (early_before < count)
-    first_before = jnp.sum((first[None, :] & earlier).astype(jnp.int32), axis=1)
-    place = jnp.where(first, first_before, count + entry - first_before)
-    place_hot = place[None, :] == entry[:, None]
-
-    def ordered(field):
-        return jnp.sum(jnp.where(place_hot, field[None, :], 0), axis=1)
-
-    source = ordered(
-        (pair_rank // deep) * (strips * deep) + ((owner ^ me) if exchange else owner) * deep + pair_rank % deep
-    )
-    top, left, step, owner_in_order = (ordered(own[:, i]) for i in (0, 1, 3, 2))
-
-    sigma = 0.1 * jnp.exp(step.astype(F32) * (math.log(100.0) / (levels - 1)))
-    u = sigma * sigma + 1.0
-    weight = u / (sigma * sigma)
-    scale_out = sigma / jnp.sqrt(u)
-    grad_scale = 2.0 * weight / (channels * cells) * scale_out
-    factors = [1.0 / jnp.sqrt(u), sigma, 1.0 / u, scale_out, grad_scale, weight / (channels * cells)]
-    factors = jnp.broadcast_to(jnp.stack(factors)[:, :, None], (6, per_strip, wide))
-    samples = lax.axis_size("segment") * lax.axis_size("dp")
-    sample = lax.axis_index("segment") * lax.axis_size("dp") + lax.axis_index("dp")
     core = lax.axis_index("segment")
-    place = jnp.concatenate([sample * strips + owner_in_order, core[None]]).astype(jnp.int32)
+    region_table = jnp.transpose(region, (0, 2, 1))
 
     slot_shape = (cells // 2, wide)
-    pieces = phases * strips if exchange else phases
-    packed = call(
-        pack_kernel,
-        [jax.ShapeDtypeStruct((phases * strips * deep // pieces,) + slot_shape, BF)] * pieces,
-        (slots, noise[0, 0]),
-        (SM, VM),
-    )
+    pieces = strips if exchange else 1
+
+    def packed(phase, region_table, noise):
+        return call(
+            functools.partial(pack_kernel, phase, exchange, most),
+            [jax.ShapeDtypeStruct((strips * deep // pieces,) + slot_shape, BF)] * pieces,
+            (region_table, noise[0, 0]),
+            (SM, VM),
+            [pltpu.SMEM((strips,), jnp.int32)],
+            limit=8,
+        )
+
+    def sent(packed_pieces):
+        if not exchange:
+            return [lax.all_to_all(packed_pieces[0], "rows", 0, 0, tiled=True)]
+        moved = [lax.ppermute(packed_pieces[d], "rows", by_distance("rows", d)) for d in range(1, strips)]
+        return [packed_pieces[0]] + moved
+
+    first_packed = packed(0, region_table, noise)
+    arrived = sent(first_packed)
+
     reg_channels = reg_conv.shape[1] // 9
     fill = -(-reg_channels // 16) * 16
     per_row = (channels, width)
-    first_packed = packed[:strips] if exchange else packed[:1]
-    coarse_above, coarse_below = after((coarse_above, coarse_below), tuple(first_packed) + (target_low,))
-    mean, mean_top = call(
+    even = me % 2 == 0
+    pairs = [(i, i ^ 1) for i in range(strips)]
+    others = [(i, ((i + 1) ^ 1) - 1) for i in range(1, strips - 1)]
+    low_edge, high_edge = own_coarse[:1], own_coarse[height - 1 :]
+    inward = lax.ppermute(jnp.where(even, high_edge, low_edge), "rows", pairs)
+    outward = lax.ppermute(jnp.where(even, low_edge, high_edge), "rows", others)
+    target_low = lax.ppermute(own_target, "rows", down)
+    inward, outward = after((inward, outward), (first_packed[0], target_low))
+    mean, mean_top, mean_last = call(
         regress_kernel,
-        [jax.ShapeDtypeStruct((height,) + per_row, BF), jax.ShapeDtypeStruct((height - 1,) + per_row, BF)],
-        (coarse_above, own_coarse, coarse_below, reg_conv.T, reg_out),
-        (VM,) * 5,
+        [jax.ShapeDtypeStruct((rows,) + per_row, BF) for rows in (height, height - 1, 1)],
+        (even.astype(jnp.int32)[None], inward, own_coarse, outward, reg_conv.T, reg_out),
+        (SM,) + (VM,) * 5,
         [pltpu.VMEM((height + 2, 3 * fill, width), BF), pltpu.VMEM((9 * fill, depth), BF)],
+        limit=12,
     )
     mean_low = lax.ppermute(mean_top, "rows", down)
 
-    arrived = []
-    for f in range(phases):
-        sent = packed[f * strips : (f + 1) * strips] if exchange else packed[f : f + 1]
-        if f > 0:
-            sent = after(tuple(sent), (mean_top,))
-        if exchange:
-            parts = [sent[0]]
-            for d in range(1, strips):
-                parts.append(lax.ppermute(sent[d], "rows", by_distance("rows", d)))
-        else:
-            parts = [lax.all_to_all(sent[0], "rows", 0, 0, tiled=True)]
-        arrived += parts
-
     conv_one, conv_two, out_proj = after((conv_one, conv_two, out_proj), (mean_top,))
-    image = jax.ShapeDtypeStruct((height, width, wide), BF)
-    image_m, image_t = call(paint_kernel, [image, image], (mean, own_target), (VM,) * 2)
     stacked = jax.ShapeDtypeStruct((12 * depth, 2 * depth), BF)
     weights = call(
         weights_kernel,
@@ -571,14 +628,33 @@
         + [jax.ShapeDtypeStruct((2 * depth, wide), BF), jax.ShapeDtypeStruct((wide, 2 * depth), BF)],
         (conv_one, conv_two, out_proj),
         (VM,) * 3,
+        limit=12,
     )
     patch_shape = jax.ShapeDtypeStruct((phases, cells // 2, count, wide), BF)
-    mean_p, target_p = call(
-        gather_kernel,
-        [patch_shape, patch_shape],
-        (top, left, image_m, image_t, mean_low, target_low),
-        (SM, SM) + (VM,) * 4,
-        [pltpu.VMEM((2 * height - 1, width, wide), F32)] * 2 + [pltpu.VMEM((cells // 2 * count, wide), F32)] * 2,
+    image = pltpu.VMEM((2 * height - 1, width, wide), F32)
+    got = pltpu.VMEM((cells // 2 * count, wide), F32)
+    table, target_p, image_m = pl.pallas_call(
+        functools.partial(target_kernel, exchange, deep),
+        out_shape=[
+            jax.ShapeDtypeStruct((5, per_strip), jnp.int32),
+            patch_shape,
+            jax.ShapeDtypeStruct((height, width, wide), BF),
+        ],
+        in_specs=[SM] + [VM] * 4,
+        out_specs=[SM, VM, VM],
+        scratch_shapes=[image, got, pltpu.SMEM((strips,), jnp.int32)],
+        compiler_params=pltpu.CompilerParams(vmem_limit_bytes=16 * MIB),
+        cost_estimate=pl.CostEstimate(flops=1000000000, bytes_accessed=1, transcendentals=0),
+    )(region_table, own_target, target_low, mean_top, mean_last)
+    later_region, later_noise = after((region_table, noise), (weights[0],))
+    arrived += sent(packed(1, later_region, later_noise))
+    mean_p = call(
+        mean_kernel,
+        patch_shape,
+        (table, image_m, mean_low),
+        (SM, VM, VM),
+        [image, got],
+        limit=16,
     )
 
     cores, groups = lax.axis_size("segment"), lax.axis_size("dp")
@@ -587,26 +663,25 @@
     unit = cores * groups * 16
     rows_all = -(-(rows_used + 16) // unit) * unit
     per_core = rows_all // cores
-    table = jax.ShapeDtypeStruct((rows_all, wide), F32)
+    sums = jax.ShapeDtypeStruct((rows_all, wide), F32)
     result = ()
     for chunk in range(phases):
         last = chunk == phases - 1
         pad = pltpu.VMEM((height + 2, height // 2 + 2, count, wide), BF)
         rim = pltpu.VMEM((height + 2, height // 2, count, wide), BF)
-        used = arrived[: (chunk + 1) * len(parts)]
+        used = arrived[: (chunk + 1) * pieces]
         slots_here = sum(piece.shape[0] for piece in used)
-        ins = (source, step, place) + tuple(used)
-        ins += (mean_p[chunk : chunk + 1], target_p[chunk : chunk + 1])
-        ins += (factors[:, chunk * count : (chunk + 1) * count], step_embed)
+        ins = (table,) + tuple(used)
+        ins += (mean_p[chunk : chunk + 1], target_p[chunk : chunk + 1], step_embed)
         ins += tuple(weights) + tuple(result)
-        outs = [table]
+        outs = [sums]
         if last:
             outs = [jax.ShapeDtypeStruct((per_core, wide), F32), jax.ShapeDtypeStruct((per_core, wide), BF)]
         result = call(
             functools.partial(chunk_kernel, chunk, last, len(used)),
             outs,
             ins,
-            (SM,) * 3 + (VM,) * (len(ins) - 3),
+            (SM,) + (VM,) * (len(ins) - 1),
             ([pltpu.VMEM((rows_all, wide), F32)] if last else [])
             + [
                 pltpu.VMEM((slots_here, cells // 2, wide), BF),
@@ -626,11 +701,13 @@
                 pltpu.VMEM((total, wide), BF),
                 pltpu.VMEM((2 * wide, total), BF),
                 pltpu.VMEM((count, wide), F32),
+                pltpu.VMEM((6, count, wide), F32),
+                pltpu.VMEM((6, levels, wide), F32),
             ],
         )
 
-    kept, sent = result
-    kept = kept + lax.ppermute(sent, "segment", by_distance("segment", 1)).astype(F32)
+    kept, given = result
+    kept = kept + lax.ppermute(given, "segment", by_distance("segment", 1)).astype(F32)
     kept = scatter_sum(kept.reshape(groups, per_core // groups, wide), "dp")
     kept = rows_sum(kept, "rows")
     piece_rows = per_core // groups
@@ -653,9 +730,10 @@
             jax.ShapeDtypeStruct(step_embed.shape, F32),
             jax.ShapeDtypeStruct((1, 1), F32),
         ],
-        (jnp.stack([core, sample * strips + me]).astype(jnp.int32), kept, other),
-        (SM, VM, VM),
+        (kept, other),
+        (VM, VM),
         [pltpu.VMEM((rows_all, wide), BF)],
+        limit=12,
     )
     return jnp.transpose(mean, (1, 0, 2))[None], owner_loss, grad_one, grad_two, grad_proj, grad_embed
 

time: 102 us -> 91.2 us (0.89)
  waiting for transfers between devices: 23.1 us -> 16 us
  local copies, waits for them, and re-layouts: 8.46 us -> 2.58 us
  Pallas kernels: 35.5 us -> 38.3 us
  other arithmetic: 2.36 us -> 1.16 us
  starting transfers between devices: 30.8 us -> 31.9 us
    pallas_call x0 -> x1, Pallas kernels: none -> 6.75 us  [per_device(): pl.pallas_call(functools.partial(target_kernel, exchange, deep), out_shap...]
    ppermute x1, waiting for transfers between devices: 6.08 us -> 0.01 us  [per_device(): mean_low = lax.ppermute(mean_top, 'rows', down)]
    pallas_call x8, Pallas kernels: 35.5 us -> 31.5 us  [call(): pl.pallas_call(kernel, out_shape=outs, in_specs=list(specs), out_specs=ja...]
    slice x5 -> x2, local copies, waits for them, and re-layouts: 2.86 us -> 0.21 us  [per_device(): ins += (mean_p[chunk:chunk + 1], target_p[chunk:chunk + 1], step_embed)]
    unnamed x28 -> x24, local copies, waits for them, and re-layouts: 4.62 us -> 2.33 us
    reduce_sum x7 -> x0, other arithmetic: 1.75 us -> none  [the longest x1 0.86 us: per_device(): mine = jnp.sum((owners == me).astype(jnp.int32), axis=1)]
  transfers between devices with their start and end apart: 21 -> 21, of which waited for: 11 -> 10; matrix products, arithmetic and copies ran while one was open for 4% -> 1% of each run, Pallas kernels for 25% -> 31%
where the time goes in v3:
time: 91.2 us; the launch traced here: 90.9 us
  Pallas kernels  38.3 us (42%)
  starting transfers between devices  31.9 us (35%)
  waiting for transfers between devices  16 us (18%)
  local copies, waits for them, and re-layouts  2.58 us (3%)
  other arithmetic  1.16 us (1%)
  between operations  0.99 us (1%)
    pallas_call x8, Pallas kernels, call(): pl.pallas_call(kernel, out_shape=outs, in_specs=list(specs), out_specs=ja...  31.5 us
    ppermute x6, starting transfers between devices, sent(): lax.ppermute(packed_pieces[d], 'rows', by_distance('rows', d))  12.9 us
    pallas_call x1, Pallas kernels, per_device(): pl.pallas_call(functools.partial(target_kernel, exchange, deep), out_shap...  6.75 us
    ppermute x3, waiting for transfers between devices, rows_sum(): values.append(lax.ppermute(values[0], axis, by_distance(axis, d)))  4.81 us
    ppermute x3, starting transfers between devices, rows_sum(): values.append(lax.ppermute(values[0], axis, by_distance(axis, d)))  4.45 us
    ppermute x3, waiting for transfers between devices, gather_all(): lax.ppermute(piece, axis, by_distance(axis, d))  4.13 us
    ppermute x3, waiting for transfers between devices, scatter_sum(): lax.ppermute(take(values, me ^ d).astype(BF), axis, by_distance(axis, d))  3.88 us
    ppermute x1, starting transfers between devices, per_device(): inward = lax.ppermute(jnp.where(even, high_edge, low_edge), 'rows', pairs)  3.72 us
  transfers between devices with their start and end apart: 21, of which 10 were waited for; matrix products, arithmetic and copies ran while one was open for 1% of the time, Pallas kernels for 31%

profile of v3, /device:TPU:0, one launch (start us, length us, event | category | flops | bytes accessed | tf_op | source)
XLA Modules:
  0.0 90.9 jit_solution(15854869711121856247)
XLA Ops:
  0.6 0.0 copy-start.1
  0.6 1.4 %collective-permute-start.2 = (bf16[12,64,256]{2,1,0:T(8,128)(2,1)}, bf16[12,64,256]{2,1,0:T(8,128)(2,1)S(1)}, u32[]{:S(2)}, u32[]{:S(2)}) collective-permute-start(bf16[12,64,256]{2,1,0:T(8,128)(2,1)} %bitcast.48), channel_id=1, source_target_pairs={{4,0},{8,4},{12,8},{5,1},{9,5},{13,9},{6,2},{10,6},{14,10},{7,3},{... | collective-permute-start | bytes 1179656 | tf_op jit(solution)/shard_map/ppermute | solution.py:611
  2.1 0.8 broadcast_select_fusion
  2.9 3.7 %collective-permute-start = (bf16[1,100,256]{2,1,0:T(8,128)(2,1)S(1)}, bf16[1,100,256]{2,1,0:T(8,128)(2,1)S(1)}, u32[]{:S(2)}, u32[]{:S(2)}) collective-permute-start(bf16[1,100,256]{2,1,0:T(8,128)(2,1)S(1)} %get-tuple-element.73), channel_id=1, source_target_pairs={{0,4},{4,0},{8,12},{12,8},{1,5},{5,1},{9,13},{13,9},{2,6},{6,2},{1... | collective-permute-start | bytes 153608 | tf_op jit(solution)/shard_map/ppermute | solution.py:609
  6.7 0.7 collective-permute-start.1
  7.3 0.0 copy-start.2
  7.3 1.6 %copy-done.2 = bf16[1,1,64,64,144]{4,3,2,1,0:T(8,128)(2,1)S(1)} copy-done((bf16[1,1,64,64,144]{4,3,2,1,0:T(8,128)(2,1)S(1)}, bf16[1,1,64,64,144]{4,3,2,1,0:T(8,128)(2,1)}, u32[]{:S(2)}) %copy-start.2) | copy-done | bytes 1179672
  8.9 0.7 copy-done.10
  9.6 2.1 %shard_map.145 = (bf16[8,72,128]{2,1,0:T(8,128)(2,1)S(1)}, bf16[8,72,128]{2,1,0:T(8,128)(2,1)S(1)}, bf16[8,72,128]{2,1,0:T(8,128)(2,1)S(1)}, bf16[8,72,128]{2,1,0:T(8,128)(2,1)S(1)}) custom-call(s32[4,4,32]{2,1,0:T(4,128)S(1)} %bitcast.51, bf16[64,64,144]{2,1,0:T(8,128)(2,1)S(1)} %bitcast.46), custom_call_target="tpu_custom_call" | custom-call | flops 1000000000 | bytes 1 | tf_op jit(solution)/shard_map/pallas_call | solution.py:29
  11.7 0.0 copy-start.6
  11.7 0.0 copy-start.9
  11.7 4.9 %collective-permute-start.3 = (bf16[8,72,128]{2,1,0:T(8,128)(2,1)S(1)}, bf16[8,72,128]{2,1,0:T(8,128)(2,1)S(1)}, u32[]{:S(2)}, u32[]{:S(2)}) collective-permute-start(bf16[8,72,128]{2,1,0:T(8,128)(2,1)S(1)} %get-tuple-element.46), channel_id=1, source_target_pairs={{0,4},{4,0},{8,12},{12,8},{1,5},{5,1},{9,13},{13,9},{2,6},{6,2},{1... | collective-permute-start | bytes 442376 | tf_op jit(solution)/shard_map/ppermute | solution.py:596
  16.7 0.0 collective-permute-start.4
  16.7 0.0 collective-permute-done.inward_ref
  16.7 2.4 %collective-permute-start.5 = (bf16[8,72,128]{2,1,0:T(8,128)(2,1)S(1)}, bf16[8,72,128]{2,1,0:T(8,128)(2,1)S(1)}, u32[]{:S(2)}, u32[]{:S(2)}) collective-permute-start(bf16[8,72,128]{2,1,0:T(8,128)(2,1)S(1)} %get-tuple-element.48), channel_id=1, source_target_pairs={{0,12},{4,8},{8,4},{12,0},{1,13},{5,9},{9,5},{13,1},{2,14},{6,10},... | collective-permute-start | bytes 442376 | tf_op jit(solution)/shard_map/ppermute | solution.py:596
  19.1 0.0 collective-permute-done.1.outward_ref
  19.1 0.0 collective-permute-done.2.tgt_low_ref
  19.1 0.0 copy-done.1
  19.1 6.7 %shard_map.146 = (bf16[12,64,256]{2,1,0:T(8,128)(2,1)}, bf16[11,64,256]{2,1,0:T(8,128)(2,1)S(1)}, bf16[1,64,256]{2,1,0:T(8,128)(2,1)S(1)}) custom-call(s32[1]{0:T(128)} %bitcast.even_ref, bf16[1,100,256]{2,1,0:T(8,128)(2,1)S(1)} %collective-permute-done.inward_ref, bf16[12,100,256]{2,1,0:T(8,128)(2,1)S(1)} %bitcast.45, ...), custom_call_target="tpu_custom_call" | custom-call | flops 1000000000 | bytes 1 | tf_op jit(solution)/shard_map/pallas_call | solution.py:29
  25.9 1.4 %collective-permute-start.9 = (bf16[11,64,256]{2,1,0:T(8,128)(2,1)S(1)}, bf16[11,64,256]{2,1,0:T(8,128)(2,1)S(1)}, u32[]{:S(2)}, u32[]{:S(2)}) collective-permute-start(bf16[11,64,256]{2,1,0:T(8,128)(2,1)S(1)} %get-tuple-element.43.top_ref), channel_id=1, source_target_pairs={{4,0},{8,4},{12,8},{5,1},{9,5},{13,9},{6,2},{10,6},{14,10},{7,3},{... | collective-permute-start | bytes 1081352 | tf_op jit(solution)/shard_map/ppermute | solution.py:621
  27.3 0.4 shard_map.148
  27.7 0.0 copy-start.4
  27.8 2.1 %shard_map.149 = (bf16[8,72,128]{2,1,0:T(8,128)(2,1)S(1)}, bf16[8,72,128]{2,1,0:T(8,128)(2,1)S(1)}, bf16[8,72,128]{2,1,0:T(8,128)(2,1)S(1)}, bf16[8,72,128]{2,1,0:T(8,128)(2,1)S(1)}) custom-call(s32[4,4,32]{2,1,0:T(4,128)S(1)} %bitcast.52, bf16[64,64,144]{2,1,0:T(8,128)(2,1)S(1)} %bitcast.47), custom_call_target="tpu_custom_call" | custom-call | flops 1000000000 | bytes 1 | tf_op jit(solution)/shard_map/pallas_call | solution.py:29
  29.9 2.7 %collective-permute-start.6 = (bf16[8,72,128]{2,1,0:T(8,128)(2,1)S(1)}, bf16[8,72,128]{2,1,0:T(8,128)(2,1)S(1)}, u32[]{:S(2)}, u32[]{:S(2)}) collective-permute-start(bf16[8,72,128]{2,1,0:T(8,128)(2,1)S(1)} %get-tuple-element.56), channel_id=1, source_target_pairs={{0,4},{4,0},{8,12},{12,8},{1,5},{5,1},{9,13},{13,9},{2,6},{6,2},{1... | collective-permute-start | bytes 442376 | tf_op jit(solution)/shard_map/ppermute | solution.py:596
  32.6 6.7 %shard_map.147 = (s32[5,32]{1,0:T(8,128)S(1)}, bf16[2,72,16,128]{3,2,1,0:T(8,128)(2,1)S(1)}, bf16[12,256,128]{2,1,0:T(8,128)(2,1)S(1)}) custom-call(s32[4,4,32]{2,1,0:T(4,128)S(1)} %bitcast.53, bf16[12,64,256]{2,1,0:T(8,128)(2,1)S(1)} %bitcast.49, bf16[12,64,256]{2,1,0:T(8,128)(2,1)S(1)} %collective-permute-done.2.tgt_low_ref, ...), custom_call_target="tpu_custom_call" | custom-call | flops 1000000000 | bytes 1 | tf_op jit(solution)/shard_map/pallas_call | solution.py:636
  39.3 0.1 fusion.9
  39.4 0.0 collective-permute-done.9.low_ref
  39.4 0.8 collective-permute-start.7
  40.2 2.1 %shard_map.150 = bf16[2,72,16,128]{3,2,1,0:T(8,128)(2,1)S(1)} custom-call(s32[5,32]{1,0:T(8,128)S(1)} %get-tuple-element.45.table_ref.refs_0_, bf16[12,256,128]{2,1,0:T(8,128)(2,1)S(1)} %get-tuple-element.59.own, bf16[11,64,256]{2,1,0:T(8,128)(2,1)S(1)} %collective-permute-done.9.low_ref), custom_call_target="tpu_custom_call" | custom-call | flops 1000000000 | bytes 1 | tf_op jit(solution)/shard_map/pallas_call | solution.py:29
  42.3 0.0 collective-permute-done.3.refs_2_
  42.4 2.1 %collective-permute-start.8 = (bf16[8,72,128]{2,1,0:T(8,128)(2,1)S(1)}, bf16[8,72,128]{2,1,0:T(8,128)(2,1)S(1)}, u32[]{:S(2)}, u32[]{:S(2)}) collective-permute-start(bf16[8,72,128]{2,1,0:T(8,128)(2,1)S(1)} %get-tuple-element.58), channel_id=1, source_target_pairs={{0,12},{4,8},{8,4},{12,0},{1,13},{5,9},{9,5},{13,1},{2,14},{6,10},... | collective-permute-start | bytes 442376 | tf_op jit(solution)/shard_map/ppermute | solution.py:596
  44.4 0.1 fusion.10
  44.5 0.0 collective-permute-done.4.refs_3_
  44.5 0.0 collective-permute-done.5.refs_4_
  44.6 8.3 %shard_map.151.refs_17_ = f32[2432,128]{1,0:T(8,128)S(1)} custom-call(s32[5,32]{1,0:T(8,128)S(1)} %get-tuple-element.45.table_ref.refs_0_, bf16[8,72,128]{2,1,0:T(8,128)(2,1)S(1)} %get-tuple-element.39.refs_1_, bf16[8,72,128]{2,1,0:T(8,128)(2,1)S(1)} %collective-permute-done.3.refs_2_, bf16[8,72,128]{2,1,0:T(8,128)(2,1)S(1)} %collective-permute-done.4.refs_3_, ...), custom_call_target="tpu_custom_call" | custom-call | flops 1000000000 | bytes 1 | tf_op jit(solution)/shard_map/pallas_call | solution.py:29
  52.9 0.0 collective-permute-done.6.refs_6_
  52.9 0.0 collective-permute-done.7.refs_7_
  52.9 0.0 collective-permute-done.8.refs_8_
  52.9 8.6 %shard_map.152 = (f32[1216,128]{1,0:T(8,128)S(1)}, bf16[1216,128]{1,0:T(8,128)(2,1)S(1)}) custom-call(s32[5,32]{1,0:T(8,128)S(1)} %get-tuple-element.45.table_ref.refs_0_, bf16[8,72,128]{2,1,0:T(8,128)(2,1)S(1)} %get-tuple-element.39.refs_1_, bf16[8,72,128]{2,1,0:T(8,128)(2,1)S(1)} %collective-permute-done.3.refs_2_, ...), custom_call_target="tpu_custom_call" | custom-call | flops 1000000000 | bytes 1 | tf_op jit(solution)/shard_map/pallas_call | solution.py:29
  61.5 0.1 collective-permute-start.10
  61.6 1.6 %collective-permute-done.10 = bf16[1216,128]{1,0:T(8,128)(2,1)S(1)} collective-permute-done((bf16[1216,128]{1,0:T(8,128)(2,1)S(1)}, bf16[1216,128]{1,0:T(8,128)(2,1)S(1)}, u32[]{:S(2)}, u32[]{:S(2)}) %collective-permute-start.10) | collective-permute-done | bytes 311328 | tf_op jit(solution)/shard_map/ppermute | solution.py:710
  63.2 0.1 convert_add_fusion
  63.3 2.5 %collective-permute-start.13 = (bf16[304,128]{1,0:T(8,128)(2,1)S(1)}, bf16[304,128]{1,0:T(8,128)(2,1)S(1)}, u32[]{:S(2)}, u32[]{:S(2)}) collective-permute-start(bf16[304,128]{1,0:T(8,128)(2,1)S(1)} %get-tuple-element.75), channel_id=1, source_target_pairs={{0,3},{1,2},{2,1},{3,0},{4,7},{5,6},{6,5},{7,4},{8,11},{9,10},{10,... | collective-permute-start | bytes 233480 | tf_op jit(solution)/shard_map/ppermute | solution.py:522
  65.8 0.5 collective-permute-start.12
  66.3 0.5 collective-permute-start.11
  66.9 1.8 %collective-permute-done.13 = bf16[304,128]{1,0:T(8,128)(2,1)S(1)} collective-permute-done((bf16[304,128]{1,0:T(8,128)(2,1)S(1)}, bf16[304,128]{1,0:T(8,128)(2,1)S(1)}, u32[]{:S(2)}, u32[]{:S(2)}) %collective-permute-start.13) | collective-permute-done | bytes 77856 | tf_op jit(solution)/shard_map/ppermute | solution.py:522
  68.7 1.6 %collective-permute-done.12 = bf16[304,128]{1,0:T(8,128)(2,1)S(1)} collective-permute-done((bf16[304,128]{1,0:T(8,128)(2,1)S(1)}, bf16[304,128]{1,0:T(8,128)(2,1)S(1)}, u32[]{:S(2)}, u32[]{:S(2)}) %collective-permute-start.12) | collective-permute-done | bytes 77856 | tf_op jit(solution)/shard_map/ppermute | solution.py:522
  70.3 0.4 collective-permute-done.11
  70.8 1.9 %collective-permute-start.16 = (bf16[304,128]{1,0:T(8,128)(2,1)S(1)}, bf16[304,128]{1,0:T(8,128)(2,1)S(1)}, u32[]{:S(2)}, u32[]{:S(2)}) collective-permute-start(bf16[304,128]{1,0:T(8,128)(2,1)S(1)} %fusion.3), channel_id=1, source_target_pairs={{0,12},{4,8},{8,4},{12,0},{1,13},{5,9},{9,5},{13,1},{2,14},{6,10},... | collective-permute-start | bytes 233480 | tf_op jit(solution)/shard_map/ppermute | solution.py:549
  72.7 0.8 collective-permute-start.15
  73.4 1.8 %collective-permute-start.14 = (bf16[304,128]{1,0:T(8,128)(2,1)S(1)}, bf16[304,128]{1,0:T(8,128)(2,1)S(1)}, u32[]{:S(2)}, u32[]{:S(2)}) collective-permute-start(bf16[304,128]{1,0:T(8,128)(2,1)S(1)} %fusion.3), channel_id=1, source_target_pairs={{0,4},{4,0},{8,12},{12,8},{1,5},{5,1},{9,13},{13,9},{2,6},{6,2},{1... | collective-permute-start | bytes 233480 | tf_op jit(solution)/shard_map/ppermute | solution.py:549
  75.2 2.5 %collective-permute-done.16 = bf16[304,128]{1,0:T(8,128)(2,1)S(1)} collective-permute-done((bf16[304,128]{1,0:T(8,128)(2,1)S(1)}, bf16[304,128]{1,0:T(8,128)(2,1)S(1)}, u32[]{:S(2)}, u32[]{:S(2)}) %collective-permute-start.16) | collective-permute-done | bytes 77856 | tf_op jit(solution)/shard_map/ppermute | solution.py:549
  77.7 2.3 %collective-permute-done.15 = bf16[304,128]{1,0:T(8,128)(2,1)S(1)} collective-permute-done((bf16[304,128]{1,0:T(8,128)(2,1)S(1)}, bf16[304,128]{1,0:T(8,128)(2,1)S(1)}, u32[]{:S(2)}, u32[]{:S(2)}) %collective-permute-start.15) | collective-permute-done | bytes 77856 | tf_op jit(solution)/shard_map/ppermute | solution.py:549
  80.0 0.0 collective-permute-done.14
  80.1 1.5 %collective-permute-start.17 = (bf16[304,128]{1,0:T(8,128)(2,1)S(1)}, bf16[304,128]{1,0:T(8,128)(2,1)S(1)}, u32[]{:S(2)}, u32[]{:S(2)}) collective-permute-start(bf16[304,128]{1,0:T(8,128)(2,1)S(1)} %reduce-precision_convert_fusion), channel_id=1, source_target_pairs={{0,3},{1,2},{2,1},{3,0},{4,7},{5,6},{6,5},{7,4},{8,11},{9,10},{10,... | collective-permute-start | bytes 233480 | tf_op jit(solution)/shard_map/ppermute | solution.py:532
  81.6 1.9 %collective-permute-start.18 = (bf16[304,128]{1,0:T(8,128)(2,1)S(1)}, bf16[304,128]{1,0:T(8,128)(2,1)S(1)}, u32[]{:S(2)}, u32[]{:S(2)}) collective-permute-start(bf16[304,128]{1,0:T(8,128)(2,1)S(1)} %reduce-precision_convert_fusion), channel_id=1, source_target_pairs={{0,2},{1,3},{2,0},{3,1},{4,6},{5,7},{6,4},{7,5},{8,10},{9,11},{10,... | collective-permute-start | bytes 233480 | tf_op jit(solution)/shard_map/ppermute | solution.py:532
  83.6 0.3 collective-permute-start.19
  83.8 2.2 %collective-permute-done.17 = bf16[304,128]{1,0:T(8,128)(2,1)S(1)} collective-permute-done((bf16[304,128]{1,0:T(8,128)(2,1)S(1)}, bf16[304,128]{1,0:T(8,128)(2,1)S(1)}, u32[]{:S(2)}, u32[]{:S(2)}) %collective-permute-start.17) | collective-permute-done | bytes 77856 | tf_op jit(solution)/shard_map/ppermute | solution.py:532
  86.1 0.4 collective-permute-done.18
  86.5 1.5 %collective-permute-done.19 = bf16[304,128]{1,0:T(8,128)(2,1)S(1)} collective-permute-done((bf16[304,128]{1,0:T(8,128)(2,1)S(1)}, bf16[304,128]{1,0:T(8,128)(2,1)S(1)}, u32[]{:S(2)}, u32[]{:S(2)}) %collective-permute-start.19) | collective-permute-done | bytes 77856 | tf_op jit(solution)/shard_map/ppermute | solution.py:532
  88.0 0.1 select_bitcast_fusion.3
  88.1 0.1 collective-permute-start.20
  88.2 1.6 %collective-permute-done.20.other_ref = bf16[1216,128]{1,0:T(8,128)(2,1)S(1)} collective-permute-done((bf16[1216,128]{1,0:T(8,128)(2,1)S(1)}, bf16[1216,128]{1,0:T(8,128)(2,1)S(1)}, u32[]{:S(2)}, u32[]{:S(2)}) %collective-permute-start.20) | collective-permute-done | bytes 311328 | tf_op jit(solution)/shard_map/ppermute | solution.py:722
  89.8 1.1 %shard_map.153 = (f32[128,1152]{1,0:T(8,128)}, f32[128,1152]{1,0:T(8,128)}, f32[64,128]{1,0:T(8,128)}, f32[32,128]{1,0:T(8,128)}, f32[1,1]{1,0:T(1,128)}) custom-call(bf16[1216,128]{1,0:T(8,128)(2,1)S(1)} %bitcast.43, bf16[1216,128]{1,0:T(8,128)(2,1)S(1)} %collective-permute-done.20.other_ref), custom_call_target="tpu_custom_call" | custom-call | flops 1000000000 | bytes 1 | tf_op jit(solution)/shard_map/pallas_call | solution.py:29
  (23 shorter events, 0.2 us)
Async XLA Ops:
  0.6 18.5 %copy-start.1 = (bf16[1,100,12,256]{3,1,2,0:T(8,128)(2,1)S(1)}, bf16[1,100,12,256]{3,1,2,0:T(8,128)(2,1)}, u32[]{:S(2)}) copy-start(bf16[1,100,12,256]{3,1,2,0:T(8,128)(2,1)} %param.10) | copy-start | bytes 1843204
  0.6 18.5 %collective-permute-start.2 = (bf16[12,64,256]{2,1,0:T(8,128)(2,1)}, bf16[12,64,256]{2,1,0:T(8,128)(2,1)S(1)}, u32[]{:S(2)}, u32[]{:S(2)}) collective-permute-start(bf16[12,64,256]{2,1,0:T(8,128)(2,1)} %bitcast.48), channel_id=1, source_target_pairs={{4,0},{8,4},{12,8},{5,1},{9,5},{13,9},{6,2},{10,6},{14,10},{7,3},{... | collective-permute-start | bytes 1179656 | tf_op jit(solution)/shard_map/ppermute | solution.py:611
  2.9 13.7 %collective-permute-start = (bf16[1,100,256]{2,1,0:T(8,128)(2,1)S(1)}, bf16[1,100,256]{2,1,0:T(8,128)(2,1)S(1)}, u32[]{:S(2)}, u32[]{:S(2)}) collective-permute-start(bf16[1,100,256]{2,1,0:T(8,128)(2,1)S(1)} %get-tuple-element.73), channel_id=1, source_target_pairs={{0,4},{4,0},{8,12},{12,8},{1,5},{5,1},{9,13},{13,9},{2,6},{6,2},{1... | collective-permute-start | bytes 153608 | tf_op jit(solution)/shard_map/ppermute | solution.py:609
  6.7 12.5 %collective-permute-start.1 = (bf16[1,100,256]{2,1,0:T(8,128)(2,1)S(1)}, bf16[1,100,256]{2,1,0:T(8,128)(2,1)S(1)}, u32[]{:S(2)}, u32[]{:S(2)}) collective-permute-start(bf16[1,100,256]{2,1,0:T(8,128)(2,1)S(1)} %get-tuple-element.72), channel_id=1, source_target_pairs={{4,8},{8,4},{5,9},{9,5},{6,10},{10,6},{7,11},{11,7},{20,24},{24,20... | collective-permute-start | bytes 153608 | tf_op jit(solution)/shard_map/ppermute | solution.py:610
  7.3 1.6 %copy-start.2 = (bf16[1,1,64,64,144]{4,3,2,1,0:T(8,128)(2,1)S(1)}, bf16[1,1,64,64,144]{4,3,2,1,0:T(8,128)(2,1)}, u32[]{:S(2)}) copy-start(bf16[1,1,64,64,144]{4,3,2,1,0:T(8,128)(2,1)} %param.12) | copy-start | bytes 3538948
  8.9 0.7 copy-start.10
  9.6 9.5 %copy-start.7 = (bf16[128,900]{0,1:T(8,128)(2,1)S(1)}, bf16[128,900]{0,1:T(8,128)(2,1)}, u32[]{:S(2)}) copy-start(bf16[128,900]{0,1:T(8,128)(2,1)} %param.14) | copy-start | bytes 691204
  9.6 9.5 %copy-start.8 = (bf16[64,128]{1,0:T(8,128)(2,1)S(1)}, bf16[64,128]{1,0:T(8,128)(2,1)}, u32[]{:S(2)}) copy-start(bf16[64,128]{1,0:T(8,128)(2,1)} %proj_ref.1) | copy-start | bytes 49156
  11.7 15.6 %copy-start.5 = (bf16[128,1152]{1,0:T(8,128)(2,1)S(1)}, bf16[128,1152]{1,0:T(8,128)(2,1)}, u32[]{:S(2)}) copy-start(bf16[128,1152]{1,0:T(8,128)(2,1)} %one_ref) | copy-start | bytes 884740
  11.7 15.6 %copy-start.6 = (bf16[128,1152]{1,0:T(8,128)(2,1)S(1)}, bf16[128,1152]{1,0:T(8,128)(2,1)}, u32[]{:S(2)}) copy-start(bf16[128,1152]{1,0:T(8,128)(2,1)} %two_ref) | copy-start | bytes 884740
  11.7 15.6 %copy-start.9 = (bf16[64,128]{1,0:T(8,128)(2,1)S(1)}, bf16[64,128]{1,0:T(8,128)(2,1)}, u32[]{:S(2)}) copy-start(bf16[64,128]{1,0:T(8,128)(2,1)} %proj_ref.2) | copy-start | bytes 49156
  11.7 30.6 %collective-permute-start.3 = (bf16[8,72,128]{2,1,0:T(8,128)(2,1)S(1)}, bf16[8,72,128]{2,1,0:T(8,128)(2,1)S(1)}, u32[]{:S(2)}, u32[]{:S(2)}) collective-permute-start(bf16[8,72,128]{2,1,0:T(8,128)(2,1)S(1)} %get-tuple-element.46), channel_id=1, source_target_pairs={{0,4},{4,0},{8,12},{12,8},{1,5},{5,1},{9,13},{13,9},{2,6},{6,2},{1... | collective-permute-start | bytes 442376 | tf_op jit(solution)/shard_map/ppermute | solution.py:596
  16.7 27.9 %collective-permute-start.4 = (bf16[8,72,128]{2,1,0:T(8,128)(2,1)S(1)}, bf16[8,72,128]{2,1,0:T(8,128)(2,1)S(1)}, u32[]{:S(2)}, u32[]{:S(2)}) collective-permute-start(bf16[8,72,128]{2,1,0:T(8,128)(2,1)S(1)} %get-tuple-element.47), channel_id=1, source_target_pairs={{0,8},{4,12},{8,0},{12,4},{1,9},{5,13},{9,1},{13,5},{2,10},{6,14},... | collective-permute-start | bytes 442376 | tf_op jit(solution)/shard_map/ppermute | solution.py:596
  16.7 27.9 %collective-permute-start.5 = (bf16[8,72,128]{2,1,0:T(8,128)(2,1)S(1)}, bf16[8,72,128]{2,1,0:T(8,128)(2,1)S(1)}, u32[]{:S(2)}, u32[]{:S(2)}) collective-permute-start(bf16[8,72,128]{2,1,0:T(8,128)(2,1)S(1)} %get-tuple-element.48), channel_id=1, source_target_pairs={{0,12},{4,8},{8,4},{12,0},{1,13},{5,9},{9,5},{13,1},{2,14},{6,10},... | collective-permute-start | bytes 442376 | tf_op jit(solution)/shard_map/ppermute | solution.py:596
  25.9 1.9 %copy-start.3 = (bf16[1,1,64,64,144]{4,3,2,1,0:T(8,128)(2,1)S(1)}, bf16[1,1,64,64,144]{4,3,2,1,0:T(8,128)(2,1)}, u32[]{:S(2)}) copy-start(bf16[1,1,64,64,144]{4,3,2,1,0:T(8,128)(2,1)} %param.12) | copy-start | bytes 3538948
  25.9 1.9 %copy-start.11 = (s32[1,4,32,4]{2,3,1,0:T(4,128)S(1)}, s32[1,4,32,4]{2,3,1,0:T(4,128)}, u32[]{:S(2)}) copy-start(s32[1,4,32,4]{2,3,1,0:T(4,128)} %param.13) | copy-start | bytes 6148
  25.9 13.6 %collective-permute-start.9 = (bf16[11,64,256]{2,1,0:T(8,128)(2,1)S(1)}, bf16[11,64,256]{2,1,0:T(8,128)(2,1)S(1)}, u32[]{:S(2)}, u32[]{:S(2)}) collective-permute-start(bf16[11,64,256]{2,1,0:T(8,128)(2,1)S(1)} %get-tuple-element.43.top_ref), channel_id=1, source_target_pairs={{4,0},{8,4},{12,8},{5,1},{9,5},{13,9},{6,2},{10,6},{14,10},{7,3},{... | collective-permute-start | bytes 1081352 | tf_op jit(solution)/shard_map/ppermute | solution.py:621
  27.7 4.8 %copy-start.4 = (bf16[1,64,12,256]{3,1,2,0:T(8,128)(2,1)S(1)}, bf16[1,64,12,256]{3,1,2,0:T(8,128)(2,1)}, u32[]{:S(2)}) copy-start(bf16[1,64,12,256]{3,1,2,0:T(8,128)(2,1)} %param.11) | copy-start | bytes 1179652
  29.9 23.0 %collective-permute-start.6 = (bf16[8,72,128]{2,1,0:T(8,128)(2,1)S(1)}, bf16[8,72,128]{2,1,0:T(8,128)(2,1)S(1)}, u32[]{:S(2)}, u32[]{:S(2)}) collective-permute-start(bf16[8,72,128]{2,1,0:T(8,128)(2,1)S(1)} %get-tuple-element.56), channel_id=1, source_target_pairs={{0,4},{4,0},{8,12},{12,8},{1,5},{5,1},{9,13},{13,9},{2,6},{6,2},{1... | collective-permute-start | bytes 442376 | tf_op jit(solution)/shard_map/ppermute | solution.py:596
  39.4 13.5 %collective-permute-start.7 = (bf16[8,72,128]{2,1,0:T(8,128)(2,1)S(1)}, bf16[8,72,128]{2,1,0:T(8,128)(2,1)S(1)}, u32[]{:S(2)}, u32[]{:S(2)}) collective-permute-start(bf16[8,72,128]{2,1,0:T(8,128)(2,1)S(1)} %get-tuple-element.57), channel_id=1, source_target_pairs={{0,8},{4,12},{8,0},{12,4},{1,9},{5,13},{9,1},{13,5},{2,10},{6,14},... | collective-permute-start | bytes 442376 | tf_op jit(solution)/shard_map/ppermute | solution.py:596
  40.2 4.4 %copy-start = (f32[32,128]{1,0:T(8,128)S(1)}, f32[32,128]{1,0:T(8,128)}, u32[]{:S(2)}) copy-start(f32[32,128]{1,0:T(8,128)} %refs_11_.1) | copy-start | bytes 49156
  42.4 10.6 %collective-permute-start.8 = (bf16[8,72,128]{2,1,0:T(8,128)(2,1)S(1)}, bf16[8,72,128]{2,1,0:T(8,128)(2,1)S(1)}, u32[]{:S(2)}, u32[]{:S(2)}) collective-permute-start(bf16[8,72,128]{2,1,0:T(8,128)(2,1)S(1)} %get-tuple-element.58), channel_id=1, source_target_pairs={{0,12},{4,8},{8,4},{12,0},{1,13},{5,9},{9,5},{13,1},{2,14},{6,10},... | collective-permute-start | bytes 442376 | tf_op jit(solution)/shard_map/ppermute | solution.py:596
  61.5 1.7 %collective-permute-start.10 = (bf16[1216,128]{1,0:T(8,128)(2,1)S(1)}, bf16[1216,128]{1,0:T(8,128)(2,1)S(1)}, u32[]{:S(2)}, u32[]{:S(2)}) collective-permute-start(bf16[1216,128]{1,0:T(8,128)(2,1)S(1)} %get-tuple-element.66), channel_id=1, source_target_pairs={{0,16},{16,0},{1,17},{17,1},{2,18},{18,2},{3,19},{19,3},{4,20},{20... | collective-permute-start | bytes 933896 | tf_op jit(solution)/shard_map/ppermute | solution.py:710
  63.3 5.4 %collective-permute-start.13 = (bf16[304,128]{1,0:T(8,128)(2,1)S(1)}, bf16[304,128]{1,0:T(8,128)(2,1)S(1)}, u32[]{:S(2)}, u32[]{:S(2)}) collective-permute-start(bf16[304,128]{1,0:T(8,128)(2,1)S(1)} %get-tuple-element.75), channel_id=1, source_target_pairs={{0,3},{1,2},{2,1},{3,0},{4,7},{5,6},{6,5},{7,4},{8,11},{9,10},{10,... | collective-permute-start | bytes 233480 | tf_op jit(solution)/shard_map/ppermute | solution.py:522
  65.8 4.5 %collective-permute-start.12 = (bf16[304,128]{1,0:T(8,128)(2,1)S(1)}, bf16[304,128]{1,0:T(8,128)(2,1)S(1)}, u32[]{:S(2)}, u32[]{:S(2)}) collective-permute-start(bf16[304,128]{1,0:T(8,128)(2,1)S(1)} %get-tuple-element.76), channel_id=1, source_target_pairs={{0,2},{1,3},{2,0},{3,1},{4,6},{5,7},{6,4},{7,5},{8,10},{9,11},{10,... | collective-permute-start | bytes 233480 | tf_op jit(solution)/shard_map/ppermute | solution.py:522
  66.3 4.4 %collective-permute-start.11 = (bf16[304,128]{1,0:T(8,128)(2,1)S(1)}, bf16[304,128]{1,0:T(8,128)(2,1)S(1)}, u32[]{:S(2)}, u32[]{:S(2)}) collective-permute-start(bf16[304,128]{1,0:T(8,128)(2,1)S(1)} %get-tuple-element.74), channel_id=1, source_target_pairs={{0,1},{1,0},{2,3},{3,2},{4,5},{5,4},{6,7},{7,6},{8,9},{9,8},{10,11... | collective-permute-start | bytes 233480 | tf_op jit(solution)/shard_map/ppermute | solution.py:522
  70.8 6.9 %collective-permute-start.16 = (bf16[304,128]{1,0:T(8,128)(2,1)S(1)}, bf16[304,128]{1,0:T(8,128)(2,1)S(1)}, u32[]{:S(2)}, u32[]{:S(2)}) collective-permute-start(bf16[304,128]{1,0:T(8,128)(2,1)S(1)} %fusion.3), channel_id=1, source_target_pairs={{0,12},{4,8},{8,4},{12,0},{1,13},{5,9},{9,5},{13,1},{2,14},{6,10},... | collective-permute-start | bytes 233480 | tf_op jit(solution)/shard_map/ppermute | solution.py:549
  72.7 7.4 %collective-permute-start.15 = (bf16[304,128]{1,0:T(8,128)(2,1)S(1)}, bf16[304,128]{1,0:T(8,128)(2,1)S(1)}, u32[]{:S(2)}, u32[]{:S(2)}) collective-permute-start(bf16[304,128]{1,0:T(8,128)(2,1)S(1)} %fusion.3), channel_id=1, source_target_pairs={{0,8},{4,12},{8,0},{12,4},{1,9},{5,13},{9,1},{13,5},{2,10},{6,14},... | collective-permute-start | bytes 233480 | tf_op jit(solution)/shard_map/ppermute | solution.py:549
  73.4 6.6 %collective-permute-start.14 = (bf16[304,128]{1,0:T(8,128)(2,1)S(1)}, bf16[304,128]{1,0:T(8,128)(2,1)S(1)}, u32[]{:S(2)}, u32[]{:S(2)}) collective-permute-start(bf16[304,128]{1,0:T(8,128)(2,1)S(1)} %fusion.3), channel_id=1, source_target_pairs={{0,4},{4,0},{8,12},{12,8},{1,5},{5,1},{9,13},{13,9},{2,6},{6,2},{1... | collective-permute-start | bytes 233480 | tf_op jit(solution)/shard_map/ppermute | solution.py:549
  80.1 5.9 %collective-permute-start.17 = (bf16[304,128]{1,0:T(8,128)(2,1)S(1)}, bf16[304,128]{1,0:T(8,128)(2,1)S(1)}, u32[]{:S(2)}, u32[]{:S(2)}) collective-permute-start(bf16[304,128]{1,0:T(8,128)(2,1)S(1)} %reduce-precision_convert_fusion), channel_id=1, source_target_pairs={{0,3},{1,2},{2,1},{3,0},{4,7},{5,6},{6,5},{7,4},{8,11},{9,10},{10,... | collective-permute-start | bytes 233480 | tf_op jit(solution)/shard_map/ppermute | solution.py:532
  81.6 4.8 %collective-permute-start.18 = (bf16[304,128]{1,0:T(8,128)(2,1)S(1)}, bf16[304,128]{1,0:T(8,128)(2,1)S(1)}, u32[]{:S(2)}, u32[]{:S(2)}) collective-permute-start(bf16[304,128]{1,0:T(8,128)(2,1)S(1)} %reduce-precision_convert_fusion), channel_id=1, source_target_pairs={{0,2},{1,3},{2,0},{3,1},{4,6},{5,7},{6,4},{7,5},{8,10},{9,11},{10,... | collective-permute-start | bytes 233480 | tf_op jit(solution)/shard_map/ppermute | solution.py:532
  83.6 4.4 %collective-permute-start.19 = (bf16[304,128]{1,0:T(8,128)(2,1)S(1)}, bf16[304,128]{1,0:T(8,128)(2,1)S(1)}, u32[]{:S(2)}, u32[]{:S(2)}) collective-permute-start(bf16[304,128]{1,0:T(8,128)(2,1)S(1)} %reduce-precision_convert_fusion), channel_id=1, source_target_pairs={{0,1},{1,0},{2,3},{3,2},{4,5},{5,4},{6,7},{7,6},{8,9},{9,8},{10,11... | collective-permute-start | bytes 233480 | tf_op jit(solution)/shard_map/ppermute | solution.py:532
  88.1 1.7 %collective-permute-start.20 = (bf16[1216,128]{1,0:T(8,128)(2,1)S(1)}, bf16[1216,128]{1,0:T(8,128)(2,1)S(1)}, u32[]{:S(2)}, u32[]{:S(2)}) collective-permute-start(bf16[1216,128]{1,0:T(8,128)(2,1)S(1)} %bitcast.42), channel_id=1, source_target_pairs={{0,16},{16,0},{1,17},{17,1},{2,18},{18,2},{3,19},{19,3},{4,20},{20... | collective-permute-start | bytes 933896 | tf_op jit(solution)/shard_map/ppermute | solution.py:722

commit v4 on v3

--- a/solution.py
+++ b/solution.py
@@ -15,6 +15,8 @@
 TN_FORM = (((0,), (0,)), ((), ()))
 MIB = 1024 * 1024
 GROUP = 4
+COSTS = (1000000000, 1000000000, 10000000000, 1000000000, 10000000000, 10000000000)
+UNROLL = 16
 
 
 def matmul(left, right):
@@ -25,7 +27,7 @@
 SM = pl.BlockSpec(memory_space=pltpu.SMEM)
 
 
-def call(kernel, outs, ins, specs, scratch=(), limit=24):
+def call(kernel, outs, ins, specs, scratch=(), limit=24, cost=0):
     return pl.pallas_call(
         kernel,
         out_shape=outs,
@@ -33,7 +35,7 @@
         out_specs=jax.tree.map(lambda _: VM, outs),
         scratch_shapes=list(scratch),
         compiler_params=pltpu.CompilerParams(vmem_limit_bytes=limit * MIB),
-        cost_estimate=pl.CostEstimate(flops=1000000000, bytes_accessed=1, transcendentals=0),
+        cost_estimate=pl.CostEstimate(flops=cost, bytes_accessed=1, transcendentals=0),
     )(*ins)
 
 
@@ -160,7 +162,7 @@
         put(r + 1, own_ref[r])
         return carry
 
-    lax.fori_loop(0, rows, fill, 0)
+    lax.fori_loop(0, rows, fill, 0, unroll=12)
 
     def one(r, carry):
         stack = cols_ref[pl.ds(r, 3)].reshape(9 * deep, width)
@@ -169,74 +171,63 @@
         mean_ref[r] = matmul(proj_ref[...], act).astype(BF)
         return carry
 
-    lax.fori_loop(0, rows, one, 0, unroll=2)
+    lax.fori_loop(0, rows, one, 0, unroll=12)
     top_ref[...] = mean_ref[0 : rows - 1]
     last_ref[...] = mean_ref[rows - 1 : rows]
 
 
-def painter(width):
-    eye = (
+def identity(width):
+    return (
         lax.broadcasted_iota(jnp.int32, (width, width), 0)
         == lax.broadcasted_iota(jnp.int32, (width, width), 1)
     ).astype(BF)
 
-    def paint(cells):
-        following = pltpu.roll(cells.astype(F32), width - 1, 1).astype(BF)
-        both = jnp.concatenate([cells, following], axis=0)
-        return lax.dot_general(eye, both, NT_FORM, preferred_element_type=F32)
-
-    return paint
-
-
-def gather(table_ref, image, got, out_ref):
-    chunks, _, count, _ = out_ref.shape
-    rows = 12
+
+def paint(eye, pieces):
+    return lax.dot_general(eye, jnp.concatenate(pieces, axis=0), NT_FORM, preferred_element_type=F32)
+
+
+def own_kernel(exchange, deep, count, region_ref, tgt_ref, top_ref, last_ref, table_ref, image, seen):
+    tables_kernel(exchange, deep, count, region_ref, table_ref, seen)
+    rows, width, wide = image.shape
+    eye = identity(width)
+    means = [top_ref[r] for r in range(rows - 1)] + [last_ref[0]]
+    for r in range(0, rows, 2):
+        both = paint(eye, [means[r], tgt_ref[r], means[r + 1], tgt_ref[r + 1]])
+        image[r] = both[:, :wide].astype(BF)
+        image[r + 1] = both[:, wide:].astype(BF)
+
+
+def gather_kernel(table_ref, own, mean_ref, tgt_ref, mp_ref, tp_ref, image, evens, odds):
+    rows, width, wide = own.shape
+    chunks, _, count, _ = mp_ref.shape
     pairs = rows // 2
+    eye = identity(width)
+    image[0:rows] = own[...].astype(F32)
+    for r in range(0, rows - 1, 2):
+        many = min(2, rows - 1 - r)
+        both = paint(eye, sum([[mean_ref[r + i], tgt_ref[r + i]] for i in range(many)], []))
+        for i in range(many):
+            image[rows + r + i] = both[:, i * wide : (i + 1) * wide]
+    half = wide // 2
+    low = lax.broadcasted_iota(jnp.int32, evens.shape, 1) < half
     for chunk in range(chunks):
 
         def patch(k, carry, chunk=chunk):
             top = table_ref[TOP, chunk * count + k]
             left = table_ref[LEFT, chunk * count + k]
             for r in range(rows):
-                got[pl.ds(r * pairs * count + k, pairs, stride=count), :] = image[
-                    top + r, pl.ds(left, pairs, stride=2), :
-                ]
+                span = pl.ds(r * pairs * count + k, pairs, stride=count)
+                evens[span, :] = image[top + r, pl.ds(left, pairs, stride=2), :]
+                odds[span, :] = image[top + r, pl.ds(left + 1, pairs, stride=2), :]
             return carry
 
-        lax.fori_loop(0, count, patch, 0, unroll=2)
-        out_ref[chunk] = got[...].astype(BF).reshape(out_ref.shape[1:])
-
-
-def target_kernel(
-    exchange, deep, region_ref, tgt_ref, tgt_low_ref, top_ref, last_ref, table_ref, tp_ref, img_m, image, got, seen
-):
-    tables_kernel(exchange, deep, tp_ref.shape[2], region_ref, table_ref, seen)
-    paint = painter(tgt_ref.shape[2])
-    rows = tgt_ref.shape[0]
-
-    def one(r, carry):
-        img_m[r] = paint(top_ref[r]).astype(BF)
-        image[r] = paint(tgt_ref[r])
-        image[rows + r] = paint(tgt_low_ref[r])
-        return carry
-
-    lax.fori_loop(0, rows - 1, one, 0)
-    img_m[rows - 1] = paint(last_ref[0]).astype(BF)
-    image[rows - 1] = paint(tgt_ref[rows - 1])
-    gather(table_ref, image, got, tp_ref)
-
-
-def mean_kernel(table_ref, own, low_ref, mp_ref, image, got):
-    rows = own.shape[0]
-    paint = painter(own.shape[1])
-    image[0:rows] = own[...].astype(F32)
-
-    def low(r, carry):
-        image[rows + r] = paint(low_ref[r])
-        return carry
-
-    lax.fori_loop(0, rows - 1, low, 0, unroll=11)
-    gather(table_ref, image, got, mp_ref)
+        lax.fori_loop(0, count, patch, 0, unroll=min(UNROLL, count))
+        even, odd = evens[...], odds[...]
+        mean = jnp.where(low, even, pltpu.roll(odd, half, 1))
+        goal = jnp.where(low, pltpu.roll(even, half, 1), odd)
+        mp_ref[chunk] = mean.astype(BF).reshape(mp_ref.shape[1:])
+        tp_ref[chunk] = goal.astype(BF).reshape(tp_ref.shape[1:])
 
 
 def chunk_kernel(chunk, last, pieces, *refs):
@@ -253,7 +244,7 @@
         refs = refs[3:]
     else:
         out_ref, refs = refs[0], refs[1:]
-    (stage, nz, xn, xm, x2n, x2m, e1, o1, e2, o2, slope1, res, noisy, act2, gout, gt, emb, fac, by_level) = refs
+    (stage, nz, xn, xm, x2n, x2m, e1, o1, e2, o2, slope1, res, noisy, act2, back, gout, gt, emb, fac, by_level) = refs
     _, cells, count, wide = mp_ref.shape
     rows = 12
     pairs = cells // rows
@@ -276,7 +267,10 @@
     half = wide // 2
 
     for ref in (xn, xm, e1, o1, e2, o2):
-        ref[...] = jnp.zeros(ref.shape, BF)
+        for at in (0, rows + 1):
+            ref[at] = jnp.zeros(ref.shape[1:], BF)
+        for at in (0, pairs + 1):
+            ref[1 : rows + 1, at] = jnp.zeros((rows,) + ref.shape[2:], BF)
     at = 0
     for ref in noise_refs:
         stage[at : at + ref.shape[0]] = ref[...]
@@ -295,9 +289,9 @@
     scale_in, sigma, skip, scale_out, grad_scale = (spread(i) for i in range(5))
     lane = lax.broadcasted_iota(jnp.int32, (1, 1, count, wide), 3)
 
-    mean_bf = mp_ref[0]
+    mean_bf = mp_ref[chunk]
     mean = mean_bf.astype(F32)
-    residual = tp_ref[0].astype(F32) - mean
+    residual = tp_ref[chunk].astype(F32) - mean
     noised = residual + sigma * nz[...].reshape(cells, count, wide)
     res[...] = residual.reshape(total, wide)
     noisy[...] = noised.reshape(total, wide)
@@ -322,23 +316,28 @@
 
     tile = group * pairs * count
     emb_pair = jnp.concatenate([emb[...], emb[...]], axis=1)[None]
-    for r in range(0, rows, group):
-        left = jnp.concatenate(sum([stack_in(r + a, group) for a in range(3)], []), axis=1)
-        pre = matmul(left, w1_ref[...]).reshape(group * pairs, count, 2 * wide) + emb_pair
+    def span_of(g):
+        return pl.ds(g * tile, tile)
+
+    def conv(stack, weight_ref, g):
+        left = jnp.concatenate(sum([stack(g * group + a, group) for a in range(3)], []), axis=1)
+        return matmul(left, weight_ref[...])
+
+    def inner(ref, g):
+        return ref.at[g * group + 1 : g * group + 1 + group, 1 : pairs + 1]
+
+    def first(g, pre):
+        pre = pre.reshape(group * pairs, count, 2 * wide) + emb_pair
         gate = jax.nn.sigmoid(pre)
-        act = (pre * gate).astype(BF)
-        slope1[r * pairs * count : r * pairs * count + tile, :] = (
-            gate * (1.0 + pre * (1.0 - gate))
-        ).reshape(tile, 2 * wide)
-        act = shape4(act, group)
-        e1[r + 1 : r + 1 + group, 1 : pairs + 1] = act[..., :wide]
-        o1[r + 1 : r + 1 + group, 1 : pairs + 1] = act[..., wide:]
-
-    loss = jnp.zeros((count, wide), F32)
-    for r in range(0, rows, group):
-        span = pl.ds(r * pairs * count, tile)
-        left = jnp.concatenate(sum([stack_eo(e1, o1, r + a, group) for a in range(3)], []), axis=1)
-        pre = matmul(left, w2_ref[...])
+        act = shape4((pre * gate).astype(BF), group)
+        slope1[span_of(g), :] = (gate * (1.0 + pre * (1.0 - gate))).reshape(tile, 2 * wide)
+        inner(e1, g)[...] = act[..., :wide]
+        inner(o1, g)[...] = act[..., wide:]
+
+    losses = []
+
+    def second(g, pre):
+        span = span_of(g)
         gate = jax.nn.sigmoid(pre)
         act = (pre * gate).astype(BF)
         slope = gate * (1.0 + pre * (1.0 - gate))
@@ -349,25 +348,52 @@
             + scale_out * output
             - res[span, :].reshape(group * pairs, count, wide)
         )
-        loss = loss + jnp.sum(error * error, axis=0)
+        losses.append(jnp.sum(error * error, axis=0))
         grad_output = (grad_scale * error).astype(BF).reshape(tile, wide)
         gout[span, :] = grad_output
-        grad_pre = (matmul(grad_output, pg_ref[...]) * slope).astype(BF)
-        grad_pre = shape4(grad_pre, group)
-        e2[r + 1 : r + 1 + group, 1 : pairs + 1] = grad_pre[..., :wide]
-        o2[r + 1 : r + 1 + group, 1 : pairs + 1] = grad_pre[..., wide:]
+        grad_pre = shape4((matmul(grad_output, pg_ref[...]) * slope).astype(BF), group)
+        inner(e2, g)[...] = grad_pre[..., :wide]
+        inner(o2, g)[...] = grad_pre[..., wide:]
+
+    partial = []
+
+    def third(g, pre):
+        span = span_of(g)
+        grad = (pre * slope1[span, :]).astype(BF)
+        back[span, :] = grad
+        partial.append(jnp.sum(grad.astype(F32).reshape(group * pairs, count, 2 * wide), axis=0))
+
+    stages = (
+        (lambda g: conv(stack_in, w1_ref, g), first),
+        (lambda g: conv(lambda at, many: stack_eo(e1, o1, at, many), w2_ref, g), second),
+        (lambda g: conv(lambda at, many: stack_eo(e2, o2, at, many), v2_ref, g), third),
+    )
+    groups = rows // group
+    depth = wide
+    pending = None
+    for index, (product, finish) in enumerate(stages):
+        for g in range(groups):
+            pre = product(g)
+            if pending is not None:
+                pending()
+            pending = functools.partial(finish, g, pre)
+        if groups < 3:
+            pending()
+            pending = None
+    proj = lax.dot_general(gout[...], act2[...], TN_FORM, preferred_element_type=F32)
+    gt[0:depth, :] = jnp.transpose(view(e2, 1, rows, 1))
+    gt[depth : 2 * depth, :] = jnp.transpose(view(o2, 1, rows, 1))
+    if pending is not None:
+        pending()
+    loss = sum(losses[1:], losses[0])
+    sums = sum(partial[1:], partial[0])
 
     def emit(at, size, value):
         if before is not None:
             value = value + before[at : at + size, :]
         out_ref[at : at + size, :] = value
 
-    depth = wide
-    proj = lax.dot_general(gout[...], act2[...], TN_FORM, preferred_element_type=F32)
     emit(18 * depth, half, proj[:half, :wide] + proj[half:, wide:])
-
-    gt[0:depth, :] = jnp.transpose(view(e2, 1, rows, 1))
-    gt[depth : 2 * depth, :] = jnp.transpose(view(o2, 1, rows, 1))
     for a in range(3):
         right = jnp.concatenate(stack_eo(e1, o1, a, rows), axis=1)
         got = matmul(gt[...], right)
@@ -377,13 +403,6 @@
         emit(base + depth, depth, h0[:, 0:wide] + h1[:, wide : 2 * wide])
         emit(base + 2 * depth, depth, h0[:, wide : 2 * wide] + h1[:, 3 * wide : 4 * wide])
 
-    sums = jnp.zeros((count, 2 * wide), F32)
-    for r in range(0, rows, group):
-        span = pl.ds(r * pairs * count, tile)
-        left = jnp.concatenate(sum([stack_eo(e2, o2, r + a, group) for a in range(3)], []), axis=1)
-        grad = (matmul(left, v2_ref[...]) * slope1[span, :]).astype(BF)
-        sums = sums + jnp.sum(grad.astype(F32).reshape(group * pairs, count, 2 * wide), axis=0)
-        act2[span, :] = grad
     emb[...] = sums[:, :wide] + sums[:, wide:]
     table = 18 * depth + half
     if before is not None:
@@ -409,7 +428,7 @@
         owned = rounded
     out_ref[levels_end : levels_end + 8, :] = owned
 
-    gt[...] = jnp.transpose(act2[...])
+    gt[...] = jnp.transpose(back[...])
     low = lax.broadcasted_iota(jnp.int32, (depth, wide), 1) < half
     for a in range(3):
         right = jnp.concatenate(stack_in(a, rows), axis=1)
@@ -588,6 +607,7 @@
             (SM, VM),
             [pltpu.SMEM((strips,), jnp.int32)],
             limit=8,
+            cost=COSTS[0],
         )
 
     def sent(packed_pieces):
@@ -609,7 +629,7 @@
     inward = lax.ppermute(jnp.where(even, high_edge, low_edge), "rows", pairs)
     outward = lax.ppermute(jnp.where(even, low_edge, high_edge), "rows", others)
     target_low = lax.ppermute(own_target, "rows", down)
-    inward, outward = after((inward, outward), (first_packed[0], target_low))
+    inward, outward = after((inward, outward), (first_packed[0],))
     mean, mean_top, mean_last = call(
         regress_kernel,
         [jax.ShapeDtypeStruct((rows,) + per_row, BF) for rows in (height, height - 1, 1)],
@@ -617,6 +637,7 @@
         (SM,) + (VM,) * 5,
         [pltpu.VMEM((height + 2, 3 * fill, width), BF), pltpu.VMEM((9 * fill, depth), BF)],
         limit=12,
+        cost=COSTS[1],
     )
     mean_low = lax.ppermute(mean_top, "rows", down)
 
@@ -629,32 +650,32 @@
         (conv_one, conv_two, out_proj),
         (VM,) * 3,
         limit=12,
+        cost=COSTS[3],
     )
     patch_shape = jax.ShapeDtypeStruct((phases, cells // 2, count, wide), BF)
-    image = pltpu.VMEM((2 * height - 1, width, wide), F32)
     got = pltpu.VMEM((cells // 2 * count, wide), F32)
-    table, target_p, image_m = pl.pallas_call(
-        functools.partial(target_kernel, exchange, deep),
+    table, image = pl.pallas_call(
+        functools.partial(own_kernel, exchange, deep, count),
         out_shape=[
             jax.ShapeDtypeStruct((5, per_strip), jnp.int32),
-            patch_shape,
             jax.ShapeDtypeStruct((height, width, wide), BF),
         ],
-        in_specs=[SM] + [VM] * 4,
-        out_specs=[SM, VM, VM],
-        scratch_shapes=[image, got, pltpu.SMEM((strips,), jnp.int32)],
+        in_specs=[SM] + [VM] * 3,
+        out_specs=[SM, VM],
+        scratch_shapes=[pltpu.SMEM((strips,), jnp.int32)],
         compiler_params=pltpu.CompilerParams(vmem_limit_bytes=16 * MIB),
-        cost_estimate=pl.CostEstimate(flops=1000000000, bytes_accessed=1, transcendentals=0),
-    )(region_table, own_target, target_low, mean_top, mean_last)
-    later_region, later_noise = after((region_table, noise), (weights[0],))
+        cost_estimate=pl.CostEstimate(flops=COSTS[2], bytes_accessed=1, transcendentals=0),
+    )(region_table, own_target, mean_top, after((mean_last,), (target_low,))[0])
+    later_region, later_noise = after((region_table, noise), (weights[0], image))
     arrived += sent(packed(1, later_region, later_noise))
-    mean_p = call(
-        mean_kernel,
-        patch_shape,
-        (table, image_m, mean_low),
-        (SM, VM, VM),
-        [image, got],
+    mean_p, target_p = call(
+        gather_kernel,
+        [patch_shape, patch_shape],
+        (table, image, mean_low, target_low),
+        (SM, VM, VM, VM),
+        [pltpu.VMEM((2 * height - 1, width, wide), F32), got, got],
         limit=16,
+        cost=COSTS[4],
     )
 
     cores, groups = lax.axis_size("segment"), lax.axis_size("dp")
@@ -672,7 +693,7 @@
         used = arrived[: (chunk + 1) * pieces]
         slots_here = sum(piece.shape[0] for piece in used)
         ins = (table,) + tuple(used)
-        ins += (mean_p[chunk : chunk + 1], target_p[chunk : chunk + 1], step_embed)
+        ins += (mean_p, target_p, step_embed)
         ins += tuple(weights) + tuple(result)
         outs = [sums]
         if last:
@@ -698,12 +719,14 @@
                 pltpu.VMEM((total, wide), F32),
                 pltpu.VMEM((total, wide), F32),
                 pltpu.VMEM((total, 2 * wide), BF),
+                pltpu.VMEM((total, 2 * wide), BF),
                 pltpu.VMEM((total, wide), BF),
                 pltpu.VMEM((2 * wide, total), BF),
                 pltpu.VMEM((count, wide), F32),
                 pltpu.VMEM((6, count, wide), F32),
                 pltpu.VMEM((6, levels, wide), F32),
             ],
+            cost=COSTS[5],
         )
 
     kept, given = result

time: 91.2 us -> 88.8 us (0.974)
  Pallas kernels: 38.3 us -> 28.2 us
  waiting for transfers between devices: 16 us -> 21.7 us
  starting transfers between devices: 31.9 us -> 34 us
    pallas_call x8, Pallas kernels: 31.5 us -> 25.9 us  [call(): pl.pallas_call(kernel, out_shape=outs, in_specs=list(specs), out_specs=ja...]
    ppermute x1, waiting for transfers between devices: 0.01 us -> 5.02 us  [per_device(): mean_low = lax.ppermute(mean_top, 'rows', down)]
    pallas_call x1, Pallas kernels: 6.75 us -> 2.28 us  [per_device(): pl.pallas_call(functools.partial(own_kernel, exchange, deep, count), out_...]
    ppermute x6, starting transfers between devices: 12.9 us -> 15 us  [sent(): lax.ppermute(packed_pieces[d], 'rows', by_distance('rows', d))]
  transfers between devices with their start and end apart: 21 -> 21, of which waited for: 10 -> 11; matrix products, arithmetic and copies ran while one was open for 1% -> 1% of each run, Pallas kernels for 31% -> 23%
where the time goes in v4:
time: 88.8 us; the launch traced here: 88.5 us
  starting transfers between devices  34 us (38%)
  Pallas kernels  28.2 us (32%)
  waiting for transfers between devices  21.7 us (24%)
  local copies, waits for them, and re-layouts  2.37 us (3%)
  other arithmetic  1.16 us (1%)
  between operations  0.97 us (1%)
    pallas_call x8, Pallas kernels, call(): pl.pallas_call(kernel, out_shape=outs, in_specs=list(specs), out_specs=ja...  25.9 us
    ppermute x6, starting transfers between devices, sent(): lax.ppermute(packed_pieces[d], 'rows', by_distance('rows', d))  15 us
    ppermute x3, waiting for transfers between devices, rows_sum(): values.append(lax.ppermute(values[0], axis, by_distance(axis, d)))  5.3 us
    ppermute x1, waiting for transfers between devices, per_device(): mean_low = lax.ppermute(mean_top, 'rows', down)  5.02 us
    ppermute x3, starting transfers between devices, rows_sum(): values.append(lax.ppermute(values[0], axis, by_distance(axis, d)))  4.45 us
    ppermute x3, waiting for transfers between devices, gather_all(): lax.ppermute(piece, axis, by_distance(axis, d))  4.36 us
    ppermute x3, waiting for transfers between devices, scatter_sum(): lax.ppermute(take(values, me ^ d).astype(BF), axis, by_distance(axis, d))  3.87 us
    ppermute x1, starting transfers between devices, per_device(): inward = lax.ppermute(jnp.where(even, high_edge, low_edge), 'rows', pairs)  3.72 us
  transfers between devices with their start and end apart: 21, of which 11 were waited for; matrix products, arithmetic and copies ran while one was open for 1% of the time, Pallas kernels for 23%

profile of v4, /device:TPU:0, one launch (start us, length us, event | category | flops | bytes accessed | tf_op | source)
XLA Modules:
  0.0 88.5 jit_solution(10679553916714130829)
XLA Ops:
  0.6 0.0 copy-start
  0.6 1.4 %collective-permute-start.2 = (bf16[12,64,256]{2,1,0:T(8,128)(2,1)}, bf16[12,64,256]{2,1,0:T(8,128)(2,1)S(1)}, u32[]{:S(2)}, u32[]{:S(2)}) collective-permute-start(bf16[12,64,256]{2,1,0:T(8,128)(2,1)} %bitcast.48), channel_id=1, source_target_pairs={{4,0},{8,4},{12,8},{5,1},{9,5},{13,9},{6,2},{10,6},{14,10},{7,3},{... | collective-permute-start | bytes 1179656 | tf_op jit(solution)/shard_map/ppermute | solution.py:631
  2.1 0.8 broadcast_select_fusion
  2.9 3.7 %collective-permute-start = (bf16[1,100,256]{2,1,0:T(8,128)(2,1)S(1)}, bf16[1,100,256]{2,1,0:T(8,128)(2,1)S(1)}, u32[]{:S(2)}, u32[]{:S(2)}) collective-permute-start(bf16[1,100,256]{2,1,0:T(8,128)(2,1)S(1)} %get-tuple-element.77), channel_id=1, source_target_pairs={{0,4},{4,0},{8,12},{12,8},{1,5},{5,1},{9,13},{13,9},{2,6},{6,2},{1... | collective-permute-start | bytes 153608 | tf_op jit(solution)/shard_map/ppermute | solution.py:629
  6.7 0.7 collective-permute-start.1
  7.3 0.0 copy-start.1
  7.3 1.6 %copy-done.1 = bf16[1,1,64,64,144]{4,3,2,1,0:T(8,128)(2,1)S(1)} copy-done((bf16[1,1,64,64,144]{4,3,2,1,0:T(8,128)(2,1)S(1)}, bf16[1,1,64,64,144]{4,3,2,1,0:T(8,128)(2,1)}, u32[]{:S(2)}) %copy-start.1) | copy-done | bytes 1179672
  8.9 0.7 copy-done.10
  9.6 2.1 %shard_map.145 = (bf16[8,72,128]{2,1,0:T(8,128)(2,1)S(1)}, bf16[8,72,128]{2,1,0:T(8,128)(2,1)S(1)}, bf16[8,72,128]{2,1,0:T(8,128)(2,1)S(1)}, bf16[8,72,128]{2,1,0:T(8,128)(2,1)S(1)}) custom-call(s32[4,4,32]{2,1,0:T(4,128)S(1)} %bitcast.51, bf16[64,64,144]{2,1,0:T(8,128)(2,1)S(1)} %bitcast.46), custom_call_target="tpu_custom_call" | custom-call | flops 1000000000 | bytes 1 | tf_op jit(solution)/shard_map/pallas_call | solution.py:31
  11.7 0.0 copy-start.5
  11.7 0.0 copy-start.8
  11.7 4.9 %collective-permute-start.3 = (bf16[8,72,128]{2,1,0:T(8,128)(2,1)S(1)}, bf16[8,72,128]{2,1,0:T(8,128)(2,1)S(1)}, u32[]{:S(2)}, u32[]{:S(2)}) collective-permute-start(bf16[8,72,128]{2,1,0:T(8,128)(2,1)S(1)} %get-tuple-element.49), channel_id=1, source_target_pairs={{0,4},{4,0},{8,12},{12,8},{1,5},{5,1},{9,13},{13,9},{2,6},{6,2},{1... | collective-permute-start | bytes 442376 | tf_op jit(solution)/shard_map/ppermute | solution.py:616
  16.7 0.0 collective-permute-start.4
  16.7 0.0 collective-permute-done.inward_ref
  16.7 2.4 %collective-permute-start.5 = (bf16[8,72,128]{2,1,0:T(8,128)(2,1)S(1)}, bf16[8,72,128]{2,1,0:T(8,128)(2,1)S(1)}, u32[]{:S(2)}, u32[]{:S(2)}) collective-permute-start(bf16[8,72,128]{2,1,0:T(8,128)(2,1)S(1)} %get-tuple-element.51), channel_id=1, source_target_pairs={{0,12},{4,8},{8,4},{12,0},{1,13},{5,9},{9,5},{13,1},{2,14},{6,10},... | collective-permute-start | bytes 442376 | tf_op jit(solution)/shard_map/ppermute | solution.py:616
  19.1 0.0 collective-permute-done.1.outward_ref
  19.1 0.0 copy-done
  19.1 0.0 copy-done.6
  19.1 0.0 copy-done.7
  19.1 4.0 %shard_map.146 = (bf16[12,64,256]{2,1,0:T(8,128)(2,1)}, bf16[11,64,256]{2,1,0:T(8,128)(2,1)S(1)}, bf16[1,64,256]{2,1,0:T(8,128)(2,1)S(1)}) custom-call(s32[1]{0:T(128)} %bitcast.even_ref, bf16[1,100,256]{2,1,0:T(8,128)(2,1)S(1)} %collective-permute-done.inward_ref, bf16[12,100,256]{2,1,0:T(8,128)(2,1)S(1)} %bitcast.45, ...), custom_call_target="tpu_custom_call" | custom-call | flops 1000000000 | bytes 1 | tf_op jit(solution)/shard_map/pallas_call | solution.py:31
  23.2 1.4 %collective-permute-start.9 = (bf16[11,64,256]{2,1,0:T(8,128)(2,1)S(1)}, bf16[11,64,256]{2,1,0:T(8,128)(2,1)S(1)}, u32[]{:S(2)}, u32[]{:S(2)}) collective-permute-start(bf16[11,64,256]{2,1,0:T(8,128)(2,1)S(1)} %get-tuple-element.45.top_ref), channel_id=1, source_target_pairs={{4,0},{8,4},{12,8},{5,1},{9,5},{13,9},{6,2},{10,6},{14,10},{7,3},{... | collective-permute-start | bytes 1081352 | tf_op jit(solution)/shard_map/ppermute | solution.py:642
  24.6 0.4 shard_map.148
  25.0 0.0 collective-permute-done.2.tgt_ref
  25.1 0.0 copy-start.2
  25.1 2.3 %shard_map.147 = (s32[5,32]{1,0:T(8,128)S(1)}, bf16[12,256,128]{2,1,0:T(8,128)(2,1)S(1)}) custom-call(s32[4,4,32]{2,1,0:T(4,128)S(1)} %bitcast.52, bf16[12,64,256]{2,1,0:T(8,128)(2,1)S(1)} %bitcast.49, bf16[11,64,256]{2,1,0:T(8,128)(2,1)S(1)} %get-tuple-element.45.top_ref, bf16[1,64,256]{2,1,0:T(8,128)(2,1)S(1)} %get-tuple-element.47.last_ref), custom_call_target="tpu_custom_call" | custom-call | flops 10000000000 | bytes 1 | tf_op jit(solution)/shard_map/pallas_call | solution.py:657
  27.4 2.3 %shard_map.149 = (bf16[8,72,128]{2,1,0:T(8,128)(2,1)S(1)}, bf16[8,72,128]{2,1,0:T(8,128)(2,1)S(1)}, bf16[8,72,128]{2,1,0:T(8,128)(2,1)S(1)}, bf16[8,72,128]{2,1,0:T(8,128)(2,1)S(1)}) custom-call(s32[4,4,32]{2,1,0:T(4,128)S(1)} %bitcast.53, bf16[64,64,144]{2,1,0:T(8,128)(2,1)S(1)} %bitcast.47), custom_call_target="tpu_custom_call" | custom-call | flops 1000000000 | bytes 1 | tf_op jit(solution)/shard_map/pallas_call | solution.py:31
  29.6 2.7 %collective-permute-start.6 = (bf16[8,72,128]{2,1,0:T(8,128)(2,1)S(1)}, bf16[8,72,128]{2,1,0:T(8,128)(2,1)S(1)}, u32[]{:S(2)}, u32[]{:S(2)}) collective-permute-start(bf16[8,72,128]{2,1,0:T(8,128)(2,1)S(1)} %get-tuple-element.60), channel_id=1, source_target_pairs={{0,4},{4,0},{8,12},{12,8},{1,5},{5,1},{9,13},{13,9},{2,6},{6,2},{1... | collective-permute-start | bytes 442376 | tf_op jit(solution)/shard_map/ppermute | solution.py:616
  32.3 5.0 %collective-permute-done.9.mean_ref = bf16[11,64,256]{2,1,0:T(8,128)(2,1)S(1)} collective-permute-done((bf16[11,64,256]{2,1,0:T(8,128)(2,1)S(1)}, bf16[11,64,256]{2,1,0:T(8,128)(2,1)S(1)}, u32[]{:S(2)}, u32[]{:S(2)}) %collective-permute-start.9) | collective-permute-done | bytes 360480 | tf_op jit(solution)/shard_map/ppermute | solution.py:642
  37.4 1.5 %collective-permute-start.7 = (bf16[8,72,128]{2,1,0:T(8,128)(2,1)S(1)}, bf16[8,72,128]{2,1,0:T(8,128)(2,1)S(1)}, u32[]{:S(2)}, u32[]{:S(2)}) collective-permute-start(bf16[8,72,128]{2,1,0:T(8,128)(2,1)S(1)} %get-tuple-element.61), channel_id=1, source_target_pairs={{0,8},{4,12},{8,0},{12,4},{1,9},{5,13},{9,1},{13,5},{2,10},{6,14},... | collective-permute-start | bytes 442376 | tf_op jit(solution)/shard_map/ppermute | solution.py:616
  38.8 2.1 %shard_map.150 = (bf16[2,72,16,128]{3,2,1,0:T(8,128)(2,1)S(1)}, bf16[2,72,16,128]{3,2,1,0:T(8,128)(2,1)S(1)}) custom-call(s32[5,32]{1,0:T(8,128)S(1)} %get-tuple-element.48.table_ref.refs_0_, bf16[12,256,128]{2,1,0:T(8,128)(2,1)S(1)} %get-tuple-element.56.own, bf16[11,64,256]{2,1,0:T(8,128)(2,1)S(1)} %collective-permute-done.9.mean_ref, ...), custom_call_target="tpu_custom_call" | custom-call | flops 10000000000 | bytes 1 | tf_op jit(solution)/shard_map/pallas_call | solution.py:31
  41.0 0.0 collective-permute-done.3.refs_2_
  41.0 3.4 %collective-permute-start.8 = (bf16[8,72,128]{2,1,0:T(8,128)(2,1)S(1)}, bf16[8,72,128]{2,1,0:T(8,128)(2,1)S(1)}, u32[]{:S(2)}, u32[]{:S(2)}) collective-permute-start(bf16[8,72,128]{2,1,0:T(8,128)(2,1)S(1)} %get-tuple-element.62), channel_id=1, source_target_pairs={{0,12},{4,8},{8,4},{12,0},{1,13},{5,9},{9,5},{13,1},{2,14},{6,10},... | collective-permute-start | bytes 442376 | tf_op jit(solution)/shard_map/ppermute | solution.py:616
  44.4 0.0 collective-permute-done.4.refs_3_
  44.4 0.0 collective-permute-done.5.refs_4_
  44.4 6.8 %shard_map.151.refs_17_ = f32[2432,128]{1,0:T(8,128)S(1)} custom-call(s32[5,32]{1,0:T(8,128)S(1)} %get-tuple-element.48.table_ref.refs_0_, bf16[8,72,128]{2,1,0:T(8,128)(2,1)S(1)} %get-tuple-element.41.refs_1_, bf16[8,72,128]{2,1,0:T(8,128)(2,1)S(1)} %collective-permute-done.3.refs_2_, bf16[8,72,128]{2,1,0:T(8,128)(2,1)S(1)} %collective-permute-done.4.refs_3_, ...), custom_call_target="tpu_custom_call" | custom-call | flops 10000000000 | bytes 1 | tf_op jit(solution)/shard_map/pallas_call | solution.py:31
  51.2 0.0 collective-permute-done.6.refs_6_
  51.2 0.0 collective-permute-done.7.refs_7_
  51.2 0.0 collective-permute-done.8.refs_8_
  51.2 7.1 %shard_map.152 = (f32[1216,128]{1,0:T(8,128)S(1)}, bf16[1216,128]{1,0:T(8,128)(2,1)S(1)}) custom-call(s32[5,32]{1,0:T(8,128)S(1)} %get-tuple-element.48.table_ref.refs_0_, bf16[8,72,128]{2,1,0:T(8,128)(2,1)S(1)} %get-tuple-element.41.refs_1_, bf16[8,72,128]{2,1,0:T(8,128)(2,1)S(1)} %collective-permute-done.3.refs_2_, ...), custom_call_target="tpu_custom_call" | custom-call | flops 10000000000 | bytes 1 | tf_op jit(solution)/shard_map/pallas_call | solution.py:31
  58.3 0.1 collective-permute-start.10
  58.4 1.6 %collective-permute-done.10 = bf16[1216,128]{1,0:T(8,128)(2,1)S(1)} collective-permute-done((bf16[1216,128]{1,0:T(8,128)(2,1)S(1)}, bf16[1216,128]{1,0:T(8,128)(2,1)S(1)}, u32[]{:S(2)}, u32[]{:S(2)}) %collective-permute-start.10) | collective-permute-done | bytes 311328 | tf_op jit(solution)/shard_map/ppermute | solution.py:733
  60.0 0.1 convert_add_fusion
  60.1 2.5 %collective-permute-start.13 = (bf16[304,128]{1,0:T(8,128)(2,1)S(1)}, bf16[304,128]{1,0:T(8,128)(2,1)S(1)}, u32[]{:S(2)}, u32[]{:S(2)}) collective-permute-start(bf16[304,128]{1,0:T(8,128)(2,1)S(1)} %get-tuple-element.79), channel_id=1, source_target_pairs={{0,3},{1,2},{2,1},{3,0},{4,7},{5,6},{6,5},{7,4},{8,11},{9,10},{10,... | collective-permute-start | bytes 233480 | tf_op jit(solution)/shard_map/ppermute | solution.py:541
  62.6 0.5 collective-permute-start.12
  63.1 0.5 collective-permute-start.11
  63.7 1.8 %collective-permute-done.13 = bf16[304,128]{1,0:T(8,128)(2,1)S(1)} collective-permute-done((bf16[304,128]{1,0:T(8,128)(2,1)S(1)}, bf16[304,128]{1,0:T(8,128)(2,1)S(1)}, u32[]{:S(2)}, u32[]{:S(2)}) %collective-permute-start.13) | collective-permute-done | bytes 77856 | tf_op jit(solution)/shard_map/ppermute | solution.py:541
  65.5 1.6 %collective-permute-done.12 = bf16[304,128]{1,0:T(8,128)(2,1)S(1)} collective-permute-done((bf16[304,128]{1,0:T(8,128)(2,1)S(1)}, bf16[304,128]{1,0:T(8,128)(2,1)S(1)}, u32[]{:S(2)}, u32[]{:S(2)}) %collective-permute-start.12) | collective-permute-done | bytes 77856 | tf_op jit(solution)/shard_map/ppermute | solution.py:541
  67.1 0.4 collective-permute-done.11
  67.6 0.5 collective-permute-start.16
  68.1 3.0 %collective-permute-start.15 = (bf16[304,128]{1,0:T(8,128)(2,1)S(1)}, bf16[304,128]{1,0:T(8,128)(2,1)S(1)}, u32[]{:S(2)}, u32[]{:S(2)}) collective-permute-start(bf16[304,128]{1,0:T(8,128)(2,1)S(1)} %fusion.3), channel_id=1, source_target_pairs={{0,8},{4,12},{8,0},{12,4},{1,9},{5,13},{9,1},{13,5},{2,10},{6,14},... | collective-permute-start | bytes 233480 | tf_op jit(solution)/shard_map/ppermute | solution.py:568
  71.1 0.9 %collective-permute-start.14 = (bf16[304,128]{1,0:T(8,128)(2,1)S(1)}, bf16[304,128]{1,0:T(8,128)(2,1)S(1)}, u32[]{:S(2)}, u32[]{:S(2)}) collective-permute-start(bf16[304,128]{1,0:T(8,128)(2,1)S(1)} %fusion.3), channel_id=1, source_target_pairs={{0,4},{4,0},{8,12},{12,8},{1,5},{5,1},{9,13},{13,9},{2,6},{6,2},{1... | collective-permute-start | bytes 233480 | tf_op jit(solution)/shard_map/ppermute | solution.py:568
  72.0 2.4 %collective-permute-done.16 = bf16[304,128]{1,0:T(8,128)(2,1)S(1)} collective-permute-done((bf16[304,128]{1,0:T(8,128)(2,1)S(1)}, bf16[304,128]{1,0:T(8,128)(2,1)S(1)}, u32[]{:S(2)}, u32[]{:S(2)}) %collective-permute-start.16) | collective-permute-done | bytes 77856 | tf_op jit(solution)/shard_map/ppermute | solution.py:568
  74.4 2.9 %collective-permute-done.15 = bf16[304,128]{1,0:T(8,128)(2,1)S(1)} collective-permute-done((bf16[304,128]{1,0:T(8,128)(2,1)S(1)}, bf16[304,128]{1,0:T(8,128)(2,1)S(1)}, u32[]{:S(2)}, u32[]{:S(2)}) %collective-permute-start.15) | collective-permute-done | bytes 77856 | tf_op jit(solution)/shard_map/ppermute | solution.py:568
  77.3 0.0 collective-permute-done.14
  77.4 1.5 %collective-permute-start.17 = (bf16[304,128]{1,0:T(8,128)(2,1)S(1)}, bf16[304,128]{1,0:T(8,128)(2,1)S(1)}, u32[]{:S(2)}, u32[]{:S(2)}) collective-permute-start(bf16[304,128]{1,0:T(8,128)(2,1)S(1)} %reduce-precision_convert_fusion), channel_id=1, source_target_pairs={{0,3},{1,2},{2,1},{3,0},{4,7},{5,6},{6,5},{7,4},{8,11},{9,10},{10,... | collective-permute-start | bytes 233480 | tf_op jit(solution)/shard_map/ppermute | solution.py:551
  78.9 2.2 %collective-permute-start.18 = (bf16[304,128]{1,0:T(8,128)(2,1)S(1)}, bf16[304,128]{1,0:T(8,128)(2,1)S(1)}, u32[]{:S(2)}, u32[]{:S(2)}) collective-permute-start(bf16[304,128]{1,0:T(8,128)(2,1)S(1)} %reduce-precision_convert_fusion), channel_id=1, source_target_pairs={{0,2},{1,3},{2,0},{3,1},{4,6},{5,7},{6,4},{7,5},{8,10},{9,11},{10,... | collective-permute-start | bytes 233480 | tf_op jit(solution)/shard_map/ppermute | solution.py:551
  81.1 0.0 collective-permute-start.19
  81.1 2.0 %collective-permute-done.17 = bf16[304,128]{1,0:T(8,128)(2,1)S(1)} collective-permute-done((bf16[304,128]{1,0:T(8,128)(2,1)S(1)}, bf16[304,128]{1,0:T(8,128)(2,1)S(1)}, u32[]{:S(2)}, u32[]{:S(2)}) %collective-permute-start.17) | collective-permute-done | bytes 77856 | tf_op jit(solution)/shard_map/ppermute | solution.py:551
  83.1 0.8 collective-permute-done.18
  83.9 1.6 %collective-permute-done.19 = bf16[304,128]{1,0:T(8,128)(2,1)S(1)} collective-permute-done((bf16[304,128]{1,0:T(8,128)(2,1)S(1)}, bf16[304,128]{1,0:T(8,128)(2,1)S(1)}, u32[]{:S(2)}, u32[]{:S(2)}) %collective-permute-start.19) | collective-permute-done | bytes 77856 | tf_op jit(solution)/shard_map/ppermute | solution.py:551
  85.5 0.1 select_bitcast_fusion.3
  85.6 0.1 collective-permute-start.20
  85.7 1.6 %collective-permute-done.20.other_ref = bf16[1216,128]{1,0:T(8,128)(2,1)S(1)} collective-permute-done((bf16[1216,128]{1,0:T(8,128)(2,1)S(1)}, bf16[1216,128]{1,0:T(8,128)(2,1)S(1)}, u32[]{:S(2)}, u32[]{:S(2)}) %collective-permute-start.20) | collective-permute-done | bytes 311328 | tf_op jit(solution)/shard_map/ppermute | solution.py:745
  87.3 1.1 %shard_map.153 = (f32[128,1152]{1,0:T(8,128)}, f32[128,1152]{1,0:T(8,128)}, f32[64,128]{1,0:T(8,128)}, f32[32,128]{1,0:T(8,128)}, f32[1,1]{1,0:T(1,128)}) custom-call(bf16[1216,128]{1,0:T(8,128)(2,1)S(1)} %bitcast.43, bf16[1216,128]{1,0:T(8,128)(2,1)S(1)} %collective-permute-done.20.other_ref), custom_call_target="tpu_custom_call" | custom-call | bytes 1 | tf_op jit(solution)/shard_map/pallas_call | solution.py:31
  (21 shorter events, 0.2 us)
Async XLA Ops:
  0.6 18.5 %copy-start = (bf16[1,100,12,256]{3,1,2,0:T(8,128)(2,1)S(1)}, bf16[1,100,12,256]{3,1,2,0:T(8,128)(2,1)}, u32[]{:S(2)}) copy-start(bf16[1,100,12,256]{3,1,2,0:T(8,128)(2,1)} %param.10) | copy-start | bytes 1843204
  0.6 24.4 %collective-permute-start.2 = (bf16[12,64,256]{2,1,0:T(8,128)(2,1)}, bf16[12,64,256]{2,1,0:T(8,128)(2,1)S(1)}, u32[]{:S(2)}, u32[]{:S(2)}) collective-permute-start(bf16[12,64,256]{2,1,0:T(8,128)(2,1)} %bitcast.48), channel_id=1, source_target_pairs={{4,0},{8,4},{12,8},{5,1},{9,5},{13,9},{6,2},{10,6},{14,10},{7,3},{... | collective-permute-start | bytes 1179656 | tf_op jit(solution)/shard_map/ppermute | solution.py:631
  2.9 13.7 %collective-permute-start = (bf16[1,100,256]{2,1,0:T(8,128)(2,1)S(1)}, bf16[1,100,256]{2,1,0:T(8,128)(2,1)S(1)}, u32[]{:S(2)}, u32[]{:S(2)}) collective-permute-start(bf16[1,100,256]{2,1,0:T(8,128)(2,1)S(1)} %get-tuple-element.77), channel_id=1, source_target_pairs={{0,4},{4,0},{8,12},{12,8},{1,5},{5,1},{9,13},{13,9},{2,6},{6,2},{1... | collective-permute-start | bytes 153608 | tf_op jit(solution)/shard_map/ppermute | solution.py:629
  6.7 12.5 %collective-permute-start.1 = (bf16[1,100,256]{2,1,0:T(8,128)(2,1)S(1)}, bf16[1,100,256]{2,1,0:T(8,128)(2,1)S(1)}, u32[]{:S(2)}, u32[]{:S(2)}) collective-permute-start(bf16[1,100,256]{2,1,0:T(8,128)(2,1)S(1)} %get-tuple-element.76), channel_id=1, source_target_pairs={{4,8},{8,4},{5,9},{9,5},{6,10},{10,6},{7,11},{11,7},{20,24},{24,20... | collective-permute-start | bytes 153608 | tf_op jit(solution)/shard_map/ppermute | solution.py:630
  7.3 1.6 %copy-start.1 = (bf16[1,1,64,64,144]{4,3,2,1,0:T(8,128)(2,1)S(1)}, bf16[1,1,64,64,144]{4,3,2,1,0:T(8,128)(2,1)}, u32[]{:S(2)}) copy-start(bf16[1,1,64,64,144]{4,3,2,1,0:T(8,128)(2,1)} %param.12) | copy-start | bytes 3538948
  8.9 0.7 copy-start.10
  9.6 9.5 %copy-start.6 = (bf16[128,900]{0,1:T(8,128)(2,1)S(1)}, bf16[128,900]{0,1:T(8,128)(2,1)}, u32[]{:S(2)}) copy-start(bf16[128,900]{0,1:T(8,128)(2,1)} %param.14) | copy-start | bytes 691204
  9.6 9.5 %copy-start.7 = (bf16[64,128]{1,0:T(8,128)(2,1)S(1)}, bf16[64,128]{1,0:T(8,128)(2,1)}, u32[]{:S(2)}) copy-start(bf16[64,128]{1,0:T(8,128)(2,1)} %proj_ref.1) | copy-start | bytes 49156
  11.7 12.9 %copy-start.4 = (bf16[128,1152]{1,0:T(8,128)(2,1)S(1)}, bf16[128,1152]{1,0:T(8,128)(2,1)}, u32[]{:S(2)}) copy-start(bf16[128,1152]{1,0:T(8,128)(2,1)} %one_ref) | copy-start | bytes 884740
  11.7 12.9 %copy-start.5 = (bf16[128,1152]{1,0:T(8,128)(2,1)S(1)}, bf16[128,1152]{1,0:T(8,128)(2,1)}, u32[]{:S(2)}) copy-start(bf16[128,1152]{1,0:T(8,128)(2,1)} %two_ref) | copy-start | bytes 884740
  11.7 12.9 %copy-start.8 = (bf16[64,128]{1,0:T(8,128)(2,1)S(1)}, bf16[64,128]{1,0:T(8,128)(2,1)}, u32[]{:S(2)}) copy-start(bf16[64,128]{1,0:T(8,128)(2,1)} %proj_ref.2) | copy-start | bytes 49156
  11.7 29.2 %collective-permute-start.3 = (bf16[8,72,128]{2,1,0:T(8,128)(2,1)S(1)}, bf16[8,72,128]{2,1,0:T(8,128)(2,1)S(1)}, u32[]{:S(2)}, u32[]{:S(2)}) collective-permute-start(bf16[8,72,128]{2,1,0:T(8,128)(2,1)S(1)} %get-tuple-element.49), channel_id=1, source_target_pairs={{0,4},{4,0},{8,12},{12,8},{1,5},{5,1},{9,13},{13,9},{2,6},{6,2},{1... | collective-permute-start | bytes 442376 | tf_op jit(solution)/shard_map/ppermute | solution.py:616
  16.7 27.8 %collective-permute-start.4 = (bf16[8,72,128]{2,1,0:T(8,128)(2,1)S(1)}, bf16[8,72,128]{2,1,0:T(8,128)(2,1)S(1)}, u32[]{:S(2)}, u32[]{:S(2)}) collective-permute-start(bf16[8,72,128]{2,1,0:T(8,128)(2,1)S(1)} %get-tuple-element.50), channel_id=1, source_target_pairs={{0,8},{4,12},{8,0},{12,4},{1,9},{5,13},{9,1},{13,5},{2,10},{6,14},... | collective-permute-start | bytes 442376 | tf_op jit(solution)/shard_map/ppermute | solution.py:616
  16.7 27.8 %collective-permute-start.5 = (bf16[8,72,128]{2,1,0:T(8,128)(2,1)S(1)}, bf16[8,72,128]{2,1,0:T(8,128)(2,1)S(1)}, u32[]{:S(2)}, u32[]{:S(2)}) collective-permute-start(bf16[8,72,128]{2,1,0:T(8,128)(2,1)S(1)} %get-tuple-element.51), channel_id=1, source_target_pairs={{0,12},{4,8},{8,4},{12,0},{1,13},{5,9},{9,5},{13,1},{2,14},{6,10},... | collective-permute-start | bytes 442376 | tf_op jit(solution)/shard_map/ppermute | solution.py:616
  23.2 1.9 %copy-start.3 = (bf16[1,64,12,256]{3,1,2,0:T(8,128)(2,1)S(1)}, bf16[1,64,12,256]{3,1,2,0:T(8,128)(2,1)}, u32[]{:S(2)}) copy-start(bf16[1,64,12,256]{3,1,2,0:T(8,128)(2,1)} %param.11) | copy-start | bytes 1179652
  23.2 1.9 %copy-start.11 = (s32[1,4,32,4]{2,3,1,0:T(4,128)S(1)}, s32[1,4,32,4]{2,3,1,0:T(4,128)}, u32[]{:S(2)}) copy-start(s32[1,4,32,4]{2,3,1,0:T(4,128)} %param.13) | copy-start | bytes 6148
  23.2 14.2 %collective-permute-start.9 = (bf16[11,64,256]{2,1,0:T(8,128)(2,1)S(1)}, bf16[11,64,256]{2,1,0:T(8,128)(2,1)S(1)}, u32[]{:S(2)}, u32[]{:S(2)}) collective-permute-start(bf16[11,64,256]{2,1,0:T(8,128)(2,1)S(1)} %get-tuple-element.45.top_ref), channel_id=1, source_target_pairs={{4,0},{8,4},{12,8},{5,1},{9,5},{13,9},{6,2},{10,6},{14,10},{7,3},{... | collective-permute-start | bytes 1081352 | tf_op jit(solution)/shard_map/ppermute | solution.py:642
  25.1 2.3 %copy-start.2 = (bf16[1,1,64,64,144]{4,3,2,1,0:T(8,128)(2,1)S(1)}, bf16[1,1,64,64,144]{4,3,2,1,0:T(8,128)(2,1)}, u32[]{:S(2)}) copy-start(bf16[1,1,64,64,144]{4,3,2,1,0:T(8,128)(2,1)} %param.12) | copy-start | bytes 3538948
  29.6 21.6 %collective-permute-start.6 = (bf16[8,72,128]{2,1,0:T(8,128)(2,1)S(1)}, bf16[8,72,128]{2,1,0:T(8,128)(2,1)S(1)}, u32[]{:S(2)}, u32[]{:S(2)}) collective-permute-start(bf16[8,72,128]{2,1,0:T(8,128)(2,1)S(1)} %get-tuple-element.60), channel_id=1, source_target_pairs={{0,4},{4,0},{8,12},{12,8},{1,5},{5,1},{9,13},{13,9},{2,6},{6,2},{1... | collective-permute-start | bytes 442376 | tf_op jit(solution)/shard_map/ppermute | solution.py:616
  37.4 13.8 %collective-permute-start.7 = (bf16[8,72,128]{2,1,0:T(8,128)(2,1)S(1)}, bf16[8,72,128]{2,1,0:T(8,128)(2,1)S(1)}, u32[]{:S(2)}, u32[]{:S(2)}) collective-permute-start(bf16[8,72,128]{2,1,0:T(8,128)(2,1)S(1)} %get-tuple-element.61), channel_id=1, source_target_pairs={{0,8},{4,12},{8,0},{12,4},{1,9},{5,13},{9,1},{13,5},{2,10},{6,14},... | collective-permute-start | bytes 442376 | tf_op jit(solution)/shard_map/ppermute | solution.py:616
  38.8 5.6 %copy-start.9 = (f32[32,128]{1,0:T(8,128)S(1)}, f32[32,128]{1,0:T(8,128)}, u32[]{:S(2)}) copy-start(f32[32,128]{1,0:T(8,128)} %refs_11_.1) | copy-start | bytes 49156
  41.0 10.2 %collective-permute-start.8 = (bf16[8,72,128]{2,1,0:T(8,128)(2,1)S(1)}, bf16[8,72,128]{2,1,0:T(8,128)(2,1)S(1)}, u32[]{:S(2)}, u32[]{:S(2)}) collective-permute-start(bf16[8,72,128]{2,1,0:T(8,128)(2,1)S(1)} %get-tuple-element.62), channel_id=1, source_target_pairs={{0,12},{4,8},{8,4},{12,0},{1,13},{5,9},{9,5},{13,1},{2,14},{6,10},... | collective-permute-start | bytes 442376 | tf_op jit(solution)/shard_map/ppermute | solution.py:616
  58.3 1.7 %collective-permute-start.10 = (bf16[1216,128]{1,0:T(8,128)(2,1)S(1)}, bf16[1216,128]{1,0:T(8,128)(2,1)S(1)}, u32[]{:S(2)}, u32[]{:S(2)}) collective-permute-start(bf16[1216,128]{1,0:T(8,128)(2,1)S(1)} %get-tuple-element.70), channel_id=1, source_target_pairs={{0,16},{16,0},{1,17},{17,1},{2,18},{18,2},{3,19},{19,3},{4,20},{20... | collective-permute-start | bytes 933896 | tf_op jit(solution)/shard_map/ppermute | solution.py:733
  60.1 5.4 %collective-permute-start.13 = (bf16[304,128]{1,0:T(8,128)(2,1)S(1)}, bf16[304,128]{1,0:T(8,128)(2,1)S(1)}, u32[]{:S(2)}, u32[]{:S(2)}) collective-permute-start(bf16[304,128]{1,0:T(8,128)(2,1)S(1)} %get-tuple-element.79), channel_id=1, source_target_pairs={{0,3},{1,2},{2,1},{3,0},{4,7},{5,6},{6,5},{7,4},{8,11},{9,10},{10,... | collective-permute-start | bytes 233480 | tf_op jit(solution)/shard_map/ppermute | solution.py:541
  62.6 4.5 %collective-permute-start.12 = (bf16[304,128]{1,0:T(8,128)(2,1)S(1)}, bf16[304,128]{1,0:T(8,128)(2,1)S(1)}, u32[]{:S(2)}, u32[]{:S(2)}) collective-permute-start(bf16[304,128]{1,0:T(8,128)(2,1)S(1)} %get-tuple-element.80), channel_id=1, source_target_pairs={{0,2},{1,3},{2,0},{3,1},{4,6},{5,7},{6,4},{7,5},{8,10},{9,11},{10,... | collective-permute-start | bytes 233480 | tf_op jit(solution)/shard_map/ppermute | solution.py:541
  63.1 4.4 %collective-permute-start.11 = (bf16[304,128]{1,0:T(8,128)(2,1)S(1)}, bf16[304,128]{1,0:T(8,128)(2,1)S(1)}, u32[]{:S(2)}, u32[]{:S(2)}) collective-permute-start(bf16[304,128]{1,0:T(8,128)(2,1)S(1)} %get-tuple-element.78), channel_id=1, source_target_pairs={{0,1},{1,0},{2,3},{3,2},{4,5},{5,4},{6,7},{7,6},{8,9},{9,8},{10,11... | collective-permute-start | bytes 233480 | tf_op jit(solution)/shard_map/ppermute | solution.py:541
  67.6 6.8 %collective-permute-start.16 = (bf16[304,128]{1,0:T(8,128)(2,1)S(1)}, bf16[304,128]{1,0:T(8,128)(2,1)S(1)}, u32[]{:S(2)}, u32[]{:S(2)}) collective-permute-start(bf16[304,128]{1,0:T(8,128)(2,1)S(1)} %fusion.3), channel_id=1, source_target_pairs={{0,12},{4,8},{8,4},{12,0},{1,13},{5,9},{9,5},{13,1},{2,14},{6,10},... | collective-permute-start | bytes 233480 | tf_op jit(solution)/shard_map/ppermute | solution.py:568
  68.1 9.2 %collective-permute-start.15 = (bf16[304,128]{1,0:T(8,128)(2,1)S(1)}, bf16[304,128]{1,0:T(8,128)(2,1)S(1)}, u32[]{:S(2)}, u32[]{:S(2)}) collective-permute-start(bf16[304,128]{1,0:T(8,128)(2,1)S(1)} %fusion.3), channel_id=1, source_target_pairs={{0,8},{4,12},{8,0},{12,4},{1,9},{5,13},{9,1},{13,5},{2,10},{6,14},... | collective-permute-start | bytes 233480 | tf_op jit(solution)/shard_map/ppermute | solution.py:568
  71.1 6.2 %collective-permute-start.14 = (bf16[304,128]{1,0:T(8,128)(2,1)S(1)}, bf16[304,128]{1,0:T(8,128)(2,1)S(1)}, u32[]{:S(2)}, u32[]{:S(2)}) collective-permute-start(bf16[304,128]{1,0:T(8,128)(2,1)S(1)} %fusion.3), channel_id=1, source_target_pairs={{0,4},{4,0},{8,12},{12,8},{1,5},{5,1},{9,13},{13,9},{2,6},{6,2},{1... | collective-permute-start | bytes 233480 | tf_op jit(solution)/shard_map/ppermute | solution.py:568
  77.4 5.7 %collective-permute-start.17 = (bf16[304,128]{1,0:T(8,128)(2,1)S(1)}, bf16[304,128]{1,0:T(8,128)(2,1)S(1)}, u32[]{:S(2)}, u32[]{:S(2)}) collective-permute-start(bf16[304,128]{1,0:T(8,128)(2,1)S(1)} %reduce-precision_convert_fusion), channel_id=1, source_target_pairs={{0,3},{1,2},{2,1},{3,0},{4,7},{5,6},{6,5},{7,4},{8,11},{9,10},{10,... | collective-permute-start | bytes 233480 | tf_op jit(solution)/shard_map/ppermute | solution.py:551
  78.9 5.0 %collective-permute-start.18 = (bf16[304,128]{1,0:T(8,128)(2,1)S(1)}, bf16[304,128]{1,0:T(8,128)(2,1)S(1)}, u32[]{:S(2)}, u32[]{:S(2)}) collective-permute-start(bf16[304,128]{1,0:T(8,128)(2,1)S(1)} %reduce-precision_convert_fusion), channel_id=1, source_target_pairs={{0,2},{1,3},{2,0},{3,1},{4,6},{5,7},{6,4},{7,5},{8,10},{9,11},{10,... | collective-permute-start | bytes 233480 | tf_op jit(solution)/shard_map/ppermute | solution.py:551
  81.1 4.4 %collective-permute-start.19 = (bf16[304,128]{1,0:T(8,128)(2,1)S(1)}, bf16[304,128]{1,0:T(8,128)(2,1)S(1)}, u32[]{:S(2)}, u32[]{:S(2)}) collective-permute-start(bf16[304,128]{1,0:T(8,128)(2,1)S(1)} %reduce-precision_convert_fusion), channel_id=1, source_target_pairs={{0,1},{1,0},{2,3},{3,2},{4,5},{5,4},{6,7},{7,6},{8,9},{9,8},{10,11... | collective-permute-start | bytes 233480 | tf_op jit(solution)/shard_map/ppermute | solution.py:551
  85.6 1.7 %collective-permute-start.20 = (bf16[1216,128]{1,0:T(8,128)(2,1)S(1)}, bf16[1216,128]{1,0:T(8,128)(2,1)S(1)}, u32[]{:S(2)}, u32[]{:S(2)}) collective-permute-start(bf16[1216,128]{1,0:T(8,128)(2,1)S(1)} %bitcast.42), channel_id=1, source_target_pairs={{0,16},{16,0},{1,17},{17,1},{2,18},{18,2},{3,19},{19,3},{4,20},{20... | collective-permute-start | bytes 933896 | tf_op jit(solution)/shard_map/ppermute | solution.py:745

commit v5 on v4

--- a/solution.py
+++ b/solution.py
@@ -613,11 +613,10 @@
     def sent(packed_pieces):
         if not exchange:
             return [lax.all_to_all(packed_pieces[0], "rows", 0, 0, tiled=True)]
-        moved = [lax.ppermute(packed_pieces[d], "rows", by_distance("rows", d)) for d in range(1, strips)]
-        return [packed_pieces[0]] + moved
+        moved = {d: lax.ppermute(packed_pieces[d], "rows", by_distance("rows", d)) for d in (3, 2, 1) if d < strips}
+        return [packed_pieces[0]] + [moved[d] for d in range(1, strips)]
 
     first_packed = packed(0, region_table, noise)
-    arrived = sent(first_packed)
 
     reg_channels = reg_conv.shape[1] // 9
     fill = -(-reg_channels // 16) * 16
@@ -640,6 +639,8 @@
         cost=COSTS[1],
     )
     mean_low = lax.ppermute(mean_top, "rows", down)
+
+    arrived = sent([p if d != 1 else after((p,), (mean_top,))[0] for d, p in enumerate(first_packed)])
 
     conv_one, conv_two, out_proj = after((conv_one, conv_two, out_proj), (mean_top,))
     stacked = jax.ShapeDtypeStruct((12 * depth, 2 * depth), BF)

time: 88.8 us -> 87.4 us (0.984)
  waiting for transfers between devices: 21.7 us -> 20.6 us
    ppermute x1, waiting for transfers between devices: 5.02 us -> 4.1 us  [per_device(): mean_low = lax.ppermute(mean_top, 'rows', down)]
where the time goes in v5:
time: 87.4 us; the launch traced here: 87.1 us
  starting transfers between devices  33.8 us (39%)
  Pallas kernels  28.2 us (32%)
  waiting for transfers between devices  20.6 us (24%)
  local copies, waits for them, and re-layouts  2.37 us (3%)
  other arithmetic  1.16 us (1%)
  between operations  0.95 us (1%)
    pallas_call x8, Pallas kernels, call(): pl.pallas_call(kernel, out_shape=outs, in_specs=list(specs), out_specs=ja...  26 us
    ppermute x6, starting transfers between devices, sent(): lax.ppermute(packed_pieces[d], 'rows', by_distance('rows', d))  14.7 us
    ppermute x3, waiting for transfers between devices, rows_sum(): values.append(lax.ppermute(values[0], axis, by_distance(axis, d)))  5.1 us
    ppermute x3, starting transfers between devices, rows_sum(): values.append(lax.ppermute(values[0], axis, by_distance(axis, d)))  4.45 us
    ppermute x3, waiting for transfers between devices, gather_all(): lax.ppermute(piece, axis, by_distance(axis, d))  4.36 us
    ppermute x1, waiting for transfers between devices, per_device(): mean_low = lax.ppermute(mean_top, 'rows', down)  4.1 us
    ppermute x3, waiting for transfers between devices, scatter_sum(): lax.ppermute(take(values, me ^ d).astype(BF), axis, by_distance(axis, d))  3.88 us
    ppermute x1, starting transfers between devices, per_device(): inward = lax.ppermute(jnp.where(even, high_edge, low_edge), 'rows', pairs)  3.72 us
  transfers between devices with their start and end apart: 21, of which 11 were waited for; matrix products, arithmetic and copies ran while one was open for 1% of the time, Pallas kernels for 23%

profile of v5, /device:TPU:0, one launch (start us, length us, event | category | flops | bytes accessed | tf_op | source)
XLA Modules:
  0.0 87.1 jit_solution(13696730143102483197)
XLA Ops:
  0.6 0.0 copy-start
  0.6 1.4 %collective-permute-start.2 = (bf16[12,64,256]{2,1,0:T(8,128)(2,1)}, bf16[12,64,256]{2,1,0:T(8,128)(2,1)S(1)}, u32[]{:S(2)}, u32[]{:S(2)}) collective-permute-start(bf16[12,64,256]{2,1,0:T(8,128)(2,1)} %bitcast.48), channel_id=1, source_target_pairs={{4,0},{8,4},{12,8},{5,1},{9,5},{13,9},{6,2},{10,6},{14,10},{7,3},{... | collective-permute-start | bytes 1179656 | tf_op jit(solution)/shard_map/ppermute | solution.py:630
  2.1 0.8 broadcast_select_fusion
  2.9 3.7 %collective-permute-start = (bf16[1,100,256]{2,1,0:T(8,128)(2,1)S(1)}, bf16[1,100,256]{2,1,0:T(8,128)(2,1)S(1)}, u32[]{:S(2)}, u32[]{:S(2)}) collective-permute-start(bf16[1,100,256]{2,1,0:T(8,128)(2,1)S(1)} %get-tuple-element.79), channel_id=1, source_target_pairs={{0,4},{4,0},{8,12},{12,8},{1,5},{5,1},{9,13},{13,9},{2,6},{6,2},{1... | collective-permute-start | bytes 153608 | tf_op jit(solution)/shard_map/ppermute | solution.py:628
  6.7 0.7 collective-permute-start.1
  7.3 0.0 copy-start.1
  7.3 1.6 %copy-done.1 = bf16[1,1,64,64,144]{4,3,2,1,0:T(8,128)(2,1)S(1)} copy-done((bf16[1,1,64,64,144]{4,3,2,1,0:T(8,128)(2,1)S(1)}, bf16[1,1,64,64,144]{4,3,2,1,0:T(8,128)(2,1)}, u32[]{:S(2)}) %copy-start.1) | copy-done | bytes 1179672
  8.9 0.7 copy-done.10
  9.6 2.1 %shard_map.145 = (bf16[8,72,128]{2,1,0:T(8,128)(2,1)S(1)}, bf16[8,72,128]{2,1,0:T(8,128)(2,1)S(1)}, bf16[8,72,128]{2,1,0:T(8,128)(2,1)S(1)}, bf16[8,72,128]{2,1,0:T(8,128)(2,1)S(1)}) custom-call(s32[4,4,32]{2,1,0:T(4,128)S(1)} %bitcast.51, bf16[64,64,144]{2,1,0:T(8,128)(2,1)S(1)} %bitcast.46), custom_call_target="tpu_custom_call" | custom-call | flops 1000000000 | bytes 1 | tf_op jit(solution)/shard_map/pallas_call | solution.py:31
  11.7 0.0 copy-start.5
  11.7 0.0 copy-start.8
  11.7 4.4 %collective-permute-start.4 = (bf16[8,72,128]{2,1,0:T(8,128)(2,1)S(1)}, bf16[8,72,128]{2,1,0:T(8,128)(2,1)S(1)}, u32[]{:S(2)}, u32[]{:S(2)}) collective-permute-start(bf16[8,72,128]{2,1,0:T(8,128)(2,1)S(1)} %get-tuple-element.52), channel_id=1, source_target_pairs={{0,8},{4,12},{8,0},{12,4},{1,9},{5,13},{9,1},{13,5},{2,10},{6,14},... | collective-permute-start | bytes 442376 | tf_op jit(solution)/shard_map/ppermute | solution.py:616
  16.1 2.9 %collective-permute-start.5 = (bf16[8,72,128]{2,1,0:T(8,128)(2,1)S(1)}, bf16[8,72,128]{2,1,0:T(8,128)(2,1)S(1)}, u32[]{:S(2)}, u32[]{:S(2)}) collective-permute-start(bf16[8,72,128]{2,1,0:T(8,128)(2,1)S(1)} %get-tuple-element.53), channel_id=1, source_target_pairs={{0,12},{4,8},{8,4},{12,0},{1,13},{5,9},{9,5},{13,1},{2,14},{6,10},... | collective-permute-start | bytes 442376 | tf_op jit(solution)/shard_map/ppermute | solution.py:616
  19.0 0.0 collective-permute-done.inward_ref
  19.0 0.0 collective-permute-done.1.outward_ref
  19.1 4.0 %shard_map.146 = (bf16[12,64,256]{2,1,0:T(8,128)(2,1)}, bf16[11,64,256]{2,1,0:T(8,128)(2,1)S(1)}, bf16[1,64,256]{2,1,0:T(8,128)(2,1)S(1)}) custom-call(s32[1]{0:T(128)} %bitcast.even_ref, bf16[1,100,256]{2,1,0:T(8,128)(2,1)S(1)} %collective-permute-done.inward_ref, bf16[12,100,256]{2,1,0:T(8,128)(2,1)S(1)} %bitcast.45, ...), custom_call_target="tpu_custom_call" | custom-call | flops 1000000000 | bytes 1 | tf_op jit(solution)/shard_map/pallas_call | solution.py:31
  23.1 1.4 %collective-permute-start.9 = (bf16[11,64,256]{2,1,0:T(8,128)(2,1)S(1)}, bf16[11,64,256]{2,1,0:T(8,128)(2,1)S(1)}, u32[]{:S(2)}, u32[]{:S(2)}) collective-permute-start(bf16[11,64,256]{2,1,0:T(8,128)(2,1)S(1)} %get-tuple-element.46.top_ref), channel_id=1, source_target_pairs={{4,0},{8,4},{12,8},{5,1},{9,5},{13,9},{6,2},{10,6},{14,10},{7,3},{... | collective-permute-start | bytes 1081352 | tf_op jit(solution)/shard_map/ppermute | solution.py:641
  24.5 2.7 %collective-permute-start.3 = (bf16[8,72,128]{2,1,0:T(8,128)(2,1)S(1)}, bf16[8,72,128]{2,1,0:T(8,128)(2,1)S(1)}, u32[]{:S(2)}, u32[]{:S(2)}) collective-permute-start(bf16[8,72,128]{2,1,0:T(8,128)(2,1)S(1)} %get-tuple-element.51), channel_id=1, source_target_pairs={{0,4},{4,0},{8,12},{12,8},{1,5},{5,1},{9,13},{13,9},{2,6},{6,2},{1... | collective-permute-start | bytes 442376 | tf_op jit(solution)/shard_map/ppermute | solution.py:616
  27.2 0.0 copy-done.4
  27.2 0.4 shard_map.148
  27.6 0.0 collective-permute-done.2.tgt_ref
  27.7 0.0 copy-start.2
  27.7 2.3 %shard_map.147 = (s32[5,32]{1,0:T(8,128)S(1)}, bf16[12,256,128]{2,1,0:T(8,128)(2,1)S(1)}) custom-call(s32[4,4,32]{2,1,0:T(4,128)S(1)} %bitcast.52, bf16[12,64,256]{2,1,0:T(8,128)(2,1)S(1)} %bitcast.49, bf16[11,64,256]{2,1,0:T(8,128)(2,1)S(1)} %get-tuple-element.46.top_ref, bf16[1,64,256]{2,1,0:T(8,128)(2,1)S(1)} %get-tuple-element.48.last_ref), custom_call_target="tpu_custom_call" | custom-call | flops 10000000000 | bytes 1 | tf_op jit(solution)/shard_map/pallas_call | solution.py:658
  30.0 0.0 copy-done.2
  30.0 2.3 %shard_map.149 = (bf16[8,72,128]{2,1,0:T(8,128)(2,1)S(1)}, bf16[8,72,128]{2,1,0:T(8,128)(2,1)S(1)}, bf16[8,72,128]{2,1,0:T(8,128)(2,1)S(1)}, bf16[8,72,128]{2,1,0:T(8,128)(2,1)S(1)}) custom-call(s32[4,4,32]{2,1,0:T(4,128)S(1)} %bitcast.53, bf16[64,64,144]{2,1,0:T(8,128)(2,1)S(1)} %bitcast.47), custom_call_target="tpu_custom_call" | custom-call | flops 1000000000 | bytes 1 | tf_op jit(solution)/shard_map/pallas_call | solution.py:31
  32.3 0.1 collective-permute-start.6
  32.4 4.1 %collective-permute-done.9.mean_ref = bf16[11,64,256]{2,1,0:T(8,128)(2,1)S(1)} collective-permute-done((bf16[11,64,256]{2,1,0:T(8,128)(2,1)S(1)}, bf16[11,64,256]{2,1,0:T(8,128)(2,1)S(1)}, u32[]{:S(2)}, u32[]{:S(2)}) %collective-permute-start.9) | collective-permute-done | bytes 360480 | tf_op jit(solution)/shard_map/ppermute | solution.py:641
  36.5 1.2 %collective-permute-start.7 = (bf16[8,72,128]{2,1,0:T(8,128)(2,1)S(1)}, bf16[8,72,128]{2,1,0:T(8,128)(2,1)S(1)}, u32[]{:S(2)}, u32[]{:S(2)}) collective-permute-start(bf16[8,72,128]{2,1,0:T(8,128)(2,1)S(1)} %get-tuple-element.63), channel_id=1, source_target_pairs={{0,8},{4,12},{8,0},{12,4},{1,9},{5,13},{9,1},{13,5},{2,10},{6,14},... | collective-permute-start | bytes 442376 | tf_op jit(solution)/shard_map/ppermute | solution.py:616
  37.7 2.1 %shard_map.150 = (bf16[2,72,16,128]{3,2,1,0:T(8,128)(2,1)S(1)}, bf16[2,72,16,128]{3,2,1,0:T(8,128)(2,1)S(1)}) custom-call(s32[5,32]{1,0:T(8,128)S(1)} %get-tuple-element.49.table_ref.refs_0_, bf16[12,256,128]{2,1,0:T(8,128)(2,1)S(1)} %get-tuple-element.58.own, bf16[11,64,256]{2,1,0:T(8,128)(2,1)S(1)} %collective-permute-done.9.mean_ref, ...), custom_call_target="tpu_custom_call" | custom-call | flops 10000000000 | bytes 1 | tf_op jit(solution)/shard_map/pallas_call | solution.py:31
  39.8 0.0 collective-permute-done.4.refs_3_
  39.9 3.4 %collective-permute-start.8 = (bf16[8,72,128]{2,1,0:T(8,128)(2,1)S(1)}, bf16[8,72,128]{2,1,0:T(8,128)(2,1)S(1)}, u32[]{:S(2)}, u32[]{:S(2)}) collective-permute-start(bf16[8,72,128]{2,1,0:T(8,128)(2,1)S(1)} %get-tuple-element.64), channel_id=1, source_target_pairs={{0,12},{4,8},{8,4},{12,0},{1,13},{5,9},{9,5},{13,1},{2,14},{6,10},... | collective-permute-start | bytes 442376 | tf_op jit(solution)/shard_map/ppermute | solution.py:616
  43.3 0.0 collective-permute-done.5.refs_4_
  43.3 0.0 collective-permute-done.3.refs_2_
  43.3 0.0 copy-done.9
  43.3 6.8 %shard_map.151.refs_17_ = f32[2432,128]{1,0:T(8,128)S(1)} custom-call(s32[5,32]{1,0:T(8,128)S(1)} %get-tuple-element.49.table_ref.refs_0_, bf16[8,72,128]{2,1,0:T(8,128)(2,1)S(1)} %get-tuple-element.42.refs_1_, bf16[8,72,128]{2,1,0:T(8,128)(2,1)S(1)} %collective-permute-done.3.refs_2_, bf16[8,72,128]{2,1,0:T(8,128)(2,1)S(1)} %collective-permute-done.4.refs_3_, ...), custom_call_target="tpu_custom_call" | custom-call | flops 10000000000 | bytes 1 | tf_op jit(solution)/shard_map/pallas_call | solution.py:31
  50.1 0.0 collective-permute-done.6.refs_6_
  50.1 0.0 collective-permute-done.7.refs_7_
  50.1 0.0 collective-permute-done.8.refs_8_
  50.1 7.1 %shard_map.152 = (f32[1216,128]{1,0:T(8,128)S(1)}, bf16[1216,128]{1,0:T(8,128)(2,1)S(1)}) custom-call(s32[5,32]{1,0:T(8,128)S(1)} %get-tuple-element.49.table_ref.refs_0_, bf16[8,72,128]{2,1,0:T(8,128)(2,1)S(1)} %get-tuple-element.42.refs_1_, bf16[8,72,128]{2,1,0:T(8,128)(2,1)S(1)} %collective-permute-done.3.refs_2_, ...), custom_call_target="tpu_custom_call" | custom-call | flops 10000000000 | bytes 1 | tf_op jit(solution)/shard_map/pallas_call | solution.py:31
  57.2 0.1 collective-permute-start.10
  57.3 1.6 %collective-permute-done.10 = bf16[1216,128]{1,0:T(8,128)(2,1)S(1)} collective-permute-done((bf16[1216,128]{1,0:T(8,128)(2,1)S(1)}, bf16[1216,128]{1,0:T(8,128)(2,1)S(1)}, u32[]{:S(2)}, u32[]{:S(2)}) %collective-permute-start.10) | collective-permute-done | bytes 311328 | tf_op jit(solution)/shard_map/ppermute | solution.py:734
  58.9 0.1 convert_add_fusion
  59.0 2.5 %collective-permute-start.13 = (bf16[304,128]{1,0:T(8,128)(2,1)S(1)}, bf16[304,128]{1,0:T(8,128)(2,1)S(1)}, u32[]{:S(2)}, u32[]{:S(2)}) collective-permute-start(bf16[304,128]{1,0:T(8,128)(2,1)S(1)} %get-tuple-element.81), channel_id=1, source_target_pairs={{0,3},{1,2},{2,1},{3,0},{4,7},{5,6},{6,5},{7,4},{8,11},{9,10},{10,... | collective-permute-start | bytes 233480 | tf_op jit(solution)/shard_map/ppermute | solution.py:541
  61.5 0.5 collective-permute-start.12
  62.0 0.5 collective-permute-start.11
  62.5 1.8 %collective-permute-done.13 = bf16[304,128]{1,0:T(8,128)(2,1)S(1)} collective-permute-done((bf16[304,128]{1,0:T(8,128)(2,1)S(1)}, bf16[304,128]{1,0:T(8,128)(2,1)S(1)}, u32[]{:S(2)}, u32[]{:S(2)}) %collective-permute-start.13) | collective-permute-done | bytes 77856 | tf_op jit(solution)/shard_map/ppermute | solution.py:541
  64.4 1.6 %collective-permute-done.12 = bf16[304,128]{1,0:T(8,128)(2,1)S(1)} collective-permute-done((bf16[304,128]{1,0:T(8,128)(2,1)S(1)}, bf16[304,128]{1,0:T(8,128)(2,1)S(1)}, u32[]{:S(2)}, u32[]{:S(2)}) %collective-permute-start.12) | collective-permute-done | bytes 77856 | tf_op jit(solution)/shard_map/ppermute | solution.py:541
  66.0 0.4 collective-permute-done.11
  66.4 0.5 collective-permute-start.16
  67.0 2.8 %collective-permute-start.15 = (bf16[304,128]{1,0:T(8,128)(2,1)S(1)}, bf16[304,128]{1,0:T(8,128)(2,1)S(1)}, u32[]{:S(2)}, u32[]{:S(2)}) collective-permute-start(bf16[304,128]{1,0:T(8,128)(2,1)S(1)} %fusion.3), channel_id=1, source_target_pairs={{0,8},{4,12},{8,0},{12,4},{1,9},{5,13},{9,1},{13,5},{2,10},{6,14},... | collective-permute-start | bytes 233480 | tf_op jit(solution)/shard_map/ppermute | solution.py:568
  69.8 1.1 %collective-permute-start.14 = (bf16[304,128]{1,0:T(8,128)(2,1)S(1)}, bf16[304,128]{1,0:T(8,128)(2,1)S(1)}, u32[]{:S(2)}, u32[]{:S(2)}) collective-permute-start(bf16[304,128]{1,0:T(8,128)(2,1)S(1)} %fusion.3), channel_id=1, source_target_pairs={{0,4},{4,0},{8,12},{12,8},{1,5},{5,1},{9,13},{13,9},{2,6},{6,2},{1... | collective-permute-start | bytes 233480 | tf_op jit(solution)/shard_map/ppermute | solution.py:568
  70.9 2.5 %collective-permute-done.16 = bf16[304,128]{1,0:T(8,128)(2,1)S(1)} collective-permute-done((bf16[304,128]{1,0:T(8,128)(2,1)S(1)}, bf16[304,128]{1,0:T(8,128)(2,1)S(1)}, u32[]{:S(2)}, u32[]{:S(2)}) %collective-permute-start.16) | collective-permute-done | bytes 77856 | tf_op jit(solution)/shard_map/ppermute | solution.py:568
  73.4 2.6 %collective-permute-done.15 = bf16[304,128]{1,0:T(8,128)(2,1)S(1)} collective-permute-done((bf16[304,128]{1,0:T(8,128)(2,1)S(1)}, bf16[304,128]{1,0:T(8,128)(2,1)S(1)}, u32[]{:S(2)}, u32[]{:S(2)}) %collective-permute-start.15) | collective-permute-done | bytes 77856 | tf_op jit(solution)/shard_map/ppermute | solution.py:568
  76.0 0.0 collective-permute-done.14
  76.1 1.4 %collective-permute-start.17 = (bf16[304,128]{1,0:T(8,128)(2,1)S(1)}, bf16[304,128]{1,0:T(8,128)(2,1)S(1)}, u32[]{:S(2)}, u32[]{:S(2)}) collective-permute-start(bf16[304,128]{1,0:T(8,128)(2,1)S(1)} %reduce-precision_convert_fusion), channel_id=1, source_target_pairs={{0,3},{1,2},{2,1},{3,0},{4,7},{5,6},{6,5},{7,4},{8,11},{9,10},{10,... | collective-permute-start | bytes 233480 | tf_op jit(solution)/shard_map/ppermute | solution.py:551
  77.5 2.2 %collective-permute-start.18 = (bf16[304,128]{1,0:T(8,128)(2,1)S(1)}, bf16[304,128]{1,0:T(8,128)(2,1)S(1)}, u32[]{:S(2)}, u32[]{:S(2)}) collective-permute-start(bf16[304,128]{1,0:T(8,128)(2,1)S(1)} %reduce-precision_convert_fusion), channel_id=1, source_target_pairs={{0,2},{1,3},{2,0},{3,1},{4,6},{5,7},{6,4},{7,5},{8,10},{9,11},{10,... | collective-permute-start | bytes 233480 | tf_op jit(solution)/shard_map/ppermute | solution.py:551
  79.7 0.0 collective-permute-start.19
  79.8 2.2 %collective-permute-done.17 = bf16[304,128]{1,0:T(8,128)(2,1)S(1)} collective-permute-done((bf16[304,128]{1,0:T(8,128)(2,1)S(1)}, bf16[304,128]{1,0:T(8,128)(2,1)S(1)}, u32[]{:S(2)}, u32[]{:S(2)}) %collective-permute-start.17) | collective-permute-done | bytes 77856 | tf_op jit(solution)/shard_map/ppermute | solution.py:551
  82.0 0.5 collective-permute-done.18
  82.5 1.7 %collective-permute-done.19 = bf16[304,128]{1,0:T(8,128)(2,1)S(1)} collective-permute-done((bf16[304,128]{1,0:T(8,128)(2,1)S(1)}, bf16[304,128]{1,0:T(8,128)(2,1)S(1)}, u32[]{:S(2)}, u32[]{:S(2)}) %collective-permute-start.19) | collective-permute-done | bytes 77856 | tf_op jit(solution)/shard_map/ppermute | solution.py:551
  84.1 0.1 select_bitcast_fusion.3
  84.3 0.1 collective-permute-start.20
  84.4 1.6 %collective-permute-done.20.other_ref = bf16[1216,128]{1,0:T(8,128)(2,1)S(1)} collective-permute-done((bf16[1216,128]{1,0:T(8,128)(2,1)S(1)}, bf16[1216,128]{1,0:T(8,128)(2,1)S(1)}, u32[]{:S(2)}, u32[]{:S(2)}) %collective-permute-start.20) | collective-permute-done | bytes 311328 | tf_op jit(solution)/shard_map/ppermute | solution.py:746
  86.0 1.1 %shard_map.153 = (f32[128,1152]{1,0:T(8,128)}, f32[128,1152]{1,0:T(8,128)}, f32[64,128]{1,0:T(8,128)}, f32[32,128]{1,0:T(8,128)}, f32[1,1]{1,0:T(1,128)}) custom-call(bf16[1216,128]{1,0:T(8,128)(2,1)S(1)} %bitcast.43, bf16[1216,128]{1,0:T(8,128)(2,1)S(1)} %collective-permute-done.20.other_ref), custom_call_target="tpu_custom_call" | custom-call | bytes 1 | tf_op jit(solution)/shard_map/pallas_call | solution.py:31
  (21 shorter events, 0.2 us)
Async XLA Ops:
  0.6 18.4 %copy-start = (bf16[1,100,12,256]{3,1,2,0:T(8,128)(2,1)S(1)}, bf16[1,100,12,256]{3,1,2,0:T(8,128)(2,1)}, u32[]{:S(2)}) copy-start(bf16[1,100,12,256]{3,1,2,0:T(8,128)(2,1)} %param.10) | copy-start | bytes 1843204
  0.6 27.0 %collective-permute-start.2 = (bf16[12,64,256]{2,1,0:T(8,128)(2,1)}, bf16[12,64,256]{2,1,0:T(8,128)(2,1)S(1)}, u32[]{:S(2)}, u32[]{:S(2)}) collective-permute-start(bf16[12,64,256]{2,1,0:T(8,128)(2,1)} %bitcast.48), channel_id=1, source_target_pairs={{4,0},{8,4},{12,8},{5,1},{9,5},{13,9},{6,2},{10,6},{14,10},{7,3},{... | collective-permute-start | bytes 1179656 | tf_op jit(solution)/shard_map/ppermute | solution.py:630
  2.9 16.1 %collective-permute-start = (bf16[1,100,256]{2,1,0:T(8,128)(2,1)S(1)}, bf16[1,100,256]{2,1,0:T(8,128)(2,1)S(1)}, u32[]{:S(2)}, u32[]{:S(2)}) collective-permute-start(bf16[1,100,256]{2,1,0:T(8,128)(2,1)S(1)} %get-tuple-element.79), channel_id=1, source_target_pairs={{0,4},{4,0},{8,12},{12,8},{1,5},{5,1},{9,13},{13,9},{2,6},{6,2},{1... | collective-permute-start | bytes 153608 | tf_op jit(solution)/shard_map/ppermute | solution.py:628
  6.7 12.4 %collective-permute-start.1 = (bf16[1,100,256]{2,1,0:T(8,128)(2,1)S(1)}, bf16[1,100,256]{2,1,0:T(8,128)(2,1)S(1)}, u32[]{:S(2)}, u32[]{:S(2)}) collective-permute-start(bf16[1,100,256]{2,1,0:T(8,128)(2,1)S(1)} %get-tuple-element.78), channel_id=1, source_target_pairs={{4,8},{8,4},{5,9},{9,5},{6,10},{10,6},{7,11},{11,7},{20,24},{24,20... | collective-permute-start | bytes 153608 | tf_op jit(solution)/shard_map/ppermute | solution.py:629
  7.3 1.6 %copy-start.1 = (bf16[1,1,64,64,144]{4,3,2,1,0:T(8,128)(2,1)S(1)}, bf16[1,1,64,64,144]{4,3,2,1,0:T(8,128)(2,1)}, u32[]{:S(2)}) copy-start(bf16[1,1,64,64,144]{4,3,2,1,0:T(8,128)(2,1)} %param.12) | copy-start | bytes 3538948
  8.9 0.7 copy-start.10
  9.6 9.4 %copy-start.6 = (bf16[128,900]{0,1:T(8,128)(2,1)S(1)}, bf16[128,900]{0,1:T(8,128)(2,1)}, u32[]{:S(2)}) copy-start(bf16[128,900]{0,1:T(8,128)(2,1)} %param.14) | copy-start | bytes 691204
  9.6 9.4 %copy-start.7 = (bf16[64,128]{1,0:T(8,128)(2,1)S(1)}, bf16[64,128]{1,0:T(8,128)(2,1)}, u32[]{:S(2)}) copy-start(bf16[64,128]{1,0:T(8,128)(2,1)} %proj_ref.1) | copy-start | bytes 49156
  11.7 15.5 %copy-start.4 = (bf16[128,1152]{1,0:T(8,128)(2,1)S(1)}, bf16[128,1152]{1,0:T(8,128)(2,1)}, u32[]{:S(2)}) copy-start(bf16[128,1152]{1,0:T(8,128)(2,1)} %one_ref) | copy-start | bytes 884740
  11.7 15.5 %copy-start.5 = (bf16[128,1152]{1,0:T(8,128)(2,1)S(1)}, bf16[128,1152]{1,0:T(8,128)(2,1)}, u32[]{:S(2)}) copy-start(bf16[128,1152]{1,0:T(8,128)(2,1)} %two_ref) | copy-start | bytes 884740
  11.7 15.5 %copy-start.8 = (bf16[64,128]{1,0:T(8,128)(2,1)S(1)}, bf16[64,128]{1,0:T(8,128)(2,1)}, u32[]{:S(2)}) copy-start(bf16[64,128]{1,0:T(8,128)(2,1)} %proj_ref.2) | copy-start | bytes 49156
  11.7 28.1 %collective-permute-start.4 = (bf16[8,72,128]{2,1,0:T(8,128)(2,1)S(1)}, bf16[8,72,128]{2,1,0:T(8,128)(2,1)S(1)}, u32[]{:S(2)}, u32[]{:S(2)}) collective-permute-start(bf16[8,72,128]{2,1,0:T(8,128)(2,1)S(1)} %get-tuple-element.52), channel_id=1, source_target_pairs={{0,8},{4,12},{8,0},{12,4},{1,9},{5,13},{9,1},{13,5},{2,10},{6,14},... | collective-permute-start | bytes 442376 | tf_op jit(solution)/shard_map/ppermute | solution.py:616
  16.1 27.2 %collective-permute-start.5 = (bf16[8,72,128]{2,1,0:T(8,128)(2,1)S(1)}, bf16[8,72,128]{2,1,0:T(8,128)(2,1)S(1)}, u32[]{:S(2)}, u32[]{:S(2)}) collective-permute-start(bf16[8,72,128]{2,1,0:T(8,128)(2,1)S(1)} %get-tuple-element.53), channel_id=1, source_target_pairs={{0,12},{4,8},{8,4},{12,0},{1,13},{5,9},{9,5},{13,1},{2,14},{6,10},... | collective-permute-start | bytes 442376 | tf_op jit(solution)/shard_map/ppermute | solution.py:616
  23.1 4.6 %copy-start.3 = (bf16[1,64,12,256]{3,1,2,0:T(8,128)(2,1)S(1)}, bf16[1,64,12,256]{3,1,2,0:T(8,128)(2,1)}, u32[]{:S(2)}) copy-start(bf16[1,64,12,256]{3,1,2,0:T(8,128)(2,1)} %param.11) | copy-start | bytes 1179652
  23.1 4.6 %copy-start.11 = (s32[1,4,32,4]{2,3,1,0:T(4,128)S(1)}, s32[1,4,32,4]{2,3,1,0:T(4,128)}, u32[]{:S(2)}) copy-start(s32[1,4,32,4]{2,3,1,0:T(4,128)} %param.13) | copy-start | bytes 6148
  23.1 13.4 %collective-permute-start.9 = (bf16[11,64,256]{2,1,0:T(8,128)(2,1)S(1)}, bf16[11,64,256]{2,1,0:T(8,128)(2,1)S(1)}, u32[]{:S(2)}, u32[]{:S(2)}) collective-permute-start(bf16[11,64,256]{2,1,0:T(8,128)(2,1)S(1)} %get-tuple-element.46.top_ref), channel_id=1, source_target_pairs={{4,0},{8,4},{12,8},{5,1},{9,5},{13,9},{6,2},{10,6},{14,10},{7,3},{... | collective-permute-start | bytes 1081352 | tf_op jit(solution)/shard_map/ppermute | solution.py:641
  24.5 18.8 %collective-permute-start.3 = (bf16[8,72,128]{2,1,0:T(8,128)(2,1)S(1)}, bf16[8,72,128]{2,1,0:T(8,128)(2,1)S(1)}, u32[]{:S(2)}, u32[]{:S(2)}) collective-permute-start(bf16[8,72,128]{2,1,0:T(8,128)(2,1)S(1)} %get-tuple-element.51), channel_id=1, source_target_pairs={{0,4},{4,0},{8,12},{12,8},{1,5},{5,1},{9,13},{13,9},{2,6},{6,2},{1... | collective-permute-start | bytes 442376 | tf_op jit(solution)/shard_map/ppermute | solution.py:616
  27.7 2.3 %copy-start.2 = (bf16[1,1,64,64,144]{4,3,2,1,0:T(8,128)(2,1)S(1)}, bf16[1,1,64,64,144]{4,3,2,1,0:T(8,128)(2,1)}, u32[]{:S(2)}) copy-start(bf16[1,1,64,64,144]{4,3,2,1,0:T(8,128)(2,1)} %param.12) | copy-start | bytes 3538948
  32.3 17.8 %collective-permute-start.6 = (bf16[8,72,128]{2,1,0:T(8,128)(2,1)S(1)}, bf16[8,72,128]{2,1,0:T(8,128)(2,1)S(1)}, u32[]{:S(2)}, u32[]{:S(2)}) collective-permute-start(bf16[8,72,128]{2,1,0:T(8,128)(2,1)S(1)} %get-tuple-element.62), channel_id=1, source_target_pairs={{0,4},{4,0},{8,12},{12,8},{1,5},{5,1},{9,13},{13,9},{2,6},{6,2},{1... | collective-permute-start | bytes 442376 | tf_op jit(solution)/shard_map/ppermute | solution.py:616
  36.5 13.6 %collective-permute-start.7 = (bf16[8,72,128]{2,1,0:T(8,128)(2,1)S(1)}, bf16[8,72,128]{2,1,0:T(8,128)(2,1)S(1)}, u32[]{:S(2)}, u32[]{:S(2)}) collective-permute-start(bf16[8,72,128]{2,1,0:T(8,128)(2,1)S(1)} %get-tuple-element.63), channel_id=1, source_target_pairs={{0,8},{4,12},{8,0},{12,4},{1,9},{5,13},{9,1},{13,5},{2,10},{6,14},... | collective-permute-start | bytes 442376 | tf_op jit(solution)/shard_map/ppermute | solution.py:616
  37.7 5.6 %copy-start.9 = (f32[32,128]{1,0:T(8,128)S(1)}, f32[32,128]{1,0:T(8,128)}, u32[]{:S(2)}) copy-start(f32[32,128]{1,0:T(8,128)} %refs_11_.1) | copy-start | bytes 49156
  39.9 10.2 %collective-permute-start.8 = (bf16[8,72,128]{2,1,0:T(8,128)(2,1)S(1)}, bf16[8,72,128]{2,1,0:T(8,128)(2,1)S(1)}, u32[]{:S(2)}, u32[]{:S(2)}) collective-permute-start(bf16[8,72,128]{2,1,0:T(8,128)(2,1)S(1)} %get-tuple-element.64), channel_id=1, source_target_pairs={{0,12},{4,8},{8,4},{12,0},{1,13},{5,9},{9,5},{13,1},{2,14},{6,10},... | collective-permute-start | bytes 442376 | tf_op jit(solution)/shard_map/ppermute | solution.py:616
  57.2 1.7 %collective-permute-start.10 = (bf16[1216,128]{1,0:T(8,128)(2,1)S(1)}, bf16[1216,128]{1,0:T(8,128)(2,1)S(1)}, u32[]{:S(2)}, u32[]{:S(2)}) collective-permute-start(bf16[1216,128]{1,0:T(8,128)(2,1)S(1)} %get-tuple-element.72), channel_id=1, source_target_pairs={{0,16},{16,0},{1,17},{17,1},{2,18},{18,2},{3,19},{19,3},{4,20},{20... | collective-permute-start | bytes 933896 | tf_op jit(solution)/shard_map/ppermute | solution.py:734
  59.0 5.4 %collective-permute-start.13 = (bf16[304,128]{1,0:T(8,128)(2,1)S(1)}, bf16[304,128]{1,0:T(8,128)(2,1)S(1)}, u32[]{:S(2)}, u32[]{:S(2)}) collective-permute-start(bf16[304,128]{1,0:T(8,128)(2,1)S(1)} %get-tuple-element.81), channel_id=1, source_target_pairs={{0,3},{1,2},{2,1},{3,0},{4,7},{5,6},{6,5},{7,4},{8,11},{9,10},{10,... | collective-permute-start | bytes 233480 | tf_op jit(solution)/shard_map/ppermute | solution.py:541
  61.5 4.5 %collective-permute-start.12 = (bf16[304,128]{1,0:T(8,128)(2,1)S(1)}, bf16[304,128]{1,0:T(8,128)(2,1)S(1)}, u32[]{:S(2)}, u32[]{:S(2)}) collective-permute-start(bf16[304,128]{1,0:T(8,128)(2,1)S(1)} %get-tuple-element.82), channel_id=1, source_target_pairs={{0,2},{1,3},{2,0},{3,1},{4,6},{5,7},{6,4},{7,5},{8,10},{9,11},{10,... | collective-permute-start | bytes 233480 | tf_op jit(solution)/shard_map/ppermute | solution.py:541
  62.0 4.4 %collective-permute-start.11 = (bf16[304,128]{1,0:T(8,128)(2,1)S(1)}, bf16[304,128]{1,0:T(8,128)(2,1)S(1)}, u32[]{:S(2)}, u32[]{:S(2)}) collective-permute-start(bf16[304,128]{1,0:T(8,128)(2,1)S(1)} %get-tuple-element.80), channel_id=1, source_target_pairs={{0,1},{1,0},{2,3},{3,2},{4,5},{5,4},{6,7},{7,6},{8,9},{9,8},{10,11... | collective-permute-start | bytes 233480 | tf_op jit(solution)/shard_map/ppermute | solution.py:541
  66.4 7.0 %collective-permute-start.16 = (bf16[304,128]{1,0:T(8,128)(2,1)S(1)}, bf16[304,128]{1,0:T(8,128)(2,1)S(1)}, u32[]{:S(2)}, u32[]{:S(2)}) collective-permute-start(bf16[304,128]{1,0:T(8,128)(2,1)S(1)} %fusion.3), channel_id=1, source_target_pairs={{0,12},{4,8},{8,4},{12,0},{1,13},{5,9},{9,5},{13,1},{2,14},{6,10},... | collective-permute-start | bytes 233480 | tf_op jit(solution)/shard_map/ppermute | solution.py:568
  67.0 9.0 %collective-permute-start.15 = (bf16[304,128]{1,0:T(8,128)(2,1)S(1)}, bf16[304,128]{1,0:T(8,128)(2,1)S(1)}, u32[]{:S(2)}, u32[]{:S(2)}) collective-permute-start(bf16[304,128]{1,0:T(8,128)(2,1)S(1)} %fusion.3), channel_id=1, source_target_pairs={{0,8},{4,12},{8,0},{12,4},{1,9},{5,13},{9,1},{13,5},{2,10},{6,14},... | collective-permute-start | bytes 233480 | tf_op jit(solution)/shard_map/ppermute | solution.py:568
  69.8 6.3 %collective-permute-start.14 = (bf16[304,128]{1,0:T(8,128)(2,1)S(1)}, bf16[304,128]{1,0:T(8,128)(2,1)S(1)}, u32[]{:S(2)}, u32[]{:S(2)}) collective-permute-start(bf16[304,128]{1,0:T(8,128)(2,1)S(1)} %fusion.3), channel_id=1, source_target_pairs={{0,4},{4,0},{8,12},{12,8},{1,5},{5,1},{9,13},{13,9},{2,6},{6,2},{1... | collective-permute-start | bytes 233480 | tf_op jit(solution)/shard_map/ppermute | solution.py:568
  76.1 5.9 %collective-permute-start.17 = (bf16[304,128]{1,0:T(8,128)(2,1)S(1)}, bf16[304,128]{1,0:T(8,128)(2,1)S(1)}, u32[]{:S(2)}, u32[]{:S(2)}) collective-permute-start(bf16[304,128]{1,0:T(8,128)(2,1)S(1)} %reduce-precision_convert_fusion), channel_id=1, source_target_pairs={{0,3},{1,2},{2,1},{3,0},{4,7},{5,6},{6,5},{7,4},{8,11},{9,10},{10,... | collective-permute-start | bytes 233480 | tf_op jit(solution)/shard_map/ppermute | solution.py:551
  77.5 4.9 %collective-permute-start.18 = (bf16[304,128]{1,0:T(8,128)(2,1)S(1)}, bf16[304,128]{1,0:T(8,128)(2,1)S(1)}, u32[]{:S(2)}, u32[]{:S(2)}) collective-permute-start(bf16[304,128]{1,0:T(8,128)(2,1)S(1)} %reduce-precision_convert_fusion), channel_id=1, source_target_pairs={{0,2},{1,3},{2,0},{3,1},{4,6},{5,7},{6,4},{7,5},{8,10},{9,11},{10,... | collective-permute-start | bytes 233480 | tf_op jit(solution)/shard_map/ppermute | solution.py:551
  79.7 4.4 %collective-permute-start.19 = (bf16[304,128]{1,0:T(8,128)(2,1)S(1)}, bf16[304,128]{1,0:T(8,128)(2,1)S(1)}, u32[]{:S(2)}, u32[]{:S(2)}) collective-permute-start(bf16[304,128]{1,0:T(8,128)(2,1)S(1)} %reduce-precision_convert_fusion), channel_id=1, source_target_pairs={{0,1},{1,0},{2,3},{3,2},{4,5},{5,4},{6,7},{7,6},{8,9},{9,8},{10,11... | collective-permute-start | bytes 233480 | tf_op jit(solution)/shard_map/ppermute | solution.py:551
  84.3 1.7 %collective-permute-start.20 = (bf16[1216,128]{1,0:T(8,128)(2,1)S(1)}, bf16[1216,128]{1,0:T(8,128)(2,1)S(1)}, u32[]{:S(2)}, u32[]{:S(2)}) collective-permute-start(bf16[1216,128]{1,0:T(8,128)(2,1)S(1)} %bitcast.42), channel_id=1, source_target_pairs={{0,16},{16,0},{1,17},{17,1},{2,18},{18,2},{3,19},{19,3},{4,20},{20... | collective-permute-start | bytes 933896 | tf_op jit(solution)/shard_map/ppermute | solution.py:746

commit v6 on v5

--- a/solution.py
+++ b/solution.py
@@ -538,7 +538,7 @@
     me = lax.axis_index(axis)
     out = take(values, me)
     arrived = [
-        lax.ppermute(take(values, me ^ d).astype(BF), axis, by_distance(axis, d)) for d in range(1, n)
+        lax.ppermute(take(values, me ^ d).astype(BF), axis, by_distance(axis, d)) for d in reversed(range(1, n))
     ]
     for piece in arrived:
         out = out + piece.astype(F32)
@@ -548,7 +548,8 @@
 def gather_all(piece, axis):
     n = lax.axis_size(axis)
     me = lax.axis_index(axis)
-    found = [piece] + [lax.ppermute(piece, axis, by_distance(axis, d)) for d in range(1, n)]
+    moved = {d: lax.ppermute(piece, axis, by_distance(axis, d)) for d in reversed(range(1, n))}
+    found = [piece] + [moved[d] for d in range(1, n)]
     return jnp.stack([sum_select(found, me, i) for i in range(n)])
 
 
@@ -564,8 +565,8 @@
     if n > 4:
         return lax.psum(piece, axis)
     values = [rounded_to_bf16(piece).astype(BF)]
-    for d in range(1, n):
-        values.append(lax.ppermute(values[0], axis, by_distance(axis, d)))
+    moved = {d: lax.ppermute(values[0], axis, by_distance(axis, d)) for d in reversed(range(1, n))}
+    values += [moved[d] for d in range(1, n)]
     values = [v.astype(F32) for v in values]
     while len(values) > 1:
         values = [values[i] + values[i + 1] for i in range(0, len(values), 2)]

time: 87.4 us -> 86.4 us (0.989)
    ppermute x3, waiting for transfers between devices: 4.36 us -> 3.14 us  [gather_all(): lax.ppermute(piece, axis, by_distance(axis, d))]
    ppermute x3, waiting for transfers between devices: 3.88 us -> 4.83 us  [scatter_sum(): lax.ppermute(take(values, me ^ d).astype(BF), axis, by_distance(axis, d))]
where the time goes in v6:
time: 86.4 us; the launch traced here: 86.1 us
  starting transfers between devices  33.7 us (39%)
  Pallas kernels  28.2 us (33%)
  waiting for transfers between devices  19.8 us (23%)
  local copies, waits for them, and re-layouts  2.37 us (3%)
  other arithmetic  1.16 us (1%)
  between operations  0.95 us (1%)
    pallas_call x8, Pallas kernels, call(): pl.pallas_call(kernel, out_shape=outs, in_specs=list(specs), out_specs=ja...  25.9 us
    ppermute x6, starting transfers between devices, sent(): lax.ppermute(packed_pieces[d], 'rows', by_distance('rows', d))  14.8 us
    ppermute x3, waiting for transfers between devices, scatter_sum(): lax.ppermute(take(values, me ^ d).astype(BF), axis, by_distance(axis, d))  4.83 us
    ppermute x3, waiting for transfers between devices, rows_sum(): lax.ppermute(values[0], axis, by_distance(axis, d))  4.52 us
    ppermute x3, starting transfers between devices, rows_sum(): lax.ppermute(values[0], axis, by_distance(axis, d))  4.45 us
    ppermute x1, waiting for transfers between devices, per_device(): mean_low = lax.ppermute(mean_top, 'rows', down)  4.1 us
    ppermute x1, starting transfers between devices, per_device(): inward = lax.ppermute(jnp.where(even, high_edge, low_edge), 'rows', pairs)  3.72 us
    ppermute x3, starting transfers between devices, gather_all(): lax.ppermute(piece, axis, by_distance(axis, d))  3.55 us
  transfers between devices with their start and end apart: 21, of which 11 were waited for; matrix products, arithmetic and copies ran while one was open for 1% of the time, Pallas kernels for 23%

profile of v6, /device:TPU:0, one launch (start us, length us, event | category | flops | bytes accessed | tf_op | source)
XLA Modules:
  0.0 86.1 jit_solution(10219856906758557974)
XLA Ops:
  0.6 1.4 %collective-permute-start.2 = (bf16[12,64,256]{2,1,0:T(8,128)(2,1)}, bf16[12,64,256]{2,1,0:T(8,128)(2,1)S(1)}, u32[]{:S(2)}, u32[]{:S(2)}) collective-permute-start(bf16[12,64,256]{2,1,0:T(8,128)(2,1)} %bitcast.48), channel_id=1, source_target_pairs={{4,0},{8,4},{12,8},{5,1},{9,5},{13,9},{6,2},{10,6},{14,10},{7,3},{... | collective-permute-start | bytes 1179656 | tf_op jit(solution)/shard_map/ppermute | solution.py:631
  2.1 0.8 broadcast_select_fusion
  2.9 3.7 %collective-permute-start = (bf16[1,100,256]{2,1,0:T(8,128)(2,1)S(1)}, bf16[1,100,256]{2,1,0:T(8,128)(2,1)S(1)}, u32[]{:S(2)}, u32[]{:S(2)}) collective-permute-start(bf16[1,100,256]{2,1,0:T(8,128)(2,1)S(1)} %get-tuple-element.79), channel_id=1, source_target_pairs={{0,4},{4,0},{8,12},{12,8},{1,5},{5,1},{9,13},{13,9},{2,6},{6,2},{1... | collective-permute-start | bytes 153608 | tf_op jit(solution)/shard_map/ppermute | solution.py:629
  6.7 0.7 collective-permute-start.1
  7.3 0.0 copy-start.1
  7.3 1.6 %copy-done.1 = bf16[1,1,64,64,144]{4,3,2,1,0:T(8,128)(2,1)S(1)} copy-done((bf16[1,1,64,64,144]{4,3,2,1,0:T(8,128)(2,1)S(1)}, bf16[1,1,64,64,144]{4,3,2,1,0:T(8,128)(2,1)}, u32[]{:S(2)}) %copy-start.1) | copy-done | bytes 1179672
  8.9 0.7 copy-done.10
  9.6 2.1 %shard_map.145 = (bf16[8,72,128]{2,1,0:T(8,128)(2,1)S(1)}, bf16[8,72,128]{2,1,0:T(8,128)(2,1)S(1)}, bf16[8,72,128]{2,1,0:T(8,128)(2,1)S(1)}, bf16[8,72,128]{2,1,0:T(8,128)(2,1)S(1)}) custom-call(s32[4,4,32]{2,1,0:T(4,128)S(1)} %bitcast.51, bf16[64,64,144]{2,1,0:T(8,128)(2,1)S(1)} %bitcast.46), custom_call_target="tpu_custom_call" | custom-call | flops 1000000000 | bytes 1 | tf_op jit(solution)/shard_map/pallas_call | solution.py:31
  11.7 0.0 copy-start.5
  11.7 0.0 copy-start.8
  11.7 4.4 %collective-permute-start.4 = (bf16[8,72,128]{2,1,0:T(8,128)(2,1)S(1)}, bf16[8,72,128]{2,1,0:T(8,128)(2,1)S(1)}, u32[]{:S(2)}, u32[]{:S(2)}) collective-permute-start(bf16[8,72,128]{2,1,0:T(8,128)(2,1)S(1)} %get-tuple-element.52), channel_id=1, source_target_pairs={{0,8},{4,12},{8,0},{12,4},{1,9},{5,13},{9,1},{13,5},{2,10},{6,14},... | collective-permute-start | bytes 442376 | tf_op jit(solution)/shard_map/ppermute | solution.py:617
  16.1 2.9 %collective-permute-start.5 = (bf16[8,72,128]{2,1,0:T(8,128)(2,1)S(1)}, bf16[8,72,128]{2,1,0:T(8,128)(2,1)S(1)}, u32[]{:S(2)}, u32[]{:S(2)}) collective-permute-start(bf16[8,72,128]{2,1,0:T(8,128)(2,1)S(1)} %get-tuple-element.53), channel_id=1, source_target_pairs={{0,12},{4,8},{8,4},{12,0},{1,13},{5,9},{9,5},{13,1},{2,14},{6,10},... | collective-permute-start | bytes 442376 | tf_op jit(solution)/shard_map/ppermute | solution.py:617
  19.0 0.0 collective-permute-done.inward_ref
  19.0 0.0 collective-permute-done.1.outward_ref
  19.0 0.0 copy-done.6
  19.0 0.0 copy-done.7
  19.1 4.0 %shard_map.146 = (bf16[12,64,256]{2,1,0:T(8,128)(2,1)}, bf16[11,64,256]{2,1,0:T(8,128)(2,1)S(1)}, bf16[1,64,256]{2,1,0:T(8,128)(2,1)S(1)}) custom-call(s32[1]{0:T(128)} %bitcast.even_ref, bf16[1,100,256]{2,1,0:T(8,128)(2,1)S(1)} %collective-permute-done.inward_ref, bf16[12,100,256]{2,1,0:T(8,128)(2,1)S(1)} %bitcast.45, ...), custom_call_target="tpu_custom_call" | custom-call | flops 1000000000 | bytes 1 | tf_op jit(solution)/shard_map/pallas_call | solution.py:31
  23.1 1.4 %collective-permute-start.9 = (bf16[11,64,256]{2,1,0:T(8,128)(2,1)S(1)}, bf16[11,64,256]{2,1,0:T(8,128)(2,1)S(1)}, u32[]{:S(2)}, u32[]{:S(2)}) collective-permute-start(bf16[11,64,256]{2,1,0:T(8,128)(2,1)S(1)} %get-tuple-element.46.top_ref), channel_id=1, source_target_pairs={{4,0},{8,4},{12,8},{5,1},{9,5},{13,9},{6,2},{10,6},{14,10},{7,3},{... | collective-permute-start | bytes 1081352 | tf_op jit(solution)/shard_map/ppermute | solution.py:642
  24.5 2.7 %collective-permute-start.3 = (bf16[8,72,128]{2,1,0:T(8,128)(2,1)S(1)}, bf16[8,72,128]{2,1,0:T(8,128)(2,1)S(1)}, u32[]{:S(2)}, u32[]{:S(2)}) collective-permute-start(bf16[8,72,128]{2,1,0:T(8,128)(2,1)S(1)} %get-tuple-element.51), channel_id=1, source_target_pairs={{0,4},{4,0},{8,12},{12,8},{1,5},{5,1},{9,13},{13,9},{2,6},{6,2},{1... | collective-permute-start | bytes 442376 | tf_op jit(solution)/shard_map/ppermute | solution.py:617
  27.2 0.0 copy-done.5
  27.2 0.4 shard_map.148
  27.6 0.0 collective-permute-done.2.tgt_ref
  27.6 0.0 copy-done.3
  27.7 0.0 copy-start.2
  27.7 2.3 %shard_map.147 = (s32[5,32]{1,0:T(8,128)S(1)}, bf16[12,256,128]{2,1,0:T(8,128)(2,1)S(1)}) custom-call(s32[4,4,32]{2,1,0:T(4,128)S(1)} %bitcast.52, bf16[12,64,256]{2,1,0:T(8,128)(2,1)S(1)} %bitcast.49, bf16[11,64,256]{2,1,0:T(8,128)(2,1)S(1)} %get-tuple-element.46.top_ref, bf16[1,64,256]{2,1,0:T(8,128)(2,1)S(1)} %get-tuple-element.48.last_ref), custom_call_target="tpu_custom_call" | custom-call | flops 10000000000 | bytes 1 | tf_op jit(solution)/shard_map/pallas_call | solution.py:659
  30.0 2.3 %shard_map.149 = (bf16[8,72,128]{2,1,0:T(8,128)(2,1)S(1)}, bf16[8,72,128]{2,1,0:T(8,128)(2,1)S(1)}, bf16[8,72,128]{2,1,0:T(8,128)(2,1)S(1)}, bf16[8,72,128]{2,1,0:T(8,128)(2,1)S(1)}) custom-call(s32[4,4,32]{2,1,0:T(4,128)S(1)} %bitcast.53, bf16[64,64,144]{2,1,0:T(8,128)(2,1)S(1)} %bitcast.47), custom_call_target="tpu_custom_call" | custom-call | flops 1000000000 | bytes 1 | tf_op jit(solution)/shard_map/pallas_call | solution.py:31
  32.3 0.1 collective-permute-start.6
  32.4 4.1 %collective-permute-done.9.mean_ref = bf16[11,64,256]{2,1,0:T(8,128)(2,1)S(1)} collective-permute-done((bf16[11,64,256]{2,1,0:T(8,128)(2,1)S(1)}, bf16[11,64,256]{2,1,0:T(8,128)(2,1)S(1)}, u32[]{:S(2)}, u32[]{:S(2)}) %collective-permute-start.9) | collective-permute-done | bytes 360480 | tf_op jit(solution)/shard_map/ppermute | solution.py:642
  36.5 1.2 %collective-permute-start.7 = (bf16[8,72,128]{2,1,0:T(8,128)(2,1)S(1)}, bf16[8,72,128]{2,1,0:T(8,128)(2,1)S(1)}, u32[]{:S(2)}, u32[]{:S(2)}) collective-permute-start(bf16[8,72,128]{2,1,0:T(8,128)(2,1)S(1)} %get-tuple-element.63), channel_id=1, source_target_pairs={{0,8},{4,12},{8,0},{12,4},{1,9},{5,13},{9,1},{13,5},{2,10},{6,14},... | collective-permute-start | bytes 442376 | tf_op jit(solution)/shard_map/ppermute | solution.py:617
  37.7 2.1 %shard_map.150 = (bf16[2,72,16,128]{3,2,1,0:T(8,128)(2,1)S(1)}, bf16[2,72,16,128]{3,2,1,0:T(8,128)(2,1)S(1)}) custom-call(s32[5,32]{1,0:T(8,128)S(1)} %get-tuple-element.49.table_ref.refs_0_, bf16[12,256,128]{2,1,0:T(8,128)(2,1)S(1)} %get-tuple-element.58.own, bf16[11,64,256]{2,1,0:T(8,128)(2,1)S(1)} %collective-permute-done.9.mean_ref, ...), custom_call_target="tpu_custom_call" | custom-call | flops 10000000000 | bytes 1 | tf_op jit(solution)/shard_map/pallas_call | solution.py:31
  39.8 0.0 collective-permute-done.4.refs_3_
  39.8 3.4 %collective-permute-start.8 = (bf16[8,72,128]{2,1,0:T(8,128)(2,1)S(1)}, bf16[8,72,128]{2,1,0:T(8,128)(2,1)S(1)}, u32[]{:S(2)}, u32[]{:S(2)}) collective-permute-start(bf16[8,72,128]{2,1,0:T(8,128)(2,1)S(1)} %get-tuple-element.64), channel_id=1, source_target_pairs={{0,12},{4,8},{8,4},{12,0},{1,13},{5,9},{9,5},{13,1},{2,14},{6,10},... | collective-permute-start | bytes 442376 | tf_op jit(solution)/shard_map/ppermute | solution.py:617
  43.3 0.0 collective-permute-done.5.refs_4_
  43.3 0.0 collective-permute-done.3.refs_2_
  43.3 6.8 %shard_map.151.refs_17_ = f32[2432,128]{1,0:T(8,128)S(1)} custom-call(s32[5,32]{1,0:T(8,128)S(1)} %get-tuple-element.49.table_ref.refs_0_, bf16[8,72,128]{2,1,0:T(8,128)(2,1)S(1)} %get-tuple-element.42.refs_1_, bf16[8,72,128]{2,1,0:T(8,128)(2,1)S(1)} %collective-permute-done.3.refs_2_, bf16[8,72,128]{2,1,0:T(8,128)(2,1)S(1)} %collective-permute-done.4.refs_3_, ...), custom_call_target="tpu_custom_call" | custom-call | flops 10000000000 | bytes 1 | tf_op jit(solution)/shard_map/pallas_call | solution.py:31
  50.1 0.0 collective-permute-done.6.refs_6_
  50.1 0.0 collective-permute-done.7.refs_7_
  50.1 0.0 collective-permute-done.8.refs_8_
  50.1 7.1 %shard_map.152 = (f32[1216,128]{1,0:T(8,128)S(1)}, bf16[1216,128]{1,0:T(8,128)(2,1)S(1)}) custom-call(s32[5,32]{1,0:T(8,128)S(1)} %get-tuple-element.49.table_ref.refs_0_, bf16[8,72,128]{2,1,0:T(8,128)(2,1)S(1)} %get-tuple-element.42.refs_1_, bf16[8,72,128]{2,1,0:T(8,128)(2,1)S(1)} %collective-permute-done.3.refs_2_, ...), custom_call_target="tpu_custom_call" | custom-call | flops 10000000000 | bytes 1 | tf_op jit(solution)/shard_map/pallas_call | solution.py:31
  57.2 0.1 collective-permute-start.10
  57.3 1.6 %collective-permute-done.10 = bf16[1216,128]{1,0:T(8,128)(2,1)S(1)} collective-permute-done((bf16[1216,128]{1,0:T(8,128)(2,1)S(1)}, bf16[1216,128]{1,0:T(8,128)(2,1)S(1)}, u32[]{:S(2)}, u32[]{:S(2)}) %collective-permute-start.10) | collective-permute-done | bytes 311328 | tf_op jit(solution)/shard_map/ppermute | solution.py:735
  58.9 0.1 convert_add_fusion
  59.0 1.6 %collective-permute-start.13 = (bf16[304,128]{1,0:T(8,128)(2,1)S(1)}, bf16[304,128]{1,0:T(8,128)(2,1)S(1)}, u32[]{:S(2)}, u32[]{:S(2)}) collective-permute-start(bf16[304,128]{1,0:T(8,128)(2,1)S(1)} %get-tuple-element.81), channel_id=1, source_target_pairs={{0,1},{1,0},{2,3},{3,2},{4,5},{5,4},{6,7},{7,6},{8,9},{9,8},{10,11... | collective-permute-start | bytes 233480 | tf_op jit(solution)/shard_map/ppermute | solution.py:541
  60.5 1.5 %collective-permute-start.12 = (bf16[304,128]{1,0:T(8,128)(2,1)S(1)}, bf16[304,128]{1,0:T(8,128)(2,1)S(1)}, u32[]{:S(2)}, u32[]{:S(2)}) collective-permute-start(bf16[304,128]{1,0:T(8,128)(2,1)S(1)} %get-tuple-element.82), channel_id=1, source_target_pairs={{0,2},{1,3},{2,0},{3,1},{4,6},{5,7},{6,4},{7,5},{8,10},{9,11},{10,... | collective-permute-start | bytes 233480 | tf_op jit(solution)/shard_map/ppermute | solution.py:541
  62.1 0.5 collective-permute-start.11
  62.5 0.9 %collective-permute-done.13 = bf16[304,128]{1,0:T(8,128)(2,1)S(1)} collective-permute-done((bf16[304,128]{1,0:T(8,128)(2,1)S(1)}, bf16[304,128]{1,0:T(8,128)(2,1)S(1)}, u32[]{:S(2)}, u32[]{:S(2)}) %collective-permute-start.13) | collective-permute-done | bytes 77856 | tf_op jit(solution)/shard_map/ppermute | solution.py:541
  63.4 1.5 %collective-permute-done.12 = bf16[304,128]{1,0:T(8,128)(2,1)S(1)} collective-permute-done((bf16[304,128]{1,0:T(8,128)(2,1)S(1)}, bf16[304,128]{1,0:T(8,128)(2,1)S(1)}, u32[]{:S(2)}, u32[]{:S(2)}) %collective-permute-start.12) | collective-permute-done | bytes 77856 | tf_op jit(solution)/shard_map/ppermute | solution.py:541
  64.9 2.4 %collective-permute-done.11 = bf16[304,128]{1,0:T(8,128)(2,1)S(1)} collective-permute-done((bf16[304,128]{1,0:T(8,128)(2,1)S(1)}, bf16[304,128]{1,0:T(8,128)(2,1)S(1)}, u32[]{:S(2)}, u32[]{:S(2)}) %collective-permute-start.11) | collective-permute-done | bytes 77856 | tf_op jit(solution)/shard_map/ppermute | solution.py:541
  67.4 0.5 collective-permute-start.16
  67.9 2.8 %collective-permute-start.15 = (bf16[304,128]{1,0:T(8,128)(2,1)S(1)}, bf16[304,128]{1,0:T(8,128)(2,1)S(1)}, u32[]{:S(2)}, u32[]{:S(2)}) collective-permute-start(bf16[304,128]{1,0:T(8,128)(2,1)S(1)} %fusion.3), channel_id=1, source_target_pairs={{0,8},{4,12},{8,0},{12,4},{1,9},{5,13},{9,1},{13,5},{2,10},{6,14},... | collective-permute-start | bytes 233480 | tf_op jit(solution)/shard_map/ppermute | solution.py:568
  70.7 1.1 %collective-permute-start.14 = (bf16[304,128]{1,0:T(8,128)(2,1)S(1)}, bf16[304,128]{1,0:T(8,128)(2,1)S(1)}, u32[]{:S(2)}, u32[]{:S(2)}) collective-permute-start(bf16[304,128]{1,0:T(8,128)(2,1)S(1)} %fusion.3), channel_id=1, source_target_pairs={{0,4},{4,0},{8,12},{12,8},{1,5},{5,1},{9,13},{13,9},{2,6},{6,2},{1... | collective-permute-start | bytes 233480 | tf_op jit(solution)/shard_map/ppermute | solution.py:568
  71.9 2.0 %collective-permute-done.16 = bf16[304,128]{1,0:T(8,128)(2,1)S(1)} collective-permute-done((bf16[304,128]{1,0:T(8,128)(2,1)S(1)}, bf16[304,128]{1,0:T(8,128)(2,1)S(1)}, u32[]{:S(2)}, u32[]{:S(2)}) %collective-permute-start.16) | collective-permute-done | bytes 77856 | tf_op jit(solution)/shard_map/ppermute | solution.py:568
  73.9 2.5 %collective-permute-done.15 = bf16[304,128]{1,0:T(8,128)(2,1)S(1)} collective-permute-done((bf16[304,128]{1,0:T(8,128)(2,1)S(1)}, bf16[304,128]{1,0:T(8,128)(2,1)S(1)}, u32[]{:S(2)}, u32[]{:S(2)}) %collective-permute-start.15) | collective-permute-done | bytes 77856 | tf_op jit(solution)/shard_map/ppermute | solution.py:568
  76.4 0.0 collective-permute-done.14
  76.5 0.8 collective-permute-start.17
  77.3 1.5 %collective-permute-start.18 = (bf16[304,128]{1,0:T(8,128)(2,1)S(1)}, bf16[304,128]{1,0:T(8,128)(2,1)S(1)}, u32[]{:S(2)}, u32[]{:S(2)}) collective-permute-start(bf16[304,128]{1,0:T(8,128)(2,1)S(1)} %reduce-precision_convert_fusion), channel_id=1, source_target_pairs={{0,2},{1,3},{2,0},{3,1},{4,6},{5,7},{6,4},{7,5},{8,10},{9,11},{10,... | collective-permute-start | bytes 233480 | tf_op jit(solution)/shard_map/ppermute | solution.py:551
  78.8 1.3 %collective-permute-start.19 = (bf16[304,128]{1,0:T(8,128)(2,1)S(1)}, bf16[304,128]{1,0:T(8,128)(2,1)S(1)}, u32[]{:S(2)}, u32[]{:S(2)}) collective-permute-start(bf16[304,128]{1,0:T(8,128)(2,1)S(1)} %reduce-precision_convert_fusion), channel_id=1, source_target_pairs={{0,1},{1,0},{2,3},{3,2},{4,5},{5,4},{6,7},{7,6},{8,9},{9,8},{10,11... | collective-permute-start | bytes 233480 | tf_op jit(solution)/shard_map/ppermute | solution.py:551
  80.0 1.9 %collective-permute-done.17 = bf16[304,128]{1,0:T(8,128)(2,1)S(1)} collective-permute-done((bf16[304,128]{1,0:T(8,128)(2,1)S(1)}, bf16[304,128]{1,0:T(8,128)(2,1)S(1)}, u32[]{:S(2)}, u32[]{:S(2)}) %collective-permute-start.17) | collective-permute-done | bytes 77856 | tf_op jit(solution)/shard_map/ppermute | solution.py:551
  81.9 0.6 collective-permute-done.18
  82.5 0.6 collective-permute-done.19
  83.2 0.1 select_bitcast_fusion.3
  83.3 0.1 collective-permute-start.20
  83.4 1.6 %collective-permute-done.20.other_ref = bf16[1216,128]{1,0:T(8,128)(2,1)S(1)} collective-permute-done((bf16[1216,128]{1,0:T(8,128)(2,1)S(1)}, bf16[1216,128]{1,0:T(8,128)(2,1)S(1)}, u32[]{:S(2)}, u32[]{:S(2)}) %collective-permute-start.20) | collective-permute-done | bytes 311328 | tf_op jit(solution)/shard_map/ppermute | solution.py:747
  85.0 1.1 %shard_map.153 = (f32[128,1152]{1,0:T(8,128)}, f32[128,1152]{1,0:T(8,128)}, f32[64,128]{1,0:T(8,128)}, f32[32,128]{1,0:T(8,128)}, f32[1,1]{1,0:T(1,128)}) custom-call(bf16[1216,128]{1,0:T(8,128)(2,1)S(1)} %bitcast.43, bf16[1216,128]{1,0:T(8,128)(2,1)S(1)} %collective-permute-done.20.other_ref), custom_call_target="tpu_custom_call" | custom-call | bytes 1 | tf_op jit(solution)/shard_map/pallas_call | solution.py:31
  (21 shorter events, 0.2 us)
Async XLA Ops:
  0.6 18.4 %copy-start = (bf16[1,100,12,256]{3,1,2,0:T(8,128)(2,1)S(1)}, bf16[1,100,12,256]{3,1,2,0:T(8,128)(2,1)}, u32[]{:S(2)}) copy-start(bf16[1,100,12,256]{3,1,2,0:T(8,128)(2,1)} %param.10) | copy-start | bytes 1843204
  0.6 27.0 %collective-permute-start.2 = (bf16[12,64,256]{2,1,0:T(8,128)(2,1)}, bf16[12,64,256]{2,1,0:T(8,128)(2,1)S(1)}, u32[]{:S(2)}, u32[]{:S(2)}) collective-permute-start(bf16[12,64,256]{2,1,0:T(8,128)(2,1)} %bitcast.48), channel_id=1, source_target_pairs={{4,0},{8,4},{12,8},{5,1},{9,5},{13,9},{6,2},{10,6},{14,10},{7,3},{... | collective-permute-start | bytes 1179656 | tf_op jit(solution)/shard_map/ppermute | solution.py:631
  2.9 16.1 %collective-permute-start = (bf16[1,100,256]{2,1,0:T(8,128)(2,1)S(1)}, bf16[1,100,256]{2,1,0:T(8,128)(2,1)S(1)}, u32[]{:S(2)}, u32[]{:S(2)}) collective-permute-start(bf16[1,100,256]{2,1,0:T(8,128)(2,1)S(1)} %get-tuple-element.79), channel_id=1, source_target_pairs={{0,4},{4,0},{8,12},{12,8},{1,5},{5,1},{9,13},{13,9},{2,6},{6,2},{1... | collective-permute-start | bytes 153608 | tf_op jit(solution)/shard_map/ppermute | solution.py:629
  6.7 12.4 %collective-permute-start.1 = (bf16[1,100,256]{2,1,0:T(8,128)(2,1)S(1)}, bf16[1,100,256]{2,1,0:T(8,128)(2,1)S(1)}, u32[]{:S(2)}, u32[]{:S(2)}) collective-permute-start(bf16[1,100,256]{2,1,0:T(8,128)(2,1)S(1)} %get-tuple-element.78), channel_id=1, source_target_pairs={{4,8},{8,4},{5,9},{9,5},{6,10},{10,6},{7,11},{11,7},{20,24},{24,20... | collective-permute-start | bytes 153608 | tf_op jit(solution)/shard_map/ppermute | solution.py:630
  7.3 1.6 %copy-start.1 = (bf16[1,1,64,64,144]{4,3,2,1,0:T(8,128)(2,1)S(1)}, bf16[1,1,64,64,144]{4,3,2,1,0:T(8,128)(2,1)}, u32[]{:S(2)}) copy-start(bf16[1,1,64,64,144]{4,3,2,1,0:T(8,128)(2,1)} %param.12) | copy-start | bytes 3538948
  8.9 0.7 copy-start.10
  9.6 9.4 %copy-start.6 = (bf16[128,900]{0,1:T(8,128)(2,1)S(1)}, bf16[128,900]{0,1:T(8,128)(2,1)}, u32[]{:S(2)}) copy-start(bf16[128,900]{0,1:T(8,128)(2,1)} %param.14) | copy-start | bytes 691204
  9.6 9.4 %copy-start.7 = (bf16[64,128]{1,0:T(8,128)(2,1)S(1)}, bf16[64,128]{1,0:T(8,128)(2,1)}, u32[]{:S(2)}) copy-start(bf16[64,128]{1,0:T(8,128)(2,1)} %proj_ref.1) | copy-start | bytes 49156
  11.7 15.5 %copy-start.4 = (bf16[128,1152]{1,0:T(8,128)(2,1)S(1)}, bf16[128,1152]{1,0:T(8,128)(2,1)}, u32[]{:S(2)}) copy-start(bf16[128,1152]{1,0:T(8,128)(2,1)} %one_ref) | copy-start | bytes 884740
  11.7 15.5 %copy-start.5 = (bf16[128,1152]{1,0:T(8,128)(2,1)S(1)}, bf16[128,1152]{1,0:T(8,128)(2,1)}, u32[]{:S(2)}) copy-start(bf16[128,1152]{1,0:T(8,128)(2,1)} %two_ref) | copy-start | bytes 884740
  11.7 15.5 %copy-start.8 = (bf16[64,128]{1,0:T(8,128)(2,1)S(1)}, bf16[64,128]{1,0:T(8,128)(2,1)}, u32[]{:S(2)}) copy-start(bf16[64,128]{1,0:T(8,128)(2,1)} %proj_ref.2) | copy-start | bytes 49156
  11.7 28.1 %collective-permute-start.4 = (bf16[8,72,128]{2,1,0:T(8,128)(2,1)S(1)}, bf16[8,72,128]{2,1,0:T(8,128)(2,1)S(1)}, u32[]{:S(2)}, u32[]{:S(2)}) collective-permute-start(bf16[8,72,128]{2,1,0:T(8,128)(2,1)S(1)} %get-tuple-element.52), channel_id=1, source_target_pairs={{0,8},{4,12},{8,0},{12,4},{1,9},{5,13},{9,1},{13,5},{2,10},{6,14},... | collective-permute-start | bytes 442376 | tf_op jit(solution)/shard_map/ppermute | solution.py:617
  16.1 27.2 %collective-permute-start.5 = (bf16[8,72,128]{2,1,0:T(8,128)(2,1)S(1)}, bf16[8,72,128]{2,1,0:T(8,128)(2,1)S(1)}, u32[]{:S(2)}, u32[]{:S(2)}) collective-permute-start(bf16[8,72,128]{2,1,0:T(8,128)(2,1)S(1)} %get-tuple-element.53), channel_id=1, source_target_pairs={{0,12},{4,8},{8,4},{12,0},{1,13},{5,9},{9,5},{13,1},{2,14},{6,10},... | collective-permute-start | bytes 442376 | tf_op jit(solution)/shard_map/ppermute | solution.py:617
  23.1 4.6 %copy-start.3 = (bf16[1,64,12,256]{3,1,2,0:T(8,128)(2,1)S(1)}, bf16[1,64,12,256]{3,1,2,0:T(8,128)(2,1)}, u32[]{:S(2)}) copy-start(bf16[1,64,12,256]{3,1,2,0:T(8,128)(2,1)} %param.11) | copy-start | bytes 1179652
  23.1 4.6 %copy-start.11 = (s32[1,4,32,4]{2,3,1,0:T(4,128)S(1)}, s32[1,4,32,4]{2,3,1,0:T(4,128)}, u32[]{:S(2)}) copy-start(s32[1,4,32,4]{2,3,1,0:T(4,128)} %param.13) | copy-start | bytes 6148
  23.1 13.4 %collective-permute-start.9 = (bf16[11,64,256]{2,1,0:T(8,128)(2,1)S(1)}, bf16[11,64,256]{2,1,0:T(8,128)(2,1)S(1)}, u32[]{:S(2)}, u32[]{:S(2)}) collective-permute-start(bf16[11,64,256]{2,1,0:T(8,128)(2,1)S(1)} %get-tuple-element.46.top_ref), channel_id=1, source_target_pairs={{4,0},{8,4},{12,8},{5,1},{9,5},{13,9},{6,2},{10,6},{14,10},{7,3},{... | collective-permute-start | bytes 1081352 | tf_op jit(solution)/shard_map/ppermute | solution.py:642
  24.5 18.8 %collective-permute-start.3 = (bf16[8,72,128]{2,1,0:T(8,128)(2,1)S(1)}, bf16[8,72,128]{2,1,0:T(8,128)(2,1)S(1)}, u32[]{:S(2)}, u32[]{:S(2)}) collective-permute-start(bf16[8,72,128]{2,1,0:T(8,128)(2,1)S(1)} %get-tuple-element.51), channel_id=1, source_target_pairs={{0,4},{4,0},{8,12},{12,8},{1,5},{5,1},{9,13},{13,9},{2,6},{6,2},{1... | collective-permute-start | bytes 442376 | tf_op jit(solution)/shard_map/ppermute | solution.py:617
  27.7 2.3 %copy-start.2 = (bf16[1,1,64,64,144]{4,3,2,1,0:T(8,128)(2,1)S(1)}, bf16[1,1,64,64,144]{4,3,2,1,0:T(8,128)(2,1)}, u32[]{:S(2)}) copy-start(bf16[1,1,64,64,144]{4,3,2,1,0:T(8,128)(2,1)} %param.12) | copy-start | bytes 3538948
  32.3 17.8 %collective-permute-start.6 = (bf16[8,72,128]{2,1,0:T(8,128)(2,1)S(1)}, bf16[8,72,128]{2,1,0:T(8,128)(2,1)S(1)}, u32[]{:S(2)}, u32[]{:S(2)}) collective-permute-start(bf16[8,72,128]{2,1,0:T(8,128)(2,1)S(1)} %get-tuple-element.62), channel_id=1, source_target_pairs={{0,4},{4,0},{8,12},{12,8},{1,5},{5,1},{9,13},{13,9},{2,6},{6,2},{1... | collective-permute-start | bytes 442376 | tf_op jit(solution)/shard_map/ppermute | solution.py:617
  36.5 13.6 %collective-permute-start.7 = (bf16[8,72,128]{2,1,0:T(8,128)(2,1)S(1)}, bf16[8,72,128]{2,1,0:T(8,128)(2,1)S(1)}, u32[]{:S(2)}, u32[]{:S(2)}) collective-permute-start(bf16[8,72,128]{2,1,0:T(8,128)(2,1)S(1)} %get-tuple-element.63), channel_id=1, source_target_pairs={{0,8},{4,12},{8,0},{12,4},{1,9},{5,13},{9,1},{13,5},{2,10},{6,14},... | collective-permute-start | bytes 442376 | tf_op jit(solution)/shard_map/ppermute | solution.py:617
  37.7 5.6 %copy-start.9 = (f32[32,128]{1,0:T(8,128)S(1)}, f32[32,128]{1,0:T(8,128)}, u32[]{:S(2)}) copy-start(f32[32,128]{1,0:T(8,128)} %refs_11_.1) | copy-start | bytes 49156
  39.8 10.2 %collective-permute-start.8 = (bf16[8,72,128]{2,1,0:T(8,128)(2,1)S(1)}, bf16[8,72,128]{2,1,0:T(8,128)(2,1)S(1)}, u32[]{:S(2)}, u32[]{:S(2)}) collective-permute-start(bf16[8,72,128]{2,1,0:T(8,128)(2,1)S(1)} %get-tuple-element.64), channel_id=1, source_target_pairs={{0,12},{4,8},{8,4},{12,0},{1,13},{5,9},{9,5},{13,1},{2,14},{6,10},... | collective-permute-start | bytes 442376 | tf_op jit(solution)/shard_map/ppermute | solution.py:617
  57.2 1.7 %collective-permute-start.10 = (bf16[1216,128]{1,0:T(8,128)(2,1)S(1)}, bf16[1216,128]{1,0:T(8,128)(2,1)S(1)}, u32[]{:S(2)}, u32[]{:S(2)}) collective-permute-start(bf16[1216,128]{1,0:T(8,128)(2,1)S(1)} %get-tuple-element.72), channel_id=1, source_target_pairs={{0,16},{16,0},{1,17},{17,1},{2,18},{18,2},{3,19},{19,3},{4,20},{20... | collective-permute-start | bytes 933896 | tf_op jit(solution)/shard_map/ppermute | solution.py:735
  59.0 4.5 %collective-permute-start.13 = (bf16[304,128]{1,0:T(8,128)(2,1)S(1)}, bf16[304,128]{1,0:T(8,128)(2,1)S(1)}, u32[]{:S(2)}, u32[]{:S(2)}) collective-permute-start(bf16[304,128]{1,0:T(8,128)(2,1)S(1)} %get-tuple-element.81), channel_id=1, source_target_pairs={{0,1},{1,0},{2,3},{3,2},{4,5},{5,4},{6,7},{7,6},{8,9},{9,8},{10,11... | collective-permute-start | bytes 233480 | tf_op jit(solution)/shard_map/ppermute | solution.py:541
  60.5 4.4 %collective-permute-start.12 = (bf16[304,128]{1,0:T(8,128)(2,1)S(1)}, bf16[304,128]{1,0:T(8,128)(2,1)S(1)}, u32[]{:S(2)}, u32[]{:S(2)}) collective-permute-start(bf16[304,128]{1,0:T(8,128)(2,1)S(1)} %get-tuple-element.82), channel_id=1, source_target_pairs={{0,2},{1,3},{2,0},{3,1},{4,6},{5,7},{6,4},{7,5},{8,10},{9,11},{10,... | collective-permute-start | bytes 233480 | tf_op jit(solution)/shard_map/ppermute | solution.py:541
  62.1 5.3 %collective-permute-start.11 = (bf16[304,128]{1,0:T(8,128)(2,1)S(1)}, bf16[304,128]{1,0:T(8,128)(2,1)S(1)}, u32[]{:S(2)}, u32[]{:S(2)}) collective-permute-start(bf16[304,128]{1,0:T(8,128)(2,1)S(1)} %get-tuple-element.80), channel_id=1, source_target_pairs={{0,3},{1,2},{2,1},{3,0},{4,7},{5,6},{6,5},{7,4},{8,11},{9,10},{10,... | collective-permute-start | bytes 233480 | tf_op jit(solution)/shard_map/ppermute | solution.py:541
  67.4 6.5 %collective-permute-start.16 = (bf16[304,128]{1,0:T(8,128)(2,1)S(1)}, bf16[304,128]{1,0:T(8,128)(2,1)S(1)}, u32[]{:S(2)}, u32[]{:S(2)}) collective-permute-start(bf16[304,128]{1,0:T(8,128)(2,1)S(1)} %fusion.3), channel_id=1, source_target_pairs={{0,12},{4,8},{8,4},{12,0},{1,13},{5,9},{9,5},{13,1},{2,14},{6,10},... | collective-permute-start | bytes 233480 | tf_op jit(solution)/shard_map/ppermute | solution.py:568
  67.9 8.4 %collective-permute-start.15 = (bf16[304,128]{1,0:T(8,128)(2,1)S(1)}, bf16[304,128]{1,0:T(8,128)(2,1)S(1)}, u32[]{:S(2)}, u32[]{:S(2)}) collective-permute-start(bf16[304,128]{1,0:T(8,128)(2,1)S(1)} %fusion.3), channel_id=1, source_target_pairs={{0,8},{4,12},{8,0},{12,4},{1,9},{5,13},{9,1},{13,5},{2,10},{6,14},... | collective-permute-start | bytes 233480 | tf_op jit(solution)/shard_map/ppermute | solution.py:568
  70.7 5.7 %collective-permute-start.14 = (bf16[304,128]{1,0:T(8,128)(2,1)S(1)}, bf16[304,128]{1,0:T(8,128)(2,1)S(1)}, u32[]{:S(2)}, u32[]{:S(2)}) collective-permute-start(bf16[304,128]{1,0:T(8,128)(2,1)S(1)} %fusion.3), channel_id=1, source_target_pairs={{0,4},{4,0},{8,12},{12,8},{1,5},{5,1},{9,13},{13,9},{2,6},{6,2},{1... | collective-permute-start | bytes 233480 | tf_op jit(solution)/shard_map/ppermute | solution.py:568
  76.5 5.5 %collective-permute-start.17 = (bf16[304,128]{1,0:T(8,128)(2,1)S(1)}, bf16[304,128]{1,0:T(8,128)(2,1)S(1)}, u32[]{:S(2)}, u32[]{:S(2)}) collective-permute-start(bf16[304,128]{1,0:T(8,128)(2,1)S(1)} %reduce-precision_convert_fusion), channel_id=1, source_target_pairs={{0,3},{1,2},{2,1},{3,0},{4,7},{5,6},{6,5},{7,4},{8,11},{9,10},{10,... | collective-permute-start | bytes 233480 | tf_op jit(solution)/shard_map/ppermute | solution.py:551
  77.3 5.2 %collective-permute-start.18 = (bf16[304,128]{1,0:T(8,128)(2,1)S(1)}, bf16[304,128]{1,0:T(8,128)(2,1)S(1)}, u32[]{:S(2)}, u32[]{:S(2)}) collective-permute-start(bf16[304,128]{1,0:T(8,128)(2,1)S(1)} %reduce-precision_convert_fusion), channel_id=1, source_target_pairs={{0,2},{1,3},{2,0},{3,1},{4,6},{5,7},{6,4},{7,5},{8,10},{9,11},{10,... | collective-permute-start | bytes 233480 | tf_op jit(solution)/shard_map/ppermute | solution.py:551
  78.8 4.4 %collective-permute-start.19 = (bf16[304,128]{1,0:T(8,128)(2,1)S(1)}, bf16[304,128]{1,0:T(8,128)(2,1)S(1)}, u32[]{:S(2)}, u32[]{:S(2)}) collective-permute-start(bf16[304,128]{1,0:T(8,128)(2,1)S(1)} %reduce-precision_convert_fusion), channel_id=1, source_target_pairs={{0,1},{1,0},{2,3},{3,2},{4,5},{5,4},{6,7},{7,6},{8,9},{9,8},{10,11... | collective-permute-start | bytes 233480 | tf_op jit(solution)/shard_map/ppermute | solution.py:551
  83.3 1.7 %collective-permute-start.20 = (bf16[1216,128]{1,0:T(8,128)(2,1)S(1)}, bf16[1216,128]{1,0:T(8,128)(2,1)S(1)}, u32[]{:S(2)}, u32[]{:S(2)}) collective-permute-start(bf16[1216,128]{1,0:T(8,128)(2,1)S(1)} %bitcast.42), channel_id=1, source_target_pairs={{0,16},{16,0},{1,17},{17,1},{2,18},{18,2},{3,19},{19,3},{4,20},{20... | collective-permute-start | bytes 933896 | tf_op jit(solution)/shard_map/ppermute | solution.py:747

commit v7 on v6

--- a/solution.py
+++ b/solution.py
@@ -203,14 +203,15 @@
     chunks, _, count, _ = mp_ref.shape
     pairs = rows // 2
     eye = identity(width)
-    image[0:rows] = own[...].astype(F32)
+    image[0:rows, 0:width] = own[...].astype(F32)
     for r in range(0, rows - 1, 2):
         many = min(2, rows - 1 - r)
         both = paint(eye, sum([[mean_ref[r + i], tgt_ref[r + i]] for i in range(many)], []))
         for i in range(many):
-            image[rows + r + i] = both[:, i * wide : (i + 1) * wide]
+            image[rows + r + i, 0:width] = both[:, i * wide : (i + 1) * wide]
     half = wide // 2
-    low = lax.broadcasted_iota(jnp.int32, evens.shape, 1) < half
+    total = rows * pairs * count
+    low = lax.broadcasted_iota(jnp.int32, (total, wide), 1) < half
     for chunk in range(chunks):
 
         def patch(k, carry, chunk=chunk):
@@ -223,7 +224,7 @@
             return carry
 
         lax.fori_loop(0, count, patch, 0, unroll=min(UNROLL, count))
-        even, odd = evens[...], odds[...]
+        even, odd = evens[0:total, :], odds[0:total, :]
         mean = jnp.where(low, even, pltpu.roll(odd, half, 1))
         goal = jnp.where(low, pltpu.roll(even, half, 1), odd)
         mp_ref[chunk] = mean.astype(BF).reshape(mp_ref.shape[1:])
@@ -262,7 +263,8 @@
     root = jnp.sqrt(u)
     scales = [1.0 / root, sig, 1.0 / u, sig / root, 2.0 * weight / values * (sig / root), weight / values]
     for i, scale in enumerate(scales):
-        by_level[i] = scale
+        by_level[i, 0:levels] = scale
+    by_level[len(scales), 0:levels] = embed_ref[...]
     group = GROUP
     half = wide // 2
 
@@ -279,12 +281,12 @@
         piece = stage[entry(SOURCE, k)]
         nz[pl.ds(k, cells, stride=count), :] = piece.astype(F32)
         step = entry(STEP, k)
-        emb[pl.ds(k, 1), :] = embed_ref[pl.ds(step, 1), :]
+        emb[pl.ds(k, 1), :] = by_level[len(scales), pl.ds(step, 1), :]
         for i in range(len(scales)):
             fac[i, pl.ds(k, 1), :] = by_level[i, pl.ds(step, 1), :]
 
     def spread(index):
-        return fac[index][None]
+        return fac[index, 0:count][None]
 
     scale_in, sigma, skip, scale_out, grad_scale = (spread(i) for i in range(5))
     lane = lax.broadcasted_iota(jnp.int32, (1, 1, count, wide), 3)
@@ -292,7 +294,7 @@
     mean_bf = mp_ref[chunk]
     mean = mean_bf.astype(F32)
     residual = tp_ref[chunk].astype(F32) - mean
-    noised = residual + sigma * nz[...].reshape(cells, count, wide)
+    noised = residual + sigma * nz[0:total, :].reshape(cells, count, wide)
     res[...] = residual.reshape(total, wide)
     noisy[...] = noised.reshape(total, wide)
     xn[1 : rows + 1, 1 : pairs + 1] = (scale_in * noised).astype(BF).reshape(rows, pairs, count, wide)
@@ -315,7 +317,7 @@
         return value.reshape(many, pairs, count, value.shape[-1])
 
     tile = group * pairs * count
-    emb_pair = jnp.concatenate([emb[...], emb[...]], axis=1)[None]
+    emb_pair = jnp.concatenate([emb[0:count, :], emb[0:count, :]], axis=1)[None]
     def span_of(g):
         return pl.ds(g * tile, tile)
 
@@ -403,7 +405,7 @@
         emit(base + depth, depth, h0[:, 0:wide] + h1[:, wide : 2 * wide])
         emit(base + 2 * depth, depth, h0[:, wide : 2 * wide] + h1[:, 3 * wide : 4 * wide])
 
-    emb[...] = sums[:, :wide] + sums[:, wide:]
+    emb[0:count, :] = sums[:, :wide] + sums[:, wide:]
     table = 18 * depth + half
     if before is not None:
         out_ref[table : table + levels, :] = before[table : table + levels, :]
@@ -415,7 +417,7 @@
 
     levels_end = table + levels
     spots = lax.broadcasted_iota(jnp.int32, (8, wide), 0) * wide + lax.broadcasted_iota(jnp.int32, (8, wide), 1)
-    sums = jnp.sum(fac[5] * loss, axis=1, keepdims=True)
+    sums = jnp.sum(fac[5, 0:count] * loss, axis=1, keepdims=True)
     owned = jnp.zeros((8, wide), F32)
     for k in range(count):
         owned = owned + jnp.where(spots == entry(PLACE, k), sums[k : k + 1], 0.0)
@@ -655,7 +657,7 @@
         cost=COSTS[3],
     )
     patch_shape = jax.ShapeDtypeStruct((phases, cells // 2, count, wide), BF)
-    got = pltpu.VMEM((cells // 2 * count, wide), F32)
+    got = pltpu.VMEM((cells // 2 * count + 8 * count, wide), F32)
     table, image = pl.pallas_call(
         functools.partial(own_kernel, exchange, deep, count),
         out_shape=[
@@ -675,7 +677,7 @@
         [patch_shape, patch_shape],
         (table, image, mean_low, target_low),
         (SM, VM, VM, VM),
-        [pltpu.VMEM((2 * height - 1, width, wide), F32), got, got],
+        [pltpu.VMEM((2 * height - 1, width + 16, wide), F32), got, got],
         limit=16,
         cost=COSTS[4],
     )
@@ -708,7 +710,7 @@
             ([pltpu.VMEM((rows_all, wide), F32)] if last else [])
             + [
                 pltpu.VMEM((slots_here, cells // 2, wide), BF),
-                pltpu.VMEM((total, wide), F32),
+                pltpu.VMEM((total + 8 * count, wide), F32),
                 pad,
                 pad,
                 rim,
@@ -724,9 +726,9 @@
                 pltpu.VMEM((total, 2 * wide), BF),
                 pltpu.VMEM((total, wide), BF),
                 pltpu.VMEM((2 * wide, total), BF),
-                pltpu.VMEM((count, wide), F32),
-                pltpu.VMEM((6, count, wide), F32),
-                pltpu.VMEM((6, levels, wide), F32),
+                pltpu.VMEM((count + 8, wide), F32),
+                pltpu.VMEM((6, count + 8, wide), F32),
+                pltpu.VMEM((7, levels + 8, wide), F32),
             ],
             cost=COSTS[5],
         )

time: 86.4 us -> 86.5 us (level)
  no operation moved by 1% of the time
where the time goes in v7:
time: 86.5 us; the launch traced here: 86.2 us
  starting transfers between devices  33.7 us (39%)
  Pallas kernels  28.2 us (33%)
  waiting for transfers between devices  19.8 us (23%)
  local copies, waits for them, and re-layouts  2.37 us (3%)
  other arithmetic  1.16 us (1%)
  between operations  0.95 us (1%)
    pallas_call x8, Pallas kernels, call(): pl.pallas_call(kernel, out_shape=outs, in_specs=list(specs), out_specs=ja...  26 us
    ppermute x6, starting transfers between devices, sent(): lax.ppermute(packed_pieces[d], 'rows', by_distance('rows', d))  14.8 us
    ppermute x3, waiting for transfers between devices, scatter_sum(): lax.ppermute(take(values, me ^ d).astype(BF), axis, by_distance(axis, d))  4.82 us
    ppermute x3, waiting for transfers between devices, rows_sum(): lax.ppermute(values[0], axis, by_distance(axis, d))  4.52 us
    ppermute x3, starting transfers between devices, rows_sum(): lax.ppermute(values[0], axis, by_distance(axis, d))  4.45 us
    ppermute x1, waiting for transfers between devices, per_device(): mean_low = lax.ppermute(mean_top, 'rows', down)  4.1 us
    ppermute x1, starting transfers between devices, per_device(): inward = lax.ppermute(jnp.where(even, high_edge, low_edge), 'rows', pairs)  3.72 us
    ppermute x3, starting transfers between devices, gather_all(): lax.ppermute(piece, axis, by_distance(axis, d))  3.55 us
  transfers between devices with their start and end apart: 21, of which 11 were waited for; matrix products, arithmetic and copies ran while one was open for 1% of the time, Pallas kernels for 23%

profile of v7, /device:TPU:0, one launch (start us, length us, event | category | flops | bytes accessed | tf_op | source)
XLA Modules:
  0.0 86.2 jit_solution(1401882644252800229)
XLA Ops:
  0.6 1.4 %collective-permute-start.2 = (bf16[12,64,256]{2,1,0:T(8,128)(2,1)}, bf16[12,64,256]{2,1,0:T(8,128)(2,1)S(1)}, u32[]{:S(2)}, u32[]{:S(2)}) collective-permute-start(bf16[12,64,256]{2,1,0:T(8,128)(2,1)} %bitcast.48), channel_id=1, source_target_pairs={{4,0},{8,4},{12,8},{5,1},{9,5},{13,9},{6,2},{10,6},{14,10},{7,3},{... | collective-permute-start | bytes 1179656 | tf_op jit(solution)/shard_map/ppermute | solution.py:633
  2.1 0.8 broadcast_select_fusion
  2.9 3.7 %collective-permute-start = (bf16[1,100,256]{2,1,0:T(8,128)(2,1)S(1)}, bf16[1,100,256]{2,1,0:T(8,128)(2,1)S(1)}, u32[]{:S(2)}, u32[]{:S(2)}) collective-permute-start(bf16[1,100,256]{2,1,0:T(8,128)(2,1)S(1)} %get-tuple-element.79), channel_id=1, source_target_pairs={{0,4},{4,0},{8,12},{12,8},{1,5},{5,1},{9,13},{13,9},{2,6},{6,2},{1... | collective-permute-start | bytes 153608 | tf_op jit(solution)/shard_map/ppermute | solution.py:631
  6.7 0.7 collective-permute-start.1
  7.3 0.0 copy-start.1
  7.3 1.6 %copy-done.1 = bf16[1,1,64,64,144]{4,3,2,1,0:T(8,128)(2,1)S(1)} copy-done((bf16[1,1,64,64,144]{4,3,2,1,0:T(8,128)(2,1)S(1)}, bf16[1,1,64,64,144]{4,3,2,1,0:T(8,128)(2,1)}, u32[]{:S(2)}) %copy-start.1) | copy-done | bytes 1179672
  8.9 0.7 copy-done.10
  9.6 2.1 %shard_map.145 = (bf16[8,72,128]{2,1,0:T(8,128)(2,1)S(1)}, bf16[8,72,128]{2,1,0:T(8,128)(2,1)S(1)}, bf16[8,72,128]{2,1,0:T(8,128)(2,1)S(1)}, bf16[8,72,128]{2,1,0:T(8,128)(2,1)S(1)}) custom-call(s32[4,4,32]{2,1,0:T(4,128)S(1)} %bitcast.51, bf16[64,64,144]{2,1,0:T(8,128)(2,1)S(1)} %bitcast.46), custom_call_target="tpu_custom_call" | custom-call | flops 1000000000 | bytes 1 | tf_op jit(solution)/shard_map/pallas_call | solution.py:31
  11.7 0.0 copy-start.5
  11.7 0.0 copy-start.8
  11.7 4.4 %collective-permute-start.4 = (bf16[8,72,128]{2,1,0:T(8,128)(2,1)S(1)}, bf16[8,72,128]{2,1,0:T(8,128)(2,1)S(1)}, u32[]{:S(2)}, u32[]{:S(2)}) collective-permute-start(bf16[8,72,128]{2,1,0:T(8,128)(2,1)S(1)} %get-tuple-element.52), channel_id=1, source_target_pairs={{0,8},{4,12},{8,0},{12,4},{1,9},{5,13},{9,1},{13,5},{2,10},{6,14},... | collective-permute-start | bytes 442376 | tf_op jit(solution)/shard_map/ppermute | solution.py:619
  16.1 2.9 %collective-permute-start.5 = (bf16[8,72,128]{2,1,0:T(8,128)(2,1)S(1)}, bf16[8,72,128]{2,1,0:T(8,128)(2,1)S(1)}, u32[]{:S(2)}, u32[]{:S(2)}) collective-permute-start(bf16[8,72,128]{2,1,0:T(8,128)(2,1)S(1)} %get-tuple-element.53), channel_id=1, source_target_pairs={{0,12},{4,8},{8,4},{12,0},{1,13},{5,9},{9,5},{13,1},{2,14},{6,10},... | collective-permute-start | bytes 442376 | tf_op jit(solution)/shard_map/ppermute | solution.py:619
  19.0 0.0 collective-permute-done.inward_ref
  19.0 0.0 collective-permute-done.1.outward_ref
  19.0 0.0 copy-done.6
  19.0 0.0 copy-done.7
  19.1 4.0 %shard_map.146 = (bf16[12,64,256]{2,1,0:T(8,128)(2,1)}, bf16[11,64,256]{2,1,0:T(8,128)(2,1)S(1)}, bf16[1,64,256]{2,1,0:T(8,128)(2,1)S(1)}) custom-call(s32[1]{0:T(128)} %bitcast.even_ref, bf16[1,100,256]{2,1,0:T(8,128)(2,1)S(1)} %collective-permute-done.inward_ref, bf16[12,100,256]{2,1,0:T(8,128)(2,1)S(1)} %bitcast.45, ...), custom_call_target="tpu_custom_call" | custom-call | flops 1000000000 | bytes 1 | tf_op jit(solution)/shard_map/pallas_call | solution.py:31
  23.1 1.4 %collective-permute-start.9 = (bf16[11,64,256]{2,1,0:T(8,128)(2,1)S(1)}, bf16[11,64,256]{2,1,0:T(8,128)(2,1)S(1)}, u32[]{:S(2)}, u32[]{:S(2)}) collective-permute-start(bf16[11,64,256]{2,1,0:T(8,128)(2,1)S(1)} %get-tuple-element.46.top_ref), channel_id=1, source_target_pairs={{4,0},{8,4},{12,8},{5,1},{9,5},{13,9},{6,2},{10,6},{14,10},{7,3},{... | collective-permute-start | bytes 1081352 | tf_op jit(solution)/shard_map/ppermute | solution.py:644
  24.5 2.7 %collective-permute-start.3 = (bf16[8,72,128]{2,1,0:T(8,128)(2,1)S(1)}, bf16[8,72,128]{2,1,0:T(8,128)(2,1)S(1)}, u32[]{:S(2)}, u32[]{:S(2)}) collective-permute-start(bf16[8,72,128]{2,1,0:T(8,128)(2,1)S(1)} %get-tuple-element.51), channel_id=1, source_target_pairs={{0,4},{4,0},{8,12},{12,8},{1,5},{5,1},{9,13},{13,9},{2,6},{6,2},{1... | collective-permute-start | bytes 442376 | tf_op jit(solution)/shard_map/ppermute | solution.py:619
  27.2 0.0 copy-done.5
  27.2 0.4 shard_map.148
  27.6 0.0 collective-permute-done.2.tgt_ref
  27.6 0.0 copy-done.3
  27.7 0.0 copy-start.2
  27.7 2.3 %shard_map.147 = (s32[5,32]{1,0:T(8,128)S(1)}, bf16[12,256,128]{2,1,0:T(8,128)(2,1)S(1)}) custom-call(s32[4,4,32]{2,1,0:T(4,128)S(1)} %bitcast.52, bf16[12,64,256]{2,1,0:T(8,128)(2,1)S(1)} %bitcast.49, bf16[11,64,256]{2,1,0:T(8,128)(2,1)S(1)} %get-tuple-element.46.top_ref, bf16[1,64,256]{2,1,0:T(8,128)(2,1)S(1)} %get-tuple-element.48.last_ref), custom_call_target="tpu_custom_call" | custom-call | flops 10000000000 | bytes 1 | tf_op jit(solution)/shard_map/pallas_call | solution.py:661
  30.0 2.3 %shard_map.149 = (bf16[8,72,128]{2,1,0:T(8,128)(2,1)S(1)}, bf16[8,72,128]{2,1,0:T(8,128)(2,1)S(1)}, bf16[8,72,128]{2,1,0:T(8,128)(2,1)S(1)}, bf16[8,72,128]{2,1,0:T(8,128)(2,1)S(1)}) custom-call(s32[4,4,32]{2,1,0:T(4,128)S(1)} %bitcast.53, bf16[64,64,144]{2,1,0:T(8,128)(2,1)S(1)} %bitcast.47), custom_call_target="tpu_custom_call" | custom-call | flops 1000000000 | bytes 1 | tf_op jit(solution)/shard_map/pallas_call | solution.py:31
  32.3 0.1 collective-permute-start.6
  32.4 4.1 %collective-permute-done.9.mean_ref = bf16[11,64,256]{2,1,0:T(8,128)(2,1)S(1)} collective-permute-done((bf16[11,64,256]{2,1,0:T(8,128)(2,1)S(1)}, bf16[11,64,256]{2,1,0:T(8,128)(2,1)S(1)}, u32[]{:S(2)}, u32[]{:S(2)}) %collective-permute-start.9) | collective-permute-done | bytes 360480 | tf_op jit(solution)/shard_map/ppermute | solution.py:644
  36.5 1.2 %collective-permute-start.7 = (bf16[8,72,128]{2,1,0:T(8,128)(2,1)S(1)}, bf16[8,72,128]{2,1,0:T(8,128)(2,1)S(1)}, u32[]{:S(2)}, u32[]{:S(2)}) collective-permute-start(bf16[8,72,128]{2,1,0:T(8,128)(2,1)S(1)} %get-tuple-element.63), channel_id=1, source_target_pairs={{0,8},{4,12},{8,0},{12,4},{1,9},{5,13},{9,1},{13,5},{2,10},{6,14},... | collective-permute-start | bytes 442376 | tf_op jit(solution)/shard_map/ppermute | solution.py:619
  37.7 2.1 %shard_map.150 = (bf16[2,72,16,128]{3,2,1,0:T(8,128)(2,1)S(1)}, bf16[2,72,16,128]{3,2,1,0:T(8,128)(2,1)S(1)}) custom-call(s32[5,32]{1,0:T(8,128)S(1)} %get-tuple-element.49.table_ref.refs_0_, bf16[12,256,128]{2,1,0:T(8,128)(2,1)S(1)} %get-tuple-element.58.own, bf16[11,64,256]{2,1,0:T(8,128)(2,1)S(1)} %collective-permute-done.9.mean_ref, ...), custom_call_target="tpu_custom_call" | custom-call | flops 10000000000 | bytes 1 | tf_op jit(solution)/shard_map/pallas_call | solution.py:31
  39.8 0.0 collective-permute-done.4.refs_3_
  39.8 3.4 %collective-permute-start.8 = (bf16[8,72,128]{2,1,0:T(8,128)(2,1)S(1)}, bf16[8,72,128]{2,1,0:T(8,128)(2,1)S(1)}, u32[]{:S(2)}, u32[]{:S(2)}) collective-permute-start(bf16[8,72,128]{2,1,0:T(8,128)(2,1)S(1)} %get-tuple-element.64), channel_id=1, source_target_pairs={{0,12},{4,8},{8,4},{12,0},{1,13},{5,9},{9,5},{13,1},{2,14},{6,10},... | collective-permute-start | bytes 442376 | tf_op jit(solution)/shard_map/ppermute | solution.py:619
  43.3 0.0 collective-permute-done.5.refs_4_
  43.3 0.0 collective-permute-done.3.refs_2_
  43.3 6.8 %shard_map.151.refs_17_ = f32[2432,128]{1,0:T(8,128)S(1)} custom-call(s32[5,32]{1,0:T(8,128)S(1)} %get-tuple-element.49.table_ref.refs_0_, bf16[8,72,128]{2,1,0:T(8,128)(2,1)S(1)} %get-tuple-element.42.refs_1_, bf16[8,72,128]{2,1,0:T(8,128)(2,1)S(1)} %collective-permute-done.3.refs_2_, bf16[8,72,128]{2,1,0:T(8,128)(2,1)S(1)} %collective-permute-done.4.refs_3_, ...), custom_call_target="tpu_custom_call" | custom-call | flops 10000000000 | bytes 1 | tf_op jit(solution)/shard_map/pallas_call | solution.py:31
  50.1 0.0 collective-permute-done.6.refs_6_
  50.1 0.0 collective-permute-done.7.refs_7_
  50.1 0.0 collective-permute-done.8.refs_8_
  50.1 7.1 %shard_map.152 = (f32[1216,128]{1,0:T(8,128)S(1)}, bf16[1216,128]{1,0:T(8,128)(2,1)S(1)}) custom-call(s32[5,32]{1,0:T(8,128)S(1)} %get-tuple-element.49.table_ref.refs_0_, bf16[8,72,128]{2,1,0:T(8,128)(2,1)S(1)} %get-tuple-element.42.refs_1_, bf16[8,72,128]{2,1,0:T(8,128)(2,1)S(1)} %collective-permute-done.3.refs_2_, ...), custom_call_target="tpu_custom_call" | custom-call | flops 10000000000 | bytes 1 | tf_op jit(solution)/shard_map/pallas_call | solution.py:31
  57.2 0.1 collective-permute-start.10
  57.3 1.6 %collective-permute-done.10 = bf16[1216,128]{1,0:T(8,128)(2,1)S(1)} collective-permute-done((bf16[1216,128]{1,0:T(8,128)(2,1)S(1)}, bf16[1216,128]{1,0:T(8,128)(2,1)S(1)}, u32[]{:S(2)}, u32[]{:S(2)}) %collective-permute-start.10) | collective-permute-done | bytes 311328 | tf_op jit(solution)/shard_map/ppermute | solution.py:737
  58.9 0.1 convert_add_fusion
  59.0 1.6 %collective-permute-start.13 = (bf16[304,128]{1,0:T(8,128)(2,1)S(1)}, bf16[304,128]{1,0:T(8,128)(2,1)S(1)}, u32[]{:S(2)}, u32[]{:S(2)}) collective-permute-start(bf16[304,128]{1,0:T(8,128)(2,1)S(1)} %get-tuple-element.81), channel_id=1, source_target_pairs={{0,1},{1,0},{2,3},{3,2},{4,5},{5,4},{6,7},{7,6},{8,9},{9,8},{10,11... | collective-permute-start | bytes 233480 | tf_op jit(solution)/shard_map/ppermute | solution.py:543
  60.6 1.5 %collective-permute-start.12 = (bf16[304,128]{1,0:T(8,128)(2,1)S(1)}, bf16[304,128]{1,0:T(8,128)(2,1)S(1)}, u32[]{:S(2)}, u32[]{:S(2)}) collective-permute-start(bf16[304,128]{1,0:T(8,128)(2,1)S(1)} %get-tuple-element.82), channel_id=1, source_target_pairs={{0,2},{1,3},{2,0},{3,1},{4,6},{5,7},{6,4},{7,5},{8,10},{9,11},{10,... | collective-permute-start | bytes 233480 | tf_op jit(solution)/shard_map/ppermute | solution.py:543
  62.1 0.5 collective-permute-start.11
  62.6 0.9 %collective-permute-done.13 = bf16[304,128]{1,0:T(8,128)(2,1)S(1)} collective-permute-done((bf16[304,128]{1,0:T(8,128)(2,1)S(1)}, bf16[304,128]{1,0:T(8,128)(2,1)S(1)}, u32[]{:S(2)}, u32[]{:S(2)}) %collective-permute-start.13) | collective-permute-done | bytes 77856 | tf_op jit(solution)/shard_map/ppermute | solution.py:543
  63.5 1.5 %collective-permute-done.12 = bf16[304,128]{1,0:T(8,128)(2,1)S(1)} collective-permute-done((bf16[304,128]{1,0:T(8,128)(2,1)S(1)}, bf16[304,128]{1,0:T(8,128)(2,1)S(1)}, u32[]{:S(2)}, u32[]{:S(2)}) %collective-permute-start.12) | collective-permute-done | bytes 77856 | tf_op jit(solution)/shard_map/ppermute | solution.py:543
  65.0 2.4 %collective-permute-done.11 = bf16[304,128]{1,0:T(8,128)(2,1)S(1)} collective-permute-done((bf16[304,128]{1,0:T(8,128)(2,1)S(1)}, bf16[304,128]{1,0:T(8,128)(2,1)S(1)}, u32[]{:S(2)}, u32[]{:S(2)}) %collective-permute-start.11) | collective-permute-done | bytes 77856 | tf_op jit(solution)/shard_map/ppermute | solution.py:543
  67.4 0.5 collective-permute-start.16
  68.0 2.8 %collective-permute-start.15 = (bf16[304,128]{1,0:T(8,128)(2,1)S(1)}, bf16[304,128]{1,0:T(8,128)(2,1)S(1)}, u32[]{:S(2)}, u32[]{:S(2)}) collective-permute-start(bf16[304,128]{1,0:T(8,128)(2,1)S(1)} %fusion.3), channel_id=1, source_target_pairs={{0,8},{4,12},{8,0},{12,4},{1,9},{5,13},{9,1},{13,5},{2,10},{6,14},... | collective-permute-start | bytes 233480 | tf_op jit(solution)/shard_map/ppermute | solution.py:570
  70.7 1.1 %collective-permute-start.14 = (bf16[304,128]{1,0:T(8,128)(2,1)S(1)}, bf16[304,128]{1,0:T(8,128)(2,1)S(1)}, u32[]{:S(2)}, u32[]{:S(2)}) collective-permute-start(bf16[304,128]{1,0:T(8,128)(2,1)S(1)} %fusion.3), channel_id=1, source_target_pairs={{0,4},{4,0},{8,12},{12,8},{1,5},{5,1},{9,13},{13,9},{2,6},{6,2},{1... | collective-permute-start | bytes 233480 | tf_op jit(solution)/shard_map/ppermute | solution.py:570
  71.9 2.0 %collective-permute-done.16 = bf16[304,128]{1,0:T(8,128)(2,1)S(1)} collective-permute-done((bf16[304,128]{1,0:T(8,128)(2,1)S(1)}, bf16[304,128]{1,0:T(8,128)(2,1)S(1)}, u32[]{:S(2)}, u32[]{:S(2)}) %collective-permute-start.16) | collective-permute-done | bytes 77856 | tf_op jit(solution)/shard_map/ppermute | solution.py:570
  73.9 2.5 %collective-permute-done.15 = bf16[304,128]{1,0:T(8,128)(2,1)S(1)} collective-permute-done((bf16[304,128]{1,0:T(8,128)(2,1)S(1)}, bf16[304,128]{1,0:T(8,128)(2,1)S(1)}, u32[]{:S(2)}, u32[]{:S(2)}) %collective-permute-start.15) | collective-permute-done | bytes 77856 | tf_op jit(solution)/shard_map/ppermute | solution.py:570
  76.4 0.0 collective-permute-done.14
  76.5 0.8 collective-permute-start.17
  77.3 1.5 %collective-permute-start.18 = (bf16[304,128]{1,0:T(8,128)(2,1)S(1)}, bf16[304,128]{1,0:T(8,128)(2,1)S(1)}, u32[]{:S(2)}, u32[]{:S(2)}) collective-permute-start(bf16[304,128]{1,0:T(8,128)(2,1)S(1)} %reduce-precision_convert_fusion), channel_id=1, source_target_pairs={{0,2},{1,3},{2,0},{3,1},{4,6},{5,7},{6,4},{7,5},{8,10},{9,11},{10,... | collective-permute-start | bytes 233480 | tf_op jit(solution)/shard_map/ppermute | solution.py:553
  78.8 1.3 %collective-permute-start.19 = (bf16[304,128]{1,0:T(8,128)(2,1)S(1)}, bf16[304,128]{1,0:T(8,128)(2,1)S(1)}, u32[]{:S(2)}, u32[]{:S(2)}) collective-permute-start(bf16[304,128]{1,0:T(8,128)(2,1)S(1)} %reduce-precision_convert_fusion), channel_id=1, source_target_pairs={{0,1},{1,0},{2,3},{3,2},{4,5},{5,4},{6,7},{7,6},{8,9},{9,8},{10,11... | collective-permute-start | bytes 233480 | tf_op jit(solution)/shard_map/ppermute | solution.py:553
  80.0 1.9 %collective-permute-done.17 = bf16[304,128]{1,0:T(8,128)(2,1)S(1)} collective-permute-done((bf16[304,128]{1,0:T(8,128)(2,1)S(1)}, bf16[304,128]{1,0:T(8,128)(2,1)S(1)}, u32[]{:S(2)}, u32[]{:S(2)}) %collective-permute-start.17) | collective-permute-done | bytes 77856 | tf_op jit(solution)/shard_map/ppermute | solution.py:553
  82.0 0.6 collective-permute-done.18
  82.5 0.6 collective-permute-done.19
  83.2 0.1 select_bitcast_fusion.3
  83.3 0.1 collective-permute-start.20
  83.4 1.6 %collective-permute-done.20.other_ref = bf16[1216,128]{1,0:T(8,128)(2,1)S(1)} collective-permute-done((bf16[1216,128]{1,0:T(8,128)(2,1)S(1)}, bf16[1216,128]{1,0:T(8,128)(2,1)S(1)}, u32[]{:S(2)}, u32[]{:S(2)}) %collective-permute-start.20) | collective-permute-done | bytes 311328 | tf_op jit(solution)/shard_map/ppermute | solution.py:749
  85.0 1.1 %shard_map.153 = (f32[128,1152]{1,0:T(8,128)}, f32[128,1152]{1,0:T(8,128)}, f32[64,128]{1,0:T(8,128)}, f32[32,128]{1,0:T(8,128)}, f32[1,1]{1,0:T(1,128)}) custom-call(bf16[1216,128]{1,0:T(8,128)(2,1)S(1)} %bitcast.43, bf16[1216,128]{1,0:T(8,128)(2,1)S(1)} %collective-permute-done.20.other_ref), custom_call_target="tpu_custom_call" | custom-call | bytes 1 | tf_op jit(solution)/shard_map/pallas_call | solution.py:31
  (21 shorter events, 0.2 us)
Async XLA Ops:
  0.6 18.4 %copy-start = (bf16[1,100,12,256]{3,1,2,0:T(8,128)(2,1)S(1)}, bf16[1,100,12,256]{3,1,2,0:T(8,128)(2,1)}, u32[]{:S(2)}) copy-start(bf16[1,100,12,256]{3,1,2,0:T(8,128)(2,1)} %param.10) | copy-start | bytes 1843204
  0.6 27.0 %collective-permute-start.2 = (bf16[12,64,256]{2,1,0:T(8,128)(2,1)}, bf16[12,64,256]{2,1,0:T(8,128)(2,1)S(1)}, u32[]{:S(2)}, u32[]{:S(2)}) collective-permute-start(bf16[12,64,256]{2,1,0:T(8,128)(2,1)} %bitcast.48), channel_id=1, source_target_pairs={{4,0},{8,4},{12,8},{5,1},{9,5},{13,9},{6,2},{10,6},{14,10},{7,3},{... | collective-permute-start | bytes 1179656 | tf_op jit(solution)/shard_map/ppermute | solution.py:633
  2.9 16.1 %collective-permute-start = (bf16[1,100,256]{2,1,0:T(8,128)(2,1)S(1)}, bf16[1,100,256]{2,1,0:T(8,128)(2,1)S(1)}, u32[]{:S(2)}, u32[]{:S(2)}) collective-permute-start(bf16[1,100,256]{2,1,0:T(8,128)(2,1)S(1)} %get-tuple-element.79), channel_id=1, source_target_pairs={{0,4},{4,0},{8,12},{12,8},{1,5},{5,1},{9,13},{13,9},{2,6},{6,2},{1... | collective-permute-start | bytes 153608 | tf_op jit(solution)/shard_map/ppermute | solution.py:631
  6.7 12.4 %collective-permute-start.1 = (bf16[1,100,256]{2,1,0:T(8,128)(2,1)S(1)}, bf16[1,100,256]{2,1,0:T(8,128)(2,1)S(1)}, u32[]{:S(2)}, u32[]{:S(2)}) collective-permute-start(bf16[1,100,256]{2,1,0:T(8,128)(2,1)S(1)} %get-tuple-element.78), channel_id=1, source_target_pairs={{4,8},{8,4},{5,9},{9,5},{6,10},{10,6},{7,11},{11,7},{20,24},{24,20... | collective-permute-start | bytes 153608 | tf_op jit(solution)/shard_map/ppermute | solution.py:632
  7.3 1.6 %copy-start.1 = (bf16[1,1,64,64,144]{4,3,2,1,0:T(8,128)(2,1)S(1)}, bf16[1,1,64,64,144]{4,3,2,1,0:T(8,128)(2,1)}, u32[]{:S(2)}) copy-start(bf16[1,1,64,64,144]{4,3,2,1,0:T(8,128)(2,1)} %param.12) | copy-start | bytes 3538948
  8.9 0.7 copy-start.10
  9.6 9.4 %copy-start.6 = (bf16[128,900]{0,1:T(8,128)(2,1)S(1)}, bf16[128,900]{0,1:T(8,128)(2,1)}, u32[]{:S(2)}) copy-start(bf16[128,900]{0,1:T(8,128)(2,1)} %param.14) | copy-start | bytes 691204
  9.6 9.4 %copy-start.7 = (bf16[64,128]{1,0:T(8,128)(2,1)S(1)}, bf16[64,128]{1,0:T(8,128)(2,1)}, u32[]{:S(2)}) copy-start(bf16[64,128]{1,0:T(8,128)(2,1)} %proj_ref.1) | copy-start | bytes 49156
  11.7 15.5 %copy-start.4 = (bf16[128,1152]{1,0:T(8,128)(2,1)S(1)}, bf16[128,1152]{1,0:T(8,128)(2,1)}, u32[]{:S(2)}) copy-start(bf16[128,1152]{1,0:T(8,128)(2,1)} %one_ref) | copy-start | bytes 884740
  11.7 15.5 %copy-start.5 = (bf16[128,1152]{1,0:T(8,128)(2,1)S(1)}, bf16[128,1152]{1,0:T(8,128)(2,1)}, u32[]{:S(2)}) copy-start(bf16[128,1152]{1,0:T(8,128)(2,1)} %two_ref) | copy-start | bytes 884740
  11.7 15.5 %copy-start.8 = (bf16[64,128]{1,0:T(8,128)(2,1)S(1)}, bf16[64,128]{1,0:T(8,128)(2,1)}, u32[]{:S(2)}) copy-start(bf16[64,128]{1,0:T(8,128)(2,1)} %proj_ref.2) | copy-start | bytes 49156
  11.7 28.1 %collective-permute-start.4 = (bf16[8,72,128]{2,1,0:T(8,128)(2,1)S(1)}, bf16[8,72,128]{2,1,0:T(8,128)(2,1)S(1)}, u32[]{:S(2)}, u32[]{:S(2)}) collective-permute-start(bf16[8,72,128]{2,1,0:T(8,128)(2,1)S(1)} %get-tuple-element.52), channel_id=1, source_target_pairs={{0,8},{4,12},{8,0},{12,4},{1,9},{5,13},{9,1},{13,5},{2,10},{6,14},... | collective-permute-start | bytes 442376 | tf_op jit(solution)/shard_map/ppermute | solution.py:619
  16.1 27.2 %collective-permute-start.5 = (bf16[8,72,128]{2,1,0:T(8,128)(2,1)S(1)}, bf16[8,72,128]{2,1,0:T(8,128)(2,1)S(1)}, u32[]{:S(2)}, u32[]{:S(2)}) collective-permute-start(bf16[8,72,128]{2,1,0:T(8,128)(2,1)S(1)} %get-tuple-element.53), channel_id=1, source_target_pairs={{0,12},{4,8},{8,4},{12,0},{1,13},{5,9},{9,5},{13,1},{2,14},{6,10},... | collective-permute-start | bytes 442376 | tf_op jit(solution)/shard_map/ppermute | solution.py:619
  23.1 4.6 %copy-start.3 = (bf16[1,64,12,256]{3,1,2,0:T(8,128)(2,1)S(1)}, bf16[1,64,12,256]{3,1,2,0:T(8,128)(2,1)}, u32[]{:S(2)}) copy-start(bf16[1,64,12,256]{3,1,2,0:T(8,128)(2,1)} %param.11) | copy-start | bytes 1179652
  23.1 4.6 %copy-start.11 = (s32[1,4,32,4]{2,3,1,0:T(4,128)S(1)}, s32[1,4,32,4]{2,3,1,0:T(4,128)}, u32[]{:S(2)}) copy-start(s32[1,4,32,4]{2,3,1,0:T(4,128)} %param.13) | copy-start | bytes 6148
  23.1 13.4 %collective-permute-start.9 = (bf16[11,64,256]{2,1,0:T(8,128)(2,1)S(1)}, bf16[11,64,256]{2,1,0:T(8,128)(2,1)S(1)}, u32[]{:S(2)}, u32[]{:S(2)}) collective-permute-start(bf16[11,64,256]{2,1,0:T(8,128)(2,1)S(1)} %get-tuple-element.46.top_ref), channel_id=1, source_target_pairs={{4,0},{8,4},{12,8},{5,1},{9,5},{13,9},{6,2},{10,6},{14,10},{7,3},{... | collective-permute-start | bytes 1081352 | tf_op jit(solution)/shard_map/ppermute | solution.py:644
  24.5 18.8 %collective-permute-start.3 = (bf16[8,72,128]{2,1,0:T(8,128)(2,1)S(1)}, bf16[8,72,128]{2,1,0:T(8,128)(2,1)S(1)}, u32[]{:S(2)}, u32[]{:S(2)}) collective-permute-start(bf16[8,72,128]{2,1,0:T(8,128)(2,1)S(1)} %get-tuple-element.51), channel_id=1, source_target_pairs={{0,4},{4,0},{8,12},{12,8},{1,5},{5,1},{9,13},{13,9},{2,6},{6,2},{1... | collective-permute-start | bytes 442376 | tf_op jit(solution)/shard_map/ppermute | solution.py:619
  27.7 2.3 %copy-start.2 = (bf16[1,1,64,64,144]{4,3,2,1,0:T(8,128)(2,1)S(1)}, bf16[1,1,64,64,144]{4,3,2,1,0:T(8,128)(2,1)}, u32[]{:S(2)}) copy-start(bf16[1,1,64,64,144]{4,3,2,1,0:T(8,128)(2,1)} %param.12) | copy-start | bytes 3538948
  32.3 17.8 %collective-permute-start.6 = (bf16[8,72,128]{2,1,0:T(8,128)(2,1)S(1)}, bf16[8,72,128]{2,1,0:T(8,128)(2,1)S(1)}, u32[]{:S(2)}, u32[]{:S(2)}) collective-permute-start(bf16[8,72,128]{2,1,0:T(8,128)(2,1)S(1)} %get-tuple-element.62), channel_id=1, source_target_pairs={{0,4},{4,0},{8,12},{12,8},{1,5},{5,1},{9,13},{13,9},{2,6},{6,2},{1... | collective-permute-start | bytes 442376 | tf_op jit(solution)/shard_map/ppermute | solution.py:619
  36.5 13.6 %collective-permute-start.7 = (bf16[8,72,128]{2,1,0:T(8,128)(2,1)S(1)}, bf16[8,72,128]{2,1,0:T(8,128)(2,1)S(1)}, u32[]{:S(2)}, u32[]{:S(2)}) collective-permute-start(bf16[8,72,128]{2,1,0:T(8,128)(2,1)S(1)} %get-tuple-element.63), channel_id=1, source_target_pairs={{0,8},{4,12},{8,0},{12,4},{1,9},{5,13},{9,1},{13,5},{2,10},{6,14},... | collective-permute-start | bytes 442376 | tf_op jit(solution)/shard_map/ppermute | solution.py:619
  37.7 5.6 %copy-start.9 = (f32[32,128]{1,0:T(8,128)S(1)}, f32[32,128]{1,0:T(8,128)}, u32[]{:S(2)}) copy-start(f32[32,128]{1,0:T(8,128)} %refs_11_.1) | copy-start | bytes 49156
  39.8 10.3 %collective-permute-start.8 = (bf16[8,72,128]{2,1,0:T(8,128)(2,1)S(1)}, bf16[8,72,128]{2,1,0:T(8,128)(2,1)S(1)}, u32[]{:S(2)}, u32[]{:S(2)}) collective-permute-start(bf16[8,72,128]{2,1,0:T(8,128)(2,1)S(1)} %get-tuple-element.64), channel_id=1, source_target_pairs={{0,12},{4,8},{8,4},{12,0},{1,13},{5,9},{9,5},{13,1},{2,14},{6,10},... | collective-permute-start | bytes 442376 | tf_op jit(solution)/shard_map/ppermute | solution.py:619
  57.2 1.7 %collective-permute-start.10 = (bf16[1216,128]{1,0:T(8,128)(2,1)S(1)}, bf16[1216,128]{1,0:T(8,128)(2,1)S(1)}, u32[]{:S(2)}, u32[]{:S(2)}) collective-permute-start(bf16[1216,128]{1,0:T(8,128)(2,1)S(1)} %get-tuple-element.72), channel_id=1, source_target_pairs={{0,16},{16,0},{1,17},{17,1},{2,18},{18,2},{3,19},{19,3},{4,20},{20... | collective-permute-start | bytes 933896 | tf_op jit(solution)/shard_map/ppermute | solution.py:737
  59.0 4.5 %collective-permute-start.13 = (bf16[304,128]{1,0:T(8,128)(2,1)S(1)}, bf16[304,128]{1,0:T(8,128)(2,1)S(1)}, u32[]{:S(2)}, u32[]{:S(2)}) collective-permute-start(bf16[304,128]{1,0:T(8,128)(2,1)S(1)} %get-tuple-element.81), channel_id=1, source_target_pairs={{0,1},{1,0},{2,3},{3,2},{4,5},{5,4},{6,7},{7,6},{8,9},{9,8},{10,11... | collective-permute-start | bytes 233480 | tf_op jit(solution)/shard_map/ppermute | solution.py:543
  60.6 4.4 %collective-permute-start.12 = (bf16[304,128]{1,0:T(8,128)(2,1)S(1)}, bf16[304,128]{1,0:T(8,128)(2,1)S(1)}, u32[]{:S(2)}, u32[]{:S(2)}) collective-permute-start(bf16[304,128]{1,0:T(8,128)(2,1)S(1)} %get-tuple-element.82), channel_id=1, source_target_pairs={{0,2},{1,3},{2,0},{3,1},{4,6},{5,7},{6,4},{7,5},{8,10},{9,11},{10,... | collective-permute-start | bytes 233480 | tf_op jit(solution)/shard_map/ppermute | solution.py:543
  62.1 5.3 %collective-permute-start.11 = (bf16[304,128]{1,0:T(8,128)(2,1)S(1)}, bf16[304,128]{1,0:T(8,128)(2,1)S(1)}, u32[]{:S(2)}, u32[]{:S(2)}) collective-permute-start(bf16[304,128]{1,0:T(8,128)(2,1)S(1)} %get-tuple-element.80), channel_id=1, source_target_pairs={{0,3},{1,2},{2,1},{3,0},{4,7},{5,6},{6,5},{7,4},{8,11},{9,10},{10,... | collective-permute-start | bytes 233480 | tf_op jit(solution)/shard_map/ppermute | solution.py:543
  67.4 6.5 %collective-permute-start.16 = (bf16[304,128]{1,0:T(8,128)(2,1)S(1)}, bf16[304,128]{1,0:T(8,128)(2,1)S(1)}, u32[]{:S(2)}, u32[]{:S(2)}) collective-permute-start(bf16[304,128]{1,0:T(8,128)(2,1)S(1)} %fusion.3), channel_id=1, source_target_pairs={{0,12},{4,8},{8,4},{12,0},{1,13},{5,9},{9,5},{13,1},{2,14},{6,10},... | collective-permute-start | bytes 233480 | tf_op jit(solution)/shard_map/ppermute | solution.py:570
  68.0 8.4 %collective-permute-start.15 = (bf16[304,128]{1,0:T(8,128)(2,1)S(1)}, bf16[304,128]{1,0:T(8,128)(2,1)S(1)}, u32[]{:S(2)}, u32[]{:S(2)}) collective-permute-start(bf16[304,128]{1,0:T(8,128)(2,1)S(1)} %fusion.3), channel_id=1, source_target_pairs={{0,8},{4,12},{8,0},{12,4},{1,9},{5,13},{9,1},{13,5},{2,10},{6,14},... | collective-permute-start | bytes 233480 | tf_op jit(solution)/shard_map/ppermute | solution.py:570
  70.7 5.7 %collective-permute-start.14 = (bf16[304,128]{1,0:T(8,128)(2,1)S(1)}, bf16[304,128]{1,0:T(8,128)(2,1)S(1)}, u32[]{:S(2)}, u32[]{:S(2)}) collective-permute-start(bf16[304,128]{1,0:T(8,128)(2,1)S(1)} %fusion.3), channel_id=1, source_target_pairs={{0,4},{4,0},{8,12},{12,8},{1,5},{5,1},{9,13},{13,9},{2,6},{6,2},{1... | collective-permute-start | bytes 233480 | tf_op jit(solution)/shard_map/ppermute | solution.py:570
  76.5 5.5 %collective-permute-start.17 = (bf16[304,128]{1,0:T(8,128)(2,1)S(1)}, bf16[304,128]{1,0:T(8,128)(2,1)S(1)}, u32[]{:S(2)}, u32[]{:S(2)}) collective-permute-start(bf16[304,128]{1,0:T(8,128)(2,1)S(1)} %reduce-precision_convert_fusion), channel_id=1, source_target_pairs={{0,3},{1,2},{2,1},{3,0},{4,7},{5,6},{6,5},{7,4},{8,11},{9,10},{10,... | collective-permute-start | bytes 233480 | tf_op jit(solution)/shard_map/ppermute | solution.py:553
  77.3 5.2 %collective-permute-start.18 = (bf16[304,128]{1,0:T(8,128)(2,1)S(1)}, bf16[304,128]{1,0:T(8,128)(2,1)S(1)}, u32[]{:S(2)}, u32[]{:S(2)}) collective-permute-start(bf16[304,128]{1,0:T(8,128)(2,1)S(1)} %reduce-precision_convert_fusion), channel_id=1, source_target_pairs={{0,2},{1,3},{2,0},{3,1},{4,6},{5,7},{6,4},{7,5},{8,10},{9,11},{10,... | collective-permute-start | bytes 233480 | tf_op jit(solution)/shard_map/ppermute | solution.py:553
  78.8 4.4 %collective-permute-start.19 = (bf16[304,128]{1,0:T(8,128)(2,1)S(1)}, bf16[304,128]{1,0:T(8,128)(2,1)S(1)}, u32[]{:S(2)}, u32[]{:S(2)}) collective-permute-start(bf16[304,128]{1,0:T(8,128)(2,1)S(1)} %reduce-precision_convert_fusion), channel_id=1, source_target_pairs={{0,1},{1,0},{2,3},{3,2},{4,5},{5,4},{6,7},{7,6},{8,9},{9,8},{10,11... | collective-permute-start | bytes 233480 | tf_op jit(solution)/shard_map/ppermute | solution.py:553
  83.3 1.7 %collective-permute-start.20 = (bf16[1216,128]{1,0:T(8,128)(2,1)S(1)}, bf16[1216,128]{1,0:T(8,128)(2,1)S(1)}, u32[]{:S(2)}, u32[]{:S(2)}) collective-permute-start(bf16[1216,128]{1,0:T(8,128)(2,1)S(1)} %bitcast.42), channel_id=1, source_target_pairs={{0,16},{16,0},{1,17},{17,1},{2,18},{18,2},{3,19},{19,3},{4,20},{20... | collective-permute-start | bytes 933896 | tf_op jit(solution)/shard_map/ppermute | solution.py:749
